TPU v7x, 32 devices: a whole 2x2x4 slice. The times are simulated.
32 devices in a mesh: dp: 4 (over z), expert: 8 (over y, x, core).
Axes of the slice: x: 2, y: 2, z: 4, core: 2. Of those that a mesh axis runs over, the one named last changes fastest.
Arguments:
- tokens: bfloat16 [4096, 2048], P(('dp', 'expert')), may hold values from -6 to 6
- cotangent: bfloat16 [4096, 2048], P(('dp', 'expert')), may hold values from -6 to 6
- lengths: int32 [32, 3], P(('dp', 'expert')), may hold values from 1 to 64, 128 in all within a row
- routes: int32 [4096, 8], P(('dp', 'expert')), may hold values from 0 to 63, all different within a row; in each aligned block of 128 rows (0 to 127, 128 to 255, ...) at most 24 rows name the same one
- w_query: bfloat16 [2048, 2048], P(('dp', 'expert')), may hold values from -0.125 to 0.125
- w_key: bfloat16 [2048, 2048], P(('dp', 'expert')), may hold values from -0.125 to 0.125
- w_value: bfloat16 [2048, 2048], P(('dp', 'expert')), may hold values from -0.125 to 0.125
- w_out: bfloat16 [2048, 2048], P(('dp', 'expert')), may hold values from -0.375 to 0.375
- w_router: bfloat16 [2048, 64], P(('dp', 'expert')), may hold values from -0.0625 to 0.0625
- gain_attn: bfloat16 [2048], P(('dp', 'expert')), may hold values from 0.5 to 1.5
- gain_query: bfloat16 [2048], P(('dp', 'expert')), may hold values from 0.5 to 1.5
- gain_key: bfloat16 [2048], P(('dp', 'expert')), may hold values from 0.5 to 1.5
- gain_mlp: bfloat16 [2048], P(('dp', 'expert')), may hold values from 0.5 to 1.5
- w_gate: bfloat16 [64, 2048, 1024], P('expert', 'dp'), may hold values from -0.125 to 0.125
- w_up: bfloat16 [64, 2048, 1024], P('expert', 'dp'), may hold values from -0.125 to 0.125
- w_down: bfloat16 [64, 1024, 2048], P('expert', 'dp'), may hold values from -2.5 to 2.5
Outputs:
- output: bfloat16 [4096, 2048], P(('dp', 'expert'))
- grad_tokens: float32 [4096, 2048], P(('dp', 'expert'))
- grad_query: float32 [2048, 2048], P(('dp', 'expert'))
- grad_key: float32 [2048, 2048], P(('dp', 'expert'))
- grad_value: float32 [2048, 2048], P(('dp', 'expert'))
- grad_out: float32 [2048, 2048], P(('dp', 'expert'))
- grad_router: float32 [2048, 64], P(('dp', 'expert'))
- grad_gain_attn: float32 [2048], P(('dp', 'expert'))
- grad_gain_query: float32 [2048], P(('dp', 'expert'))
- grad_gain_key: float32 [2048], P(('dp', 'expert'))
- grad_gain_mlp: float32 [2048], P(('dp', 'expert'))
- grad_gate: float32 [64, 2048, 1024], P('expert', 'dp')
- grad_up: float32 [64, 2048, 1024], P('expert', 'dp')
- grad_down: float32 [64, 1024, 2048], P('expert', 'dp')
Inputs may be any that keep to these rules, and one draw needn't show every extreme that they name: The lengths of one device sum to 128; the longest of each device is exactly 64. `routes`: a token names 8 different experts; among the tokens of one device no expert is named more than 24 times, a bound that some block reaches.
All inputs are finite; a program needn't handle non-finite values.
Results may differ from a plain program's by a relative error of at most 0.015.
Values may be sent and summed in bfloat16 or wider, within the bound.
A program may use at most 640 MiB of HBM per device.

v0:
```python
import jax
import jax.numpy as jnp
from jax import lax
from jax.sharding import PartitionSpec as P

D = 2048
HEADS = 16
HD = 128
TOPK = 8
CAP = 24


eps = 1e-05


def product(left, right, form):
    return jnp.einsum(form, left, right, preferred_element_type=jnp.float32)


def rms_forward(values, gain):
    inverse = lax.rsqrt(jnp.mean(values * values, axis=-1, keepdims=True) + eps)
    return (values * inverse * gain, inverse)


def rms_backward(values, inverse, gain, grad):
    scaled = grad * gain
    inner = jnp.mean(scaled * values, axis=-1, keepdims=True)
    grad_values = inverse * scaled - values * (inverse * inverse * inverse) * inner
    grad_gain = jnp.sum(grad * values * inverse, axis=0)
    return (grad_values, grad_gain)


def layout(lengths_row, count):
    places = jnp.arange(count, dtype=jnp.int32)
    ends = jnp.cumsum(lengths_row, dtype=jnp.int32)
    passed = (places[:, None] >= ends[None, :]).astype(jnp.int32)
    segment = jnp.sum(passed, axis=1, dtype=jnp.int32)
    start = jnp.sum(passed * lengths_row[None, :], axis=1, dtype=jnp.int32)
    return (segment, places - start, places)


def rotate(values, cosine, sine):
    count = values.shape[0]
    heads = values.reshape(count, HEADS, HD)
    half = HD // 2
    first = heads[..., :half]
    second = heads[..., half:]
    turned = jnp.concatenate(
        [first * cosine - second * sine, second * cosine + first * sine], axis=-1
    )
    return turned.reshape(count, D)


def shards(
    tokens,
    cotangent,
    lengths,
    routes,
    w_query,
    w_key,
    w_value,
    w_out,
    w_router,
    gain_attn,
    gain_query,
    gain_key,
    gain_mlp,
    w_gate,
    w_up,
    w_down,
):
    (
        query_weight,
        key_weight,
        value_weight,
        out_weight,
        router_weight,
        attn_low,
        query_gain_low,
        key_gain_low,
        mlp_low_gain,
    ) = (
        lax.all_gather(w_query, ("dp", "expert"), axis=0, tiled=True),
        lax.all_gather(w_key, ("dp", "expert"), axis=0, tiled=True),
        lax.all_gather(w_value, ("dp", "expert"), axis=0, tiled=True),
        lax.all_gather(w_out, ("dp", "expert"), axis=0, tiled=True),
        lax.all_gather(w_router, ("dp", "expert"), axis=0, tiled=True),
        lax.all_gather(gain_attn, ("dp", "expert"), axis=0, tiled=True),
        lax.all_gather(gain_query, ("dp", "expert"), axis=0, tiled=True),
        lax.all_gather(gain_key, ("dp", "expert"), axis=0, tiled=True),
        lax.all_gather(gain_mlp, ("dp", "expert"), axis=0, tiled=True),
    )
    attn_gain = attn_low.astype(jnp.float32)
    query_gain = query_gain_low.astype(jnp.float32)
    key_gain = key_gain_low.astype(jnp.float32)
    mlp_gain = mlp_low_gain.astype(jnp.float32)
    inputs = tokens.astype(jnp.float32)
    count = inputs.shape[0]
    segment, position, places = layout(lengths[0], count)
    half = HD // 2
    freq = 10000.0 ** (-2.0 * jnp.arange(half, dtype=jnp.float32) / HD)
    angle = position.astype(jnp.float32)[:, None] * freq[None, :]
    cosine = jnp.cos(angle)[:, None, :]
    sine = jnp.sin(angle)[:, None, :]
    scale = HD ** (-0.5)
    normed, attn_inverse = rms_forward(inputs, attn_gain)
    normed_low = normed.astype(jnp.bfloat16)
    query_raw = product(normed_low, query_weight, "td,de->te")
    key_raw = product(normed_low, key_weight, "td,de->te")
    value_low = product(normed_low, value_weight, "td,de->te").astype(jnp.bfloat16)
    query_normed, query_inverse = rms_forward(query_raw, query_gain)
    key_normed, key_inverse = rms_forward(key_raw, key_gain)
    query_low = rotate(query_normed, cosine, sine).astype(jnp.bfloat16).reshape(count, HEADS, HD)
    key_low = rotate(key_normed, cosine, sine).astype(jnp.bfloat16).reshape(count, HEADS, HD)
    value_heads = value_low.reshape(count, HEADS, HD)
    allowed = (segment[:, None] == segment[None, :]) & (places[None, :] <= places[:, None])
    scores = product(query_low, key_low, "qhd,khd->hqk") * scale
    scores = jnp.where(allowed[None], scores, -1e30)
    probs = jax.nn.softmax(scores, axis=-1)
    probs_low = probs.astype(jnp.bfloat16)
    attended_low = (
        product(probs_low, value_heads, "hqk,khd->qhd").reshape(count, D).astype(jnp.bfloat16)
    )
    middle = inputs + product(attended_low, out_weight, "td,de->te")
    mlp_normed, mlp_inverse = rms_forward(middle, mlp_gain)
    mlp_low = mlp_normed.astype(jnp.bfloat16)
    router = jax.nn.softmax(product(mlp_low, router_weight, "td,de->te"), axis=-1)
    experts_all = router.shape[1]
    columns = jnp.arange(experts_all, dtype=jnp.int32)
    chosen = (routes[:, :, None] == columns[None, None, :]).astype(jnp.float32)
    gates = jnp.sum(router[:, None, :] * chosen, axis=2)
    flat = routes.reshape(-1)
    entries = flat.shape[0]
    capacity = CAP
    onehot = (flat[:, None] == columns[None, :]).astype(jnp.int32)
    slot = jnp.sum(
        (jnp.cumsum(onehot, axis=0, dtype=jnp.int32) - onehot) * onehot, axis=1, dtype=jnp.int32
    )
    target = flat * capacity + slot
    table = (
        jnp.full((experts_all * capacity,), -1, jnp.int32)
        .at[target]
        .set(jnp.arange(entries, dtype=jnp.int32))
    )
    filled = table >= 0
    source = jnp.where(filled, table, 0)
    nothing = jnp.zeros((), jnp.bfloat16)
    send = jnp.where(filled[:, None], mlp_low[source // TOPK], nothing).reshape(
        experts_all, capacity, D
    )
    received = lax.all_to_all(send, "expert", split_axis=0, concat_axis=1, tiled=True)
    gate_full, up_full, down_full = (
        lax.all_gather(w_gate, "dp", axis=1, tiled=True),
        lax.all_gather(w_up, "dp", axis=1, tiled=True),
        lax.all_gather(w_down, "dp", axis=1, tiled=True),
    )
    gate_mid = product(received, gate_full, "erd,edf->erf")
    up_mid = product(received, up_full, "erd,edf->erf")
    sigmoid = jax.nn.sigmoid(gate_mid)
    hidden_low = (gate_mid * sigmoid * up_mid).astype(jnp.bfloat16)
    result_low = product(hidden_low, down_full, "erf,efd->erd").astype(jnp.bfloat16)
    returned = lax.all_to_all(
        result_low, "expert", split_axis=1, concat_axis=0, tiled=True
    ).reshape(experts_all * capacity, D)
    picked = returned[target].reshape(count, TOPK, D)
    output = (middle + product(gates, picked, "tk,tkd->td")).astype(jnp.bfloat16)
    grad_final = cotangent.astype(jnp.float32)
    grad_gates = product(grad_final, picked, "td,tkd->tk")
    grad_picked = (
        (gates[:, :, None] * grad_final[:, None, :]).astype(jnp.bfloat16).reshape(entries, D)
    )
    grad_send = jnp.where(filled[:, None], grad_picked[source], nothing).reshape(
        experts_all, capacity, D
    )
    grad_received = lax.all_to_all(grad_send, "expert", split_axis=0, concat_axis=1, tiled=True)
    grad_hidden = product(grad_received, down_full, "erd,efd->erf")
    grad_gate_low = (grad_hidden * up_mid * sigmoid * (1.0 + gate_mid * (1.0 - sigmoid))).astype(
        jnp.bfloat16
    )
    grad_up_low = (grad_hidden * gate_mid * sigmoid).astype(jnp.bfloat16)
    grad_rows = (
        product(grad_gate_low, gate_full, "erf,edf->erd")
        + product(grad_up_low, up_full, "erf,edf->erd")
    ).astype(jnp.bfloat16)
    grad_down_full = product(hidden_low, grad_received, "erf,erd->efd")
    back_rows = lax.all_to_all(
        grad_rows, "expert", split_axis=1, concat_axis=0, tiled=True
    ).reshape(experts_all * capacity, D)
    grad_mlp = jnp.sum(back_rows[target].reshape(count, TOPK, D).astype(jnp.float32), axis=1)
    grad_gate_full = product(received, grad_gate_low, "erd,erf->edf")
    grad_up_full = product(received, grad_up_low, "erd,erf->edf")
    grad_gate_part, grad_up_part, grad_down_part = (
        lax.psum_scatter(
            grad_gate_full.astype(jnp.bfloat16), "dp", scatter_dimension=1, tiled=True
        ).astype(jnp.float32),
        lax.psum_scatter(
            grad_up_full.astype(jnp.bfloat16), "dp", scatter_dimension=1, tiled=True
        ).astype(jnp.float32),
        lax.psum_scatter(
            grad_down_full.astype(jnp.bfloat16), "dp", scatter_dimension=1, tiled=True
        ).astype(jnp.float32),
    )
    grad_router_probs = jnp.sum(grad_gates[:, :, None] * chosen, axis=1)
    grad_logits = router * (
        grad_router_probs - jnp.sum(router * grad_router_probs, axis=1, keepdims=True)
    )
    grad_logits_low = grad_logits.astype(jnp.bfloat16)
    grad_router_full = product(mlp_low, grad_logits_low, "td,te->de")
    grad_mlp = grad_mlp + product(grad_logits_low, router_weight, "te,de->td")
    grad_middle_part, grad_mlp_gain = rms_backward(middle, mlp_inverse, mlp_gain, grad_mlp)
    grad_middle = grad_final + grad_middle_part
    grad_branch_low = grad_middle.astype(jnp.bfloat16)
    grad_out_full = product(attended_low, grad_branch_low, "td,te->de")
    grad_attended = (
        product(grad_branch_low, out_weight, "te,de->td")
        .astype(jnp.bfloat16)
        .reshape(count, HEADS, HD)
    )
    grad_weights = product(grad_attended, value_heads, "qhd,khd->hqk")
    grad_scores = probs * (grad_weights - jnp.sum(probs * grad_weights, axis=-1, keepdims=True))
    grad_scores_low = grad_scores.astype(jnp.bfloat16)
    grad_query_turn = product(grad_scores_low, key_low, "hqk,khd->qhd").reshape(count, D) * scale
    grad_key_turn = product(grad_scores_low, query_low, "hqk,qhd->khd").reshape(count, D) * scale
    grad_value_low = (
        product(probs_low, grad_attended, "hqk,qhd->khd").reshape(count, D).astype(jnp.bfloat16)
    )
    grad_query_raw, grad_query_gain = rms_backward(
        query_raw, query_inverse, query_gain, rotate(grad_query_turn, cosine, -sine)
    )
    grad_key_raw, grad_key_gain = rms_backward(
        key_raw, key_inverse, key_gain, rotate(grad_key_turn, cosine, -sine)
    )
    grad_query_low = grad_query_raw.astype(jnp.bfloat16)
    grad_key_low = grad_key_raw.astype(jnp.bfloat16)
    grad_query_full = product(normed_low, grad_query_low, "td,te->de")
    grad_key_full = product(normed_low, grad_key_low, "td,te->de")
    grad_value_full = product(normed_low, grad_value_low, "td,te->de")
    grad_normed = (
        product(grad_query_low, query_weight, "te,de->td")
        + product(grad_key_low, key_weight, "te,de->td")
        + product(grad_value_low, value_weight, "te,de->td")
    )
    grad_inputs_part, grad_attn_gain = rms_backward(inputs, attn_inverse, attn_gain, grad_normed)
    grad_inputs = grad_middle + grad_inputs_part
    (
        grad_query_part,
        grad_key_part,
        grad_value_part,
        grad_out_part,
        grad_router_part,
        grad_attn_part,
        grad_query_gain_part,
        grad_key_gain_part,
        grad_mlp_gain_part,
    ) = (
        lax.psum_scatter(grad_query_full, ("dp", "expert"), scatter_dimension=0, tiled=True),
        lax.psum_scatter(grad_key_full, ("dp", "expert"), scatter_dimension=0, tiled=True),
        lax.psum_scatter(grad_value_full, ("dp", "expert"), scatter_dimension=0, tiled=True),
        lax.psum_scatter(grad_out_full, ("dp", "expert"), scatter_dimension=0, tiled=True),
        lax.psum_scatter(grad_router_full, ("dp", "expert"), scatter_dimension=0, tiled=True),
        lax.psum_scatter(grad_attn_gain, ("dp", "expert"), scatter_dimension=0, tiled=True),
        lax.psum_scatter(grad_query_gain, ("dp", "expert"), scatter_dimension=0, tiled=True),
        lax.psum_scatter(grad_key_gain, ("dp", "expert"), scatter_dimension=0, tiled=True),
        lax.psum_scatter(grad_mlp_gain, ("dp", "expert"), scatter_dimension=0, tiled=True),
    )
    return (
        output,
        grad_inputs,
        grad_query_part,
        grad_key_part,
        grad_value_part,
        grad_out_part,
        grad_router_part,
        grad_attn_part,
        grad_query_gain_part,
        grad_key_gain_part,
        grad_mlp_gain_part,
        grad_gate_part,
        grad_up_part,
        grad_down_part,
    )


def solution(mesh):
    return jax.shard_map(
        shards,
        mesh=mesh,
        in_specs=(
            P(("dp", "expert"), None),
            P(("dp", "expert"), None),
            P(("dp", "expert"), None),
            P(("dp", "expert"), None),
            P(("dp", "expert"), None),
            P(("dp", "expert"), None),
            P(("dp", "expert"), None),
            P(("dp", "expert"), None),
            P(("dp", "expert"), None),
            P(("dp", "expert")),
            P(("dp", "expert")),
            P(("dp", "expert")),
            P(("dp", "expert")),
            P("expert", "dp", None),
            P("expert", "dp", None),
            P("expert", "dp", None),
        ),
        out_specs=(
            P(("dp", "expert"), None),
            P(("dp", "expert"), None),
            P(("dp", "expert"), None),
            P(("dp", "expert"), None),
            P(("dp", "expert"), None),
            P(("dp", "expert"), None),
            P(("dp", "expert"), None),
            P(("dp", "expert")),
            P(("dp", "expert")),
            P(("dp", "expert")),
            P(("dp", "expert")),
            P("expert", "dp", None),
            P("expert", "dp", None),
            P("expert", "dp", None),
        ),
        check_vma=False,
    )
```

profile of v0, /device:TPU:0, one launch (start us, length us, event | category | flops | bytes accessed | tf_op | source)
XLA Modules:
  0.0 4838.2 jit_solution(8131444242675643257)
XLA Ops:
  13.3 42.5 all-reduce.9
  56.1 18.0 reduce-window.19
  74.9 4.6 scatter_custom_fusion
  81.6 9.6 all-gather.12.cloned.1.call-done
  91.2 4.8 multiply_reduce_fusion.6
  97.4 72.8 %all-gather.10.cloned.1.call-done = bf16[2048,2048]{1,0:T(8,128)(2,1)} async-done(((bf16[64,2048]{1,0:T(8,128)(2,1)}), bf16[2048,2048]{1,0:T(8,128)(2,1)}) %all-gather.10.cloned.1.call-update) | async-done | bytes 8388624 | tf_op jit(solution)/shard_map/all_gather | solution.py:83
  170.3 4.8 multiply_reduce_fusion.7
  180.3 68.9 %all-gather.8.cloned.1.call-done = bf16[2048,2048]{1,0:T(8,128)(2,1)} async-done(((bf16[64,2048]{1,0:T(8,128)(2,1)}), bf16[2048,2048]{1,0:T(8,128)(2,1)}) %all-gather.8.cloned.1.call-update) | async-done | bytes 8388624 | tf_op jit(solution)/shard_map/all_gather | solution.py:85
  249.2 5.5 fusion.11
  256.9 71.1 %all-gather.14.cloned.1.call-done = bf16[2048,2048]{1,0:T(8,128)(2,1)} async-done(((bf16[64,2048]{1,0:T(8,128)(2,1)}), bf16[2048,2048]{1,0:T(8,128)(2,1)}) %all-gather.14.cloned.1.call-update) | async-done | bytes 8388624 | tf_op jit(solution)/shard_map/all_gather | solution.py:86
  328.0 4.7 multiply_reduce_fusion.5
  333.9 7.5 gather_fusion
  341.4 4.4 broadcast_select_fusion.1
  345.8 74.2 %all_to_all.66 = bf16[64,24,2048]{2,1,0:T(8,128)(2,1)S(1)} all-to-all(bf16[64,24,2048]{2,1,0:T(8,128)(2,1)S(1)} %broadcast_select_fusion.1), channel_id=1, replica_groups=mesh['dp'=4,'expert'=8] {'expert'}, dimensions={0} | all-to-all | bytes 12582912 | tf_op jit(solution)/shard_map/all_to_all | solution.py:151
  420.0 3.3 copy.123
  423.3 466.1 %all-gather.16.cloned.1.call-done = bf16[8,2048,1024]{2,1,0:T(8,128)(2,1)} async-done(((bf16[8,512,1024]{2,1,0:T(8,128)(2,1)}), bf16[8,2048,1024]{2,1,0:T(8,128)(2,1)}) %all-gather.16.cloned.1.call-update) | async-done | bytes 33554448 | tf_op jit(solution)/shard_map/all_gather | solution.py:153
  889.4 23.4 fusion.72
  912.9 537.6 %all-gather.18.cloned.1.call-done = bf16[8,2048,1024]{2,1,0:T(8,128)(2,1)} async-done(((bf16[8,512,1024]{2,1,0:T(8,128)(2,1)}), bf16[8,2048,1024]{2,1,0:T(8,128)(2,1)}) %all-gather.18.cloned.1.call-update) | async-done | bytes 33554448 | tf_op jit(solution)/shard_map/all_gather | solution.py:154
  1450.5 27.1 multiply_convert_fusion.2
  1477.6 534.1 %all-gather.20.cloned.1.call-done = bf16[8,1024,2048]{2,1,0:T(8,128)(2,1)} async-done(((bf16[8,256,2048]{2,1,0:T(8,128)(2,1)}), bf16[8,1024,2048]{2,1,0:T(8,128)(2,1)}) %all-gather.20.cloned.1.call-update) | async-done | bytes 33554448 | tf_op jit(solution)/shard_map/all_gather | solution.py:155
  2011.7 17.6 convolution_convert_fusion.3
  2029.3 8.9 copy.124
  2038.2 4.9 all-to-all-start.1
  2043.2 102.5 %all_gather.44 = bf16[2048,64]{1,0:T(8,128)(2,1)S(1)} all-gather(bf16[64,64]{1,0:T(8,128)(2,1)S(1)} %copy-done.50), channel_id=1, replica_groups=mesh['dp'=4,'expert'=8] {'dp','expert'}, dimensions={0}, use_global_device_ids=true | all-gather | bytes 270336 | tf_op jit(solution)/shard_map/all_gather | solution.py:87
  2147.2 9.5 copy.125
  2156.7 12.7 gather_fusion.1
  2169.4 4.9 fusion.2
  2177.6 15.4 gather_fusion.2
  2193.0 3.3 broadcast_select_fusion
  2196.3 74.1 %all_to_all.67 = bf16[64,24,2048]{2,1,0:T(8,128)(2,1)S(1)} all-to-all(bf16[64,24,2048]{2,1,0:T(8,128)(2,1)S(1)} %broadcast_select_fusion), channel_id=1, replica_groups=mesh['dp'=4,'expert'=8] {'expert'}, dimensions={0} | all-to-all | bytes 12582912 | tf_op jit(solution)/shard_map/all_to_all | solution.py:175
  2273.6 16.0 convolution_convert_fusion
  2289.7 22.9 multiply_convert_fusion
  2312.7 16.9 convolution_convert_fusion.2
  2329.7 17.5 convolution_convert_fusion.1
  2347.2 21.0 fusion.73
  2368.2 21.2 add_convert_fusion
  2389.4 8.9 copy.128
  2398.4 4.9 all-to-all-start.3
  2405.3 4.5 fusion.4
  2409.7 65.2 %all-to-all-done.3 = bf16[8,192,2048]{2,0,1:T(8,128)(2,1)} async-done(((bf16[8,192,2048]{2,0,1:T(8,128)(2,1)}), bf16[8,192,2048]{2,0,1:T(8,128)(2,1)}, u32[]{:S(2)}, u32[]{:S(2)}) %all-to-all-start.3) | async-done | bytes 6291488 | tf_op jit(solution)/shard_map/all_to_all | solution.py:186
  2474.9 9.6 copy.129
  2484.5 12.6 gather_fusion.3
  2497.1 5.5 convert_reduce_fusion
  2504.8 8.1 fusion.35
  2513.2 7.3 convolution_convert_fusion.4
  2522.6 3.1 convolution_convert_fusion.6
  2525.7 9.2 fusion.57
  2543.4 8.3 fusion.59
  2557.0 8.3 fusion.61
  2565.4 6.8 fusion.74
  2572.2 6.4 convolution_add_fusion.2
  2578.7 3.1 fusion.20
  2581.7 41.8 all-reduce.8
  2627.3 211.9 %reduce-scatter.23.cloned.1.call-done = bf16[8,256,2048]{2,1,0:T(8,128)(2,1)} async-done(((bf16[8,1024,2048]{2,1,0:T(8,128)(2,1)}), bf16[8,256,2048]{2,1,0:T(8,128)(2,1)}) %reduce-scatter.23.cloned.1.call-update) | async-done | bytes 8388624 | tf_op jit(solution)/shard_map/reduce_scatter | solution.py:199
  2839.2 11.8 convert_element_type.174
  2851.0 543.5 %reduce-scatter.19.cloned.1.call-done = bf16[8,512,1024]{2,1,0:T(8,128)(2,1)} async-done(((bf16[8,2048,1024]{2,1,0:T(8,128)(2,1)}), bf16[8,512,1024]{2,1,0:T(8,128)(2,1)}) %reduce-scatter.19.cloned.1.call-update) | async-done | bytes 8388624 | tf_op jit(solution)/shard_map/reduce_scatter | solution.py:193
  3394.5 11.9 convert_element_type.170
  3406.4 543.1 %reduce-scatter.21.cloned.1.call-done = bf16[8,512,1024]{2,1,0:T(8,128)(2,1)} async-done(((bf16[8,2048,1024]{2,1,0:T(8,128)(2,1)}), bf16[8,512,1024]{2,1,0:T(8,128)(2,1)}) %reduce-scatter.21.cloned.1.call-update) | async-done | bytes 8388624 | tf_op jit(solution)/shard_map/reduce_scatter | solution.py:196
  3949.5 11.7 convert_element_type.172
  3961.2 126.7 %reduce-scatter.17.cloned.1.call-done = f32[64,64]{1,0:T(8,128)} async-done(((f32[2048,64]{1,0:T(8,128)}), f32[64,64]{1,0:T(8,128)}) %reduce-scatter.17.cloned.1.call-update) | async-done | bytes 16400 | tf_op jit(solution)/shard_map/reduce_scatter | solution.py:260
  4087.9 181.5 %reduce-scatter.15.cloned.1.call-done = f32[64,2048]{1,0:T(8,128)} async-done(((f32[2048,2048]{1,0:T(8,128)}), f32[64,2048]{1,0:T(8,128)}) %reduce-scatter.15.cloned.1.call-update) | async-done | bytes 524304 | tf_op jit(solution)/shard_map/reduce_scatter | solution.py:259
  4269.4 187.5 %reduce-scatter.13.cloned.1.call-done = f32[64,2048]{1,0:T(8,128)} async-done(((f32[2048,2048]{1,0:T(8,128)}), f32[64,2048]{1,0:T(8,128)}) %reduce-scatter.13.cloned.1.call-update) | async-done | bytes 524304 | tf_op jit(solution)/shard_map/reduce_scatter | solution.py:258
  4456.9 187.2 %reduce-scatter.11.cloned.1.call-done = f32[64,2048]{1,0:T(8,128)} async-done(((f32[2048,2048]{1,0:T(8,128)}), f32[64,2048]{1,0:T(8,128)}) %reduce-scatter.11.cloned.1.call-update) | async-done | bytes 524304 | tf_op jit(solution)/shard_map/reduce_scatter | solution.py:257
  4644.2 187.3 %reduce-scatter.9.cloned.1.call-done = f32[64,2048]{1,0:T(8,128)} async-done(((f32[2048,2048]{1,0:T(8,128)}), f32[64,2048]{1,0:T(8,128)}) %reduce-scatter.9.cloned.1.call-update) | async-done | bytes 524304 | tf_op jit(solution)/shard_map/reduce_scatter | solution.py:256
  (270 shorter events, 50.9 us)
Async XLA Ops:
  7.2 84.0 %all-gather.12.cloned.1.call-start = ((), (), s32[]{:S(2)}) async-start(), calls=%async_computation.14 | async-start | bytes 8650752 | tf_op jit(solution)/shard_map/all_gather | solution.py:84
  7.9 162.3 %all-gather.10.cloned.1.call-start = ((), (), s32[]{:S(2)}) async-start(), calls=%async_computation.13 | async-start | bytes 8650752 | tf_op jit(solution)/shard_map/all_gather | solution.py:83
  8.7 240.5 %all-gather.8.cloned.1.call-start = ((), (), s32[]{:S(2)}) async-start(), calls=%async_computation.12 | async-start | bytes 8650752 | tf_op jit(solution)/shard_map/all_gather | solution.py:85
  9.4 318.6 %all-gather.14.cloned.1.call-start = ((), (), s32[]{:S(2)}) async-start(), calls=%async_computation.15 | async-start | bytes 8650752 | tf_op jit(solution)/shard_map/all_gather | solution.py:86
  10.0 879.5 %all-gather.16.cloned.1.call-start = ((), (), s32[]{:S(2)}) async-start(), calls=%async_computation.16 | async-start | bytes 41943040 | tf_op jit(solution)/shard_map/all_gather | solution.py:153
  10.6 1439.9 %all-gather.18.cloned.1.call-start = ((), (), s32[]{:S(2)}) async-start(), calls=%async_computation.17 | async-start | bytes 41943040 | tf_op jit(solution)/shard_map/all_gather | solution.py:154
  11.2 44.7 copy-start.68
  11.2 68.6 %copy-start.2 = (bf16[128,2048]{1,0:T(8,128)(2,1)S(1)}, bf16[128,2048]{1,0:T(8,128)(2,1)}, u32[]{:S(2)}) copy-start(bf16[128,2048]{1,0:T(8,128)(2,1)} %param.16) | copy-start | bytes 1572868
  11.2 2000.5 %all-gather.20.cloned.1.call-start = ((), (), s32[]{:S(2)}) async-start(), calls=%async_computation.18 | async-start | bytes 41943040 | tf_op jit(solution)/shard_map/all_gather | solution.py:155
  55.8 193.4 %copy-start.18 = (f32[2048]{0:T(1024)}, f32[2048]{0:T(1024)S(1)}, u32[]{:S(2)}) copy-start(f32[2048]{0:T(1024)S(1)} %convert_element_type.135) | copy-start | bytes 24580
  55.8 40.7 copy-start.39
  55.8 119.8 %copy-start.37 = (f32[2048]{0:T(1024)}, f32[2048]{0:T(1024)S(1)}, u32[]{:S(2)}) copy-start(f32[2048]{0:T(1024)S(1)} %convert_element_type.139) | copy-start | bytes 24580
  55.9 277.5 %copy-start.41 = (f32[2048]{0:T(1024)}, f32[2048]{0:T(1024)S(1)}, u32[]{:S(2)}) copy-start(f32[2048]{0:T(1024)S(1)} %convert_element_type.146) | copy-start | bytes 24580
  80.6 168.6 %copy-start.43 = (f32[128]{0:T(128)}, f32[128]{0:T(128)S(1)}, u32[]{:S(2)}) copy-start(f32[128]{0:T(128)S(1)} %get-tuple-element.60) | copy-start | bytes 1540
  80.7 174.0 %copy-start.51 = (pred[128,128]{0,1:T(8,128)(4,1)}, pred[128,128]{0,1:T(8,128)(4,1)S(1)}, u32[]{:S(2)}) copy-start(pred[128,128]{0,1:T(8,128)(4,1)S(1)} %fusion.41) | copy-start | bytes 49156
  81.6 95.5 %copy-start.33 = (f32[128,64]{1,0:T(8,128)}, f32[128,64]{1,0:T(8,128)S(1)}, u32[]{:S(2)}) copy-start(f32[128,64]{1,0:T(8,128)S(1)} %get-tuple-element.58) | copy-start | bytes 98308
  178.5 76.2 %copy-start.22 = (bf16[128,16,64]{2,0,1:T(8,128)(2,1)}, bf16[128,16,64]{2,0,1:T(8,128)(2,1)S(1)}, u32[]{:S(2)}) copy-start(bf16[128,16,64]{2,0,1:T(8,128)(2,1)S(1)} %get-tuple-element.36) | copy-start | bytes 786436
  178.5 76.2 %copy-start.24 = (bf16[128,16,64]{2,0,1:T(8,128)(2,1)}, bf16[128,16,64]{2,0,1:T(8,128)(2,1)S(1)}, u32[]{:S(2)}) copy-start(bf16[128,16,64]{2,0,1:T(8,128)(2,1)S(1)} %get-tuple-element.37) | copy-start | bytes 786436
  178.5 76.2 %copy-start.26 = (bf16[128,16,64]{2,0,1:T(8,128)(2,1)}, bf16[128,16,64]{2,0,1:T(8,128)(2,1)S(1)}, u32[]{:S(2)}) copy-start(bf16[128,16,64]{2,0,1:T(8,128)(2,1)S(1)} %get-tuple-element.52) | copy-start | bytes 786436
  178.5 76.2 %copy-start.28 = (bf16[128,16,64]{2,0,1:T(8,128)(2,1)}, bf16[128,16,64]{2,0,1:T(8,128)(2,1)S(1)}, u32[]{:S(2)}) copy-start(bf16[128,16,64]{2,0,1:T(8,128)(2,1)S(1)} %get-tuple-element.53) | copy-start | bytes 786436
  180.3 74.4 %copy-start.54 = (f32[16,128]{1,0:T(8,128)}, f32[16,128]{1,0:T(8,128)S(1)}, u32[]{:S(2)}) copy-start(f32[16,128]{1,0:T(8,128)S(1)} %get-tuple-element.71) | copy-start | bytes 24580
  256.9 75.9 %copy-start.15 = (bf16[16,128,128]{2,1,0:T(8,128)(2,1)}, bf16[16,128,128]{2,1,0:T(8,128)(2,1)S(1)}, u32[]{:S(2)}) copy-start(bf16[16,128,128]{2,1,0:T(8,128)(2,1)S(1)} %convolution_convert_fusion.7) | copy-start | bytes 1572868
  333.3 8.1 copy-start.62
  333.9 1811.9 %copy-start = (bf16[128,2048]{1,0:T(8,128)(2,1)}, bf16[128,2048]{1,0:T(8,128)(2,1)S(1)}, u32[]{:S(2)}) copy-start(bf16[128,2048]{1,0:T(8,128)(2,1)S(1)} %multiply_convert_fusion.4) | copy-start | bytes 1572868
  2038.2 109.0 %all-to-all-start.1 = ((bf16[8,192,2048]{2,0,1:T(8,128)(2,1)}), bf16[8,192,2048]{2,0,1:T(8,128)(2,1)}, u32[]{:S(2)}, u32[]{:S(2)}) async-start(bf16[8,192,2048]{2,0,1:T(8,128)(2,1)} %copy.124), calls=%async_computation.1 | async-start | bytes 12582912 | tf_op jit(solution)/shard_map/all_to_all | solution.py:162
  2043.1 796.1 %reduce-scatter.23.cloned.1.call-start = ((), (), s32[]{:S(2)}) async-start(), calls=%async_computation.26 | async-start | bytes 41943040 | tf_op jit(solution)/shard_map/reduce_scatter | solution.py:199
  2145.7 10.9 copy-start.45
  2146.5 10.1 copy-start.52
  2147.1 9.5 copy-start.56
  2175.0 18.0 copy-start.47
  2289.7 1104.8 %reduce-scatter.19.cloned.1.call-start = ((), (), s32[]{:S(2)}) async-start(), calls=%async_computation.24 | async-start | bytes 41943040 | tf_op jit(solution)/shard_map/reduce_scatter | solution.py:193
  2329.6 1619.9 %reduce-scatter.21.cloned.1.call-start = ((), (), s32[]{:S(2)}) async-start(), calls=%async_computation.25 | async-start | bytes 41943040 | tf_op jit(solution)/shard_map/reduce_scatter | solution.py:196
  2398.4 5.2 copy-start.32
  2398.4 5.2 copy-start.35
  2398.4 5.2 copy-start.53
  2398.4 5.2 copy-start.57
  2398.4 5.2 copy-start.1
  2398.4 76.5 %all-to-all-start.3 = ((bf16[8,192,2048]{2,0,1:T(8,128)(2,1)}), bf16[8,192,2048]{2,0,1:T(8,128)(2,1)}, u32[]{:S(2)}, u32[]{:S(2)}) async-start(bf16[8,192,2048]{2,0,1:T(8,128)(2,1)} %copy.128), calls=%async_computation.3 | async-start | bytes 12582912 | tf_op jit(solution)/shard_map/all_to_all | solution.py:186
  2403.3 1684.6 %reduce-scatter.17.cloned.1.call-start = ((), (), s32[]{:S(2)}) async-start(), calls=%async_computation.23 | async-start | bytes 1081344 | tf_op jit(solution)/shard_map/reduce_scatter | solution.py:260
  2405.0 1864.4 %reduce-scatter.15.cloned.1.call-start = ((), (), s32[]{:S(2)}) async-start(), calls=%async_computation.22 | async-start | bytes 17301504 | tf_op jit(solution)/shard_map/reduce_scatter | solution.py:259
  2474.9 9.6 copy-start.46
  2484.5 18.1 copy-start.6
  2484.5 18.1 copy-start.12
  2484.5 18.1 copy-start.42
  2484.5 18.1 copy-start.63
  2497.1 6.1 copy-start.17
  2497.1 6.1 copy-start.21
  2497.1 6.1 copy-start.67
  2497.1 7.7 copy-start.16
  2512.9 9.7 copy-start.23
  2512.9 9.7 copy-start.25
  2512.9 9.7 copy-start.27
  2512.9 9.7 copy-start.55
  2512.9 12.8 copy-start.3
  2512.9 12.8 copy-start.19
  2512.9 12.8 copy-start.44
  2512.9 1944.0 %reduce-scatter.13.cloned.1.call-start = ((), (), s32[]{:S(2)}) async-start(), calls=%async_computation.21 | async-start | bytes 17301504 | tf_op jit(solution)/shard_map/reduce_scatter | solution.py:258
  2535.0 2109.2 %reduce-scatter.11.cloned.1.call-start = ((), (), s32[]{:S(2)}) async-start(), calls=%async_computation.20 | async-start | bytes 17301504 | tf_op jit(solution)/shard_map/reduce_scatter | solution.py:257
  2551.7 2279.8 %reduce-scatter.9.cloned.1.call-start = ((), (), s32[]{:S(2)}) async-start(), calls=%async_computation.19 | async-start | bytes 17301504 | tf_op jit(solution)/shard_map/reduce_scatter | solution.py:256
  2565.3 6.8 copy-start.14
  2565.4 13.3 slice-start
  2572.2 6.5 slice-start.1
  2572.2 6.5 copy-start.30
  2578.7 47.2 copy-start.64
  (28 other events, 62.9 us)
Sparse Core Ops, SparseCore 0:
  10.9 80.2 all-gather.11
  94.1 76.1 all-gather.9
  173.1 76.0 all-gather.7
  251.9 76.0 all-gather.13
  329.4 559.9 all-gather.15
  890.9 559.5 all-gather.17
  1452.1 559.5 all-gather.19
  2289.8 549.3 reduce-scatter.22
  2841.7 552.7 reduce-scatter.18
  3396.7 552.7 reduce-scatter.20
  3952.4 135.4 reduce-scatter.16
  4090.6 178.7 reduce-scatter.14
  4272.3 184.6 reduce-scatter.12
  4459.6 184.4 reduce-scatter.10
  4646.9 184.5 reduce-scatter.8
where the time goes:
time: 4840 us
  waiting for transfers between devices  4000 us (83%)
  blocking collectives  335 us (7%)
  matrix products  283 us (6%)
  local copies, waits for them, and re-layouts  108 us (2%)
  other arithmetic  87.3 us (2%)
    reduce_scatter x1, waiting for transfers between devices, shards(): lax.psum_scatter(grad_gate_full.astype(jnp.bfloat16), 'dp', scatter_dimen...  543 us
    reduce_scatter x1, waiting for transfers between devices, shards(): lax.psum_scatter(grad_up_full.astype(jnp.bfloat16), 'dp', scatter_dimensi...  543 us
    all_gather x1, waiting for transfers between devices, shards(): lax.all_gather(w_up, 'dp', axis=1, tiled=True)  538 us
    all_gather x1, waiting for transfers between devices, shards(): lax.all_gather(w_down, 'dp', axis=1, tiled=True)  534 us
    all_gather x1, waiting for transfers between devices, shards(): lax.all_gather(w_gate, 'dp', axis=1, tiled=True)  466 us
    dot_general x31, matrix products, product(): return jnp.einsum(form, left, right, preferred_element_type=jnp.float32)  281 us
    reduce_scatter x1, waiting for transfers between devices, shards(): lax.psum_scatter(grad_down_full.astype(jnp.bfloat16), 'dp', scatter_dimen...  212 us
    reduce_scatter x1, waiting for transfers between devices, shards(): lax.psum_scatter(grad_value_full, ('dp', 'expert'), scatter_dimension=0,...  188 us
  transfers between devices with their start and end apart: 17, of which 16 were waited for; matrix products, arithmetic and copies ran while one was open for 8% of the time, Pallas kernels for 0%

commit v1 on v0

v1 whole, which is shorter than its diff:
```python
import functools

import jax
import jax.numpy as jnp
from jax import lax
from jax.sharding import PartitionSpec as P

D = 2048
HEADS = 16
HD = 128
TOPK = 8
CAP = 24


eps = 1e-05


def product(left, right, form):
    return jnp.einsum(form, left, right, preferred_element_type=jnp.float32)


def rms_forward(values, gain):
    inverse = lax.rsqrt(jnp.mean(values * values, axis=-1, keepdims=True) + eps)
    return (values * inverse * gain, inverse)


def rms_backward(values, inverse, gain, grad):
    scaled = grad * gain
    inner = jnp.mean(scaled * values, axis=-1, keepdims=True)
    grad_values = inverse * scaled - values * (inverse * inverse * inverse) * inner
    grad_gain = jnp.sum(grad * values * inverse, axis=0)
    return (grad_values, grad_gain)


def layout(lengths_row, count):
    places = jnp.arange(count, dtype=jnp.int32)
    ends = jnp.cumsum(lengths_row, dtype=jnp.int32)
    passed = (places[:, None] >= ends[None, :]).astype(jnp.int32)
    segment = jnp.sum(passed, axis=1, dtype=jnp.int32)
    start = jnp.sum(passed * lengths_row[None, :], axis=1, dtype=jnp.int32)
    return (segment, places - start, places)


def rotate(values, cosine, sine):
    count = values.shape[0]
    heads = values.reshape(count, HEADS, HD)
    half = HD // 2
    first = heads[..., :half]
    second = heads[..., half:]
    turned = jnp.concatenate(
        [first * cosine - second * sine, second * cosine + first * sine], axis=-1
    )
    return turned.reshape(count, D)


def spread(weights, axis, size):
    me = lax.axis_index(axis)
    experts, rows, columns = weights[0].shape
    part = columns // size
    whole = jnp.zeros((experts, size, rows, len(weights) * part), weights[0].dtype)
    for step in range(size):
        to = (me + step) % size
        piece = jnp.concatenate(
            [lax.dynamic_slice_in_dim(one, to * part, part, 2) for one in weights], axis=2
        )
        if step:
            piece = lax.ppermute(piece, axis, [(i, (i + step) % size) for i in range(size)])
        whole = lax.dynamic_update_slice_in_dim(whole, piece[:, None], (me - step) % size, 1)
    return whole.reshape(experts, size * rows, len(weights) * part)


def collect(grads, axis, size, number):
    me = lax.axis_index(axis)
    experts, rows, columns = grads.shape
    rows = rows // size
    part = columns // number
    wholes = [jnp.zeros((experts, rows, size, part), grads.dtype) for i in range(number)]
    for step in range(size):
        to = (me + step) % size
        piece = lax.dynamic_slice_in_dim(grads, to * rows, rows, 1)
        if step:
            piece = lax.ppermute(piece, axis, [(i, (i + step) % size) for i in range(size)])
        at = (me - step) % size
        wholes = [
            lax.dynamic_update_slice_in_dim(
                one, piece[:, :, None, i * part : (i + 1) * part], at, 2
            )
            for i, one in enumerate(wholes)
        ]
    return [one.reshape(experts, rows, size * part) for one in wholes]


def shards(
    n_dp,
    n_expert,
    tokens,
    cotangent,
    lengths,
    routes,
    w_query,
    w_key,
    w_value,
    w_out,
    w_router,
    gain_attn,
    gain_query,
    gain_key,
    gain_mlp,
    w_gate,
    w_up,
    w_down,
):
    both = ("dp", "expert")
    groups = n_dp * n_expert
    bf16 = jnp.bfloat16
    number = w_gate.shape[0]
    ff = w_gate.shape[2]
    part = ff // n_dp
    experts_all = w_router.shape[1]
    width = 128
    small = jnp.concatenate(
        [
            w_router,
            gain_attn[:, None],
            gain_query[:, None],
            gain_key[:, None],
            gain_mlp[:, None],
            jnp.zeros((w_router.shape[0], width - experts_all - 4), bf16),
        ],
        axis=1,
    )
    query_small = lax.all_gather(
        jnp.concatenate([w_query, small], axis=1), both, axis=0, tiled=True
    )
    query_weight = query_small[:, :D]
    small_all = query_small[:, D:]
    key_weight = lax.all_gather(w_key, both, axis=0, tiled=True)
    value_weight = lax.all_gather(w_value, both, axis=0, tiled=True)
    out_weight = lax.all_gather(w_out, both, axis=0, tiled=True)
    routes_all = lax.all_gather(routes, both, axis=0, tiled=True)
    cotangent_all = lax.all_gather(cotangent, both, axis=0, tiled=True)
    gate_up = spread([w_gate, w_up], "dp", n_dp)
    router_weight = small_all[:, :experts_all]
    gains = small_all[:, experts_all : experts_all + 4].astype(jnp.float32)
    attn_gain, query_gain, key_gain, mlp_gain = (gains[:, i] for i in range(4))
    inputs = tokens.astype(jnp.float32)
    count = inputs.shape[0]
    segment, position, places = layout(lengths[0], count)
    half = HD // 2
    freq = 10000.0 ** (-2.0 * jnp.arange(half, dtype=jnp.float32) / HD)
    angle = position.astype(jnp.float32)[:, None] * freq[None, :]
    cosine = jnp.cos(angle)[:, None, :]
    sine = jnp.sin(angle)[:, None, :]
    scale = HD ** (-0.5)
    normed, attn_inverse = rms_forward(inputs, attn_gain)
    normed_low = normed.astype(bf16)
    query_raw = product(normed_low, query_weight, "td,de->te")
    key_raw = product(normed_low, key_weight, "td,de->te")
    value_low = product(normed_low, value_weight, "td,de->te").astype(bf16)
    query_normed, query_inverse = rms_forward(query_raw, query_gain)
    key_normed, key_inverse = rms_forward(key_raw, key_gain)
    query_low = rotate(query_normed, cosine, sine).astype(bf16).reshape(count, HEADS, HD)
    key_low = rotate(key_normed, cosine, sine).astype(bf16).reshape(count, HEADS, HD)
    value_heads = value_low.reshape(count, HEADS, HD)
    allowed = (segment[:, None] == segment[None, :]) & (places[None, :] <= places[:, None])
    scores = product(query_low, key_low, "qhd,khd->hqk") * scale
    scores = jnp.where(allowed[None], scores, -1e30)
    probs = jax.nn.softmax(scores, axis=-1)
    probs_low = probs.astype(bf16)
    attended_low = product(probs_low, value_heads, "hqk,khd->qhd").reshape(count, D).astype(bf16)
    middle = inputs + product(attended_low, out_weight, "td,de->te")
    mlp_normed, mlp_inverse = rms_forward(middle, mlp_gain)
    mlp_low = mlp_normed.astype(bf16)
    router = jax.nn.softmax(product(mlp_low, router_weight, "td,de->te"), axis=-1)

    mlp_all = lax.all_gather(mlp_low, both, axis=0, tiled=True)
    router_all = jax.nn.softmax(product(mlp_all, router_weight, "td,de->te"), axis=-1)
    first = lax.axis_index("expert") * number
    own = lax.dynamic_slice_in_dim(router_all, first, number, 1).reshape(groups, count, number)
    names = first + jnp.arange(number, dtype=jnp.int32)
    hit = jnp.any(
        routes_all.reshape(groups, count, TOPK)[..., None] == names[None, None, None, :], axis=2
    )
    before = jnp.tril(jnp.ones((count, count), bf16), -1)
    slot = product(before, hit.astype(bf16), "ts,bse->bte").astype(jnp.int32)
    slot = jnp.where(hit, slot, -1)
    slots = jnp.arange(CAP, dtype=jnp.int32)
    table = jnp.transpose(slot, (0, 2, 1))[:, :, None, :] == slots[None, None, :, None]
    pick = table.astype(bf16)
    gates = jnp.sum(
        jnp.where(table, jnp.transpose(own, (0, 2, 1))[:, :, None, :], 0.0), axis=3
    )
    rows = product(pick, mlp_all.reshape(groups, count, D), "bect,btd->becd").astype(bf16)
    grows = product(pick, cotangent_all.reshape(groups, count, D), "bect,btd->becd").astype(bf16)
    mids = product(rows, gate_up, "becd,edf->becf")
    gate_mid = mids[..., :part]
    up_mid = mids[..., part:]
    sigmoid = jax.nn.sigmoid(gate_mid)
    silu = gate_mid * sigmoid
    hidden = silu * up_mid
    hidden_low = hidden.astype(bf16)
    result = product(hidden_low, w_down, "becf,efd->becd")
    weighted = (result * gates[..., None]).astype(bf16)
    part_out = product(pick, weighted, "bect,becd->btd").reshape(groups * count, D).astype(bf16)
    grad_plain = product(grows, w_down, "becd,efd->becf")
    grad_gates = jnp.sum(grad_plain * hidden_low.astype(jnp.float32), axis=3)
    grad_hidden = grad_plain * gates[..., None]
    grad_gate_low = (grad_hidden * up_mid * sigmoid * (1.0 + gate_mid * (1.0 - sigmoid))).astype(
        bf16
    )
    grad_up_low = (grad_hidden * silu).astype(bf16)
    grad_mids = jnp.concatenate([grad_gate_low, grad_up_low], axis=3)
    grad_rows = product(grad_mids, gate_up, "becf,edf->becd").astype(bf16)
    part_grad = product(pick, grad_rows, "bect,becd->btd").reshape(groups * count, D)
    part_probs = jnp.sum(
        jnp.where(table, grad_gates[..., None], 0.0), axis=2
    )
    part_probs = jnp.transpose(part_probs, (0, 2, 1)).reshape(groups * count, number)
    spare = jnp.zeros((groups * count, width), jnp.float32)
    part_probs = lax.dynamic_update_slice_in_dim(spare, part_probs, first, 1)
    back = lax.psum_scatter(
        jnp.concatenate([part_grad, part_probs], axis=1).astype(bf16),
        both,
        scatter_dimension=0,
        tiled=True,
    ).astype(jnp.float32)
    grad_down_part = product((hidden * gates[..., None]).astype(bf16), grows, "becf,becd->efd")
    grad_gate_up = product(rows, grad_mids, "becd,becf->edf").astype(bf16)
    grad_gate_part, grad_up_part = collect(grad_gate_up, "dp", n_dp, 2)
    grad_gate_part = grad_gate_part.astype(jnp.float32)
    grad_up_part = grad_up_part.astype(jnp.float32)
    summed = lax.psum_scatter(part_out, both, scatter_dimension=0, tiled=True)
    output = (middle + summed.astype(jnp.float32)).astype(bf16)

    grad_final = cotangent.astype(jnp.float32)
    grad_mlp = back[:, :D]
    grad_router_probs = back[:, D : D + experts_all]
    grad_logits = router * (
        grad_router_probs - jnp.sum(router * grad_router_probs, axis=1, keepdims=True)
    )
    grad_logits_low = grad_logits.astype(bf16)
    grad_router_full = product(mlp_low, grad_logits_low, "td,te->de")
    grad_mlp = grad_mlp + product(grad_logits_low, router_weight, "te,de->td")
    grad_middle_part, grad_mlp_gain = rms_backward(middle, mlp_inverse, mlp_gain, grad_mlp)
    grad_middle = grad_final + grad_middle_part
    grad_branch_low = grad_middle.astype(bf16)
    grad_out_full = product(attended_low, grad_branch_low, "td,te->de")
    grad_attended = (
        product(grad_branch_low, out_weight, "te,de->td").astype(bf16).reshape(count, HEADS, HD)
    )
    grad_weights = product(grad_attended, value_heads, "qhd,khd->hqk")
    grad_scores = probs * (grad_weights - jnp.sum(probs * grad_weights, axis=-1, keepdims=True))
    grad_scores_low = grad_scores.astype(bf16)
    grad_query_turn = product(grad_scores_low, key_low, "hqk,khd->qhd").reshape(count, D) * scale
    grad_key_turn = product(grad_scores_low, query_low, "hqk,qhd->khd").reshape(count, D) * scale
    grad_value_low = (
        product(probs_low, grad_attended, "hqk,qhd->khd").reshape(count, D).astype(bf16)
    )
    grad_query_raw, grad_query_gain = rms_backward(
        query_raw, query_inverse, query_gain, rotate(grad_query_turn, cosine, -sine)
    )
    grad_key_raw, grad_key_gain = rms_backward(
        key_raw, key_inverse, key_gain, rotate(grad_key_turn, cosine, -sine)
    )
    grad_query_low = grad_query_raw.astype(bf16)
    grad_key_low = grad_key_raw.astype(bf16)
    grad_query_full = product(normed_low, grad_query_low, "td,te->de")
    grad_key_full = product(normed_low, grad_key_low, "td,te->de")
    grad_value_full = product(normed_low, grad_value_low, "td,te->de")
    grad_normed = (
        product(grad_query_low, query_weight, "te,de->td")
        + product(grad_key_low, key_weight, "te,de->td")
        + product(grad_value_low, value_weight, "te,de->td")
    )
    grad_inputs_part, grad_attn_gain = rms_backward(inputs, attn_inverse, attn_gain, grad_normed)
    grad_inputs = grad_middle + grad_inputs_part

    def scattered(value):
        return lax.psum_scatter(value.astype(bf16), both, scatter_dimension=0, tiled=True).astype(
            jnp.float32
        )

    grad_out_part = scattered(grad_out_full)
    grad_value_part = scattered(grad_value_full)
    grad_key_part = scattered(grad_key_full)
    small_grads = jnp.concatenate(
        [
            grad_router_full,
            grad_attn_gain[:, None],
            grad_query_gain[:, None],
            grad_key_gain[:, None],
            grad_mlp_gain[:, None],
            jnp.zeros((D, width - experts_all - 4), jnp.float32),
        ],
        axis=1,
    )
    query_part = scattered(jnp.concatenate([grad_query_full, small_grads], axis=1))
    grad_query_part = query_part[:, :D]
    grad_router_part = query_part[:, D : D + experts_all]
    gain_parts = [query_part[:, D + experts_all + i] for i in range(4)]
    return (
        output,
        grad_inputs,
        grad_query_part,
        grad_key_part,
        grad_value_part,
        grad_out_part,
        grad_router_part,
        gain_parts[0],
        gain_parts[1],
        gain_parts[2],
        gain_parts[3],
        grad_gate_part,
        grad_up_part,
        grad_down_part,
    )


def solution(mesh):
    return jax.shard_map(
        functools.partial(shards, mesh.shape["dp"], mesh.shape["expert"]),
        mesh=mesh,
        in_specs=(
            P(("dp", "expert"), None),
            P(("dp", "expert"), None),
            P(("dp", "expert"), None),
            P(("dp", "expert"), None),
            P(("dp", "expert"), None),
            P(("dp", "expert"), None),
            P(("dp", "expert"), None),
            P(("dp", "expert"), None),
            P(("dp", "expert"), None),
            P(("dp", "expert")),
            P(("dp", "expert")),
            P(("dp", "expert")),
            P(("dp", "expert")),
            P("expert", "dp", None),
            P("expert", "dp", None),
            P("expert", "dp", None),
        ),
        out_specs=(
            P(("dp", "expert"), None),
            P(("dp", "expert"), None),
            P(("dp", "expert"), None),
            P(("dp", "expert"), None),
            P(("dp", "expert"), None),
            P(("dp", "expert"), None),
            P(("dp", "expert"), None),
            P(("dp", "expert")),
            P(("dp", "expert")),
            P(("dp", "expert")),
            P(("dp", "expert")),
            P("expert", "dp", None),
            P("expert", "dp", None),
            P("expert", "dp", None),
        ),
        check_vma=False,
    )
```

time: 4840 us -> 2310 us (0.48)
  waiting for transfers between devices: 4000 us -> 1230 us
  local copies, waits for them, and re-layouts: 108 us -> 295 us
  matrix products: 283 us -> 336 us
    reduce_scatter x8 -> x5, waiting for transfers between devices: 2170 us -> 430 us  [the longest x1 182 us: shards(): summed = lax.psum_scatter(part_out, both, scatter_dimension=0, tiled=True)]
    all_gather x7 -> x6, waiting for transfers between devices: 1760 us -> 430 us  [the longest x1 113 us: shards(): mlp_all = lax.all_gather(mlp_low, both, axis=0, tiled=True)]
    all_gather x1, blocking collectives: 102 us -> 325 us  [shards(): routes_all = lax.all_gather(routes, both, axis=0, tiled=True)]
    ppermute x0 -> x6, waiting for transfers between devices: none -> 220 us  [the longest x3 220 us: collect(): lax.ppermute(piece, axis, [(i, (i + step) % size) for i in range(size)])]
    all_to_all x2 -> x0, blocking collectives: 148 us -> none  [the longest x1 74.2 us: shards(): lax.all_to_all(send, 'expert', split_axis=0, concat_axis=1, tiled=True)]
    unnamed x15 -> x13, waiting for transfers between devices: 4.46 us -> 149 us
    dynamic_update_slice x0 -> x12, local copies, waits for them, and re-layouts: none -> 140 us  [the longest x7 116 us: collect(): lax.dynamic_update_slice_in_dim(one, piece[:, :, None, i * part:(i + 1) *...]
    unnamed x2 -> x0, blocking collectives: 84.3 us -> none
  transfers between devices with their start and end apart: 17 -> 18, of which waited for: 16 -> 12; matrix products, arithmetic and copies ran while one was open for 8% -> 23% of each run, Pallas kernels for 0% -> 0%
where the time goes in v1:
time: 2310 us; the launch traced here: 2290 us
  waiting for transfers between devices  1230 us (53%)
  matrix products  336 us (15%)
  blocking collectives  325 us (14%)
  local copies, waits for them, and re-layouts  295 us (13%)
  other arithmetic  76.1 us (3%)
    dot_general x32, matrix products, product(): return jnp.einsum(form, left, right, preferred_element_type=jnp.float32)  335 us
    all_gather x1, blocking collectives, shards(): routes_all = lax.all_gather(routes, both, axis=0, tiled=True)  325 us
    ppermute x3, waiting for transfers between devices, collect(): lax.ppermute(piece, axis, [(i, (i + step) % size) for i in range(size)])  220 us
    reduce_scatter x1, waiting for transfers between devices, shards(): summed = lax.psum_scatter(part_out, both, scatter_dimension=0, tiled=True)  182 us
    unnamed x13, waiting for transfers between devices  149 us
    reduce_scatter x1, waiting for transfers between devices, shards(): lax.psum_scatter(jnp.concatenate([part_grad, part_probs], axis=1).astype(...  146 us
    dynamic_update_slice x7, local copies, waits for them, and re-layouts, collect(): lax.dynamic_update_slice_in_dim(one, piece[:, :, None, i * part:(i + 1) *...  116 us
    all_gather x1, waiting for transfers between devices, shards(): mlp_all = lax.all_gather(mlp_low, both, axis=0, tiled=True)  113 us
  transfers between devices with their start and end apart: 18, of which 12 were waited for; matrix products, arithmetic and copies ran while one was open for 23% of the time, Pallas kernels for 0%

profile of v1, /device:TPU:0, one launch (start us, length us, event | category | flops | bytes accessed | tf_op | source)
XLA Modules:
  0.0 2286.8 jit_solution(1482397978998856430)
XLA Ops:
  19.2 75.3 %all-gather.7.cloned.1.call-done = bf16[2048,2176]{1,0:T(8,128)(2,1)} async-done(((bf16[64,2176]{1,0:T(8,128)(2,1)}), bf16[2048,2176]{1,0:T(8,128)(2,1)}) %all-gather.7.cloned.1.call-update) | async-done | bytes 8912912 | tf_op jit(solution)/shard_map/all_gather | solution.py:132
  97.8 4.8 multiply_reduce_fusion.7
  103.2 70.3 %all-gather.11.cloned.1.call-done = bf16[2048,2048]{1,0:T(8,128)(2,1)} async-done(((bf16[64,2048]{1,0:T(8,128)(2,1)}), bf16[2048,2048]{1,0:T(8,128)(2,1)}) %all-gather.11.cloned.1.call-update) | async-done | bytes 8388624 | tf_op jit(solution)/shard_map/all_gather | solution.py:137
  173.5 4.8 multiply_reduce_fusion.6
  183.7 68.7 %all-gather.9.cloned.1.call-done = bf16[2048,2048]{1,0:T(8,128)(2,1)} async-done(((bf16[64,2048]{1,0:T(8,128)(2,1)}), bf16[2048,2048]{1,0:T(8,128)(2,1)}) %all-gather.9.cloned.1.call-update) | async-done | bytes 8388624 | tf_op jit(solution)/shard_map/all_gather | solution.py:138
  252.4 5.5 fusion.62
  260.0 71.1 %all-gather.13.cloned.1.call-done = bf16[2048,2048]{1,0:T(8,128)(2,1)} async-done(((bf16[64,2048]{1,0:T(8,128)(2,1)}), bf16[2048,2048]{1,0:T(8,128)(2,1)}) %all-gather.13.cloned.1.call-update) | async-done | bytes 8388624 | tf_op jit(solution)/shard_map/all_gather | solution.py:139
  331.2 4.9 multiply_reduce_fusion.5
  338.3 8.5 constant_dynamic-slice_fusion.3
  360.9 6.5 copy.161
  367.4 325.2 %all_gather.25 = s32[4096,8]{0,1:T(8,128)S(1)} all-gather(s32[128,8]{0,1:T(8,128)S(1)} %copy-done.53), channel_id=1, replica_groups=mesh['dp'=4,'expert'=8] {'dp','expert'}, dimensions={0}, use_global_device_ids=true | all-gather | bytes 135168 | tf_op jit(solution)/shard_map/all_gather | solution.py:140
  693.1 4.5 bitcast_dynamic-update-slice_fusion.2
  697.6 4.5 bitcast_dynamic-update-slice_fusion.1
  702.1 4.6 bitcast_dynamic-update-slice_fusion
  706.7 31.6 %all-gather.17.cloned.1.call-done = bf16[4096,2048]{1,0:T(8,128)(2,1)} async-done(((bf16[128,2048]{1,0:T(8,128)(2,1)}), bf16[4096,2048]{1,0:T(8,128)(2,1)}) %all-gather.17.cloned.1.call-update) | async-done | bytes 16777232 | tf_op jit(solution)/shard_map/all_gather | solution.py:141
  738.3 17.3 convolution_convert_fusion
  755.6 17.2 fusion.8
  772.9 112.6 %all-gather.15.cloned.1.call-done = bf16[4096,2048]{1,0:T(8,128)(2,1)} async-done(((bf16[128,2048]{1,0:T(8,128)(2,1)}), bf16[4096,2048]{1,0:T(8,128)(2,1)}) %all-gather.15.cloned.1.call-update) | async-done | bytes 16777232 | tf_op jit(solution)/shard_map/all_gather | solution.py:176
  885.5 17.1 convolution_convert_fusion.1
  902.6 35.3 %fusion.33 = f32[32,8,24,512]{3,0,2,1:T(8,128)} fusion(bf16[8,2048,512,1]{2,1,3,0:T(8,128)(2,1)} %bitcast.221, bf16[32,8,24,2048]{3,2,1,0:T(8,128)(2,1)} %convolution_convert_fusion.1), kind=kOutput, calls=%fused_computation.45 | convolution fusion | flops 12884901888 | bytes 54525952 | tf_op jit(solution)/shard_map/becd,edf->becf/dot_general | solution.py:19
  937.9 9.3 fusion.28
  947.3 11.0 fusion.125
  961.1 8.5 multiply_convert_fusion.2
  969.6 3.3 pad_maximum_fusion.1
  972.9 26.2 %fusion.31 = bf16[8,2048,32,24]{1,3,0,2:T(8,128)(2,1)} fusion(bf16[8,2048,512,1]{2,1,0,3:T(8,128)(2,1)} %bitcast.222, bf16[32,8,24,512]{3,0,2,1:T(8,128)(2,1)} %pad_maximum_fusion.1), kind=kOutput, calls=%fused_computation.43 | convolution fusion | flops 12884901888 | bytes 48234496 | tf_op jit(solution)/shard_map/becf,edf->becd/dot_general | solution.py:19
  999.1 16.7 bitcast_convert_fusion.1
  1016.4 3.9 dynamic_update_slice.43
  1020.3 15.6 pad_maximum_fusion
  1036.0 23.0 %fusion.19 = f32[8,32,24,2048]{3,2,0,1:T(8,128)} fusion(bf16[8,256,2048]{2,1,0:T(8,128)(2,1)} %param.31, bf16[32,8,24,256]{3,0,2,1:T(8,128)(2,1)} %get-tuple-element.89), kind=kOutput, calls=%fused_computation.21 | convolution fusion | flops 6442450944 | bytes 61865984 | tf_op jit(solution)/shard_map/becf,efd->becd/dot_general | solution.py:19
  1059.1 23.9 %bitcast_convert_fusion.2 = bf16[32,128,2048]{2,1,0:T(8,128)(2,1)} fusion(f32[8,32,24,2048]{3,2,0,1:T(8,128)} %fusion.19, f32[32,8,24]{2,1,0:T(8,128)S(1)} %copy-done.30, s32[32,8,128]{2,1,0:T(8,128)S(1)} %fusion.63), kind=kOutput, calls=%fused_computation.5 | convolution fusion | flops 3255566336 | bytes 67264512 | tf_op jit(solution)/shard_map/bect,becd->btd/dot_general | solution.py:19
  1085.7 146.0 %reduce-scatter.11.cloned.1.call-done = bf16[128,2176]{1,0:T(8,128)(2,1)} async-done(((bf16[4096,2176]{1,0:T(8,128)(2,1)}), bf16[128,2176]{1,0:T(8,128)(2,1)}) %reduce-scatter.11.cloned.1.call-update) | async-done | bytes 557072 | tf_op jit(solution)/shard_map/reduce_scatter | solution.py:221
  1236.4 182.3 %reduce-scatter.9.cloned.1.call-done = bf16[128,2048]{1,0:T(8,128)(2,1)} async-done(((bf16[4096,2048]{1,0:T(8,128)(2,1)}), bf16[128,2048]{1,0:T(8,128)(2,1)}) %reduce-scatter.9.cloned.1.call-update) | async-done | bytes 524304 | tf_op jit(solution)/shard_map/reduce_scatter | solution.py:232
  1421.4 5.6 convolution_convert_fusion.2
  1427.3 7.2 convolution_convert_fusion.6
  1444.1 5.7 convolution_convert_fusion.4
  1449.8 3.3 convolution_convert_fusion.9
  1453.1 6.9 convolution_convert_fusion.3
  1464.4 6.6 fusion.127
  1471.0 2.9 fusion.128
  1473.9 4.0 fusion.72
  1479.2 5.8 convolution_convert_fusion.5
  1485.1 38.5 %concatenate.51 = bf16[2048,2176]{0,1:T(8,128)(2,1)} concatenate(bf16[2048,2048]{0,1:T(8,128)(2,1)} %convolution_convert_fusion.5, bf16[2048,64]{0,1:T(8,128)(2,1)S(1)} %convolution_convert_fusion.8, bf16[2048,1]{0,1:T(2,128)(2,1)S(1)} %broadcast_in_dim.175, bf16[2048,1]{0,1:T(2,128)(2,1)S(1)} %broadcast_in_dim.176, bf16[2048,1]{0,1:T(2,128)(2,1)S(1)} %broadcast_in_dim.177, ...), dimensions={1} | concatenate | bytes 17825792 | tf_op jit(solution)/shard_map/concatenate | solution.py:297
  1523.6 11.8 copy.208
  1535.4 28.5 %bitcast_convert_fusion = bf16[8,2048,512]{1,2,0:T(8,128)(2,1)} fusion(bf16[32,8,24,2048]{3,2,1,0:T(8,128)(2,1)} %convolution_convert_fusion.1, bf16[32,8,24,512]{3,0,2,1:T(8,128)(2,1)} %pad_maximum_fusion.1), kind=kOutput, calls=%fused_computation.3 | convolution fusion | flops 12893290496 | bytes 48234496 | tf_op jit(solution)/shard_map/becd,becf->edf/dot_general | solution.py:19
  1563.9 9.4 constant_dynamic-slice_fusion
  1574.4 2.9 collective-permute-start.5
  1577.3 4.2 broadcast.224.clone.1
  1581.5 3.1 fusion.52
  1584.6 4.3 broadcast.224.clone
  1589.0 3.1 fusion.48
  1592.1 39.9 %fusion.25 = f32[8,256,2048]{2,1,0:T(8,128)} fusion(bf16[32,8,24,2048]{3,2,1,0:T(8,128)(2,1)} %convolution_convert_fusion, f32[32,8,24]{0,2,1:T(8,128)S(1)} %copy-done.36, f32[32,8,24,512]{3,0,2,1:T(8,128)} %fusion.33), kind=kOutput, calls=%fused_computation.31 | convolution fusion | flops 6453460992 | bytes 54550528 | tf_op jit(solution)/shard_map/becf,becd->efd/dot_general | solution.py:19
  1632.0 55.7 %collective-permute-done.3 = bf16[8,512,512]{1,2,0:T(8,128)(2,1)} collective-permute-done((bf16[8,512,512]{1,2,0:T(8,128)(2,1)}, bf16[8,512,512]{1,2,0:T(8,128)(2,1)}, u32[]{:S(2)}, u32[]{:S(2)}) %collective-permute-start.3) | collective-permute-done | bytes 4194336 | tf_op jit(solution)/shard_map/ppermute | solution.py:82
  1687.6 4.6 fusion.47
  1692.3 164.3 %collective-permute-done.4 = bf16[8,512,512]{1,2,0:T(8,128)(2,1)} collective-permute-done((bf16[8,512,512]{1,2,0:T(8,128)(2,1)}, bf16[8,512,512]{1,2,0:T(8,128)(2,1)}, u32[]{:S(2)}, u32[]{:S(2)}) %collective-permute-start.4) | collective-permute-done | bytes 4194336 | tf_op jit(solution)/shard_map/ppermute | solution.py:82
  1856.6 4.6 fusion.46
  1861.2 13.9 copy.188
  1876.9 7.2 copy.189
  1884.1 83.4 %dynamic_update_slice.51 = bf16[8,512,4,256]{3,2,1,0:T(4,128)(2,1)} dynamic-update-slice(bf16[8,512,4,256]{3,2,1,0:T(4,128)(2,1)} %copy.188, bf16[8,512,1,256]{3,2,1,0:T(2,128)(2,1)} %copy.189, s32[]{:T(128)} %constant.117.clone.1, s32[]{:T(128)} %constant.117.clone.1, s32[]{:T(128)S(6)} %select_n.141, s32[]{:T(128)} %constant.117.clone.1) | dynamic-update-slice | bytes 4194308 | tf_op jit(solution)/shard_map/dynamic_update_slice | solution.py:85
  1967.4 14.9 reshape.340
  1982.3 3.1 fusion.49
  1985.4 14.8 copy.187
  2000.2 20.9 reshape.339
  2026.1 102.1 %reduce-scatter.15.cloned.1.call-done = bf16[64,2048]{1,0:T(8,128)(2,1)} async-done(((bf16[2048,2048]{1,0:T(8,128)(2,1)}), bf16[64,2048]{1,0:T(8,128)(2,1)}) %reduce-scatter.15.cloned.1.call-update) | async-done | bytes 262160 | tf_op jit(solution)/shard_map/reduce_scatter | solution.py:279
  2130.0 146.0 %reduce-scatter.19.cloned.1.call-done = bf16[64,2176]{1,0:T(8,128)(2,1)} async-done(((bf16[2048,2176]{1,0:T(8,128)(2,1)}), bf16[64,2176]{1,0:T(8,128)(2,1)}) %reduce-scatter.19.cloned.1.call-update) | async-done | bytes 278544
  (250 shorter events, 82.1 us)
Async XLA Ops:
  7.2 90.6 %copy-start = (bf16[128,2048]{1,0:T(8,128)(2,1)S(1)}, bf16[128,2048]{1,0:T(8,128)(2,1)}, u32[]{:S(2)}) copy-start(bf16[128,2048]{1,0:T(8,128)(2,1)} %param.16) | copy-start | bytes 1572868
  7.2 87.3 %all-gather.7.cloned.1.call-start = ((), (), s32[]{:S(2)}) async-start(), calls=%async_computation.6 | async-start | bytes 9191424 | tf_op jit(solution)/shard_map/all_gather | solution.py:132
  12.1 161.4 %all-gather.11.cloned.1.call-start = ((), (), s32[]{:S(2)}) async-start(), calls=%async_computation.8 | async-start | bytes 8650752 | tf_op jit(solution)/shard_map/all_gather | solution.py:137
  12.9 239.5 %all-gather.9.cloned.1.call-start = ((), (), s32[]{:S(2)}) async-start(), calls=%async_computation.7 | async-start | bytes 8650752 | tf_op jit(solution)/shard_map/all_gather | solution.py:138
  13.6 317.6 %all-gather.13.cloned.1.call-start = ((), (), s32[]{:S(2)}) async-start(), calls=%async_computation.9 | async-start | bytes 8650752 | tf_op jit(solution)/shard_map/all_gather | solution.py:139
  14.2 724.1 %all-gather.17.cloned.1.call-start = ((), (), s32[]{:S(2)}) async-start(), calls=%async_computation.12 | async-start | bytes 17301504 | tf_op jit(solution)/shard_map/all_gather | solution.py:141
  14.8 870.7 %all-gather.15.cloned.1.call-start = ((), (), s32[]{:S(2)}) async-start(), calls=%async_computation.10 | async-start | bytes 17301504 | tf_op jit(solution)/shard_map/all_gather | solution.py:176
  18.2 234.2 %copy-start.44 = (f32[128]{0:T(128)}, f32[128]{0:T(128)S(1)}, u32[]{:S(2)}) copy-start(f32[128]{0:T(128)S(1)} %get-tuple-element.133) | copy-start | bytes 1540
  18.3 239.6 %copy-start.46 = (pred[128,128]{0,1:T(8,128)(4,1)}, pred[128,128]{0,1:T(8,128)(4,1)S(1)}, u32[]{:S(2)}) copy-start(pred[128,128]{0,1:T(8,128)(4,1)S(1)} %fusion.92) | copy-start | bytes 49156
  19.2 161.2 %copy-start.32 = (f32[128,64]{1,0:T(8,128)}, f32[128,64]{1,0:T(8,128)S(1)}, u32[]{:S(2)}) copy-start(f32[128,64]{1,0:T(8,128)S(1)} %get-tuple-element.131) | copy-start | bytes 98308
  97.8 81.1 %copy-start.38 = (f32[2048]{0:T(1024)}, f32[2048]{0:T(1024)S(1)}, u32[]{:S(2)}) copy-start(f32[2048]{0:T(1024)S(1)} %get-tuple-element.80) | copy-start | bytes 24580
  97.8 81.1 %copy-start.40 = (f32[2048]{0:T(1024)}, f32[2048]{0:T(1024)S(1)}, u32[]{:S(2)}) copy-start(f32[2048]{0:T(1024)S(1)} %get-tuple-element.79) | copy-start | bytes 24580
  97.8 154.6 %copy-start.15 = (f32[2048]{0:T(1024)}, f32[2048]{0:T(1024)S(1)}, u32[]{:S(2)}) copy-start(f32[2048]{0:T(1024)S(1)} %get-tuple-element.81) | copy-start | bytes 24580
  97.8 238.9 %copy-start.42 = (f32[2048]{0:T(1024)}, f32[2048]{0:T(1024)S(1)}, u32[]{:S(2)}) copy-start(f32[2048]{0:T(1024)S(1)} %get-tuple-element.78) | copy-start | bytes 24580
  102.6 76.5 %copy-start.6 = (f32[128,2048]{1,0:T(8,128)}, f32[128,2048]{1,0:T(8,128)S(1)}, u32[]{:S(2)}) copy-start(f32[128,2048]{1,0:T(8,128)S(1)} %get-tuple-element.141) | copy-start | bytes 3145732
  103.2 76.0 %copy-start.49 = (f32[128]{0:T(128)}, f32[128]{0:T(128)S(1)}, u32[]{:S(2)}) copy-start(f32[128]{0:T(128)S(1)} %get-tuple-element.135) | copy-start | bytes 1540
  181.9 76.0 %copy-start.17 = (bf16[128,16,64]{2,0,1:T(8,128)(2,1)}, bf16[128,16,64]{2,0,1:T(8,128)(2,1)S(1)}, u32[]{:S(2)}) copy-start(bf16[128,16,64]{2,0,1:T(8,128)(2,1)S(1)} %get-tuple-element.107) | copy-start | bytes 786436
  181.9 76.0 %copy-start.20 = (bf16[128,16,64]{2,0,1:T(8,128)(2,1)}, bf16[128,16,64]{2,0,1:T(8,128)(2,1)S(1)}, u32[]{:S(2)}) copy-start(bf16[128,16,64]{2,0,1:T(8,128)(2,1)S(1)} %get-tuple-element.108) | copy-start | bytes 786436
  181.9 76.0 %copy-start.23 = (bf16[128,16,64]{2,0,1:T(8,128)(2,1)}, bf16[128,16,64]{2,0,1:T(8,128)(2,1)S(1)}, u32[]{:S(2)}) copy-start(bf16[128,16,64]{2,0,1:T(8,128)(2,1)S(1)} %get-tuple-element.127) | copy-start | bytes 786436
  181.9 76.0 %copy-start.25 = (bf16[128,16,64]{2,0,1:T(8,128)(2,1)}, bf16[128,16,64]{2,0,1:T(8,128)(2,1)S(1)}, u32[]{:S(2)}) copy-start(bf16[128,16,64]{2,0,1:T(8,128)(2,1)S(1)} %get-tuple-element.128) | copy-start | bytes 786436
  183.7 76.3 %copy-start.47 = (f32[16,128]{1,0:T(8,128)}, f32[16,128]{1,0:T(8,128)S(1)}, u32[]{:S(2)}) copy-start(f32[16,128]{1,0:T(8,128)S(1)} %get-tuple-element.144) | copy-start | bytes 24580
  260.0 76.1 %copy-start.12 = (bf16[16,128,128]{2,1,0:T(8,128)(2,1)}, bf16[16,128,128]{2,1,0:T(8,128)(2,1)S(1)}, u32[]{:S(2)}) copy-start(bf16[16,128,128]{2,1,0:T(8,128)(2,1)S(1)} %convolution_convert_fusion.10) | copy-start | bytes 1572868
  338.2 893.5 %reduce-scatter.11.cloned.1.call-start = ((), (), s32[]{:S(2)}) async-start(), calls=%async_computation.13 | async-start | bytes 18382848 | tf_op jit(solution)/shard_map/reduce_scatter | solution.py:221
  349.2 343.9 %collective-permute-start = (bf16[8,512,512]{2,1,0:T(8,128)(2,1)}, bf16[8,512,512]{2,1,0:T(8,128)(2,1)}, u32[]{:S(2)}, u32[]{:S(2)}) collective-permute-start(bf16[8,512,512]{2,1,0:T(8,128)(2,1)} %pad_maximum_fusion.2), channel_id=1, source_target_pairs={{0,8},{8,16},{16,24},{24,0},{1,9},{9,17},{17,25},{25,1},{2,10},{10... | collective-permute-start | bytes 12582920 | tf_op jit(solution)/shard_map/ppermute | solution.py:67
  353.1 344.5 %collective-permute-start.1 = (bf16[8,512,512]{2,1,0:T(8,128)(2,1)}, bf16[8,512,512]{2,1,0:T(8,128)(2,1)}, u32[]{:S(2)}, u32[]{:S(2)}) collective-permute-start(bf16[8,512,512]{2,1,0:T(8,128)(2,1)} %pad_maximum_fusion.3), channel_id=1, source_target_pairs={{0,16},{8,24},{16,0},{24,8},{1,17},{9,25},{17,1},{25,9},{2,18},{10... | collective-permute-start | bytes 12582920 | tf_op jit(solution)/shard_map/ppermute | solution.py:67
  356.3 345.9 %collective-permute-start.2 = (bf16[8,512,512]{2,1,0:T(8,128)(2,1)}, bf16[8,512,512]{2,1,0:T(8,128)(2,1)}, u32[]{:S(2)}, u32[]{:S(2)}) collective-permute-start(bf16[8,512,512]{2,1,0:T(8,128)(2,1)} %pad_maximum_fusion.4), channel_id=1, source_target_pairs={{0,24},{8,0},{16,8},{24,16},{1,25},{9,1},{17,9},{25,17},{2,26},{10... | collective-permute-start | bytes 12582920 | tf_op jit(solution)/shard_map/ppermute | solution.py:67
  360.9 6.6 copy-start.53
  961.0 8.6 copy-start.29
  961.1 8.5 copy-start.35
  1036.0 382.7 %reduce-scatter.9.cloned.1.call-start = ((), (), s32[]{:S(2)}) async-start(), calls=%async_computation.11 | async-start | bytes 17301504 | tf_op jit(solution)/shard_map/reduce_scatter | solution.py:232
  1036.0 23.0 %copy-start.30 = (f32[32,8,24]{2,1,0:T(8,128)S(1)}, f32[32,8,24]{2,1,0:T(8,128)}, u32[]{:S(2)}) copy-start(f32[32,8,24]{2,1,0:T(8,128)} %copy-done.29) | copy-start | bytes 73732
  1082.9 150.8 %copy-start.9 = (f32[128,2048]{1,0:T(8,128)S(1)}, f32[128,2048]{1,0:T(8,128)}, u32[]{:S(2)}) copy-start(f32[128,2048]{1,0:T(8,128)} %copy-done.8) | copy-start | bytes 3145732
  1082.9 150.8 %copy-start.43 = (f32[2048]{0:T(1024)S(1)}, f32[2048]{0:T(1024)}, u32[]{:S(2)}) copy-start(f32[2048]{0:T(1024)} %copy-done.42) | copy-start | bytes 24580
  1082.9 150.8 %copy-start.55 = (f32[128]{0:T(128)S(1)}, f32[128]{0:T(128)}, u32[]{:S(2)}) copy-start(f32[128]{0:T(128)} %copy-done.54) | copy-start | bytes 1540
  1082.9 335.8 %copy-start.59 = (f32[128]{0:T(128)S(1)}, f32[128]{0:T(128)}, u32[]{:S(2)}) copy-start(f32[128]{0:T(128)} %get-tuple-element.138) | copy-start | bytes 1540
  1083.0 338.4 %copy-start.13 = (bf16[16,128,128]{2,1,0:T(8,128)(2,1)S(1)}, bf16[16,128,128]{2,1,0:T(8,128)(2,1)}, u32[]{:S(2)}) copy-start(bf16[16,128,128]{2,1,0:T(8,128)(2,1)} %copy-done.12) | copy-start | bytes 1572868
  1083.0 939.5 %reduce-scatter.17.cloned.1.call-start = ((), (), s32[]{:S(2)}) async-start(), calls=%async_computation.16 | async-start | bytes 8650752 | tf_op jit(solution)/shard_map/reduce_scatter | solution.py:279
  1421.4 6.0 copy-start.2
  1427.0 9.0 copy-start.48
  1427.0 12.4 copy-start.18
  1427.0 12.4 copy-start.21
  1427.1 12.9 copy-start.24
  1427.1 597.3 %reduce-scatter.13.cloned.1.call-start = ((), (), s32[]{:S(2)}) async-start(), calls=%async_computation.14 | async-start | bytes 8650752 | tf_op jit(solution)/shard_map/reduce_scatter | solution.py:279
  1434.6 6.0 copy-start.33
  1434.6 6.0 copy-start.37
  1444.0 5.8 copy-start.19
  1444.0 5.8 copy-start.22
  1449.8 678.5 %reduce-scatter.15.cloned.1.call-start = ((), (), s32[]{:S(2)}) async-start(), calls=%async_computation.15 | async-start | bytes 8650752 | tf_op jit(solution)/shard_map/reduce_scatter | solution.py:279
  1453.1 7.4 copy-start.7
  1453.1 7.4 copy-start.39
  1453.1 7.4 copy-start.50
  1460.0 816.0 %reduce-scatter.19.cloned.1.call-start = ((), (), s32[]{:S(2)}) async-start(), calls=%async_computation.17 | async-start | bytes 9191424
  1460.6 10.4 slice-start
  1460.6 10.4 copy-start.27
  1462.5 11.4 slice-start.2
  1464.4 6.6 slice-start.1
  1464.4 9.5 slice-start.3
  1573.4 114.2 %collective-permute-start.3 = (bf16[8,512,512]{1,2,0:T(8,128)(2,1)}, bf16[8,512,512]{1,2,0:T(8,128)(2,1)}, u32[]{:S(2)}, u32[]{:S(2)}) collective-permute-start(bf16[8,512,512]{1,2,0:T(8,128)(2,1)} %get-tuple-element.94), channel_id=1, source_target_pairs={{0,8},{8,16},{16,24},{24,0},{1,9},{9,17},{17,25},{25,1},{2,10},{10... | collective-permute-start | bytes 12582920 | tf_op jit(solution)/shard_map/ppermute | solution.py:82
  1573.4 283.2 %collective-permute-start.4 = (bf16[8,512,512]{1,2,0:T(8,128)(2,1)}, bf16[8,512,512]{1,2,0:T(8,128)(2,1)}, u32[]{:S(2)}, u32[]{:S(2)}) collective-permute-start(bf16[8,512,512]{1,2,0:T(8,128)(2,1)} %get-tuple-element.93), channel_id=1, source_target_pairs={{0,16},{8,24},{16,0},{24,8},{1,17},{9,25},{17,1},{25,9},{2,18},{10... | collective-permute-start | bytes 12582920 | tf_op jit(solution)/shard_map/ppermute | solution.py:82
  1574.4 300.6 %collective-permute-start.5 = (bf16[8,512,512]{1,2,0:T(8,128)(2,1)}, bf16[8,512,512]{1,2,0:T(8,128)(2,1)}, u32[]{:S(2)}, u32[]{:S(2)}) collective-permute-start(bf16[8,512,512]{1,2,0:T(8,128)(2,1)} %get-tuple-element.92), channel_id=1, source_target_pairs={{0,24},{8,0},{16,8},{24,16},{1,25},{9,1},{17,9},{25,17},{2,26},{10... | collective-permute-start | bytes 12582920 | tf_op jit(solution)/shard_map/ppermute | solution.py:82
  1581.5 10.6 copy-start.36
  2000.2 20.9 copy-start.3
  2000.2 20.9 copy-start.31
  2000.2 20.9 copy-start.56
  (19 other events, 51.4 us)
Sparse Core Ops, SparseCore 0:
  12.2 82.2 all-gather.6
  97.4 76.0 all-gather.10
  176.4 75.9 all-gather.8
  255.1 76.0 all-gather.12
  333.9 404.3 all-gather.16
  741.6 143.8 all-gather.14
  1036.1 195.5 reduce-scatter.10
  1234.5 184.1 reduce-scatter.8
  1427.2 150.3 reduce-scatter.16
  1579.7 367.4 reduce-scatter.12
  1949.5 178.6 reduce-scatter.14
  2130.4 145.5 reduce-scatter.18

commit v2 on v1

--- a/solution.py
+++ b/solution.py
@@ -3,6 +3,8 @@
 import jax
 import jax.numpy as jnp
 from jax import lax
+from jax.experimental import pallas as pl
+from jax.experimental.pallas import tpu as pltpu
 from jax.sharding import PartitionSpec as P
 
 D = 2048
@@ -53,41 +55,419 @@
     return turned.reshape(count, D)
 
 
-def spread(weights, axis, size):
-    me = lax.axis_index(axis)
-    experts, rows, columns = weights[0].shape
-    part = columns // size
-    whole = jnp.zeros((experts, size, rows, len(weights) * part), weights[0].dtype)
-    for step in range(size):
-        to = (me + step) % size
-        piece = jnp.concatenate(
-            [lax.dynamic_slice_in_dim(one, to * part, part, 2) for one in weights], axis=2
+MESH = pl.DeviceIdType.MESH
+
+
+def place_of():
+    z = lax.axis_index("dp")
+    j = lax.axis_index("expert")
+    return z, j, j // 2, j % 2
+
+
+def greet(n_dp, n_expert):
+    z, j, chip, core = place_of()
+    chips = n_expert // 2
+    barrier = pltpu.get_barrier_semaphore()
+    for k in range(1, n_dp):
+        pl.semaphore_signal(
+            barrier, inc=1, device_id=((z + k) % n_dp, j), device_id_type=MESH
         )
-        if step:
-            piece = lax.ppermute(piece, axis, [(i, (i + step) % size) for i in range(size)])
-        whole = lax.dynamic_update_slice_in_dim(whole, piece[:, None], (me - step) % size, 1)
-    return whole.reshape(experts, size * rows, len(weights) * part)
-
-
-def collect(grads, axis, size, number):
-    me = lax.axis_index(axis)
-    experts, rows, columns = grads.shape
-    rows = rows // size
-    part = columns // number
-    wholes = [jnp.zeros((experts, rows, size, part), grads.dtype) for i in range(number)]
-    for step in range(size):
-        to = (me + step) % size
-        piece = lax.dynamic_slice_in_dim(grads, to * rows, rows, 1)
-        if step:
-            piece = lax.ppermute(piece, axis, [(i, (i + step) % size) for i in range(size)])
-        at = (me - step) % size
-        wholes = [
-            lax.dynamic_update_slice_in_dim(
-                one, piece[:, :, None, i * part : (i + 1) * part], at, 2
+    for k in range(1, chips):
+        other = ((chip + k) % chips) * 2 + core
+        pl.semaphore_signal(barrier, inc=1, device_id=(z, other), device_id_type=MESH)
+    pl.semaphore_signal(
+        barrier, inc=1, device_id=(z, chip * 2 + 1 - core), device_id_type=MESH
+    )
+    pl.semaphore_wait(barrier, n_dp - 1 + chips - 1 + 1)
+
+
+def remote(source, target, send, receive, device):
+    return pltpu.make_async_remote_copy(
+        src_ref=source,
+        dst_ref=target,
+        send_sem=send,
+        recv_sem=receive,
+        device_id=device,
+        device_id_type=MESH,
+    )
+
+
+def exchange(n_dp, pairs, send, receive, local):
+    z, j, chip, core = place_of()
+    copies = []
+    for i, (source, target) in enumerate(pairs):
+        for k in range(1, n_dp):
+            to = (z + k) % n_dp
+            copies.append(
+                remote(source(to), target(z), send.at[i, k], receive.at[i, k], (to, j))
             )
-            for i, one in enumerate(wholes)
-        ]
-    return [one.reshape(experts, rows, size * part) for one in wholes]
+        copies.append(pltpu.make_async_copy(source(z), target(z), local.at[i]))
+    return copies
+
+
+def gather_kernel(n_dp, n_expert, n_items, places, cuts, n_cut, n_out, *refs):
+    z, j, chip, core = place_of()
+    chips = n_expert // 2
+    sources = refs[:n_items]
+    cut_in = refs[n_items : n_items + n_cut]
+    at = n_items + n_cut
+    targets = refs[at : at + n_items]
+    cut_out = refs[at + n_items : at + n_items + n_out]
+    (
+        send_c,
+        recv_c,
+        send_b,
+        recv_b,
+        send_a,
+        recv_a,
+        local,
+        send_x,
+        recv_x,
+        local_x,
+    ) = refs[at + n_items + n_out :]
+    greet(n_dp, n_expert)
+    mate = (z, chip * 2 + 1 - core)
+
+    def slot(i, plane, column):
+        return places[i](targets[i], plane * n_expert + column)
+
+    def hand(i, plane, source):
+        for k in range(1, chips):
+            other = ((chip + k) % chips) * 2 + core
+            remote(
+                source, slot(i, plane, j), send_b.at[i, plane, k], recv_b.at[i, plane, k], (z, other)
+            ).start()
+        remote(
+            source, slot(i, plane, j), send_a.at[i, plane, 0], recv_a.at[i, plane, 0], mate
+        ).start()
+
+    def along(i, plane, source, way, step):
+        return remote(
+            source, slot(i, plane, j), send_c.at[i, way, plane], recv_c.at[i, plane], (z + step, j)
+        )
+
+    for i in range(n_items):
+
+        @pl.when(z < n_dp - 1)
+        def _():
+            along(i, z, sources[i], 0, 1).start()
+
+        @pl.when(z > 0)
+        def _():
+            along(i, z, sources[i], 1, -1).start()
+
+        hand(i, z, sources[i])
+        pltpu.make_async_copy(sources[i], slot(i, z, j), local.at[i]).start()
+    copies = exchange(n_dp, cuts(cut_in, cut_out), send_x, recv_x, local_x)
+    for copy in copies:
+        copy.start()
+
+    def arrived(i, plane):
+        for k in range(1, chips):
+            column = ((chip + chips - k) % chips) * 2 + core
+            block = slot(i, plane, column)
+            remote(block, block, send_b.at[i, plane, k], recv_b.at[i, plane, k], mate).wait_recv()
+            remote(block, block, send_a.at[i, plane, k], recv_a.at[i, plane, k], mate).start()
+
+    for d in range(1, n_dp):
+
+        @pl.when(z >= d)
+        def _():
+            for i in range(n_items):
+                block = slot(i, z - d, j)
+                along(i, z - d, block, 0, 1).wait_recv()
+
+                @pl.when(z < n_dp - 1)
+                def _():
+                    along(i, z - d, block, 0, 1).start()
+
+                hand(i, z - d, block)
+
+        @pl.when(z + d < n_dp)
+        def _():
+            for i in range(n_items):
+                block = slot(i, z + d, j)
+                along(i, z + d, block, 1, -1).wait_recv()
+
+                @pl.when(z > 0)
+                def _():
+                    along(i, z + d, block, 1, -1).start()
+
+                hand(i, z + d, block)
+
+        if d == 1:
+            for i in range(n_items):
+                arrived(i, z)
+        else:
+
+            @pl.when(z >= d - 1)
+            def _():
+                for i in range(n_items):
+                    arrived(i, z - d + 1)
+
+            @pl.when(z + d - 1 < n_dp)
+            def _():
+                for i in range(n_items):
+                    arrived(i, z + d - 1)
+
+    @pl.when(z >= n_dp - 1)
+    def _():
+        for i in range(n_items):
+            arrived(i, z - n_dp + 1)
+
+    @pl.when(z + n_dp - 1 < n_dp)
+    def _():
+        for i in range(n_items):
+            arrived(i, z + n_dp - 1)
+
+    for i in range(n_items):
+        for plane in range(n_dp):
+            for k in range(chips):
+                column = ((chip + chips - k) % chips) * 2 + 1 - core
+                block = slot(i, plane, column)
+                remote(
+                    block, block, send_a.at[i, plane, k], recv_a.at[i, plane, k], mate
+                ).wait_recv()
+    for i in range(n_items):
+        for plane in range(n_dp):
+            block = slot(i, plane, j)
+            for k in range(1, chips):
+                remote(
+                    block, block, send_b.at[i, plane, k], recv_b.at[i, plane, k], mate
+                ).wait_send()
+            for k in range(chips):
+                remote(
+                    block, block, send_a.at[i, plane, k], recv_a.at[i, plane, k], mate
+                ).wait_send()
+
+            @pl.when((z < n_dp - 1) & (z >= plane))
+            def _():
+                along(i, plane, block, 0, 1).wait_send()
+
+            @pl.when((z > 0) & (z <= plane))
+            def _():
+                along(i, plane, block, 1, -1).wait_send()
+
+        pltpu.make_async_copy(sources[i], slot(i, z, j), local.at[i]).wait()
+    for copy in copies:
+        copy.wait()
+
+
+def gather_call(n_dp, n_expert, items, shapes, places, cut_in, cut_shapes, cuts, aliases, number):
+    chips = n_expert // 2
+    n, m = len(items), len(cut_shapes)
+    dma = pltpu.SemaphoreType.DMA
+    anywhere = pl.BlockSpec(memory_space=pl.ANY)
+    return pl.pallas_call(
+        functools.partial(gather_kernel, n_dp, n_expert, n, places, cuts, len(cut_in), m),
+        out_shape=[*shapes, *cut_shapes],
+        in_specs=[anywhere] * (n + len(cut_in)),
+        out_specs=[anywhere] * (n + m),
+        scratch_shapes=[
+            dma((n, 2, n_dp)),
+            dma((n, n_dp)),
+            dma((n, n_dp, chips)),
+            dma((n, n_dp, chips)),
+            dma((n, n_dp, chips)),
+            dma((n, n_dp, chips)),
+            dma((n,)),
+            dma((max(m, 1), n_dp)),
+            dma((max(m, 1), n_dp)),
+            dma((max(m, 1),)),
+        ],
+        input_output_aliases=aliases,
+        compiler_params=pltpu.CompilerParams(collective_id=number, has_side_effects=True),
+    )(*items, *cut_in)
+
+
+def scatter_kernel(n_dp, n_expert, n_items, n_cut, cuts, *refs):
+    z, j, chip, core = place_of()
+    chips = n_expert // 2
+    sources = refs[:n_items]
+    cut_in = refs[n_items : n_items + n_cut]
+    at = n_items + n_cut
+    targets = refs[at : at + n_items]
+    cut_out = refs[at + n_items : at + n_items + n_cut]
+    at = at + n_items + n_cut
+    halves = refs[at : at + n_items]
+    got_a = refs[at + n_items : at + 2 * n_items]
+    got_b = refs[at + 2 * n_items : at + 3 * n_items]
+    got_c = refs[at + 3 * n_items : at + 4 * n_items]
+    (
+        send_a,
+        recv_a,
+        send_b,
+        recv_b,
+        send_c,
+        recv_c,
+        local,
+        send_x,
+        recv_x,
+        local_x,
+    ) = refs[at + 4 * n_items :]
+    greet(n_dp, n_expert)
+    mate = (z, chip * 2 + 1 - core)
+    order = [*range(1, chips), 0]
+
+    def to_mate(i, k):
+        column = ((chip + k) % chips) * 2
+        return remote(
+            sources[i].at[:, column + 1 - core],
+            got_a[i].at[k],
+            send_a.at[i, k],
+            recv_a.at[i, k],
+            mate,
+        )
+
+    def load(i, k):
+        column = ((chip + k) % chips) * 2
+        return pltpu.make_async_copy(
+            sources[i].at[:, column + core], halves[i].at[k], local.at[i, k]
+        )
+
+    def to_chip(i, k):
+        other = ((chip + k) % chips) * 2 + core
+        return remote(
+            halves[i].at[k], got_b[i].at[k - 1], send_b.at[i, k], recv_b.at[i, k], (z, other)
+        )
+
+    def to_plane(i, k):
+        to = (z + k) % n_dp
+        return remote(
+            halves[i].at[0, to], got_c[i].at[k - 1], send_c.at[i, k], recv_c.at[i, k], (to, j)
+        )
+
+    for i in range(n_items):
+        for k in order:
+            to_mate(i, k).start()
+            load(i, k).start()
+    copies = exchange(n_dp, cuts(cut_in, cut_out), send_x, recv_x, local_x)
+    for copy in copies:
+        copy.start()
+
+    def loop(rows, body):
+        def step(n, unused):
+            body(pl.ds(pl.multiple_of(n * 16, 16), 16))
+            return unused
+
+        lax.fori_loop(0, rows // 16, step, 0)
+
+    f32 = jnp.float32
+    for i in range(n_items):
+        rows = halves[i].shape[2]
+        for k in order:
+            load(i, k).wait()
+            to_mate(i, k).wait_recv()
+            if k == 0:
+                continue
+
+            def one(n, unused):
+                plane = n // (rows // 16)
+                at = pl.ds(pl.multiple_of((n % (rows // 16)) * 16, 16), 16)
+                total = halves[i][k, plane, at].astype(f32) + got_a[i][k, plane, at].astype(f32)
+                halves[i][k, plane, at] = total.astype(halves[i].dtype)
+                return unused
+
+            lax.fori_loop(0, n_dp * (rows // 16), one, 0)
+            to_chip(i, k).start()
+    for i in range(n_items):
+        rows = halves[i].shape[2]
+        for k in range(1, chips):
+            to_chip(i, k).wait_recv()
+        for k in [*range(1, n_dp), 0]:
+            plane = (z + k) % n_dp
+
+            def body(at):
+                total = halves[i][0, plane, at].astype(f32) + got_a[i][0, plane, at].astype(f32)
+                for other in range(chips - 1):
+                    total = total + got_b[i][other, plane, at].astype(f32)
+                halves[i][0, plane, at] = total.astype(halves[i].dtype)
+
+            loop(rows, body)
+            if k:
+                to_plane(i, k).start()
+    for i in range(n_items):
+        rows = halves[i].shape[2]
+        for k in range(1, n_dp):
+            to_plane(i, k).wait_recv()
+
+        def body(at):
+            total = halves[i][0, z, at].astype(f32)
+            for k in range(n_dp - 1):
+                total = total + got_c[i][k, at].astype(f32)
+            targets[i][at] = total
+
+        loop(rows, body)
+    for i in range(n_items):
+        for k in range(chips):
+            to_mate(i, k).wait_send()
+            if k:
+                to_chip(i, k).wait_send()
+        for k in range(1, n_dp):
+            to_plane(i, k).wait_send()
+    for copy in copies:
+        copy.wait()
+
+
+def scatter_call(n_dp, n_expert, items, cut_in, cut_shapes, cuts, number):
+    chips = n_expert // 2
+    n, m = len(items), len(cut_shapes)
+    dma = pltpu.SemaphoreType.DMA
+    anywhere = pl.BlockSpec(memory_space=pl.ANY)
+    blocks = [item.shape[2:] for item in items]
+    bf16 = jnp.bfloat16
+    return pl.pallas_call(
+        functools.partial(scatter_kernel, n_dp, n_expert, n, m, cuts),
+        out_shape=[*[jax.ShapeDtypeStruct(block, jnp.float32) for block in blocks], *cut_shapes],
+        in_specs=[anywhere] * (n + m),
+        out_specs=[pl.BlockSpec(memory_space=pltpu.VMEM)] * n + [anywhere] * m,
+        scratch_shapes=[
+            *[pltpu.VMEM((chips, n_dp, *block), bf16) for block in blocks],
+            *[pltpu.VMEM((chips, n_dp, *block), bf16) for block in blocks],
+            *[pltpu.VMEM((chips - 1, n_dp, *block), bf16) for block in blocks],
+            *[pltpu.VMEM((n_dp - 1, *block), bf16) for block in blocks],
+            dma((n, chips)),
+            dma((n, chips)),
+            dma((n, chips)),
+            dma((n, chips)),
+            dma((n, n_dp)),
+            dma((n, n_dp)),
+            dma((n, chips)),
+            dma((max(m, 1), n_dp)),
+            dma((max(m, 1), n_dp)),
+            dma((max(m, 1),)),
+        ],
+        compiler_params=pltpu.CompilerParams(
+            collective_id=number, has_side_effects=True, vmem_limit_bytes=60 * 1024 * 1024
+        ),
+    )(*items, *cut_in)
+
+def scatter_all(n_dp, n_expert, items, cut_in, cut_shapes, cuts, number):
+    chips = n_expert // 2
+    blocks = (3 * chips - 1) * n_dp + n_dp + 2
+    need = sum(blocks * item.shape[2] * item.shape[3] * 2 for item in items)
+    pieces = -(-need // (56 * 1024 * 1024))
+    tiles = [item.shape[3] // 128 for item in items]
+    results = [[] for item in items]
+    extra = []
+    for piece in range(pieces):
+        ends = [(t * piece // pieces * 128, t * (piece + 1) // pieces * 128) for t in tiles]
+        used = [i for i, (low, high) in enumerate(ends) if high > low]
+        first = piece == 0
+        outs = scatter_call(
+            n_dp,
+            n_expert,
+            [items[i][..., ends[i][0] : ends[i][1]] if pieces > 1 else items[i] for i in used],
+            cut_in if first else [],
+            cut_shapes if first else [],
+            cuts if first else lambda ins, outs: [],
+            number + piece,
+        )
+        for i, out in zip(used, outs):
+            results[i].append(out)
+        if first:
+            extra = outs[len(used) :]
+    return [one[0] if len(one) == 1 else jnp.concatenate(one, axis=1) for one in results], extra
 
 
 def shards(
@@ -110,7 +490,6 @@
     w_up,
     w_down,
 ):
-    both = ("dp", "expert")
     groups = n_dp * n_expert
     bf16 = jnp.bfloat16
     number = w_gate.shape[0]
@@ -129,22 +508,69 @@
         ],
         axis=1,
     )
-    query_small = lax.all_gather(
-        jnp.concatenate([w_query, small], axis=1), both, axis=0, tiled=True
-    )
-    query_weight = query_small[:, :D]
-    small_all = query_small[:, D:]
-    key_weight = lax.all_gather(w_key, both, axis=0, tiled=True)
-    value_weight = lax.all_gather(w_value, both, axis=0, tiled=True)
-    out_weight = lax.all_gather(w_out, both, axis=0, tiled=True)
-    routes_all = lax.all_gather(routes, both, axis=0, tiled=True)
-    cotangent_all = lax.all_gather(cotangent, both, axis=0, tiled=True)
-    gate_up = spread([w_gate, w_up], "dp", n_dp)
+    hits = jnp.any(
+        routes[:, :, None] == jnp.arange(width, dtype=jnp.int32)[None, None, :], axis=1
+    ).astype(bf16)
+    count = tokens.shape[0]
+    rows_each = w_query.shape[0]
+    extras = jnp.concatenate(
+        [cotangent, hits, jnp.pad(small, ((0, count - rows_each), (0, 0)))], axis=1
+    )
+    weights = jnp.stack([w_query, w_key, w_value, w_out])
+    depth = w_gate.shape[1]
+    early = number * 5 // 8
+    cut_shape = jax.ShapeDtypeStruct((number, n_dp * depth, part), bf16)
+
+    def row_block(size):
+        return lambda ref, block: ref.at[pl.ds(pl.multiple_of(block * size, 16), size)]
+
+    def recut(low, high):
+        def cuts(ins, outs):
+            def pair(n):
+                def source(to):
+                    columns = pl.ds(pl.multiple_of(to * part, part), part)
+                    return ins[n].at[pl.ds(low, high - low), :, columns]
+
+                def target(at):
+                    here = pl.ds(pl.multiple_of(at * depth, depth), depth)
+                    return outs[n].at[pl.ds(low, high - low), here]
+
+                return source, target
+
+            return [pair(0), pair(1)]
+
+        return cuts
+
+    weights_all, extras_all, gate_early, up_early = gather_call(
+        n_dp,
+        n_expert,
+        [weights, extras],
+        [
+            jax.ShapeDtypeStruct((4, groups * rows_each, D), bf16),
+            jax.ShapeDtypeStruct((groups * count, D + 2 * width), bf16),
+        ],
+        [
+            lambda ref, block: ref.at[
+                :, pl.ds(pl.multiple_of(block * rows_each, 16), rows_each)
+            ],
+            row_block(count),
+        ],
+        [w_gate, w_up],
+        [cut_shape, cut_shape],
+        recut(0, early),
+        {},
+        0,
+    )
+    query_weight, key_weight, value_weight, out_weight = (weights_all[i] for i in range(4))
+    small_all = (
+        extras_all[:, D + width :].reshape(groups, count, width)[:, :rows_each].reshape(-1, width)
+    )
+    cotangent_all = extras_all[:, :D]
+    hits_all = extras_all[:, D : D + experts_all]
     router_weight = small_all[:, :experts_all]
     gains = small_all[:, experts_all : experts_all + 4].astype(jnp.float32)
     attn_gain, query_gain, key_gain, mlp_gain = (gains[:, i] for i in range(4))
     inputs = tokens.astype(jnp.float32)
-    count = inputs.shape[0]
     segment, position, places = layout(lengths[0], count)
     half = HD // 2
     freq = 10000.0 ** (-2.0 * jnp.arange(half, dtype=jnp.float32) / HD)
@@ -173,17 +599,26 @@
     mlp_low = mlp_normed.astype(bf16)
     router = jax.nn.softmax(product(mlp_low, router_weight, "td,de->te"), axis=-1)
 
-    mlp_all = lax.all_gather(mlp_low, both, axis=0, tiled=True)
+    mlp_all, gate_cut, up_cut = gather_call(
+        n_dp,
+        n_expert,
+        [mlp_low],
+        [jax.ShapeDtypeStruct((groups * count, D), bf16)],
+        [row_block(count)],
+        [w_gate, w_up, gate_early, up_early],
+        [cut_shape, cut_shape],
+        recut(early, number),
+        {3: 1, 4: 2},
+        1,
+    )
+    gate_up = jnp.concatenate([gate_cut, up_cut], axis=2)
     router_all = jax.nn.softmax(product(mlp_all, router_weight, "td,de->te"), axis=-1)
     first = lax.axis_index("expert") * number
     own = lax.dynamic_slice_in_dim(router_all, first, number, 1).reshape(groups, count, number)
-    names = first + jnp.arange(number, dtype=jnp.int32)
-    hit = jnp.any(
-        routes_all.reshape(groups, count, TOPK)[..., None] == names[None, None, None, :], axis=2
-    )
+    hit = lax.dynamic_slice_in_dim(hits_all, first, number, 1).reshape(groups, count, number)
     before = jnp.tril(jnp.ones((count, count), bf16), -1)
-    slot = product(before, hit.astype(bf16), "ts,bse->bte").astype(jnp.int32)
-    slot = jnp.where(hit, slot, -1)
+    slot = product(before, hit, "ts,bse->bte").astype(jnp.int32)
+    slot = jnp.where(hit > 0, slot, -1)
     slots = jnp.arange(CAP, dtype=jnp.int32)
     table = jnp.transpose(slot, (0, 2, 1))[:, :, None, :] == slots[None, None, :, None]
     pick = table.astype(bf16)
@@ -218,19 +653,48 @@
     part_probs = jnp.transpose(part_probs, (0, 2, 1)).reshape(groups * count, number)
     spare = jnp.zeros((groups * count, width), jnp.float32)
     part_probs = lax.dynamic_update_slice_in_dim(spare, part_probs, first, 1)
-    back = lax.psum_scatter(
-        jnp.concatenate([part_grad, part_probs], axis=1).astype(bf16),
-        both,
-        scatter_dimension=0,
-        tiled=True,
-    ).astype(jnp.float32)
     grad_down_part = product((hidden * gates[..., None]).astype(bf16), grows, "becf,becd->efd")
     grad_gate_up = product(rows, grad_mids, "becd,becf->edf").astype(bf16)
-    grad_gate_part, grad_up_part = collect(grad_gate_up, "dp", n_dp, 2)
-    grad_gate_part = grad_gate_part.astype(jnp.float32)
-    grad_up_part = grad_up_part.astype(jnp.float32)
-    summed = lax.psum_scatter(part_out, both, scatter_dimension=0, tiled=True)
-    output = (middle + summed.astype(jnp.float32)).astype(bf16)
+    grad_gate_cut = grad_gate_up[..., :part]
+    grad_up_cut = grad_gate_up[..., part:]
+
+    def way_back(low, high):
+        def cuts(ins, outs):
+            def pair(n):
+                def source(to):
+                    here = pl.ds(pl.multiple_of(to * depth, depth), depth)
+                    return ins[n].at[pl.ds(low, high - low), here]
+
+                def target(at):
+                    columns = pl.ds(pl.multiple_of(at * part, part), part)
+                    return outs[n].at[:, :, columns]
+
+                return source, target
+
+            return [pair(0), pair(1)]
+
+        return cuts
+
+    def way_shape(size):
+        return jax.ShapeDtypeStruct((size, depth, ff), bf16)
+
+    back_items = [
+        jnp.concatenate([part_grad, part_probs], axis=1)
+        .astype(bf16)
+        .reshape(n_dp, n_expert, count, D + width),
+        part_out.reshape(n_dp, n_expert, count, D),
+    ]
+    sooner = number * 3 // 8
+    (back, summed), (gate_first, up_first) = scatter_all(
+        n_dp,
+        n_expert,
+        back_items,
+        [grad_gate_cut, grad_up_cut],
+        [way_shape(sooner)] * 2,
+        way_back(0, sooner),
+        8,
+    )
+    output = (middle + summed).astype(bf16)
 
     grad_final = cotangent.astype(jnp.float32)
     grad_mlp = back[:, :D]
@@ -275,14 +739,6 @@
     grad_inputs_part, grad_attn_gain = rms_backward(inputs, attn_inverse, attn_gain, grad_normed)
     grad_inputs = grad_middle + grad_inputs_part
 
-    def scattered(value):
-        return lax.psum_scatter(value.astype(bf16), both, scatter_dimension=0, tiled=True).astype(
-            jnp.float32
-        )
-
-    grad_out_part = scattered(grad_out_full)
-    grad_value_part = scattered(grad_value_full)
-    grad_key_part = scattered(grad_key_full)
     small_grads = jnp.concatenate(
         [
             grad_router_full,
@@ -294,10 +750,33 @@
         ],
         axis=1,
     )
-    query_part = scattered(jnp.concatenate([grad_query_full, small_grads], axis=1))
-    grad_query_part = query_part[:, :D]
-    grad_router_part = query_part[:, D : D + experts_all]
-    gain_parts = [query_part[:, D + experts_all + i] for i in range(4)]
+
+    def blocks_of(value):
+        return value.astype(bf16).reshape(n_dp, n_expert, rows_each, -1)
+
+    sums, (gate_last, up_last) = scatter_all(
+        n_dp,
+        n_expert,
+        [
+            blocks_of(value)
+            for value in (
+                grad_out_full,
+                grad_value_full,
+                grad_key_full,
+                grad_query_full,
+                small_grads,
+            )
+        ],
+        [grad_gate_cut, grad_up_cut],
+        [way_shape(number - sooner)] * 2,
+        way_back(sooner, number),
+        16,
+    )
+    grad_out_part, grad_value_part, grad_key_part, grad_query_part, small_part = sums
+    grad_router_part = small_part[:, :experts_all]
+    gain_parts = [small_part[:, experts_all + i] for i in range(4)]
+    grad_gate_part = jnp.concatenate([gate_first, gate_last], axis=0).astype(jnp.float32)
+    grad_up_part = jnp.concatenate([up_first, up_last], axis=0).astype(jnp.float32)
     return (
         output,
         grad_inputs,

time: 2310 us -> 1620 us (0.70)
  waiting for transfers between devices: 1230 us -> 0 us
  Pallas kernels: 0 us -> 1160 us
  blocking collectives: 325 us -> 0 us
  local copies, waits for them, and re-layouts: 295 us -> 82.4 us
  matrix products: 336 us -> 306 us
    pallas_call x0 -> x4, Pallas kernels: none -> 1160 us  [the longest x2 588 us: gather_call(): pl.pallas_call(functools.partial(gather_kernel, n_dp, n_expert, n, places...]
    reduce_scatter x5 -> x0, waiting for transfers between devices: 430 us -> none  [the longest x1 182 us: shards(): summed = lax.psum_scatter(part_out, both, scatter_dimension=0, tiled=True)]
    all_gather x6 -> x0, waiting for transfers between devices: 430 us -> none  [the longest x1 113 us: shards(): mlp_all = lax.all_gather(mlp_low, both, axis=0, tiled=True)]
    all_gather x1 -> x0, blocking collectives: 325 us -> none  [shards(): routes_all = lax.all_gather(routes, both, axis=0, tiled=True)]
    ppermute x6 -> x0, waiting for transfers between devices: 220 us -> none  [the longest x3 220 us: collect(): lax.ppermute(piece, axis, [(i, (i + step) % size) for i in range(size)])]
    unnamed x13 -> x0, waiting for transfers between devices: 149 us -> none
    dynamic_update_slice x11 -> x0, local copies, waits for them, and re-layouts: 136 us -> none  [the longest x7 116 us: collect(): lax.dynamic_update_slice_in_dim(one, piece[:, :, None, i * part:(i + 1) *...]
    convert_element_type x3 -> x0, local copies, waits for them, and re-layouts: 50.6 us -> none  [the longest x2 35.7 us: shards(): grad_gate_part = grad_gate_part.astype(jnp.float32)]
  transfers between devices with their start and end apart: 18 -> 0, of which waited for: 12 -> 0; matrix products, arithmetic and copies ran while one was open for 23% -> 0% of each run, Pallas kernels for 0% -> 0%
where the time goes in v2:
time: 1620 us
  Pallas kernels  1160 us (72%)
  matrix products  306 us (19%)
  local copies, waits for them, and re-layouts  82.4 us (5%)
  other arithmetic  70.1 us (4%)
    pallas_call x2, Pallas kernels, gather_call(): pl.pallas_call(functools.partial(gather_kernel, n_dp, n_expert, n, places...  588 us
    pallas_call x2, Pallas kernels, scatter_call(): pl.pallas_call(functools.partial(scatter_kernel, n_dp, n_expert, n, m, cu...  571 us
    dot_general x32, matrix products, product(): return jnp.einsum(form, left, right, preferred_element_type=jnp.float32)  304 us

profile of v2, /device:TPU:0, one launch (start us, length us, event | category | flops | bytes accessed | tf_op | source)
XLA Modules:
  0.0 1619.5 jit_solution(6178348299713321688)
XLA Ops:
  1.5 1.2 fusion.94
  10.0 1.9 fusion.107.refs_1_
  11.9 2.3 pad_maximum_fusion.2.refs_0_
  14.2 386.4 %shard_map.263 = (bf16[4,2048,2048]{2,1,0:T(8,128)(2,1)}, bf16[4096,2304]{1,0:T(8,128)(2,1)}, bf16[8,2048,256]{2,1,0:T(8,128)(2,1)}, bf16[8,2048,256]{2,1,0:T(8,128)(2,1)}) custom-call(bf16[4,64,2048]{2,1,0:T(8,128)(2,1)} %pad_maximum_fusion.2.refs_0_, bf16[128,2304]{1,0:T(8,128)(2,1)} %fusion.107.refs_1_, bf16[8,512,1024]{2,1,0:T(8,128)(2,1)} %refs_1_.1, ...), custom_call_target="tpu_custom_call" | custom-call | tf_op jit(solution)/shard_map/pallas_call | solution.py:261
  400.6 1.3 slice.113
  403.1 1.3 slice.99
  404.4 14.7 slice.115
  419.4 2.0 slice_reduce_fusion
  421.4 5.5 fusion.87
  426.9 4.8 multiply_reduce_fusion.7
  433.0 4.8 multiply_reduce_fusion.6
  439.5 1.4 subtract_convert_fusion.3
  440.9 1.8 fusion.156
  442.7 2.9 convolution_convert_fusion.8
  445.6 4.9 multiply_reduce_fusion.5
  453.1 16.9 %convolution_convert_fusion.1 = bf16[32,8,24,2048]{3,2,1,0:T(8,128)(2,1)} fusion(bf16[32,128,2048,1]{2,1,3,0:T(8,128)(2,1)} %bitcast.221, s32[32,8,128]{2,1,0:T(8,128)S(1)} %fusion.93), kind=kOutput, calls=%fused_computation.22 | convolution fusion | flops 3234594816 | bytes 42074112 | tf_op jit(solution)/shard_map/bect,btd->becd/dot_general | solution.py:21
  470.0 202.0 %shard_map.264 = (bf16[4096,2048]{1,0:T(8,128)(2,1)}, bf16[8,2048,256]{2,1,0:T(8,128)(2,1)}, bf16[8,2048,256]{2,1,0:T(8,128)(2,1)}) custom-call(bf16[128,2048]{1,0:T(8,128)(2,1)} %copy-done.6, bf16[8,512,1024]{2,1,0:T(8,128)(2,1)} %refs_1_.1, bf16[8,512,1024]{2,1,0:T(8,128)(2,1)} %refs_2_.3, ...), custom_call_target="tpu_custom_call", output_to_operand_aliasing={{1}: (3, {}), {2}: (4, {})} | custom-call | tf_op jit(solution)/shard_map/pallas_call | solution.py:261
  672.0 11.0 fusion.157
  683.2 7.3 constant_dynamic-update-slice_fusion.1
  690.5 7.3 constant_dynamic-update-slice_fusion
  697.8 17.1 %convolution_convert_fusion = bf16[32,8,24,2048]{3,2,1,0:T(8,128)(2,1)} fusion(bf16[32,128,2048,1]{2,1,3,0:T(8,128)(2,1)} %bitcast.220, s32[32,8,128]{2,1,0:T(8,128)S(1)} %fusion.93), kind=kOutput, calls=%fused_computation.21 | convolution fusion | flops 3234594816 | bytes 42074112 | tf_op jit(solution)/shard_map/bect,btd->becd/dot_general | solution.py:21
  714.9 23.6 %fusion.55 = f32[32,8,24,512]{3,2,0,1:T(8,128)} fusion(bf16[32,8,24,2048]{3,2,1,0:T(8,128)(2,1)} %convolution_convert_fusion, bf16[8,2048,512]{2,1,0:T(8,128)(2,1)} %constant_dynamic-update-slice_fusion), kind=kOutput, calls=%fused_computation.69 | convolution fusion | flops 12884901888 | bytes 54525952 | tf_op jit(solution)/shard_map/becd,edf->becf/dot_general | solution.py:21
  738.5 22.4 %fusion.51 = (f32[32,8,24]{2,0,1:T(8,128)S(1)}, bf16[32,8,24,256]{3,2,0,1:T(8,128)(2,1)}, f32[8,32,24,256]{3,2,1,0:T(8,128)}) fusion(f32[32,8,24,512]{3,2,0,1:T(8,128)} %fusion.55, bf16[8,256,2048]{2,1,0:T(8,128)(2,1)} %param.31, bf16[32,8,24,2048]{3,2,1,0:T(8,128)(2,1)} %convolution_convert_fusion.1), kind=kOutput, calls=%fused_computation.60 | convolution fusion | flops 6456600576 | bytes 55599104 | tf_op jit(solution)/shard_map/becd,efd->becf/dot_general | solution.py:21
  761.0 2.7 select_reduce_fusion.1
  764.4 23.0 %fusion.48 = f32[8,256,2048]{2,1,0:T(8,128)} fusion(bf16[32,8,24,2048]{3,2,1,0:T(8,128)(2,1)} %convolution_convert_fusion.1, f32[32,8,24]{2,0,1:T(8,128)S(1)} %copy.234, f32[32,8,24,512]{3,2,0,1:T(8,128)} %fusion.55), kind=kOutput, calls=%fused_computation.56 | convolution fusion | flops 6453460992 | bytes 54550528 | tf_op jit(solution)/shard_map/becf,becd->efd/dot_general | solution.py:21
  787.4 9.8 multiply_convert_fusion.2
  797.2 21.8 %bitcast_convert_fusion = bf16[8,2048,512]{2,1,0:T(8,128)(2,1)} fusion(bf16[32,8,24,2048]{3,2,1,0:T(8,128)(2,1)} %convolution_convert_fusion, bf16[32,8,24,256]{3,2,0,1:T(8,128)(2,1)} %get-tuple-element.75, bf16[32,8,24,256]{3,2,0,1:T(8,128)(2,1)S(1)} %get-tuple-element.74), kind=kOutput, calls=%fused_computation.3 | convolution fusion | flops 12905873408 | bytes 48234496 | tf_op jit(solution)/shard_map/becd,becf->edf/dot_general | solution.py:21
  819.0 11.4 fusion.153
  831.0 3.9 dynamic_update_slice.3
  834.9 24.0 %fusion.15 = bf16[8,2048,32,24]{1,3,0,2:T(8,128)(2,1)} fusion(bf16[8,2048,512]{2,1,0:T(8,128)(2,1)} %constant_dynamic-update-slice_fusion, bf16[32,8,24,256]{3,2,0,1:T(8,128)(2,1)} %get-tuple-element.75, bf16[32,8,24,256]{3,2,0,1:T(8,128)(2,1)} %copy-done.15), kind=kOutput, calls=%fused_computation.19 | convolution fusion | flops 12897484800 | bytes 48234496 | tf_op jit(solution)/shard_map/becf,edf->becd/dot_general | solution.py:21
  859.0 16.7 %bitcast_convert_fusion.2 = bf16[32,128,2048]{2,1,0:T(8,128)(2,1)} fusion(bf16[8,2048,32,24]{1,3,0,2:T(8,128)(2,1)} %fusion.15, s32[32,8,128]{2,1,0:T(8,128)S(1)} %copy-done.11), kind=kOutput, calls=%fused_computation.5 | convolution fusion | flops 3230400512 | bytes 42074112 | tf_op jit(solution)/shard_map/bect,becd->btd/dot_general | solution.py:21
  875.6 14.2 pad_maximum_fusion.refs_0_
  889.9 22.1 %fusion.22 = f32[8,32,24,2048]{3,2,0,1:T(8,128)} fusion(bf16[8,256,2048]{2,1,0:T(8,128)(2,1)} %param.31, bf16[32,8,24,256]{3,2,0,1:T(8,128)(2,1)} %get-tuple-element.71), kind=kOutput, calls=%fused_computation.26 | convolution fusion | flops 6442450944 | bytes 61865984 | tf_op jit(solution)/shard_map/becf,efd->becd/dot_general | solution.py:21
  912.0 23.5 %bitcast_convert_fusion.1 = bf16[32,128,2048]{2,1,0:T(8,128)(2,1)} fusion(f32[8,32,24,2048]{3,2,0,1:T(8,128)} %fusion.22, f32[32,8,24]{2,1,0:T(8,128)S(1)} %copy-done.32, s32[32,8,128]{2,1,0:T(8,128)S(1)} %copy-done.11), kind=kOutput, calls=%fused_computation.4 | convolution fusion | flops 3255566336 | bytes 67264512 | tf_op jit(solution)/shard_map/bect,becd->btd/dot_general | solution.py:21
  935.6 237.5 %shard_map.265 = (f32[128,2176]{1,0:T(8,128)}, f32[128,2048]{1,0:T(8,128)}, bf16[3,512,1024]{2,1,0:T(8,128)(2,1)}, bf16[3,512,1024]{2,1,0:T(8,128)(2,1)}) custom-call(bf16[4,8,128,2176]{3,2,1,0:T(8,128)(2,1)} %pad_maximum_fusion.refs_0_, bf16[4,8,128,2048]{3,2,1,0:T(8,128)(2,1)} %bitcast.222, bf16[8,2048,256]{2,1,0:T(8,128)(2,1)} %get-tuple-element.77.refs_2_.refs_5_, ...), custom_call_target="tpu_custom_call" | custom-call | tf_op jit(solution)/shard_map/pallas_call | solution.py:419
  1173.1 1.0 multiply_reduce_fusion.8
  1174.1 1.2 convolution_convert_fusion.6
  1175.4 1.8 multiply_reduce_fusion
  1177.2 2.4 subtract_add_fusion
  1180.7 1.8 concatenate.78
  1182.5 7.1 fusion.74
  1189.5 2.0 copy.283
  1191.6 3.0 convolution_convert_fusion.7
  1194.6 1.8 multiply_reduce_fusion.3
  1196.6 1.6 multiply_convert_fusion.4
  1203.2 1.8 concatenate.76
  1205.0 6.4 fusion.28
  1211.5 6.4 fusion.65
  1218.0 5.6 fusion.102
  1223.6 1.4 fusion.99
  1225.0 1.8 concatenate.75
  1227.8 3.9 concatenate.72.refs_4_
  1231.7 6.8 convolution_convert_fusion.5
  1238.5 5.9 convolution_convert_fusion.4
  1244.4 5.7 convolution_convert_fusion.2
  1250.1 5.7 convolution_convert_fusion.3
  1255.7 333.2 %shard_map.266 = (f32[64,2048]{1,0:T(8,128)}, f32[64,2048]{1,0:T(8,128)}, f32[64,2048]{1,0:T(8,128)}, f32[64,2048]{1,0:T(8,128)}, f32[64,128]{1,0:T(8,128)}, /*i...) custom-call(bf16[4,8,64,2048]{3,2,1,0:T(8,128)(2,1)} %bitcast.224, bf16[4,8,64,2048]{3,2,1,0:T(8,128)(2,1)} %bitcast.225, ...), custom_call_target="tpu_custom_call" | custom-call | tf_op jit(solution)/shard_map/pallas_call | solution.py:419
  1588.9 1.7 slice_reduce_fusion.4
  1590.6 10.8 maximum_convert_fusion
  1601.4 9.7 maximum_convert_fusion.1
  1611.2 1.9 copy.340
  1613.0 1.9 copy.341
  1614.9 1.9 copy.342
  1616.8 1.9 copy.343
  (191 shorter events, 24.1 us)
Async XLA Ops:
  3.2 429.7 %copy-start.50 = (f32[128]{0:T(128)}, f32[128]{0:T(128)S(1)}, u32[]{:S(2)}) copy-start(f32[128]{0:T(128)S(1)} %get-tuple-element.100) | copy-start | bytes 1540
  4.1 438.7 %copy-start.52 = (pred[128,128]{0,1:T(8,128)(4,1)}, pred[128,128]{0,1:T(8,128)(4,1)S(1)}, u32[]{:S(2)}) copy-start(pred[128,128]{0,1:T(8,128)(4,1)S(1)} %fusion.124) | copy-start | bytes 49156
  10.0 429.5 %copy-start.38 = (f32[128,64]{1,0:T(8,128)}, f32[128,64]{1,0:T(8,128)S(1)}, u32[]{:S(2)}) copy-start(f32[128,64]{1,0:T(8,128)S(1)} %get-tuple-element.98) | copy-start | bytes 98308
  403.1 358.0 %copy-start.10 = (s32[32,8,128]{2,1,0:T(8,128)}, s32[32,8,128]{2,1,0:T(8,128)S(1)}, u32[]{:S(2)}) copy-start(s32[32,8,128]{2,1,0:T(8,128)S(1)} %fusion.93) | copy-start | bytes 393220
  404.4 17.0 %copy-start = (bf16[128,2048]{1,0:T(8,128)(2,1)S(1)}, bf16[128,2048]{1,0:T(8,128)(2,1)}, u32[]{:S(2)}) copy-start(bf16[128,2048]{1,0:T(8,128)(2,1)} %param.16) | copy-start | bytes 1572868
  419.2 252.8 %copy-start.8 = (bf16[32,64,128]{2,1,0:T(8,128)(2,1)}, bf16[32,64,128]{2,1,0:T(8,128)(2,1)S(1)}, u32[]{:S(2)}) copy-start(bf16[32,64,128]{2,1,0:T(8,128)(2,1)S(1)} %slice.132) | copy-start | bytes 1572868
  421.4 10.9 copy-start.44
  421.4 11.6 copy-start.35
  421.4 17.0 %copy-start.46 = (f32[2048]{0:T(1024)}, f32[2048]{0:T(1024)S(1)}, u32[]{:S(2)}) copy-start(f32[2048]{0:T(1024)S(1)} %get-tuple-element.59) | copy-start | bytes 24580
  421.4 29.8 %copy-start.48 = (f32[2048]{0:T(1024)}, f32[2048]{0:T(1024)S(1)}, u32[]{:S(2)}) copy-start(f32[2048]{0:T(1024)S(1)} %get-tuple-element.58) | copy-start | bytes 24580
  431.7 6.1 copy-start.2
  432.3 5.5 copy-start.57
  438.4 1.1 copy-start.59
  440.9 9.7 copy-start.16
  440.9 9.7 copy-start.18
  440.9 9.7 copy-start.20
  440.9 9.7 copy-start.22
  442.7 7.9 copy-start.53
  451.8 18.2 %copy-start.6 = (bf16[128,2048]{1,0:T(8,128)(2,1)}, bf16[128,2048]{1,0:T(8,128)(2,1)S(1)}, u32[]{:S(2)}) copy-start(bf16[128,2048]{1,0:T(8,128)(2,1)S(1)} %multiply_convert_fusion.5.refs_0_) | copy-start | bytes 1572868
  452.3 17.7 %copy-start.55 = (f32[128]{0:T(128)}, f32[128]{0:T(128)S(1)}, u32[]{:S(2)}) copy-start(f32[128]{0:T(128)S(1)} %get-tuple-element.118) | copy-start | bytes 1540
  452.4 17.6 %copy-start.33 = (f32[128,64]{1,0:T(8,128)}, f32[128,64]{1,0:T(8,128)S(1)}, u32[]{:S(2)}) copy-start(f32[128,64]{1,0:T(8,128)S(1)} %copy.242) | copy-start | bytes 98308
  797.2 21.8 %copy-start.15 = (bf16[32,8,24,256]{3,2,0,1:T(8,128)(2,1)}, bf16[32,8,24,256]{3,2,0,1:T(8,128)(2,1)S(1)}, u32[]{:S(2)}) copy-start(bf16[32,8,24,256]{3,2,0,1:T(8,128)(2,1)S(1)} %get-tuple-element.74) | copy-start | bytes 9437188
  819.0 11.4 copy-start.43
  834.9 24.0 %copy-start.11 = (s32[32,8,128]{2,1,0:T(8,128)S(1)}, s32[32,8,128]{2,1,0:T(8,128)}, u32[]{:S(2)}) copy-start(s32[32,8,128]{2,1,0:T(8,128)} %copy-done.10) | copy-start | bytes 393220
  889.9 22.1 %copy-start.32 = (f32[32,8,24]{2,1,0:T(8,128)S(1)}, f32[32,8,24]{2,1,0:T(8,128)}, u32[]{:S(2)}) copy-start(f32[32,8,24]{2,1,0:T(8,128)} %copy-done.31) | copy-start | bytes 73732
  935.5 237.6 %copy-start.34 = (f32[128,64]{1,0:T(8,128)S(1)}, f32[128,64]{1,0:T(8,128)}, u32[]{:S(2)}) copy-start(f32[128,64]{1,0:T(8,128)} %copy-done.33) | copy-start | bytes 98308
  935.5 237.6 %copy-start.56 = (f32[128]{0:T(128)S(1)}, f32[128]{0:T(128)}, u32[]{:S(2)}) copy-start(f32[128]{0:T(128)} %copy-done.55) | copy-start | bytes 1540
  935.5 237.6 %copy-start.61 = (f32[128]{0:T(128)S(1)}, f32[128]{0:T(128)}, u32[]{:S(2)}) copy-start(f32[128]{0:T(128)} %fusion.127) | copy-start | bytes 1540
  935.5 238.6 %copy-start.7 = (bf16[128,2048]{1,0:T(8,128)(2,1)S(1)}, bf16[128,2048]{1,0:T(8,128)(2,1)}, u32[]{:S(2)}) copy-start(bf16[128,2048]{1,0:T(8,128)(2,1)} %copy-done.6) | copy-start | bytes 1572868
  935.5 239.9 %copy-start.9 = (bf16[32,64,128]{2,1,0:T(8,128)(2,1)S(1)}, bf16[32,64,128]{2,1,0:T(8,128)(2,1)}, u32[]{:S(2)}) copy-start(bf16[32,64,128]{2,1,0:T(8,128)(2,1)} %copy-done.8) | copy-start | bytes 1572868
  935.5 239.8 %copy-start.13 = (f32[128,2048]{1,0:T(8,128)S(1)}, f32[128,2048]{1,0:T(8,128)}, u32[]{:S(2)}) copy-start(f32[128,2048]{1,0:T(8,128)} %copy-done.12) | copy-start | bytes 3145732
  935.5 239.8 %copy-start.49 = (f32[2048]{0:T(1024)S(1)}, f32[2048]{0:T(1024)}, u32[]{:S(2)}) copy-start(f32[2048]{0:T(1024)} %copy-done.48) | copy-start | bytes 24580
  935.5 239.8 %copy-start.63 = (f32[128]{0:T(128)S(1)}, f32[128]{0:T(128)}, u32[]{:S(2)}) copy-start(f32[128]{0:T(128)} %copy-done.62) | copy-start | bytes 1540
  935.5 241.7 %copy-start.24 = (bf16[128,2048]{1,0:T(8,128)(2,1)S(1)}, bf16[128,2048]{1,0:T(8,128)(2,1)}, u32[]{:S(2)}) copy-start(bf16[128,2048]{1,0:T(8,128)(2,1)} %param.17) | copy-start | bytes 1572868
  935.5 241.7 %copy-start.67 = (f32[128]{0:T(128)S(1)}, f32[128]{0:T(128)}, u32[]{:S(2)}) copy-start(f32[128]{0:T(128)} %get-tuple-element.105) | copy-start | bytes 1540
  1179.6 12.0 copy-start.17
  1179.6 12.0 copy-start.19
  1179.6 12.0 copy-start.21
  1179.6 12.0 copy-start.23
  1179.6 12.0 copy-start.54
  1191.6 7.6 copy-start.39
  1191.6 7.6 copy-start.42
  1196.5 3.7 copy-start.3
  1196.5 3.7 copy-start.5
  1196.5 3.7 copy-start.45
  1196.5 3.7 copy-start.47
  1196.5 3.7 copy-start.58
  1196.6 3.7 copy-start.60
  1198.6 2.5 copy-start.66
  1199.2 2.5 copy-start.65
  1201.7 3.4 copy-start.27
  1202.2 9.3 copy-start.29
  1211.5 6.4 copy-start.1
  1211.5 6.4 copy-start.36
  1211.5 6.4 copy-start.40
  1211.5 6.4 copy-start.51
  1217.9 5.7 copy-start.64
  1217.9 9.8 copy-start.25
  1218.0 9.8 copy-start.26
  1231.7 6.8 copy-start.41
  1238.5 5.9 copy-start.30
  1244.4 5.7 copy-start.28
  1590.6 10.8 copy-start.14
  1601.4 17.2 %copy-start.37 = (f32[64,128]{1,0:T(8,128)S(1)}, f32[64,128]{1,0:T(8,128)}, u32[]{:S(2)}) copy-start(f32[64,128]{1,0:T(8,128)} %get-tuple-element.45) | copy-start | bytes 98308
  (4 other events, 3.7 us)

commit v3 on v2

--- a/solution.py
+++ b/solution.py
@@ -468,6 +468,239 @@
         if first:
             extra = outs[len(used) :]
     return [one[0] if len(one) == 1 else jnp.concatenate(one, axis=1) for one in results], extra
+
+
+def dot(left, right, dims):
+    return lax.dot_general(
+        left, right, ((dims[:1], dims[1:]), ((), ())), preferred_element_type=jnp.float32
+    )
+
+
+def picks(slots_ref, number):
+    pair = slots_ref.shape[2]
+    rows = lax.broadcasted_iota(jnp.int32, (2 * CAP, pair), 0)
+    return [slots_ref[0, e : e + 1, :] == rows for e in range(number)]
+
+
+def pick_kernel(number, experts_all, slots_ref, x_ref, g_ref, router_ref, rows_ref, grows_ref, gates_ref):
+    chosen = picks(slots_ref, number)
+    pick = jnp.concatenate(chosen, axis=0).astype(jnp.bfloat16)
+    size = 2 * CAP
+    x = x_ref[...]
+    logits = dot(router_ref[...], x, (0, 1))
+    names = lax.broadcasted_iota(jnp.int32, logits.shape, 0)
+    logits = jnp.where(names < experts_all, logits, -1e30)
+    weights = jnp.exp(logits - jnp.max(logits, axis=0, keepdims=True))
+    probs = weights / jnp.sum(weights, axis=0, keepdims=True)
+    for e in range(number):
+        gate = jnp.sum(jnp.where(chosen[e], probs[e : e + 1, :], 0.0), axis=1, keepdims=True)
+        gates_ref[e] = jnp.broadcast_to(gate, (size, 128))
+    picked = dot(pick, x, (1, 0)).astype(jnp.bfloat16)
+    for e in range(number):
+        rows_ref[e] = picked[e * size : (e + 1) * size]
+    picked = dot(pick, g_ref[...], (1, 0)).astype(jnp.bfloat16)
+    for e in range(number):
+        grows_ref[e] = picked[e * size : (e + 1) * size]
+
+
+def expert_kernel(
+    steps,
+    half,
+    first_ref,
+    x_ref,
+    g_ref,
+    gates_ref,
+    gate_ref,
+    up_ref,
+    down_ref,
+    y_ref,
+    dx_ref,
+    probs_ref,
+    dgate_ref,
+    dup_ref,
+    ddown_ref,
+    sum_gate,
+    sum_up,
+):
+    bf16 = jnp.bfloat16
+    x, g = x_ref[0], g_ref[0]
+    rows, width = x.shape
+    gate = gates_ref[0][:, :1]
+    gate_mid = dot(x, gate_ref[0], (1, 0))
+    up_mid = dot(x, up_ref[0], (1, 0))
+    sigmoid = 1.0 / (1.0 + jnp.exp(-gate_mid))
+    silu = gate_mid * sigmoid
+    hidden = silu * up_mid
+    hidden_low = hidden.astype(bf16)
+    grad_plain = dot(g, down_ref[0], (1, 1))
+    grad_gates = jnp.sum(grad_plain * hidden_low.astype(jnp.float32), axis=1, keepdims=True)
+    high = grad_gates.astype(bf16).astype(jnp.float32)
+    lane = lax.broadcasted_iota(jnp.int32, (rows, 128), 1)
+    name = first_ref[0] + pl.program_id(0)
+    probs_ref[0] = (
+        jnp.where(lane == name, high, 0.0) + jnp.where(lane == name + half, grad_gates - high, 0.0)
+    ).astype(bf16)
+    grad_hidden = grad_plain * gate
+    grad_gate = (
+        grad_hidden * up_mid * sigmoid * (1.0 + gate_mid * (1.0 - sigmoid))
+    ).astype(bf16)
+    grad_up = (grad_hidden * silu).astype(bf16)
+    scaled = (hidden * gate).astype(bf16)
+    piece = 512
+    for at in range(0, width, piece):
+        y_ref[0, :, at : at + piece] = (
+            dot(hidden_low, down_ref[0, :, at : at + piece], (1, 0)) * gate
+        ).astype(bf16)
+        dx_ref[0, :, at : at + piece] = (
+            dot(grad_gate, gate_ref[0, at : at + piece, :], (1, 1))
+            + dot(grad_up, up_ref[0, at : at + piece, :], (1, 1))
+        ).astype(bf16)
+    step = pl.program_id(1)
+    for at in range(0, width, piece):
+        x_part = x_ref[0, :, at : at + piece]
+        here_gate = dot(x_part, grad_gate, (0, 0))
+        here_up = dot(x_part, grad_up, (0, 0))
+        here_down = dot(scaled, g_ref[0, :, at : at + piece], (0, 0))
+        if steps == 1:
+            dgate_ref[0, at : at + piece, :] = here_gate.astype(bf16)
+            dup_ref[0, at : at + piece, :] = here_up.astype(bf16)
+            ddown_ref[0, :, at : at + piece] = here_down
+            continue
+
+        @pl.when(step == 0)
+        def _():
+            sum_gate[at : at + piece, :] = here_gate
+            sum_up[at : at + piece, :] = here_up
+            ddown_ref[0, :, at : at + piece] = here_down
+
+        @pl.when(step > 0)
+        def _():
+            sum_gate[at : at + piece, :] += here_gate
+            sum_up[at : at + piece, :] += here_up
+            ddown_ref[0, :, at : at + piece] += here_down
+
+        @pl.when(step == steps - 1)
+        def _():
+            dgate_ref[0, at : at + piece, :] = sum_gate[at : at + piece, :].astype(bf16)
+            dup_ref[0, at : at + piece, :] = sum_up[at : at + piece, :].astype(bf16)
+
+
+def place_kernel(number, slots_ref, y_ref, dx_ref, probs_ref, out_ref, back_ref):
+    pick = jnp.concatenate(picks(slots_ref, number), axis=0).astype(jnp.bfloat16)
+    width = out_ref.shape[1]
+    piece = 512
+    flat = number * 2 * CAP
+    for at in range(0, width, piece):
+        part = y_ref[:, :, at : at + piece].reshape(flat, piece)
+        out_ref[:, at : at + piece] = dot(pick, part, (0, 0)).astype(jnp.bfloat16)
+        part = dx_ref[:, :, at : at + piece].reshape(flat, piece)
+        back_ref[:, at : at + piece] = dot(pick, part, (0, 0)).astype(jnp.bfloat16)
+    part = probs_ref[...].reshape(flat, 128)
+    back_ref[:, width:] = dot(pick, part, (0, 0)).astype(jnp.bfloat16)
+
+
+BIG = 60 * 1024 * 1024
+
+
+def pick_call(number, experts_all, slots, x_all, g_all, router):
+    pairs, _, pair = slots.shape
+    bf16 = jnp.bfloat16
+    size = 2 * CAP
+    rows = pl.BlockSpec((number, size, D), lambda p: (0, p, 0))
+    tokens = pl.BlockSpec((pair, D), lambda p: (p, 0))
+    return pl.pallas_call(
+        functools.partial(pick_kernel, number, experts_all),
+        grid=(pairs,),
+        in_specs=[
+            pl.BlockSpec((1, number, pair), lambda p: (p, 0, 0)),
+            tokens,
+            tokens,
+            pl.BlockSpec(router.shape, lambda p: (0, 0)),
+        ],
+        out_specs=[rows, rows, pl.BlockSpec((number, size, 128), lambda p: (0, p, 0))],
+        out_shape=[
+            jax.ShapeDtypeStruct((number, pairs * size, D), bf16),
+            jax.ShapeDtypeStruct((number, pairs * size, D), bf16),
+            jax.ShapeDtypeStruct((number, pairs * size, 128), jnp.float32),
+        ],
+        compiler_params=pltpu.CompilerParams(vmem_limit_bytes=BIG),
+    )(slots, x_all, g_all, router)
+
+
+def expert_call(first, half, rows, grows, gates, gate, up, down):
+    number, depth, _ = rows.shape
+    part = gate.shape[2]
+    size = depth
+    while size > 768:
+        size //= 2
+    steps = depth // size
+    bf16 = jnp.bfloat16
+    f32 = jnp.float32
+
+    def by_rows(width):
+        return pl.BlockSpec((1, size, width), lambda e, r: (e, r, 0))
+
+    def whole(*shape):
+        return pl.BlockSpec((1, *shape), lambda e, r: (e, 0, 0))
+
+    keep = (D, part) if steps > 1 else (16, 128)
+    return pl.pallas_call(
+        functools.partial(expert_kernel, steps, half),
+        grid=(number, steps),
+        in_specs=[
+            pl.BlockSpec(memory_space=pltpu.SMEM),
+            by_rows(D),
+            by_rows(D),
+            by_rows(128),
+            whole(D, part),
+            whole(D, part),
+            whole(part, D),
+        ],
+        out_specs=[
+            by_rows(D),
+            by_rows(D),
+            by_rows(128),
+            whole(D, part),
+            whole(D, part),
+            whole(part, D),
+        ],
+        out_shape=[
+            jax.ShapeDtypeStruct((number, depth, D), bf16),
+            jax.ShapeDtypeStruct((number, depth, D), bf16),
+            jax.ShapeDtypeStruct((number, depth, 128), bf16),
+            jax.ShapeDtypeStruct((number, D, part), bf16),
+            jax.ShapeDtypeStruct((number, D, part), bf16),
+            jax.ShapeDtypeStruct((number, part, D), f32),
+        ],
+        scratch_shapes=[pltpu.VMEM(keep, f32), pltpu.VMEM(keep, f32)],
+        compiler_params=pltpu.CompilerParams(vmem_limit_bytes=BIG),
+    )(first, rows, grows, gates, gate, up, down)
+
+
+def place_call(number, slots, y, dx, probs):
+    pairs, _, pair = slots.shape
+    bf16 = jnp.bfloat16
+    size = 2 * CAP
+    rows = pl.BlockSpec((number, size, D), lambda p: (0, p, 0))
+    return pl.pallas_call(
+        functools.partial(place_kernel, number),
+        grid=(pairs,),
+        in_specs=[
+            pl.BlockSpec((1, number, pair), lambda p: (p, 0, 0)),
+            rows,
+            rows,
+            pl.BlockSpec((number, size, 128), lambda p: (0, p, 0)),
+        ],
+        out_specs=[
+            pl.BlockSpec((pair, D), lambda p: (p, 0)),
+            pl.BlockSpec((pair, D + 128), lambda p: (p, 0)),
+        ],
+        out_shape=[
+            jax.ShapeDtypeStruct((pairs * pair, D), bf16),
+            jax.ShapeDtypeStruct((pairs * pair, D + 128), bf16),
+        ],
+        compiler_params=pltpu.CompilerParams(vmem_limit_bytes=BIG),
+    )(slots, y, dx, probs)
 
 
 def shards(
@@ -565,7 +798,6 @@
     small_all = (
         extras_all[:, D + width :].reshape(groups, count, width)[:, :rows_each].reshape(-1, width)
     )
-    cotangent_all = extras_all[:, :D]
     hits_all = extras_all[:, D : D + experts_all]
     router_weight = small_all[:, :experts_all]
     gains = small_all[:, experts_all : experts_all + 4].astype(jnp.float32)
@@ -611,52 +843,23 @@
         {3: 1, 4: 2},
         1,
     )
-    gate_up = jnp.concatenate([gate_cut, up_cut], axis=2)
-    router_all = jax.nn.softmax(product(mlp_all, router_weight, "td,de->te"), axis=-1)
     first = lax.axis_index("expert") * number
-    own = lax.dynamic_slice_in_dim(router_all, first, number, 1).reshape(groups, count, number)
     hit = lax.dynamic_slice_in_dim(hits_all, first, number, 1).reshape(groups, count, number)
     before = jnp.tril(jnp.ones((count, count), bf16), -1)
-    slot = product(before, hit, "ts,bse->bte").astype(jnp.int32)
-    slot = jnp.where(hit > 0, slot, -1)
-    slots = jnp.arange(CAP, dtype=jnp.int32)
-    table = jnp.transpose(slot, (0, 2, 1))[:, :, None, :] == slots[None, None, :, None]
-    pick = table.astype(bf16)
-    gates = jnp.sum(
-        jnp.where(table, jnp.transpose(own, (0, 2, 1))[:, :, None, :], 0.0), axis=3
-    )
-    rows = product(pick, mlp_all.reshape(groups, count, D), "bect,btd->becd").astype(bf16)
-    grows = product(pick, cotangent_all.reshape(groups, count, D), "bect,btd->becd").astype(bf16)
-    mids = product(rows, gate_up, "becd,edf->becf")
-    gate_mid = mids[..., :part]
-    up_mid = mids[..., part:]
-    sigmoid = jax.nn.sigmoid(gate_mid)
-    silu = gate_mid * sigmoid
-    hidden = silu * up_mid
-    hidden_low = hidden.astype(bf16)
-    result = product(hidden_low, w_down, "becf,efd->becd")
-    weighted = (result * gates[..., None]).astype(bf16)
-    part_out = product(pick, weighted, "bect,becd->btd").reshape(groups * count, D).astype(bf16)
-    grad_plain = product(grows, w_down, "becd,efd->becf")
-    grad_gates = jnp.sum(grad_plain * hidden_low.astype(jnp.float32), axis=3)
-    grad_hidden = grad_plain * gates[..., None]
-    grad_gate_low = (grad_hidden * up_mid * sigmoid * (1.0 + gate_mid * (1.0 - sigmoid))).astype(
-        bf16
-    )
-    grad_up_low = (grad_hidden * silu).astype(bf16)
-    grad_mids = jnp.concatenate([grad_gate_low, grad_up_low], axis=3)
-    grad_rows = product(grad_mids, gate_up, "becf,edf->becd").astype(bf16)
-    part_grad = product(pick, grad_rows, "bect,becd->btd").reshape(groups * count, D)
-    part_probs = jnp.sum(
-        jnp.where(table, grad_gates[..., None], 0.0), axis=2
-    )
-    part_probs = jnp.transpose(part_probs, (0, 2, 1)).reshape(groups * count, number)
-    spare = jnp.zeros((groups * count, width), jnp.float32)
-    part_probs = lax.dynamic_update_slice_in_dim(spare, part_probs, first, 1)
-    grad_down_part = product((hidden * gates[..., None]).astype(bf16), grows, "becf,becd->efd")
-    grad_gate_up = product(rows, grad_mids, "becd,becf->edf").astype(bf16)
-    grad_gate_cut = grad_gate_up[..., :part]
-    grad_up_cut = grad_gate_up[..., part:]
+    slot = product(before, hit, "ts,bse->bet").astype(jnp.int32)
+    slot = jnp.where(jnp.transpose(hit, (0, 2, 1)) > 0, slot, -1)
+    slot = slot.reshape(groups // 2, 2, number, count)
+    shift = jnp.array([0, CAP], jnp.int32)[None, :, None, None]
+    slots = jnp.transpose(jnp.where(slot < 0, -1, slot + shift), (0, 2, 1, 3))
+    slots = slots.reshape(groups // 2, number, 2 * count)
+    router_own = jnp.pad(
+        jnp.roll(router_weight, -first, axis=1), ((0, 0), (0, width - experts_all))
+    )
+    rows, grows, gates = pick_call(number, experts_all, slots, mlp_all, extras_all, router_own)
+    weighted, grad_rows, grad_gates, grad_gate_cut, grad_up_cut, grad_down_part = expert_call(
+        first[None], experts_all, rows, grows, gates, gate_cut, up_cut, w_down
+    )
+    part_out, part_back = place_call(number, slots, weighted, grad_rows, grad_gates)
 
     def way_back(low, high):
         def cuts(ins, outs):
@@ -679,9 +882,7 @@
         return jax.ShapeDtypeStruct((size, depth, ff), bf16)
 
     back_items = [
-        jnp.concatenate([part_grad, part_probs], axis=1)
-        .astype(bf16)
-        .reshape(n_dp, n_expert, count, D + width),
+        part_back.reshape(n_dp, n_expert, count, D + width),
         part_out.reshape(n_dp, n_expert, count, D),
     ]
     sooner = number * 3 // 8
@@ -698,7 +899,7 @@
 
     grad_final = cotangent.astype(jnp.float32)
     grad_mlp = back[:, :D]
-    grad_router_probs = back[:, D : D + experts_all]
+    grad_router_probs = back[:, D : D + experts_all] + back[:, D + experts_all :]
     grad_logits = router * (
         grad_router_probs - jnp.sum(router * grad_router_probs, axis=1, keepdims=True)
     )

time: 1620 us -> 1490 us (0.920)
  matrix products: 306 us -> 92.3 us
  Pallas kernels: 1160 us -> 1310 us
  local copies, waits for them, and re-layouts: 82.4 us -> 32.6 us
  other arithmetic: 70.1 us -> 43.7 us
    dot_general x32 -> x21, matrix products: 304 us -> 88.9 us  [product(): return jnp.einsum(form, left, right, preferred_element_type=jnp.float32)]
    pallas_call x0 -> x3, Pallas kernels: none -> 153 us  [the longest x1 76.5 us: expert_call(): pl.pallas_call(functools.partial(expert_kernel, steps, half), grid=(numbe...]
    slice x2 -> x0, local copies, waits for them, and re-layouts: 26.1 us -> none  [the longest x1 14.7 us: shards(): cotangent_all = extras_all[:, :D]]
where the time goes in v3:
time: 1490 us; the launch traced here: 1480 us
  Pallas kernels  1310 us (88%)
  matrix products  92.3 us (6%)
  other arithmetic  43.7 us (3%)
  local copies, waits for them, and re-layouts  32.6 us (2%)
    pallas_call x2, Pallas kernels, gather_call(): pl.pallas_call(functools.partial(gather_kernel, n_dp, n_expert, n, places...  588 us
    pallas_call x2, Pallas kernels, scatter_call(): pl.pallas_call(functools.partial(scatter_kernel, n_dp, n_expert, n, m, cu...  567 us
    dot_general x21, matrix products, product(): return jnp.einsum(form, left, right, preferred_element_type=jnp.float32)  88.9 us
    pallas_call x1, Pallas kernels, expert_call(): pl.pallas_call(functools.partial(expert_kernel, steps, half), grid=(numbe...  76.5 us
    pallas_call x1, Pallas kernels, place_call(): pl.pallas_call(functools.partial(place_kernel, number), grid=(pairs,), in...  38.3 us
    pallas_call x1, Pallas kernels, pick_call(): pl.pallas_call(functools.partial(pick_kernel, number, experts_all), grid=...  38.2 us

profile of v3, /device:TPU:0, one launch (start us, length us, event | category | flops | bytes accessed | tf_op | source)
XLA Modules:
  0.0 1478.7 jit_solution(9776018502981867254)
XLA Ops:
  0.6 2.3 pad_maximum_fusion.refs_0_
  2.9 0.8 copy.89
  3.7 0.8 copy.90
  4.5 0.8 copy.91
  5.2 0.8 copy.92
  6.0 0.8 concatenate.45
  6.8 0.8 copy.88
  7.9 1.9 fusion.63.refs_1_
  9.8 386.4 %shard_map.272 = (bf16[4,2048,2048]{2,1,0:T(8,128)(2,1)}, bf16[4096,2304]{1,0:T(8,128)(2,1)}, bf16[8,2048,256]{2,1,0:T(8,128)(2,1)}, bf16[8,2048,256]{2,1,0:T(8,128)(2,1)}) custom-call(bf16[4,64,2048]{2,1,0:T(8,128)(2,1)} %pad_maximum_fusion.refs_0_, bf16[128,2304]{1,0:T(8,128)(2,1)} %fusion.63.refs_1_, bf16[8,512,1024]{2,1,0:T(8,128)(2,1)} %refs_1_.1, ...), custom_call_target="tpu_custom_call" | custom-call | tf_op jit(solution)/shard_map/pallas_call | solution.py:261
  396.2 1.4 slice.87
  397.8 2.0 slice_reduce_fusion
  400.0 5.5 fusion.45
  405.9 4.8 multiply_reduce_fusion.7
  411.7 4.8 multiply_reduce_fusion.6
  417.2 2.8 subtract_convert_fusion.3
  420.0 3.3 fusion.105
  423.3 3.5 convolution_convert_fusion.6
  426.9 6.2 multiply_reduce_fusion.5
  433.1 2.3 slice.101
  435.4 2.5 constant_dynamic-slice_fusion
  437.9 1.5 copy.99
  439.4 1.7 fusion.49
  441.9 2.2 multiply_convert_fusion.1.refs_0_
  444.1 202.0 %shard_map.273 = (bf16[4096,2048]{1,0:T(8,128)(2,1)}, bf16[8,2048,256]{2,1,0:T(8,128)(2,1)}, bf16[8,2048,256]{2,1,0:T(8,128)(2,1)}) custom-call(bf16[128,2048]{1,0:T(8,128)(2,1)} %multiply_convert_fusion.1.refs_0_, bf16[8,512,1024]{2,1,0:T(8,128)(2,1)} %refs_1_.1, bf16[8,512,1024]{2,1,0:T(8,128)(2,1)} %refs_2_.3, ...), custom_call_target="tpu_custom_call", output_to_operand_aliasing={{1}: (3, {}), {2}: (4, {})} | custom-call | tf_op jit(solution)/shard_map/pallas_call | solution.py:261
  646.6 0.9 pad.9.router_ref
  647.5 38.2 %shard_map.274 = (bf16[8,768,2048]{2,1,0:T(8,128)(2,1)}, bf16[8,768,2048]{2,1,0:T(8,128)(2,1)}, f32[8,768,128]{2,1,0:T(8,128)}) custom-call(s32[16,8,256]{2,1,0:T(8,128)} %select_bitcast_fusion.slots_ref, bf16[4096,2048]{1,0:T(8,128)(2,1)} %get-tuple-element.47.x_ref, bf16[4096,2304]{1,0:T(8,128)(2,1)} %get-tuple-element.43.g_ref, ...), custom_call_target="tpu_custom_call" | custom-call | tf_op jit(solution)/shard_map/pallas_call | solution.py:611
  685.7 76.5 %shard_map.275 = (bf16[8,768,2048]{2,1,0:T(8,128)(2,1)}, bf16[8,768,2048]{2,1,0:T(8,128)(2,1)}, bf16[8,768,128]{2,1,0:T(8,128)(2,1)}, bf16[8,2048,256]{2,1,0:T(8...) custom-call(s32[1]{0:T(128)} %bitcast.25.first_ref, bf16[8,768,2048]{2,1,0:T(8,128)(2,1)} %get-tuple-element.48.x_ref, ...), custom_call_target="tpu_custom_call" | custom-call | tf_op jit(solution)/shard_map/pallas_call | solution.py:647
  762.2 38.3 %shard_map.276 = (bf16[4096,2048]{1,0:T(8,128)(2,1)}, bf16[4096,2176]{1,0:T(8,128)(2,1)}) custom-call(s32[16,8,256]{2,1,0:T(8,128)} %select_bitcast_fusion.slots_ref, bf16[8,768,2048]{2,1,0:T(8,128)(2,1)} %get-tuple-element.53.y_ref, bf16[8,768,2048]{2,1,0:T(8,128)(2,1)} %get-tuple-element.54.dx_ref, bf16[8,768,128]{2,1,0:T(8,128)(2,1)} %get-tuple-element.55.probs_ref), custom_call_target="tpu_custom_call" | custom-call | tf_op jit(solution)/shard_map/pallas_call | solution.py:685
  800.5 234.0 %shard_map.277 = (f32[128,2176]{1,0:T(8,128)}, f32[128,2048]{1,0:T(8,128)}, bf16[3,512,1024]{2,1,0:T(8,128)(2,1)}, bf16[3,512,1024]{2,1,0:T(8,128)(2,1)}) custom-call(bf16[4,8,128,2176]{3,2,1,0:T(8,128)(2,1)} %bitcast.151, bf16[4,8,128,2048]{3,2,1,0:T(8,128)(2,1)} %bitcast.152, bf16[8,2048,256]{2,1,0:T(8,128)(2,1)} %get-tuple-element.58.refs_2_.refs_5_, ...), custom_call_target="tpu_custom_call" | custom-call | tf_op jit(solution)/shard_map/pallas_call | solution.py:419
  1035.3 1.1 multiply_reduce_fusion.8
  1036.4 2.3 multiply_reduce_fusion
  1038.7 2.9 subtract_add_fusion
  1041.6 1.0 copy-done.1
  1042.6 7.1 fusion.37
  1049.7 2.0 copy.130
  1051.7 1.9 multiply_reduce_fusion.3
  1053.6 1.4 multiply_convert_fusion
  1055.1 1.8 fusion.43
  1057.3 0.9 multiply_subtract_fusion.1
  1058.3 0.9 fusion.60
  1059.8 6.5 fusion.5
  1066.9 0.8 copy-done.12
  1067.7 7.3 fusion.28
  1075.0 3.5 convolution_convert_fusion.5
  1078.5 6.9 fusion.58
  1085.4 1.4 fusion.55
  1086.9 5.7 convolution_convert_fusion.3
  1092.6 5.7 convolution_convert_fusion.2
  1098.3 5.7 convolution_convert_fusion.1
  1103.9 5.9 convolution_convert_fusion
  1109.9 1.3 convolution_convert_fusion.4
  1111.5 1.0 concatenate.60
  1112.5 1.0 concatenate.61
  1113.5 1.0 concatenate.62
  1114.5 1.0 concatenate.63
  1115.7 2.3 concatenate.57.refs_4_
  1118.0 333.2 %shard_map.278 = (f32[64,2048]{1,0:T(8,128)}, f32[64,2048]{1,0:T(8,128)}, f32[64,2048]{1,0:T(8,128)}, f32[64,2048]{1,0:T(8,128)}, f32[64,128]{1,0:T(8,128)}, /*i...) custom-call(bf16[4,8,64,2048]{3,2,1,0:T(8,128)(2,1)} %bitcast.147, bf16[4,8,64,2048]{3,2,1,0:T(8,128)(2,1)} %bitcast.148, ...), custom_call_target="tpu_custom_call" | custom-call | tf_op jit(solution)/shard_map/pallas_call | solution.py:419
  1451.2 1.7 slice_reduce_fusion.4
  1452.9 10.7 maximum_convert_fusion
  1463.6 10.8 maximum_convert_fusion.1
  1474.4 0.8 copy.167
  1475.2 0.8 copy.168
  1476.0 0.8 copy.169
  1476.8 0.8 copy.170
  (81 shorter events, 7.4 us)
Async XLA Ops:
  396.2 3.6 copy-start
  397.6 248.5 %copy-start.4 = (bf16[32,64,128]{2,1,0:T(8,128)(2,1)}, bf16[32,64,128]{2,1,0:T(8,128)(2,1)S(1)}, u32[]{:S(2)}) copy-start(bf16[32,64,128]{2,1,0:T(8,128)(2,1)S(1)} %slice.116) | copy-start | bytes 1572868
  397.8 7.7 copy-start.21
  800.5 234.1 %copy-start.3 = (bf16[128,2048]{1,0:T(8,128)(2,1)S(1)}, bf16[128,2048]{1,0:T(8,128)(2,1)}, u32[]{:S(2)}) copy-start(bf16[128,2048]{1,0:T(8,128)(2,1)} %multiply_convert_fusion.1.refs_0_) | copy-start | bytes 1572868
  800.5 234.1 %copy-start.5 = (bf16[32,64,128]{2,1,0:T(8,128)(2,1)S(1)}, bf16[32,64,128]{2,1,0:T(8,128)(2,1)}, u32[]{:S(2)}) copy-start(bf16[32,64,128]{2,1,0:T(8,128)(2,1)} %copy-done.4) | copy-start | bytes 1572868
  1041.6 1.0 copy-start.1
  1051.7 5.1 copy-start.6
  1051.7 5.1 copy-start.8
  1059.7 7.1 copy-start.10
  1066.2 8.7 copy-start.7
  1066.2 8.7 copy-start.9
  1066.9 0.8 copy-start.12
  1078.5 7.0 copy-start.2
  1078.5 8.4 copy-start.14
  1085.4 7.2 copy-start.16
  1092.6 5.7 copy-start.11
  1098.3 5.7 copy-start.13
  1463.6 10.9 copy-start.20
  1463.6 11.7 copy-start.19
  1463.6 12.4 copy-start.18
  1463.6 13.2 copy-start.17
  1463.6 14.0 copy-start.15

commit v4 on v3

--- a/solution.py
+++ b/solution.py
@@ -56,12 +56,20 @@
 
 
 MESH = pl.DeviceIdType.MESH
+BIG = 60 * 1024 * 1024
 
 
 def place_of():
     z = lax.axis_index("dp")
     j = lax.axis_index("expert")
     return z, j, j // 2, j % 2
+
+
+def other_chips(chip, chips):
+    if chips == 4:
+        square = [chip, chip + 1 - 2 * (chip % 2), chip + 2 - 4 * (chip // 2), 3 - chip]
+        return lambda k: square[k], lambda k: square[k]
+    return lambda k: (chip + k) % chips, lambda k: (chip + chips - k) % chips
 
 
 def greet(n_dp, n_expert):
@@ -108,6 +116,8 @@
 def gather_kernel(n_dp, n_expert, n_items, places, cuts, n_cut, n_out, *refs):
     z, j, chip, core = place_of()
     chips = n_expert // 2
+    square = chips == 4
+    to_chip, from_chip = other_chips(chip, chips)
     sources = refs[:n_items]
     cut_in = refs[n_items : n_items + n_cut]
     at = n_items + n_cut
@@ -127,16 +137,23 @@
     ) = refs[at + n_items + n_out :]
     greet(n_dp, n_expert)
     mate = (z, chip * 2 + 1 - core)
+    near = (1, 2) if square else tuple(range(1, chips))
 
     def slot(i, plane, column):
         return places[i](targets[i], plane * n_expert + column)
 
+    def pass_on(i, plane, source, column, k, chip_to):
+        return remote(
+            source,
+            slot(i, plane, column),
+            send_b.at[i, plane, k],
+            recv_b.at[i, plane, k],
+            (z, chip_to * 2 + core),
+        )
+
     def hand(i, plane, source):
-        for k in range(1, chips):
-            other = ((chip + k) % chips) * 2 + core
-            remote(
-                source, slot(i, plane, j), send_b.at[i, plane, k], recv_b.at[i, plane, k], (z, other)
-            ).start()
+        for k in near:
+            pass_on(i, plane, source, j, k, to_chip(k)).start()
         remote(
             source, slot(i, plane, j), send_a.at[i, plane, 0], recv_a.at[i, plane, 0], mate
         ).start()
@@ -146,6 +163,19 @@
             source, slot(i, plane, j), send_c.at[i, way, plane], recv_c.at[i, plane], (z + step, j)
         )
 
+    def at_distance(d, body):
+        if d == 0:
+            body(z, 0)
+            return
+
+        @pl.when(z >= d)
+        def _():
+            body(z - d, 0)
+
+        @pl.when(z + d < n_dp)
+        def _():
+            body(z + d, 1)
+
     for i in range(n_items):
 
         @pl.when(z < n_dp - 1)
@@ -158,72 +188,56 @@
 
         hand(i, z, sources[i])
         pltpu.make_async_copy(sources[i], slot(i, z, j), local.at[i]).start()
+
+    def relay(plane, way):
+        step = -1 if way else 1
+        for i in range(n_items):
+            block = slot(i, plane, j)
+            along(i, plane, block, way, step).wait_recv()
+
+            @pl.when(z > 0 if way else z < n_dp - 1)
+            def _():
+                along(i, plane, block, way, step).start()
+
+            hand(i, plane, block)
+
+    for d in range(1, n_dp):
+        at_distance(d, relay)
     copies = exchange(n_dp, cuts(cut_in, cut_out), send_x, recv_x, local_x)
     for copy in copies:
         copy.start()
 
-    def arrived(i, plane):
-        for k in range(1, chips):
-            column = ((chip + chips - k) % chips) * 2 + core
-            block = slot(i, plane, column)
-            remote(block, block, send_b.at[i, plane, k], recv_b.at[i, plane, k], mate).wait_recv()
-            remote(block, block, send_a.at[i, plane, k], recv_a.at[i, plane, k], mate).start()
-
-    for d in range(1, n_dp):
-
-        @pl.when(z >= d)
-        def _():
-            for i in range(n_items):
-                block = slot(i, z - d, j)
-                along(i, z - d, block, 0, 1).wait_recv()
-
-                @pl.when(z < n_dp - 1)
-                def _():
-                    along(i, z - d, block, 0, 1).start()
-
-                hand(i, z - d, block)
-
-        @pl.when(z + d < n_dp)
-        def _():
-            for i in range(n_items):
-                block = slot(i, z + d, j)
-                along(i, z + d, block, 1, -1).wait_recv()
-
-                @pl.when(z > 0)
-                def _():
-                    along(i, z + d, block, 1, -1).start()
-
-                hand(i, z + d, block)
-
-        if d == 1:
-            for i in range(n_items):
-                arrived(i, z)
-        else:
-
-            @pl.when(z >= d - 1)
-            def _():
-                for i in range(n_items):
-                    arrived(i, z - d + 1)
-
-            @pl.when(z + d - 1 < n_dp)
-            def _():
-                for i in range(n_items):
-                    arrived(i, z + d - 1)
-
-    @pl.when(z >= n_dp - 1)
-    def _():
+    def arrive(i, plane, k):
+        column = from_chip(k) * 2 + core
+        block = slot(i, plane, column)
+        pass_on(i, plane, block, column, k, chip).wait_recv()
+        remote(block, block, send_a.at[i, plane, k], recv_a.at[i, plane, k], mate).start()
+        return block, column
+
+    def arrived(plane, way):
         for i in range(n_items):
-            arrived(i, z - n_dp + 1)
-
-    @pl.when(z + n_dp - 1 < n_dp)
-    def _():
+            for k in near:
+                block, column = arrive(i, plane, k)
+                if square:
+
+                    @pl.when(plane % 2 == k - 1)
+                    def _():
+                        pass_on(i, plane, block, column, 3, to_chip(3 - k)).start()
+
+    def crossed(plane, way):
         for i in range(n_items):
-            arrived(i, z + n_dp - 1)
+            arrive(i, plane, 3)
+
+    for d in range(n_dp):
+        at_distance(d, arrived)
+    if square:
+        for d in range(n_dp):
+            at_distance(d, crossed)
 
     for i in range(n_items):
         for plane in range(n_dp):
             for k in range(chips):
-                column = ((chip + chips - k) % chips) * 2 + 1 - core
+                column = (from_chip(k) if k else chip) * 2 + 1 - core
                 block = slot(i, plane, column)
                 remote(
                     block, block, send_a.at[i, plane, k], recv_a.at[i, plane, k], mate
@@ -232,9 +246,7 @@
         for plane in range(n_dp):
             block = slot(i, plane, j)
             for k in range(1, chips):
-                remote(
-                    block, block, send_b.at[i, plane, k], recv_b.at[i, plane, k], mate
-                ).wait_send()
+                pass_on(i, plane, block, j, k, chip).wait_send()
             for k in range(chips):
                 remote(
                     block, block, send_a.at[i, plane, k], recv_a.at[i, plane, k], mate
@@ -280,19 +292,21 @@
     )(*items, *cut_in)
 
 
-def scatter_kernel(n_dp, n_expert, n_items, n_cut, cuts, *refs):
+def scatter_kernel(n_dp, n_expert, n_items, n_cut, n_out, cuts, rings, n_rings, *refs):
     z, j, chip, core = place_of()
     chips = n_expert // 2
-    sources = refs[:n_items]
-    cut_in = refs[n_items : n_items + n_cut]
-    at = n_items + n_cut
-    targets = refs[at : at + n_items]
-    cut_out = refs[at + n_items : at + n_items + n_cut]
-    at = at + n_items + n_cut
-    halves = refs[at : at + n_items]
-    got_a = refs[at + n_items : at + 2 * n_items]
-    got_b = refs[at + 2 * n_items : at + 3 * n_items]
-    got_c = refs[at + 3 * n_items : at + 4 * n_items]
+    square = chips == 4
+    to_chip, from_chip = other_chips(chip, chips)
+    refs = list(refs)
+
+    def take(count):
+        taken = refs[:count]
+        del refs[:count]
+        return taken
+
+    sources, cut_in, targets, cut_out = take(n_items), take(n_cut), take(n_items), take(n_out)
+    ring, got_a, got_b, got_c = take(n_rings), take(n_items), take(n_items), take(n_items)
+    transit = take(n_items)
     (
         send_a,
         recv_a,
@@ -300,109 +314,182 @@
         recv_b,
         send_c,
         recv_c,
+        send_t,
+        recv_t,
         local,
         send_x,
         recv_x,
         local_x,
-    ) = refs[at + 4 * n_items :]
+    ) = refs
     greet(n_dp, n_expert)
     mate = (z, chip * 2 + 1 - core)
-    order = [*range(1, chips), 0]
+    order = [3, 1, 2, 0] if square else [*range(1, chips), 0]
+    half = n_dp // 2
+    low, high = pl.ds(0, half), pl.ds(half, n_dp - half)
+
+    def chip_of(k):
+        return to_chip(k) if k else chip
 
     def to_mate(i, k):
-        column = ((chip + k) % chips) * 2
         return remote(
-            sources[i].at[:, column + 1 - core],
+            sources[i].at[:, chip_of(k) * 2 + 1 - core],
             got_a[i].at[k],
             send_a.at[i, k],
             recv_a.at[i, k],
             mate,
         )
 
-    def load(i, k):
-        column = ((chip + k) % chips) * 2
+    turn = [0] * n_rings
+    loads = []
+    for i in range(n_items):
+        for k in order:
+            loads.append((i, k, turn[rings[i]] % 2))
+            turn[rings[i]] += 1
+
+    def load(i, k, at):
         return pltpu.make_async_copy(
-            sources[i].at[:, column + core], halves[i].at[k], local.at[i, k]
+            sources[i].at[:, chip_of(k) * 2 + core], ring[rings[i]].at[at], local.at[rings[i], at]
         )
 
-    def to_chip(i, k):
-        other = ((chip + k) % chips) * 2 + core
+    def send_near(i, k, part, number):
         return remote(
-            halves[i].at[k], got_b[i].at[k - 1], send_b.at[i, k], recv_b.at[i, k], (z, other)
+            got_a[i].at[k, part],
+            got_b[i].at[k - 1, part],
+            send_b.at[i, number],
+            recv_b.at[i, number],
+            (z, to_chip(k) * 2 + core),
+        )
+
+    def send_over(i, k, part):
+        return remote(
+            got_a[i].at[3, part],
+            transit[i].at[k - 1],
+            send_t.at[i, k],
+            recv_t.at[i, k],
+            (z, to_chip(k) * 2 + core),
+        )
+
+    def send_far(i, k):
+        return remote(
+            got_a[i].at[k],
+            got_b[i].at[k - 1],
+            send_b.at[i, k],
+            recv_b.at[i, k],
+            (z, to_chip(k) * 2 + core),
         )
 
     def to_plane(i, k):
         to = (z + k) % n_dp
         return remote(
-            halves[i].at[0, to], got_c[i].at[k - 1], send_c.at[i, k], recv_c.at[i, k], (to, j)
+            got_a[i].at[0, to], got_c[i].at[k - 1], send_c.at[i, k], recv_c.at[i, k], (to, j)
         )
+
+    f32 = jnp.float32
+
+    def add(i, planes, target, terms):
+        rows = got_a[i].shape[2]
+        per = rows // 16
+
+        def step(n, unused):
+            plane = n // per
+            at = pl.ds(pl.multiple_of((n % per) * 16, 16), 16)
+            total = terms[0](plane, at).astype(f32)
+            for term in terms[1:]:
+                total = total + term(plane, at).astype(f32)
+            target(plane, at, total)
+            return unused
+
+        lax.fori_loop(0, planes * per, step, 0)
+
+    def grow(i, k, first, planes, term):
+        def target(plane, at, total):
+            got_a[i][k, plane + first, at] = total.astype(got_a[i].dtype)
+
+        add(i, planes, target, [lambda plane, at: got_a[i][k, plane + first, at], term])
 
     for i in range(n_items):
         for k in order:
             to_mate(i, k).start()
-            load(i, k).start()
+    started = 0
+    ahead = [0] * n_rings
+    for i, k, at in loads:
+        if ahead[rings[i]] < 2:
+            load(i, k, at).start()
+            ahead[rings[i]] += 1
     copies = exchange(n_dp, cuts(cut_in, cut_out), send_x, recv_x, local_x)
     for copy in copies:
         copy.start()
 
-    def loop(rows, body):
-        def step(n, unused):
-            body(pl.ds(pl.multiple_of(n * 16, 16), 16))
-            return unused
-
-        lax.fori_loop(0, rows // 16, step, 0)
-
-    f32 = jnp.float32
+    for n, (i, k, at) in enumerate(loads):
+        load(i, k, at).wait()
+        to_mate(i, k).wait_recv()
+        grow(i, k, 0, n_dp, lambda plane, rows: ring[rings[i]][at, plane, rows])
+        later = [one for one in loads[n + 1 :] if rings[one[0]] == rings[i]]
+        if len(later) >= 2:
+            load(*later[1]).start()
+        if not k:
+            continue
+        if not square:
+            send_far(i, k).start()
+        elif k == 3:
+            send_over(i, 1, low).start()
+            send_over(i, 2, high).start()
+        elif k == 1:
+            send_near(i, 1, low, 0).start()
+        else:
+            send_near(i, 2, high, 1).start()
+    if square:
+        for i in range(n_items):
+            send_over(i, 2, high).wait_recv()
+            grow(i, 1, half, n_dp - half, lambda plane, rows: transit[i][1, plane, rows])
+            send_near(i, 1, high, 2).start()
+            send_over(i, 1, low).wait_recv()
+            grow(i, 2, 0, half, lambda plane, rows: transit[i][0, plane, rows])
+            send_near(i, 2, low, 3).start()
     for i in range(n_items):
-        rows = halves[i].shape[2]
-        for k in order:
-            load(i, k).wait()
-            to_mate(i, k).wait_recv()
-            if k == 0:
-                continue
-
-            def one(n, unused):
-                plane = n // (rows // 16)
-                at = pl.ds(pl.multiple_of((n % (rows // 16)) * 16, 16), 16)
-                total = halves[i][k, plane, at].astype(f32) + got_a[i][k, plane, at].astype(f32)
-                halves[i][k, plane, at] = total.astype(halves[i].dtype)
-                return unused
-
-            lax.fori_loop(0, n_dp * (rows // 16), one, 0)
-            to_chip(i, k).start()
-    for i in range(n_items):
-        rows = halves[i].shape[2]
-        for k in range(1, chips):
-            to_chip(i, k).wait_recv()
+        if square:
+            send_near(i, 1, low, 0).wait_recv()
+            send_near(i, 2, high, 1).wait_recv()
+            send_near(i, 1, high, 2).wait_recv()
+            send_near(i, 2, low, 3).wait_recv()
+        else:
+            for k in range(1, chips):
+                send_far(i, k).wait_recv()
+        heard = 2 if square else chips - 1
         for k in [*range(1, n_dp), 0]:
             plane = (z + k) % n_dp
 
-            def body(at):
-                total = halves[i][0, plane, at].astype(f32) + got_a[i][0, plane, at].astype(f32)
-                for other in range(chips - 1):
-                    total = total + got_b[i][other, plane, at].astype(f32)
-                halves[i][0, plane, at] = total.astype(halves[i].dtype)
-
-            loop(rows, body)
+            def target(unused, at, total):
+                got_a[i][0, plane, at] = total.astype(got_a[i].dtype)
+
+            terms = [lambda unused, at: got_a[i][0, plane, at]]
+            for other in range(heard):
+                terms.append(lambda unused, at, other=other: got_b[i][other, plane, at])
+            add(i, 1, target, terms)
             if k:
                 to_plane(i, k).start()
     for i in range(n_items):
-        rows = halves[i].shape[2]
         for k in range(1, n_dp):
             to_plane(i, k).wait_recv()
 
-        def body(at):
-            total = halves[i][0, z, at].astype(f32)
-            for k in range(n_dp - 1):
-                total = total + got_c[i][k, at].astype(f32)
+        def target(unused, at, total):
             targets[i][at] = total
 
-        loop(rows, body)
+        terms = [lambda unused, at: got_a[i][0, z, at]]
+        for k in range(n_dp - 1):
+            terms.append(lambda unused, at, k=k: got_c[i][k, at])
+        add(i, 1, target, terms)
     for i in range(n_items):
         for k in range(chips):
             to_mate(i, k).wait_send()
-            if k:
-                to_chip(i, k).wait_send()
+        if square:
+            for k, part in ((1, low), (2, high)):
+                send_over(i, k, part).wait_send()
+            for k, part, number in ((1, low, 0), (2, high, 1), (1, high, 2), (2, low, 3)):
+                send_near(i, k, part, number).wait_send()
+        else:
+            for k in range(1, chips):
+                send_far(i, k).wait_send()
         for k in range(1, n_dp):
             to_plane(i, k).wait_send()
     for copy in copies:
@@ -411,42 +498,54 @@
 
 def scatter_call(n_dp, n_expert, items, cut_in, cut_shapes, cuts, number):
     chips = n_expert // 2
+    square = chips == 4
     n, m = len(items), len(cut_shapes)
     dma = pltpu.SemaphoreType.DMA
     anywhere = pl.BlockSpec(memory_space=pl.ANY)
     blocks = [item.shape[2:] for item in items]
+    kinds = sorted(set(blocks))
+    rings = [kinds.index(block) for block in blocks]
     bf16 = jnp.bfloat16
+    heard = 2 if square else chips - 1
     return pl.pallas_call(
-        functools.partial(scatter_kernel, n_dp, n_expert, n, m, cuts),
+        functools.partial(
+            scatter_kernel, n_dp, n_expert, n, len(cut_in), m, cuts, rings, len(kinds)
+        ),
         out_shape=[*[jax.ShapeDtypeStruct(block, jnp.float32) for block in blocks], *cut_shapes],
-        in_specs=[anywhere] * (n + m),
+        in_specs=[anywhere] * (n + len(cut_in)),
         out_specs=[pl.BlockSpec(memory_space=pltpu.VMEM)] * n + [anywhere] * m,
         scratch_shapes=[
+            *[pltpu.VMEM((2, n_dp, *kind), bf16) for kind in kinds],
             *[pltpu.VMEM((chips, n_dp, *block), bf16) for block in blocks],
-            *[pltpu.VMEM((chips, n_dp, *block), bf16) for block in blocks],
-            *[pltpu.VMEM((chips - 1, n_dp, *block), bf16) for block in blocks],
+            *[pltpu.VMEM((heard, n_dp, *block), bf16) for block in blocks],
             *[pltpu.VMEM((n_dp - 1, *block), bf16) for block in blocks],
+            *[pltpu.VMEM((2, n_dp // 2, *(block if square else (16, 128))), bf16) for block in blocks],
             dma((n, chips)),
             dma((n, chips)),
             dma((n, chips)),
             dma((n, chips)),
             dma((n, n_dp)),
             dma((n, n_dp)),
-            dma((n, chips)),
+            dma((n, 3)),
+            dma((n, 3)),
+            dma((len(kinds), 2)),
             dma((max(m, 1), n_dp)),
             dma((max(m, 1), n_dp)),
             dma((max(m, 1),)),
         ],
         compiler_params=pltpu.CompilerParams(
-            collective_id=number, has_side_effects=True, vmem_limit_bytes=60 * 1024 * 1024
+            collective_id=number, has_side_effects=True, vmem_limit_bytes=62 * 1024 * 1024
         ),
     )(*items, *cut_in)
 
+
 def scatter_all(n_dp, n_expert, items, cut_in, cut_shapes, cuts, number):
     chips = n_expert // 2
-    blocks = (3 * chips - 1) * n_dp + n_dp + 2
+    blocks = (2 * chips if chips != 4 else 7) * n_dp + n_dp + 3
     need = sum(blocks * item.shape[2] * item.shape[3] * 2 for item in items)
-    pieces = -(-need // (56 * 1024 * 1024))
+    kinds = {item.shape[2:] for item in items}
+    need += sum(2 * n_dp * kind[0] * kind[1] * 2 for kind in kinds)
+    pieces = -(-need // (61 * 1024 * 1024))
     tiles = [item.shape[3] // 128 for item in items]
     results = [[] for item in items]
     extra = []
@@ -599,9 +698,6 @@
     back_ref[:, width:] = dot(pick, part, (0, 0)).astype(jnp.bfloat16)
 
 
-BIG = 60 * 1024 * 1024
-
-
 def pick_call(number, experts_all, slots, x_all, g_all, router):
     pairs, _, pair = slots.shape
     bf16 = jnp.bfloat16
@@ -746,12 +842,10 @@
     ).astype(bf16)
     count = tokens.shape[0]
     rows_each = w_query.shape[0]
-    extras = jnp.concatenate(
-        [cotangent, hits, jnp.pad(small, ((0, count - rows_each), (0, 0)))], axis=1
-    )
+    extras = jnp.concatenate([hits, jnp.pad(small, ((0, count - rows_each), (0, 0)))], axis=1)
     weights = jnp.stack([w_query, w_key, w_value, w_out])
     depth = w_gate.shape[1]
-    early = number * 5 // 8
+    early = number // 4
     cut_shape = jax.ShapeDtypeStruct((number, n_dp * depth, part), bf16)
 
     def row_block(size):
@@ -780,7 +874,7 @@
         [weights, extras],
         [
             jax.ShapeDtypeStruct((4, groups * rows_each, D), bf16),
-            jax.ShapeDtypeStruct((groups * count, D + 2 * width), bf16),
+            jax.ShapeDtypeStruct((groups * count, 2 * width), bf16),
         ],
         [
             lambda ref, block: ref.at[
@@ -796,9 +890,9 @@
     )
     query_weight, key_weight, value_weight, out_weight = (weights_all[i] for i in range(4))
     small_all = (
-        extras_all[:, D + width :].reshape(groups, count, width)[:, :rows_each].reshape(-1, width)
-    )
-    hits_all = extras_all[:, D : D + experts_all]
+        extras_all[:, width:].reshape(groups, count, width)[:, :rows_each].reshape(-1, width)
+    )
+    hits_all = extras_all[:, :experts_all]
     router_weight = small_all[:, :experts_all]
     gains = small_all[:, experts_all : experts_all + 4].astype(jnp.float32)
     attn_gain, query_gain, key_gain, mlp_gain = (gains[:, i] for i in range(4))
@@ -831,16 +925,16 @@
     mlp_low = mlp_normed.astype(bf16)
     router = jax.nn.softmax(product(mlp_low, router_weight, "td,de->te"), axis=-1)
 
-    mlp_all, gate_cut, up_cut = gather_call(
+    mlp_all, cotangent_all, gate_cut, up_cut = gather_call(
         n_dp,
         n_expert,
-        [mlp_low],
-        [jax.ShapeDtypeStruct((groups * count, D), bf16)],
-        [row_block(count)],
+        [mlp_low, cotangent],
+        [jax.ShapeDtypeStruct((groups * count, D), bf16)] * 2,
+        [row_block(count)] * 2,
         [w_gate, w_up, gate_early, up_early],
         [cut_shape, cut_shape],
         recut(early, number),
-        {3: 1, 4: 2},
+        {4: 2, 5: 3},
         1,
     )
     first = lax.axis_index("expert") * number
@@ -855,7 +949,7 @@
     router_own = jnp.pad(
         jnp.roll(router_weight, -first, axis=1), ((0, 0), (0, width - experts_all))
     )
-    rows, grows, gates = pick_call(number, experts_all, slots, mlp_all, extras_all, router_own)
+    rows, grows, gates = pick_call(number, experts_all, slots, mlp_all, cotangent_all, router_own)
     weighted, grad_rows, grad_gates, grad_gate_cut, grad_up_cut, grad_down_part = expert_call(
         first[None], experts_all, rows, grows, gates, gate_cut, up_cut, w_down
     )
@@ -881,12 +975,9 @@
     def way_shape(size):
         return jax.ShapeDtypeStruct((size, depth, ff), bf16)
 
-    back_items = [
-        part_back.reshape(n_dp, n_expert, count, D + width),
-        part_out.reshape(n_dp, n_expert, count, D),
-    ]
-    sooner = number * 3 // 8
-    (back, summed), (gate_first, up_first) = scatter_all(
+    back_items = [part_back.reshape(n_dp, n_expert, count, D + width)]
+    sooner = number // 4
+    (back,), (gate_first, up_first) = scatter_all(
         n_dp,
         n_expert,
         back_items,
@@ -895,7 +986,6 @@
         way_back(0, sooner),
         8,
     )
-    output = (middle + summed).astype(bf16)
 
     grad_final = cotangent.astype(jnp.float32)
     grad_mlp = back[:, :D]
@@ -967,13 +1057,15 @@
                 grad_query_full,
                 small_grads,
             )
-        ],
+        ]
+        + [part_out.reshape(n_dp, n_expert, count, D)],
         [grad_gate_cut, grad_up_cut],
         [way_shape(number - sooner)] * 2,
         way_back(sooner, number),
         16,
     )
-    grad_out_part, grad_value_part, grad_key_part, grad_query_part, small_part = sums
+    grad_out_part, grad_value_part, grad_key_part, grad_query_part, small_part, summed = sums
+    output = (middle + summed).astype(bf16)
     grad_router_part = small_part[:, :experts_all]
     gain_parts = [small_part[:, experts_all + i] for i in range(4)]
     grad_gate_part = jnp.concatenate([gate_first, gate_last], axis=0).astype(jnp.float32)

time: 1490 us -> 1390 us (0.933)
  Pallas kernels: 1310 us -> 1220 us
    pallas_call x2, Pallas kernels: 588 us -> 518 us  [gather_call(): pl.pallas_call(functools.partial(gather_kernel, n_dp, n_expert, n, places...]
    pallas_call x2, Pallas kernels: 567 us -> 546 us  [scatter_call(): pl.pallas_call(functools.partial(scatter_kernel, n_dp, n_expert, n, len(c...]
where the time goes in v4:
time: 1390 us; the launch traced here: 1380 us
  Pallas kernels  1220 us (88%)
  matrix products  80.8 us (6%)
  other arithmetic  44.4 us (3%)
  local copies, waits for them, and re-layouts  32.9 us (2%)
    pallas_call x2, Pallas kernels, scatter_call(): pl.pallas_call(functools.partial(scatter_kernel, n_dp, n_expert, n, len(c...  546 us
    pallas_call x2, Pallas kernels, gather_call(): pl.pallas_call(functools.partial(gather_kernel, n_dp, n_expert, n, places...  518 us
    dot_general x21, matrix products, product(): return jnp.einsum(form, left, right, preferred_element_type=jnp.float32)  78.5 us
    pallas_call x1, Pallas kernels, expert_call(): pl.pallas_call(functools.partial(expert_kernel, steps, half), grid=(numbe...  76.5 us
    pallas_call x1, Pallas kernels, place_call(): pl.pallas_call(functools.partial(place_kernel, number), grid=(pairs,), in...  38.3 us
    pallas_call x1, Pallas kernels, pick_call(): pl.pallas_call(functools.partial(pick_kernel, number, experts_all), grid=...  38.2 us

profile of v4, /device:TPU:0, one launch (start us, length us, event | category | flops | bytes accessed | tf_op | source)
XLA Modules:
  0.0 1377.1 jit_solution(9950176177409715372)
XLA Ops:
  0.6 2.3 pad_maximum_fusion.refs_0_
  2.9 0.8 copy.88
  4.0 0.8 copy.89
  4.8 0.8 copy.90
  5.5 0.8 copy.91
  6.3 0.8 copy.92
  7.1 0.8 concatenate.45
  7.9 0.6 fusion.80.refs_1_
  8.5 184.6 %shard_map.272 = (bf16[4,2048,2048]{2,1,0:T(8,128)(2,1)}, bf16[4096,256]{1,0:T(8,128)(2,1)}, bf16[8,2048,256]{2,1,0:T(8,128)(2,1)}, bf16[8,2048,256]{2,1,0:T(8,128)(2,1)}) custom-call(bf16[4,64,2048]{2,1,0:T(8,128)(2,1)} %pad_maximum_fusion.refs_0_, bf16[128,256]{1,0:T(8,128)(2,1)} %fusion.80.refs_1_, bf16[8,512,1024]{2,1,0:T(8,128)(2,1)} %refs_2_.3, ...), custom_call_target="tpu_custom_call" | custom-call | tf_op jit(solution)/shard_map/pallas_call | solution.py:273
  193.1 1.4 slice.87
  194.7 2.0 slice_reduce_fusion
  196.9 0.5 multiply_multiply_fusion
  197.4 4.8 multiply_reduce_fusion.6
  202.9 4.8 multiply_reduce_fusion.7
  207.7 1.0 copy-done.5
  209.1 1.6 fusion.110
  211.3 4.2 subtract_convert_fusion.3
  215.6 2.4 fusion.112
  218.0 5.1 fusion.48
  223.5 5.3 multiply_reduce_fusion.5
  228.8 1.1 multiply_convert_fusion.1.refs_0_
  229.9 333.9 %shard_map.273 = (bf16[4096,2048]{1,0:T(8,128)(2,1)}, bf16[4096,2048]{1,0:T(8,128)(2,1)}, bf16[8,2048,256]{2,1,0:T(8,128)(2,1)}, bf16[8,2048,256]{2,1,0:T(8,128)(2,1)}) custom-call(bf16[128,2048]{1,0:T(8,128)(2,1)} %multiply_convert_fusion.1.refs_0_, bf16[128,2048]{1,0:T(8,128)(2,1)} %refs_1_.1, ...), custom_call_target="tpu_custom_call", output_to_operand_aliasing={{2}: (4, {}), {3}: (5, {})} | custom-call | tf_op jit(solution)/shard_map/pallas_call | solution.py:273
  563.9 0.6 dynamic-slice_maximum_fusion
  564.4 0.9 pad.9.router_ref
  565.3 1.3 slice.101
  567.8 0.7 select_bitcast_fusion.slots_ref
  568.5 38.2 %shard_map.274 = (bf16[8,768,2048]{2,1,0:T(8,128)(2,1)}, bf16[8,768,2048]{2,1,0:T(8,128)(2,1)}, f32[8,768,128]{2,1,0:T(8,128)}) custom-call(s32[16,8,256]{2,1,0:T(8,128)} %select_bitcast_fusion.slots_ref, bf16[4096,2048]{1,0:T(8,128)(2,1)} %get-tuple-element.48.x_ref, bf16[4096,2048]{1,0:T(8,128)(2,1)} %get-tuple-element.49.g_ref, ...), custom_call_target="tpu_custom_call" | custom-call | tf_op jit(solution)/shard_map/pallas_call | solution.py:707
  606.7 76.5 %shard_map.275 = (bf16[8,768,2048]{2,1,0:T(8,128)(2,1)}, bf16[8,768,2048]{2,1,0:T(8,128)(2,1)}, bf16[8,768,128]{2,1,0:T(8,128)(2,1)}, bf16[8,2048,256]{2,1,0:T(8...) custom-call(s32[1]{0:T(128)} %bitcast.26.first_ref, bf16[8,768,2048]{2,1,0:T(8,128)(2,1)} %get-tuple-element.50.x_ref, ...), custom_call_target="tpu_custom_call" | custom-call | tf_op jit(solution)/shard_map/pallas_call | solution.py:743
  683.2 38.3 %shard_map.276 = (bf16[4096,2048]{1,0:T(8,128)(2,1)}, bf16[4096,2176]{1,0:T(8,128)(2,1)}) custom-call(s32[16,8,256]{2,1,0:T(8,128)} %select_bitcast_fusion.slots_ref, bf16[8,768,2048]{2,1,0:T(8,128)(2,1)} %get-tuple-element.55.y_ref, bf16[8,768,2048]{2,1,0:T(8,128)(2,1)} %get-tuple-element.56.dx_ref, bf16[8,768,128]{2,1,0:T(8,128)(2,1)} %get-tuple-element.57.probs_ref), custom_call_target="tpu_custom_call" | custom-call | tf_op jit(solution)/shard_map/pallas_call | solution.py:781
  721.5 133.7 %shard_map.277 = (f32[128,2176]{1,0:T(8,128)}, bf16[2,512,1024]{2,1,0:T(8,128)(2,1)}, bf16[2,512,1024]{2,1,0:T(8,128)(2,1)}) custom-call(bf16[4,8,128,2176]{3,2,1,0:T(8,128)(2,1)} %bitcast.159, bf16[8,2048,256]{2,1,0:T(8,128)(2,1)} %get-tuple-element.59.refs_1_.refs_6_, bf16[8,2048,256]{2,1,0:T(8,128)(2,1)} %get-tuple-element.60.refs_2_.refs_7_), custom_call_target="tpu_custom_call" | custom-call | tf_op jit(solution)/shard_map/pallas_call | solution.py:510
  855.2 1.6 fusion.113
  857.1 1.1 multiply_reduce_fusion.8
  858.2 2.0 multiply_reduce_fusion
  860.3 1.8 subtract_add_fusion
  862.1 6.4 fusion.45
  869.9 0.6 fusion.43
  870.4 0.9 multiply_subtract_fusion
  871.4 1.0 fusion.62
  872.9 6.5 fusion.5
  879.4 0.6 subtract_convert_fusion
  880.0 6.5 fusion.28
  887.1 7.8 fusion.60
  894.8 1.0 concatenate.60
  895.8 1.3 convolution_convert_fusion.4
  897.4 1.8 concatenate.61
  899.2 1.8 concatenate.62
  901.1 1.8 concatenate.63
  902.9 0.9 broadcast_in_dim.52
  903.8 4.0 concatenate.57.refs_4_
  907.9 6.8 convolution_convert_fusion
  914.6 5.7 convolution_convert_fusion.1
  920.3 5.7 convolution_convert_fusion.2
  926.0 5.6 convolution_convert_fusion.3
  931.5 412.2 %shard_map.278 = (f32[64,2048]{1,0:T(8,128)}, f32[64,2048]{1,0:T(8,128)}, f32[64,2048]{1,0:T(8,128)}, f32[64,2048]{1,0:T(8,128)}, f32[64,128]{1,0:T(8,128)}, /*i...) custom-call(bf16[4,8,64,2048]{3,2,1,0:T(8,128)(2,1)} %bitcast.158, ...), custom_call_target="tpu_custom_call" | custom-call | tf_op jit(solution)/shard_map/pallas_call | solution.py:510
  1343.7 10.7 maximum_convert_fusion.1
  1354.4 10.7 maximum_convert_fusion
  1365.1 2.7 fusion.59
  1367.8 2.1 add_convert_fusion
  1370.0 0.7 slice_reduce_fusion.4
  1370.7 1.9 copy.177
  1372.6 1.9 copy.178
  1374.5 0.8 copy.179
  1375.3 0.8 copy.180
  1376.0 0.6 copy.181
  (95 shorter events, 6.8 us)
Async XLA Ops:
  193.1 3.6 copy-start
  194.5 369.4 %copy-start.8 = (bf16[32,64,128]{2,1,0:T(8,128)(2,1)}, bf16[32,64,128]{2,1,0:T(8,128)(2,1)S(1)}, u32[]{:S(2)}) copy-start(bf16[32,64,128]{2,1,0:T(8,128)(2,1)S(1)} %slice.116) | copy-start | bytes 1572868
  202.2 5.5 copy-start.3
  202.9 7.8 copy-start.26
  207.7 1.0 copy-start.5
  218.0 5.5 copy-start.18
  223.1 6.8 copy-start.27
  223.5 340.4 %copy-start.16 = (bf16[16,128,128]{2,1,0:T(8,128)(2,1)}, bf16[16,128,128]{2,1,0:T(8,128)(2,1)S(1)}, u32[]{:S(2)}) copy-start(bf16[16,128,128]{2,1,0:T(8,128)(2,1)S(1)} %convolution_convert_fusion.6) | copy-start | bytes 1572868
  228.7 629.5 %copy-start.1 = (f32[128,2048]{1,0:T(8,128)}, f32[128,2048]{1,0:T(8,128)S(1)}, u32[]{:S(2)}) copy-start(f32[128,2048]{1,0:T(8,128)S(1)} %get-tuple-element.126) | copy-start | bytes 3145732
  860.2 8.3 copy-start.19
  860.2 8.3 copy-start.28
  862.1 7.2 copy-start.11
  862.1 7.2 copy-start.12
  862.1 7.7 copy-start.9
  862.1 7.7 copy-start.10
  869.1 2.3 copy-start.4
  869.1 2.3 copy-start.6
  872.9 13.6 copy-start.13
  880.0 14.8 %copy-start.15 = (bf16[128,2048]{1,0:T(8,128)(2,1)}, bf16[128,2048]{1,0:T(8,128)(2,1)S(1)}, u32[]{:S(2)}) copy-start(bf16[128,2048]{1,0:T(8,128)(2,1)S(1)} %subtract_convert_fusion) | copy-start | bytes 1572868
  886.5 9.3 copy-start.7
  887.0 7.8 copy-start.21
  907.9 6.8 copy-start.14
  914.6 5.7 copy-start.22
  920.3 5.7 copy-start.17
  1354.3 10.8 copy-start.25
  1354.3 13.5 copy-start.2
  1354.3 15.6 %copy-start.20 = (f32[64,128]{1,0:T(8,128)S(1)}, f32[64,128]{1,0:T(8,128)}, u32[]{:S(2)}) copy-start(f32[64,128]{1,0:T(8,128)} %get-tuple-element.68) | copy-start | bytes 98308
  1365.1 9.4 copy-start.24
  1365.1 10.2 copy-start.23

commit v5 on v4

--- a/solution.py
+++ b/solution.py
@@ -113,7 +113,18 @@
     return copies
 
 
-def gather_kernel(n_dp, n_expert, n_items, places, cuts, n_cut, n_out, *refs):
+def moves(pairs, local):
+    return [
+        pltpu.make_async_copy(source, target, local.at[i])
+        for i, (source, target) in enumerate(pairs)
+    ]
+
+
+def nothing(ins, outs):
+    return []
+
+
+def gather_kernel(n_dp, n_expert, n_items, places, cuts, puts, n_cut, n_out, *refs):
     z, j, chip, core = place_of()
     chips = n_expert // 2
     square = chips == 4
@@ -134,6 +145,7 @@
         send_x,
         recv_x,
         local_x,
+        local_y,
     ) = refs[at + n_items + n_out :]
     greet(n_dp, n_expert)
     mate = (z, chip * 2 + 1 - core)
@@ -204,6 +216,7 @@
     for d in range(1, n_dp):
         at_distance(d, relay)
     copies = exchange(n_dp, cuts(cut_in, cut_out), send_x, recv_x, local_x)
+    copies += moves(puts(cut_in, cut_out), local_y)
     for copy in copies:
         copy.start()
 
@@ -265,13 +278,15 @@
         copy.wait()
 
 
-def gather_call(n_dp, n_expert, items, shapes, places, cut_in, cut_shapes, cuts, aliases, number):
+def gather_call(
+    n_dp, n_expert, items, shapes, places, cut_in, cut_shapes, cuts, aliases, number, puts=nothing
+):
     chips = n_expert // 2
     n, m = len(items), len(cut_shapes)
     dma = pltpu.SemaphoreType.DMA
     anywhere = pl.BlockSpec(memory_space=pl.ANY)
     return pl.pallas_call(
-        functools.partial(gather_kernel, n_dp, n_expert, n, places, cuts, len(cut_in), m),
+        functools.partial(gather_kernel, n_dp, n_expert, n, places, cuts, puts, len(cut_in), m),
         out_shape=[*shapes, *cut_shapes],
         in_specs=[anywhere] * (n + len(cut_in)),
         out_specs=[anywhere] * (n + m),
@@ -283,16 +298,17 @@
             dma((n, n_dp, chips)),
             dma((n, n_dp, chips)),
             dma((n,)),
-            dma((max(m, 1), n_dp)),
-            dma((max(m, 1), n_dp)),
-            dma((max(m, 1),)),
+            dma((4, n_dp)),
+            dma((4, n_dp)),
+            dma((4,)),
+            dma((4 * n_dp,)),
         ],
         input_output_aliases=aliases,
         compiler_params=pltpu.CompilerParams(collective_id=number, has_side_effects=True),
     )(*items, *cut_in)
 
 
-def scatter_kernel(n_dp, n_expert, n_items, n_cut, n_out, cuts, rings, n_rings, *refs):
+def scatter_kernel(n_dp, n_expert, n_items, n_cut, n_out, cuts, puts, rings, n_rings, *refs):
     z, j, chip, core = place_of()
     chips = n_expert // 2
     square = chips == 4
@@ -320,6 +336,7 @@
         send_x,
         recv_x,
         local_x,
+        local_y,
     ) = refs
     greet(n_dp, n_expert)
     mate = (z, chip * 2 + 1 - core)
@@ -378,10 +395,19 @@
             (z, to_chip(k) * 2 + core),
         )
 
-    def to_plane(i, k):
-        to = (z + k) % n_dp
+    def along(i, plane, way):
+        slot = n_dp - (z - 1) + plane if way else plane - (z + 1)
         return remote(
-            got_a[i].at[0, to], got_c[i].at[k - 1], send_c.at[i, k], recv_c.at[i, k], (to, j)
+            got_a[i].at[0, plane],
+            got_c[i].at[slot],
+            send_c.at[i, plane],
+            recv_c.at[i, slot],
+            (z - 1 if way else z + 1, j),
+        )
+
+    def from_along(i, slot):
+        return remote(
+            got_c[i].at[slot], got_c[i].at[slot], send_c.at[i, 0], recv_c.at[i, slot], mate
         )
 
     f32 = jnp.float32
@@ -417,6 +443,7 @@
             load(i, k, at).start()
             ahead[rings[i]] += 1
     copies = exchange(n_dp, cuts(cut_in, cut_out), send_x, recv_x, local_x)
+    copies += moves(puts(cut_in, cut_out), local_y)
     for copy in copies:
         copy.start()
 
@@ -456,29 +483,47 @@
             for k in range(1, chips):
                 send_far(i, k).wait_recv()
         heard = 2 if square else chips - 1
-        for k in [*range(1, n_dp), 0]:
-            plane = (z + k) % n_dp
-
-            def target(unused, at, total):
-                got_a[i][0, plane, at] = total.astype(got_a[i].dtype)
-
-            terms = [lambda unused, at: got_a[i][0, plane, at]]
-            for other in range(heard):
-                terms.append(lambda unused, at, other=other: got_b[i][other, plane, at])
-            add(i, 1, target, terms)
-            if k:
-                to_plane(i, k).start()
+
+        def target(plane, at, total):
+            got_a[i][0, plane, at] = total.astype(got_a[i].dtype)
+
+        terms = [lambda plane, at: got_a[i][0, plane, at]]
+        for other in range(heard):
+            terms.append(lambda plane, at, other=other: got_b[i][other, plane, at])
+        add(i, n_dp, target, terms)
+        for d in range(n_dp - 1, 0, -1):
+            for way in (0, 1):
+                plane = z - d if way else z + d
+                arrives = z < n_dp - 1 if way else z > 0
+                slot = n_dp - z + plane if way else plane - z
+
+                @pl.when(plane >= 0 if way else plane < n_dp)
+                def _():
+                    @pl.when(arrives)
+                    def _():
+                        from_along(i, slot).wait_recv()
+                        grow(i, 0, plane, 1, lambda unused, at: got_c[i][slot, at])
+
+                    along(i, plane, way).start()
+
     for i in range(n_items):
-        for k in range(1, n_dp):
-            to_plane(i, k).wait_recv()
-
-        def target(unused, at, total):
+
+        def own(unused, at, total):
             targets[i][at] = total
 
-        terms = [lambda unused, at: got_a[i][0, z, at]]
-        for k in range(n_dp - 1):
-            terms.append(lambda unused, at, k=k: got_c[i][k, at])
-        add(i, 1, target, terms)
+        add(i, 1, own, [lambda unused, at: got_a[i][0, z, at]])
+        for slot, arrives in ((0, z > 0), (n_dp, z < n_dp - 1)):
+
+            @pl.when(arrives)
+            def _():
+                from_along(i, slot).wait_recv()
+                add(
+                    i,
+                    1,
+                    own,
+                    [lambda unused, at: targets[i][at], lambda unused, at: got_c[i][slot, at]],
+                )
+
     for i in range(n_items):
         for k in range(chips):
             to_mate(i, k).wait_send()
@@ -490,13 +535,25 @@
         else:
             for k in range(1, chips):
                 send_far(i, k).wait_send()
-        for k in range(1, n_dp):
-            to_plane(i, k).wait_send()
+        for plane in range(n_dp):
+
+            @pl.when(z != plane)
+            def _():
+                remote(
+                    got_a[i].at[0, plane],
+                    got_c[i].at[0],
+                    send_c.at[i, plane],
+                    recv_c.at[i, 0],
+                    mate,
+                ).wait_send()
+
     for copy in copies:
         copy.wait()
 
 
-def scatter_call(n_dp, n_expert, items, cut_in, cut_shapes, cuts, number):
+def scatter_call(
+    n_dp, n_expert, items, cut_in, cut_shapes, cuts, number, aliases, puts=nothing
+):
     chips = n_expert // 2
     square = chips == 4
     n, m = len(items), len(cut_shapes)
@@ -509,7 +566,7 @@
     heard = 2 if square else chips - 1
     return pl.pallas_call(
         functools.partial(
-            scatter_kernel, n_dp, n_expert, n, len(cut_in), m, cuts, rings, len(kinds)
+            scatter_kernel, n_dp, n_expert, n, len(cut_in), m, cuts, puts, rings, len(kinds)
         ),
         out_shape=[*[jax.ShapeDtypeStruct(block, jnp.float32) for block in blocks], *cut_shapes],
         in_specs=[anywhere] * (n + len(cut_in)),
@@ -518,30 +575,34 @@
             *[pltpu.VMEM((2, n_dp, *kind), bf16) for kind in kinds],
             *[pltpu.VMEM((chips, n_dp, *block), bf16) for block in blocks],
             *[pltpu.VMEM((heard, n_dp, *block), bf16) for block in blocks],
-            *[pltpu.VMEM((n_dp - 1, *block), bf16) for block in blocks],
+            *[pltpu.VMEM((n_dp + 1, *block), bf16) for block in blocks],
             *[pltpu.VMEM((2, n_dp // 2, *(block if square else (16, 128))), bf16) for block in blocks],
             dma((n, chips)),
             dma((n, chips)),
             dma((n, chips)),
             dma((n, chips)),
             dma((n, n_dp)),
-            dma((n, n_dp)),
+            dma((n, n_dp + 1)),
             dma((n, 3)),
             dma((n, 3)),
             dma((len(kinds), 2)),
-            dma((max(m, 1), n_dp)),
-            dma((max(m, 1), n_dp)),
-            dma((max(m, 1),)),
+            dma((4, n_dp)),
+            dma((4, n_dp)),
+            dma((4,)),
+            dma((4 * n_dp,)),
         ],
+        input_output_aliases=aliases,
         compiler_params=pltpu.CompilerParams(
             collective_id=number, has_side_effects=True, vmem_limit_bytes=62 * 1024 * 1024
         ),
     )(*items, *cut_in)
 
 
-def scatter_all(n_dp, n_expert, items, cut_in, cut_shapes, cuts, number):
+def scatter_all(
+    n_dp, n_expert, items, cut_in, cut_shapes, cuts, number, aliases=(), puts=nothing
+):
     chips = n_expert // 2
-    blocks = (2 * chips if chips != 4 else 7) * n_dp + n_dp + 3
+    blocks = (2 * chips - 1 if chips != 4 else 7) * n_dp + n_dp + 3
     need = sum(blocks * item.shape[2] * item.shape[3] * 2 for item in items)
     kinds = {item.shape[2:] for item in items}
     need += sum(2 * n_dp * kind[0] * kind[1] * 2 for kind in kinds)
@@ -559,8 +620,10 @@
             [items[i][..., ends[i][0] : ends[i][1]] if pieces > 1 else items[i] for i in used],
             cut_in if first else [],
             cut_shapes if first else [],
-            cuts if first else lambda ins, outs: [],
+            cuts if first else nothing,
             number + piece,
+            {len(used) + a: len(used) + b for a, b in aliases} if first else {},
+            puts if first else nothing,
         )
         for i, out in zip(used, outs):
             results[i].append(out)
@@ -602,31 +665,43 @@
         grows_ref[e] = picked[e * size : (e + 1) * size]
 
 
-def expert_kernel(
-    steps,
-    half,
-    first_ref,
-    x_ref,
-    g_ref,
-    gates_ref,
-    gate_ref,
-    up_ref,
-    down_ref,
-    y_ref,
-    dx_ref,
-    probs_ref,
-    dgate_ref,
-    dup_ref,
-    ddown_ref,
-    sum_gate,
-    sum_up,
-):
+def expert_kernel(steps, half, n_weights, n_into, names_ref, x_ref, g_ref, gates_ref, *refs):
+    weights, refs = refs[:n_weights], refs[n_weights:]
+    down_ref, refs = refs[0], refs[1 + n_into :]
+    (
+        y_ref,
+        dx_ref,
+        probs_ref,
+        dgate_ref,
+        dup_ref,
+        ddown_ref,
+        sum_gate,
+        sum_up,
+    ) = refs
     bf16 = jnp.bfloat16
-    x, g = x_ref[0], g_ref[0]
-    rows, width = x.shape
+    g = g_ref[0]
+    rows, width = x_ref.shape[1:]
+    part = dgate_ref.shape[2]
     gate = gates_ref[0][:, :1]
-    gate_mid = dot(x, gate_ref[0], (1, 0))
-    up_mid = dot(x, up_ref[0], (1, 0))
+    if n_weights == 2:
+        piece = 512
+        gate_ref, up_ref = weights
+        gate_mid = dot(x_ref[0], gate_ref[0], (1, 0))
+        up_mid = dot(x_ref[0], up_ref[0], (1, 0))
+        spans = [
+            (pl.ds(at, piece), gate_ref, up_ref, pl.ds(at, piece), pl.ds(0, part), pl.ds(0, part))
+            for at in range(0, width, piece)
+        ]
+    else:
+        piece = width // n_weights
+        spans = []
+        gate_mid = up_mid = 0.0
+        for n, ref in enumerate(weights):
+            span = pl.ds(pl.multiple_of(names_ref[1 + n], piece), piece)
+            x_part = x_ref[0, :, span]
+            gate_mid = gate_mid + dot(x_part, ref[0, :, :part], (1, 0))
+            up_mid = up_mid + dot(x_part, ref[0, :, part:], (1, 0))
+            spans.append((span, ref, ref, pl.ds(0, piece), pl.ds(0, part), pl.ds(part, part)))
     sigmoid = 1.0 / (1.0 + jnp.exp(-gate_mid))
     silu = gate_mid * sigmoid
     hidden = silu * up_mid
@@ -635,7 +710,7 @@
     grad_gates = jnp.sum(grad_plain * hidden_low.astype(jnp.float32), axis=1, keepdims=True)
     high = grad_gates.astype(bf16).astype(jnp.float32)
     lane = lax.broadcasted_iota(jnp.int32, (rows, 128), 1)
-    name = first_ref[0] + pl.program_id(0)
+    name = names_ref[0] + pl.program_id(0)
     probs_ref[0] = (
         jnp.where(lane == name, high, 0.0) + jnp.where(lane == name + half, grad_gates - high, 0.0)
     ).astype(bf16)
@@ -645,43 +720,43 @@
     ).astype(bf16)
     grad_up = (grad_hidden * silu).astype(bf16)
     scaled = (hidden * gate).astype(bf16)
-    piece = 512
     for at in range(0, width, piece):
         y_ref[0, :, at : at + piece] = (
             dot(hidden_low, down_ref[0, :, at : at + piece], (1, 0)) * gate
         ).astype(bf16)
-        dx_ref[0, :, at : at + piece] = (
-            dot(grad_gate, gate_ref[0, at : at + piece, :], (1, 1))
-            + dot(grad_up, up_ref[0, at : at + piece, :], (1, 1))
+    for span, gate_ref, up_ref, here, gate_columns, up_columns in spans:
+        dx_ref[0, :, span] = (
+            dot(grad_gate, gate_ref[0, here, gate_columns], (1, 1))
+            + dot(grad_up, up_ref[0, here, up_columns], (1, 1))
         ).astype(bf16)
     step = pl.program_id(1)
-    for at in range(0, width, piece):
-        x_part = x_ref[0, :, at : at + piece]
+    for span, *unused in spans:
+        x_part = x_ref[0, :, span]
         here_gate = dot(x_part, grad_gate, (0, 0))
         here_up = dot(x_part, grad_up, (0, 0))
-        here_down = dot(scaled, g_ref[0, :, at : at + piece], (0, 0))
+        here_down = dot(scaled, g_ref[0, :, span], (0, 0))
         if steps == 1:
-            dgate_ref[0, at : at + piece, :] = here_gate.astype(bf16)
-            dup_ref[0, at : at + piece, :] = here_up.astype(bf16)
-            ddown_ref[0, :, at : at + piece] = here_down
+            dgate_ref[0, span, :] = here_gate.astype(bf16)
+            dup_ref[0, span, :] = here_up.astype(bf16)
+            ddown_ref[0, :, span] = here_down
             continue
 
         @pl.when(step == 0)
         def _():
-            sum_gate[at : at + piece, :] = here_gate
-            sum_up[at : at + piece, :] = here_up
-            ddown_ref[0, :, at : at + piece] = here_down
+            sum_gate[span, :] = here_gate
+            sum_up[span, :] = here_up
+            ddown_ref[0, :, span] = here_down
 
         @pl.when(step > 0)
         def _():
-            sum_gate[at : at + piece, :] += here_gate
-            sum_up[at : at + piece, :] += here_up
-            ddown_ref[0, :, at : at + piece] += here_down
+            sum_gate[span, :] += here_gate
+            sum_up[span, :] += here_up
+            ddown_ref[0, :, span] += here_down
 
         @pl.when(step == steps - 1)
         def _():
-            dgate_ref[0, at : at + piece, :] = sum_gate[at : at + piece, :].astype(bf16)
-            dup_ref[0, at : at + piece, :] = sum_up[at : at + piece, :].astype(bf16)
+            dgate_ref[0, span, :] = sum_gate[span, :].astype(bf16)
+            dup_ref[0, span, :] = sum_up[span, :].astype(bf16)
 
 
 def place_kernel(number, slots_ref, y_ref, dx_ref, probs_ref, out_ref, back_ref):
@@ -723,9 +798,9 @@
     )(slots, x_all, g_all, router)
 
 
-def expert_call(first, half, rows, grows, gates, gate, up, down):
-    number, depth, _ = rows.shape
-    part = gate.shape[2]
+def expert_call(names, half, low, number, rows, grows, gates, weights, down, into=()):
+    total, depth, _ = rows.shape
+    part = down.shape[1]
     size = depth
     while size > 768:
         size //= 2
@@ -733,44 +808,50 @@
     bf16 = jnp.bfloat16
     f32 = jnp.float32
 
-    def by_rows(width):
-        return pl.BlockSpec((1, size, width), lambda e, r: (e, r, 0))
+    def from_rows(width):
+        return pl.BlockSpec((1, size, width), lambda e, r: (e + low, r, 0))
 
     def whole(*shape):
         return pl.BlockSpec((1, *shape), lambda e, r: (e, 0, 0))
 
+    def from_whole(*shape):
+        return pl.BlockSpec((1, *shape), lambda e, r: (e + low, 0, 0))
+
     keep = (D, part) if steps > 1 else (16, 128)
     return pl.pallas_call(
-        functools.partial(expert_kernel, steps, half),
+        functools.partial(expert_kernel, steps, half, len(weights), len(into)),
         grid=(number, steps),
         in_specs=[
             pl.BlockSpec(memory_space=pltpu.SMEM),
-            by_rows(D),
-            by_rows(D),
-            by_rows(128),
+            from_rows(D),
+            from_rows(D),
+            from_rows(128),
+            *[(from_whole if len(weights) == 2 else whole)(*one.shape[1:]) for one in weights],
+            from_whole(part, D),
+            *[pl.BlockSpec(memory_space=pl.ANY)] * len(into),
+        ],
+        out_specs=[
+            from_rows(D),
+            from_rows(D),
+            from_rows(128),
             whole(D, part),
             whole(D, part),
-            whole(part, D),
-        ],
-        out_specs=[
-            by_rows(D),
-            by_rows(D),
-            by_rows(128),
-            whole(D, part),
-            whole(D, part),
-            whole(part, D),
+            from_whole(part, D),
         ],
         out_shape=[
-            jax.ShapeDtypeStruct((number, depth, D), bf16),
-            jax.ShapeDtypeStruct((number, depth, D), bf16),
-            jax.ShapeDtypeStruct((number, depth, 128), bf16),
+            jax.ShapeDtypeStruct((total, depth, D), bf16),
+            jax.ShapeDtypeStruct((total, depth, D), bf16),
+            jax.ShapeDtypeStruct((total, depth, 128), bf16),
             jax.ShapeDtypeStruct((number, D, part), bf16),
             jax.ShapeDtypeStruct((number, D, part), bf16),
-            jax.ShapeDtypeStruct((number, part, D), f32),
+            jax.ShapeDtypeStruct((total, part, D), f32),
         ],
+        input_output_aliases={
+            5 + len(weights) + i: out for i, out in zip(range(len(into)), (0, 1, 2, 5))
+        },
         scratch_shapes=[pltpu.VMEM(keep, f32), pltpu.VMEM(keep, f32)],
         compiler_params=pltpu.CompilerParams(vmem_limit_bytes=BIG),
-    )(first, rows, grows, gates, gate, up, down)
+    )(names, rows, grows, gates, *weights, down, *into)
 
 
 def place_call(number, slots, y, dx, probs):
@@ -846,27 +927,72 @@
     weights = jnp.stack([w_query, w_key, w_value, w_out])
     depth = w_gate.shape[1]
     early = number // 4
+    beside = early + number // 8
+    late = number - number // 4
+    back_beside = number // 8
+    back_third = back_beside + number // 4
+    back_late = back_third + number // 8
+    me = lax.axis_index("dp")
     cut_shape = jax.ShapeDtypeStruct((number, n_dp * depth, part), bf16)
 
     def row_block(size):
         return lambda ref, block: ref.at[pl.ds(pl.multiple_of(block * size, 16), size)]
+
+    def columns_at(at):
+        return pl.ds(pl.multiple_of(at * part, part), part)
+
+    def rows_at(at):
+        return pl.ds(pl.multiple_of(at * depth, depth), depth)
 
     def recut(low, high):
         def cuts(ins, outs):
             def pair(n):
-                def source(to):
-                    columns = pl.ds(pl.multiple_of(to * part, part), part)
-                    return ins[n].at[pl.ds(low, high - low), :, columns]
-
-                def target(at):
-                    here = pl.ds(pl.multiple_of(at * depth, depth), depth)
-                    return outs[n].at[pl.ds(low, high - low), here]
-
-                return source, target
+                chosen = pl.ds(low, high - low)
+                return (
+                    lambda to: ins[n].at[chosen, :, columns_at(to)],
+                    lambda at: outs[n].at[chosen, rows_at(at)],
+                )
 
             return [pair(0), pair(1)]
 
         return cuts
+
+    def permuted(pieces, after):
+        *pieces, unused = lax.optimization_barrier((*pieces, after))
+        return [pieces[0]] + [
+            lax.ppermute(pieces[k], "dp", [(i, (i + k) % n_dp) for i in range(n_dp)])
+            for k in range(1, n_dp)
+        ]
+
+    def weight_pieces(low, high, after):
+        return permuted(
+            [
+                jnp.concatenate(
+                    [
+                        lax.dynamic_slice_in_dim(one[low:high], (me + k) % n_dp * part, part, 2)
+                        for one in (w_gate, w_up)
+                    ],
+                    axis=2,
+                )
+                for k in range(n_dp)
+            ],
+            after,
+        )
+
+    def grad_pieces(gate, up, low, high, after):
+        return permuted(
+            [
+                jnp.concatenate(
+                    [
+                        lax.dynamic_slice_in_dim(one[low:high], (me + k) % n_dp * depth, depth, 1)
+                        for one in (gate, up)
+                    ],
+                    axis=2,
+                )
+                for k in range(n_dp)
+            ],
+            after,
+        )
 
     weights_all, extras_all, gate_early, up_early = gather_call(
         n_dp,
@@ -925,18 +1051,35 @@
     mlp_low = mlp_normed.astype(bf16)
     router = jax.nn.softmax(product(mlp_low, router_weight, "td,de->te"), axis=-1)
 
+    pieces = []
+    if beside > early:
+        pieces = weight_pieces(early, beside, extras_all)
+        mlp_low, *pieces = lax.optimization_barrier((mlp_low, *pieces))
+
+    def put_weights(ins, outs):
+        chosen = pl.ds(early, beside - early)
+        pairs = []
+        for k, piece in enumerate(ins[4:]):
+            here = rows_at((lax.axis_index("dp") + n_dp - k) % n_dp)
+            for n in range(2):
+                columns = piece.at[:, :, pl.ds(n * part, part)]
+                pairs.append((columns, outs[n].at[chosen, here]))
+        return pairs
+
     mlp_all, cotangent_all, gate_cut, up_cut = gather_call(
         n_dp,
         n_expert,
         [mlp_low, cotangent],
         [jax.ShapeDtypeStruct((groups * count, D), bf16)] * 2,
         [row_block(count)] * 2,
-        [w_gate, w_up, gate_early, up_early],
+        [w_gate, w_up, gate_early, up_early, *pieces],
         [cut_shape, cut_shape],
-        recut(early, number),
+        recut(beside, late),
         {4: 2, 5: 3},
         1,
-    )
+        put_weights,
+    )
+    late_pieces = weight_pieces(late, number, mlp_all)
     first = lax.axis_index("expert") * number
     hit = lax.dynamic_slice_in_dim(hits_all, first, number, 1).reshape(groups, count, number)
     before = jnp.tril(jnp.ones((count, count), bf16), -1)
@@ -950,42 +1093,70 @@
         jnp.roll(router_weight, -first, axis=1), ((0, 0), (0, width - experts_all))
     )
     rows, grows, gates = pick_call(number, experts_all, slots, mlp_all, cotangent_all, router_own)
-    weighted, grad_rows, grad_gates, grad_gate_cut, grad_up_cut, grad_down_part = expert_call(
-        first[None], experts_all, rows, grows, gates, gate_cut, up_cut, w_down
+    *outs, gate_soon, up_soon, down_soon = expert_call(
+        first[None],
+        experts_all,
+        0,
+        late,
+        rows,
+        grows,
+        gates,
+        [gate_cut, up_cut],
+        w_down,
+    )
+    offsets = [(me + n_dp - k) % n_dp * depth for k in range(n_dp)]
+    weighted, grad_rows, grad_gates, gate_rest, up_rest, grad_down_part = expert_call(
+        jnp.stack([first + late, *offsets]),
+        experts_all,
+        late,
+        number - late,
+        rows,
+        grows,
+        gates,
+        late_pieces,
+        w_down,
+        [*outs, down_soon],
     )
     part_out, part_back = place_call(number, slots, weighted, grad_rows, grad_gates)
 
-    def way_back(low, high):
-        def cuts(ins, outs):
-            def pair(n):
-                def source(to):
-                    here = pl.ds(pl.multiple_of(to * depth, depth), depth)
-                    return ins[n].at[pl.ds(low, high - low), here]
-
-                def target(at):
-                    columns = pl.ds(pl.multiple_of(at * part, part), part)
-                    return outs[n].at[:, :, columns]
-
-                return source, target
-
-            return [pair(0), pair(1)]
-
-        return cuts
-
-    def way_shape(size):
-        return jax.ShapeDtypeStruct((size, depth, ff), bf16)
-
-    back_items = [part_back.reshape(n_dp, n_expert, count, D + width)]
-    sooner = number // 4
-    (back,), (gate_first, up_first) = scatter_all(
+    def ways(low, high, at, ins, outs):
+        def pair(n):
+            return (
+                lambda to: ins[n].at[pl.ds(low, high - low), rows_at(to)],
+                lambda here: outs[n].at[pl.ds(low + at, high - low), :, columns_at(here)],
+            )
+
+        return [pair(0), pair(1)]
+
+    def put_grads(low, high, pieces, outs):
+        pairs = []
+        for k, piece in enumerate(pieces):
+            here = columns_at((lax.axis_index("dp") + n_dp - k) % n_dp)
+            for n in range(2):
+                columns = piece.at[:, :, pl.ds(n * part, part)]
+                pairs.append((columns, outs[n].at[pl.ds(low, high - low), :, here]))
+        return pairs
+
+    pieces = []
+    if back_beside:
+        pieces = grad_pieces(gate_soon, up_soon, 0, back_beside, gate_soon)
+        part_back, *pieces = lax.optimization_barrier((part_back, *pieces))
+    way_shapes = [jax.ShapeDtypeStruct((number, depth, ff), bf16)] * 2
+    (back,), (gate_third, up_third) = scatter_all(
         n_dp,
         n_expert,
-        back_items,
-        [grad_gate_cut, grad_up_cut],
-        [way_shape(sooner)] * 2,
-        way_back(0, sooner),
+        [part_back.reshape(n_dp, n_expert, count, D + width)],
+        [gate_soon, up_soon, *pieces],
+        way_shapes,
+        lambda ins, outs: ways(back_beside, back_third, 0, ins, outs),
         8,
-    )
+        (),
+        lambda ins, outs: put_grads(0, back_beside, ins[2:], outs),
+    )
+    pieces = []
+    if back_late > back_third:
+        pieces = grad_pieces(gate_soon, up_soon, back_third, back_late, back)
+        part_out, *pieces = lax.optimization_barrier((part_out, *pieces))
 
     grad_final = cotangent.astype(jnp.float32)
     grad_mlp = back[:, :D]
@@ -1045,7 +1216,7 @@
     def blocks_of(value):
         return value.astype(bf16).reshape(n_dp, n_expert, rows_each, -1)
 
-    sums, (gate_last, up_last) = scatter_all(
+    sums, (gate_back, up_back) = scatter_all(
         n_dp,
         n_expert,
         [
@@ -1059,17 +1230,20 @@
             )
         ]
         + [part_out.reshape(n_dp, n_expert, count, D)],
-        [grad_gate_cut, grad_up_cut],
-        [way_shape(number - sooner)] * 2,
-        way_back(sooner, number),
+        [gate_third, up_third, gate_soon, up_soon, gate_rest, up_rest, *pieces],
+        way_shapes,
+        lambda ins, outs: ways(back_late, late, 0, ins[2:4], outs)
+        + ways(0, number - late, late, ins[4:6], outs),
         16,
+        ((0, 0), (1, 1)),
+        lambda ins, outs: put_grads(back_third, back_late, ins[6:], outs),
     )
     grad_out_part, grad_value_part, grad_key_part, grad_query_part, small_part, summed = sums
     output = (middle + summed).astype(bf16)
     grad_router_part = small_part[:, :experts_all]
     gain_parts = [small_part[:, experts_all + i] for i in range(4)]
-    grad_gate_part = jnp.concatenate([gate_first, gate_last], axis=0).astype(jnp.float32)
-    grad_up_part = jnp.concatenate([up_first, up_last], axis=0).astype(jnp.float32)
+    grad_gate_part = gate_back.astype(jnp.float32)
+    grad_up_part = up_back.astype(jnp.float32)
     return (
         output,
         grad_inputs,

time: 1390 us -> 1220 us (0.88)
  Pallas kernels: 1220 us -> 968 us
  waiting for transfers between devices: 0 us -> 25.6 us
  other arithmetic: 44.4 us -> 64.6 us
  starting transfers between devices: 0 us -> 17.7 us
  local copies, waits for them, and re-layouts: 32.9 us -> 48 us
    pallas_call x2, Pallas kernels: 546 us -> 403 us  [scatter_call(): pl.pallas_call(functools.partial(scatter_kernel, n_dp, n_expert, n, len(c...]
    pallas_call x2, Pallas kernels: 518 us -> 413 us  [gather_call(): pl.pallas_call(functools.partial(gather_kernel, n_dp, n_expert, n, places...]
    ppermute x0 -> x12, waiting for transfers between devices: none -> 25.6 us  [permuted(): lax.ppermute(pieces[k], 'dp', [(i, (i + k) % n_dp) for i in range(n_dp)])]
    concatenate x0 -> x16, other arithmetic: none -> 19 us  [the longest x8 12.3 us: weight_pieces(): jnp.concatenate([lax.dynamic_slice_in_dim(one[low:high], (me + k) % n_dp...]
    ppermute x0 -> x12, starting transfers between devices: none -> 17.7 us  [permuted(): lax.ppermute(pieces[k], 'dp', [(i, (i + k) % n_dp) for i in range(n_dp)])]
    pallas_call x1 -> x2, Pallas kernels: 76.5 us -> 75.9 us  [expert_call(): pl.pallas_call(functools.partial(expert_kernel, steps, half, len(weights)...]
  transfers between devices with their start and end apart: 0 -> 12, of which waited for: 0 -> 2; matrix products, arithmetic and copies ran while one was open for 0% -> 7% of each run, Pallas kernels for 0% -> 13%
where the time goes in v5:
time: 1220 us; the launch traced here: 1210 us
  Pallas kernels  968 us (79%)
  matrix products  84.6 us (7%)
  other arithmetic  64.6 us (5%)
  local copies, waits for them, and re-layouts  48 us (4%)
  waiting for transfers between devices  25.6 us (2%)
  starting transfers between devices  17.7 us (1%)
    pallas_call x2, Pallas kernels, gather_call(): pl.pallas_call(functools.partial(gather_kernel, n_dp, n_expert, n, places...  413 us
    pallas_call x2, Pallas kernels, scatter_call(): pl.pallas_call(functools.partial(scatter_kernel, n_dp, n_expert, n, len(c...  403 us
    dot_general x21, matrix products, product(): return jnp.einsum(form, left, right, preferred_element_type=jnp.float32)  82.8 us
    pallas_call x2, Pallas kernels, expert_call(): pl.pallas_call(functools.partial(expert_kernel, steps, half, len(weights)...  75.9 us
    pallas_call x1, Pallas kernels, place_call(): pl.pallas_call(functools.partial(place_kernel, number), grid=(pairs,), in...  38.3 us
    pallas_call x1, Pallas kernels, pick_call(): pl.pallas_call(functools.partial(pick_kernel, number, experts_all), grid=...  38.1 us
    ppermute x12, waiting for transfers between devices, permuted(): lax.ppermute(pieces[k], 'dp', [(i, (i + k) % n_dp) for i in range(n_dp)])  25.6 us
  transfers between devices with their start and end apart: 12, of which 2 were waited for; matrix products, arithmetic and copies ran while one was open for 7% of the time, Pallas kernels for 13%

profile of v5, /device:TPU:0, one launch (start us, length us, event | category | flops | bytes accessed | tf_op | source)
XLA Modules:
  0.0 1210.8 jit_solution(12391978455286573008)
XLA Ops:
  4.9 1.3 slice.152
  6.2 1.3 slice.151
  10.0 2.1 pad_maximum_fusion.refs_0_
  12.1 184.9 %shard_map.272 = (bf16[4,2048,2048]{2,1,0:T(8,128)(2,1)}, bf16[4096,256]{1,0:T(8,128)(2,1)}, bf16[8,2048,256]{2,1,0:T(8,128)(2,1)}, bf16[8,2048,256]{2,1,0:T(8,128)(2,1)}) custom-call(bf16[4,64,2048]{2,1,0:T(8,128)(2,1)} %pad_maximum_fusion.refs_0_, bf16[128,256]{1,0:T(8,128)(2,1)} %fusion.80.refs_1_, bf16[8,512,1024]{2,1,0:T(8,128)(2,1)} %refs_2_.4, ...), custom_call_target="tpu_custom_call" | custom-call | tf_op jit(solution)/shard_map/pallas_call | solution.py:288
  200.4 4.0 collective-permute-start.2
  204.4 1.3 slice.135
  206.7 2.0 slice_reduce_fusion
  209.4 5.5 fusion.48
  214.9 4.8 multiply_reduce_fusion.7
  219.8 5.2 multiply_reduce_fusion.6
  225.0 1.1 slice.149
  226.1 3.1 slice.155
  232.9 1.4 subtract_convert_fusion.3
  234.3 1.8 fusion.114
  236.2 1.7 convolution_convert_fusion.6
  238.7 5.7 multiply_reduce_fusion.5
  245.0 3.1 constant_dynamic-slice_fusion.16
  248.1 1.4 constant_dynamic-slice_fusion.17
  249.8 1.6 fusion.115
  251.5 1.6 constant_dynamic-slice_fusion.32
  253.1 1.9 dynamic-slice_maximum_fusion
  254.9 2.3 pad_maximum_fusion.1.refs_0_
  257.2 2.3 pad_maximum_fusion.2
  259.5 2.3 pad_maximum_fusion.3
  261.7 2.1 pad_maximum_fusion.4
  267.2 228.4 %shard_map.273 = (bf16[4096,2048]{1,0:T(8,128)(2,1)}, bf16[4096,2048]{1,0:T(8,128)(2,1)}, bf16[8,2048,256]{2,1,0:T(8,128)(2,1)}, bf16[8,2048,256]{2,1,0:T(8,128)(2,1)}) custom-call(bf16[128,2048]{1,0:T(8,128)(2,1)} %copy-done.7, bf16[128,2048]{1,0:T(8,128)(2,1)} %refs_1_.1, ...), custom_call_target="tpu_custom_call", output_to_operand_aliasing={{2}: (4, {}), {3}: (5, {})} | custom-call | tf_op jit(solution)/shard_map/pallas_call | solution.py:288
  495.7 3.7 collective-permute-start.5
  499.4 38.1 %shard_map.274 = (bf16[8,768,2048]{2,1,0:T(8,128)(2,1)}, bf16[8,768,2048]{2,1,0:T(8,128)(2,1)}, f32[8,768,128]{2,1,0:T(8,128)}) custom-call(s32[16,8,256]{2,1,0:T(8,128)} %select_bitcast_fusion.slots_ref, bf16[4096,2048]{1,0:T(8,128)(2,1)} %get-tuple-element.94.x_ref, bf16[4096,2048]{1,0:T(8,128)(2,1)} %get-tuple-element.95.g_ref, ...), custom_call_target="tpu_custom_call" | custom-call | tf_op jit(solution)/shard_map/pallas_call | solution.py:782
  537.5 52.1 %shard_map.275 = (bf16[8,768,2048]{2,1,0:T(8,128)(2,1)}, bf16[8,768,2048]{2,1,0:T(8,128)(2,1)}, bf16[8,768,128]{2,1,0:T(8,128)(2,1)}, bf16[6,2048,256]{2,1,0:T(8...) custom-call(s32[1]{0:T(128)} %bitcast.32.names_ref, bf16[8,768,2048]{2,1,0:T(8,128)(2,1)} %get-tuple-element.96.x_ref, ...), custom_call_target="tpu_custom_call" | custom-call | tf_op jit(solution)/shard_map/pallas_call | solution.py:821
  589.7 1.7 fusion.111
  591.4 1.7 fusion.110
  597.1 1.5 collective-permute-start.7
  598.6 3.3 collective-permute-start.8
  606.4 23.7 %shard_map.276 = (bf16[8,768,2048]{2,1,0:T(8,128)(2,1)}, bf16[8,768,2048]{2,1,0:T(8,128)(2,1)}, bf16[8,768,128]{2,1,0:T(8,128)(2,1)}, bf16[2,2048,256]{2,1,0:T(8...) custom-call(s32[5]{0:T(128)} %stack.43.names_ref, ...), custom_call_target="tpu_custom_call", output_to_operand_aliasing={{0}: (9, {}), {1}: (10, {}), {2}: (11, {}), {5}: (12, {})} | custom-call | tf_op jit(solution)/shard_map/pallas_call | solution.py:821
  630.2 38.3 %shard_map.277 = (bf16[4096,2048]{1,0:T(8,128)(2,1)}, bf16[4096,2176]{1,0:T(8,128)(2,1)}) custom-call(s32[16,8,256]{2,1,0:T(8,128)} %select_bitcast_fusion.slots_ref, bf16[8,768,2048]{2,1,0:T(8,128)(2,1)} %get-tuple-element.109.y_ref, bf16[8,768,2048]{2,1,0:T(8,128)(2,1)} %get-tuple-element.110.dx_ref, bf16[8,768,128]{2,1,0:T(8,128)(2,1)} %get-tuple-element.111.probs_ref), custom_call_target="tpu_custom_call" | custom-call | tf_op jit(solution)/shard_map/pallas_call | solution.py:862
  668.6 123.7 %shard_map.278 = (f32[128,2176]{1,0:T(8,128)}, bf16[8,512,1024]{2,1,0:T(8,128)(2,1)}, bf16[8,512,1024]{2,1,0:T(8,128)(2,1)}) custom-call(bf16[4,8,128,2176]{3,2,1,0:T(8,128)(2,1)} %bitcast.164, bf16[6,2048,256]{2,1,0:T(8,128)(2,1)} %get-tuple-element.113.refs_1_.refs_8_, bf16[6,2048,256]{2,1,0:T(8,128)(2,1)} %get-tuple-element.114.refs_2_.refs_9_, ...), custom_call_target="tpu_custom_call" | custom-call | tf_op jit(solution)/shard_map/pallas_call | solution.py:567
  792.3 1.1 multiply_reduce_fusion.8
  793.5 2.8 multiply_reduce_fusion
  796.2 1.6 subtract_add_fusion
  797.8 6.8 convolution_convert_fusion.3
  804.6 6.4 fusion.45
  813.5 1.3 convolution_convert_fusion.4
  817.3 5.9 convolution_convert_fusion.1
  823.3 7.3 fusion.5
  830.5 5.7 convolution_convert_fusion.2
  836.8 5.8 convolution_convert_fusion
  842.9 6.5 fusion.28
  849.4 7.4 fusion.60
  856.8 1.2 concatenate.116
  858.1 1.0 concatenate.117
  859.1 1.8 concatenate.118
  860.9 1.8 concatenate.119
  862.7 2.2 collective-permute-start.9
  864.9 1.2 collective-permute-start.10
  866.1 1.1 collective-permute-start.11
  868.2 4.0 concatenate.111.refs_4_
  872.2 2.6 fusion.59
  874.8 5.0 collective-permute-done.9.refs_13_
  879.8 20.5 %collective-permute-done.10.refs_14_ = bf16[1,512,512]{2,1,0:T(8,128)(2,1)} collective-permute-done((bf16[1,512,512]{2,1,0:T(8,128)(2,1)}, bf16[1,512,512]{2,1,0:T(8,128)(2,1)}, u32[]{:S(2)}, u32[]{:S(2)}) %collective-permute-start.10) | collective-permute-done | bytes 524320 | tf_op jit(solution)/shard_map/ppermute | solution.py:963
  900.4 278.8 %shard_map.279 = (f32[64,2048]{1,0:T(8,128)}, f32[64,2048]{1,0:T(8,128)}, f32[64,2048]{1,0:T(8,128)}, f32[64,2048]{1,0:T(8,128)}, f32[64,128]{1,0:T(8,128)}, /*i...) custom-call(bf16[4,8,64,2048]{3,2,1,0:T(8,128)(2,1)} %bitcast.160, ...), custom_call_target="tpu_custom_call", output_to_operand_aliasing={{6}: (6, {}), {7}: (7, {})} | custom-call | tf_op jit(solution)/shard_map/pallas_call | solution.py:567
  1179.2 2.1 add_convert_fusion
  1181.4 1.7 slice_reduce_fusion.4
  1183.0 11.7 convert_element_type.136
  1194.7 11.8 convert_element_type.137
  (223 shorter events, 39.5 us)
Async XLA Ops:
  0.6 8.6 copy-start.44
  0.7 9.3 copy-start.38
  0.7 9.3 copy-start.39
  12.1 184.9 %copy-start.26 = (bf16[1,512,256]{2,1,0:T(8,128)(2,1)S(1)}, bf16[1,512,256]{2,1,0:T(8,128)(2,1)}, u32[]{:S(2)}) copy-start(bf16[1,512,256]{2,1,0:T(8,128)(2,1)} %get-tuple-element.209) | copy-start | bytes 786436
  12.1 184.9 %copy-start.27 = (bf16[1,512,256]{2,1,0:T(8,128)(2,1)S(1)}, bf16[1,512,256]{2,1,0:T(8,128)(2,1)}, u32[]{:S(2)}) copy-start(bf16[1,512,256]{2,1,0:T(8,128)(2,1)} %get-tuple-element.205) | copy-start | bytes 786436
  197.0 11.7 copy-start
  200.4 66.8 %collective-permute-start = (bf16[1,512,512]{2,1,0:T(8,128)(2,1)}, bf16[1,512,512]{2,1,0:T(8,128)(2,1)}, u32[]{:S(2)}, u32[]{:S(2)}) collective-permute-start(bf16[1,512,512]{2,1,0:T(8,128)(2,1)} %pad_maximum_fusion.8), channel_id=1, source_target_pairs={{0,8},{8,16},{16,24},{24,0},{1,9},{9,17},{17,25},{25,1},{2,10},{10... | collective-permute-start | bytes 1572872 | tf_op jit(solution)/shard_map/ppermute | solution.py:963
  200.4 66.8 %collective-permute-start.1 = (bf16[1,512,512]{2,1,0:T(8,128)(2,1)}, bf16[1,512,512]{2,1,0:T(8,128)(2,1)}, u32[]{:S(2)}, u32[]{:S(2)}) collective-permute-start(bf16[1,512,512]{2,1,0:T(8,128)(2,1)} %pad_maximum_fusion.9), channel_id=1, source_target_pairs={{0,16},{8,24},{16,0},{24,8},{1,17},{9,25},{17,1},{25,9},{2,18},{10... | collective-permute-start | bytes 1572872 | tf_op jit(solution)/shard_map/ppermute | solution.py:963
  200.4 66.8 %collective-permute-start.2 = (bf16[1,512,512]{2,1,0:T(8,128)(2,1)}, bf16[1,512,512]{2,1,0:T(8,128)(2,1)}, u32[]{:S(2)}, u32[]{:S(2)}) collective-permute-start(bf16[1,512,512]{2,1,0:T(8,128)(2,1)} %pad_maximum_fusion.10), channel_id=1, source_target_pairs={{0,24},{8,0},{16,8},{24,16},{1,25},{9,1},{17,9},{25,17},{2,26},{10... | collective-permute-start | bytes 1572872 | tf_op jit(solution)/shard_map/ppermute | solution.py:963
  208.7 11.0 copy-start.28
  208.7 40.9 %copy-start.40 = (f32[2048]{0:T(1024)}, f32[2048]{0:T(1024)S(1)}, u32[]{:S(2)}) copy-start(f32[2048]{0:T(1024)S(1)} %get-tuple-element.156) | copy-start | bytes 24580
  209.4 10.3 copy-start.42
  219.7 10.3 copy-start.3
  219.7 5.2 copy-start.20
  224.9 6.3 copy-start.5
  224.9 4.2 copy-start.63
  231.3 3.1 copy-start.52
  236.2 12.0 copy-start.45
  237.9 10.2 slice-start
  245.0 4.6 copy-start.57
  245.0 4.6 copy-start.1
  249.6 12.2 %copy-start.21 = (bf16[2,512,256]{2,1,0:T(8,128)(2,1)S(1)}, bf16[2,512,256]{2,1,0:T(8,128)(2,1)}, u32[]{:S(2)}) copy-start(bf16[2,512,256]{2,1,0:T(8,128)(2,1)} %get-tuple-element.178) | copy-start | bytes 1572868
  249.8 17.4 %copy-start.7 = (bf16[128,2048]{1,0:T(8,128)(2,1)}, bf16[128,2048]{1,0:T(8,128)(2,1)S(1)}, u32[]{:S(2)}) copy-start(bf16[128,2048]{1,0:T(8,128)(2,1)S(1)} %multiply_convert_fusion.1.refs_0_) | copy-start | bytes 1572868
  251.4 14.6 %copy-start.47 = (f32[128]{0:T(128)}, f32[128]{0:T(128)S(1)}, u32[]{:S(2)}) copy-start(f32[128]{0:T(128)S(1)} %get-tuple-element.237) | copy-start | bytes 1540
  264.0 529.4 %copy-start.54 = (f32[128]{0:T(128)}, f32[128]{0:T(128)S(1)}, u32[]{:S(2)}) copy-start(f32[128]{0:T(128)S(1)} %fusion.84) | copy-start | bytes 1540
  495.6 103.0 %collective-permute-start.3 = (bf16[2,512,512]{2,1,0:T(8,128)(2,1)}, bf16[2,512,512]{2,1,0:T(8,128)(2,1)S(1)}, u32[]{:S(2)}, u32[]{:S(2)}) collective-permute-start(bf16[2,512,512]{2,1,0:T(8,128)(2,1)} %pad_maximum_fusion.2), channel_id=1, source_target_pairs={{0,8},{8,16},{16,24},{24,0},{1,9},{9,17},{17,25},{25,1},{2,10},{10... | collective-permute-start | bytes 3145736 | tf_op jit(solution)/shard_map/ppermute | solution.py:963
  495.6 109.8 %collective-permute-start.4 = (bf16[2,512,512]{2,1,0:T(8,128)(2,1)}, bf16[2,512,512]{2,1,0:T(8,128)(2,1)S(1)}, u32[]{:S(2)}, u32[]{:S(2)}) collective-permute-start(bf16[2,512,512]{2,1,0:T(8,128)(2,1)} %pad_maximum_fusion.3), channel_id=1, source_target_pairs={{0,16},{8,24},{16,0},{24,8},{1,17},{9,25},{17,1},{25,9},{2,18},{10... | collective-permute-start | bytes 3145736 | tf_op jit(solution)/shard_map/ppermute | solution.py:963
  495.7 109.7 %collective-permute-start.5 = (bf16[2,512,512]{2,1,0:T(8,128)(2,1)}, bf16[2,512,512]{2,1,0:T(8,128)(2,1)}, u32[]{:S(2)}, u32[]{:S(2)}) collective-permute-start(bf16[2,512,512]{2,1,0:T(8,128)(2,1)} %pad_maximum_fusion.4), channel_id=1, source_target_pairs={{0,24},{8,0},{16,8},{24,16},{1,25},{9,1},{17,9},{25,17},{2,26},{10... | collective-permute-start | bytes 3145736 | tf_op jit(solution)/shard_map/ppermute | solution.py:963
  596.5 72.0 %collective-permute-start.6 = (bf16[1,512,512]{2,1,0:T(8,128)(2,1)}, bf16[1,512,512]{2,1,0:T(8,128)(2,1)}, u32[]{:S(2)}, u32[]{:S(2)}) collective-permute-start(bf16[1,512,512]{2,1,0:T(8,128)(2,1)} %pad_maximum_fusion.12), channel_id=1, source_target_pairs={{0,8},{8,16},{16,24},{24,0},{1,9},{9,17},{17,25},{25,1},{2,10},{10... | collective-permute-start | bytes 1572872 | tf_op jit(solution)/shard_map/ppermute | solution.py:963
  597.1 71.4 %collective-permute-start.7 = (bf16[1,512,512]{2,1,0:T(8,128)(2,1)}, bf16[1,512,512]{2,1,0:T(8,128)(2,1)}, u32[]{:S(2)}, u32[]{:S(2)}) collective-permute-start(bf16[1,512,512]{2,1,0:T(8,128)(2,1)} %pad_maximum_fusion.13), channel_id=1, source_target_pairs={{0,16},{8,24},{16,0},{24,8},{1,17},{9,25},{17,1},{25,9},{2,18},{10... | collective-permute-start | bytes 1572872 | tf_op jit(solution)/shard_map/ppermute | solution.py:963
  598.6 6.9 copy-start.23
  598.6 69.9 %collective-permute-start.8 = (bf16[1,512,512]{2,1,0:T(8,128)(2,1)}, bf16[1,512,512]{2,1,0:T(8,128)(2,1)}, u32[]{:S(2)}, u32[]{:S(2)}) collective-permute-start(bf16[1,512,512]{2,1,0:T(8,128)(2,1)} %pad_maximum_fusion.14), channel_id=1, source_target_pairs={{0,24},{8,0},{16,8},{24,16},{1,25},{9,1},{17,9},{25,17},{2,26},{10... | collective-permute-start | bytes 1572872 | tf_op jit(solution)/shard_map/ppermute | solution.py:963
  668.5 123.8 %copy-start.48 = (f32[128]{0:T(128)S(1)}, f32[128]{0:T(128)}, u32[]{:S(2)}) copy-start(f32[128]{0:T(128)} %copy-done.47) | copy-start | bytes 1540
  668.5 124.9 %copy-start.10 = (bf16[32,64,128]{2,1,0:T(8,128)(2,1)S(1)}, bf16[32,64,128]{2,1,0:T(8,128)(2,1)}, u32[]{:S(2)}) copy-start(bf16[32,64,128]{2,1,0:T(8,128)(2,1)} %copy-done.9) | copy-start | bytes 1572868
  668.5 124.9 %copy-start.41 = (f32[2048]{0:T(1024)S(1)}, f32[2048]{0:T(1024)}, u32[]{:S(2)}) copy-start(f32[2048]{0:T(1024)} %copy-done.40) | copy-start | bytes 24580
  668.5 124.9 %copy-start.58 = (f32[128]{0:T(128)S(1)}, f32[128]{0:T(128)}, u32[]{:S(2)}) copy-start(f32[128]{0:T(128)} %copy-done.57) | copy-start | bytes 1540
  668.5 127.7 %copy-start.11 = (bf16[128,2048]{1,0:T(8,128)(2,1)S(1)}, bf16[128,2048]{1,0:T(8,128)(2,1)}, u32[]{:S(2)}) copy-start(bf16[128,2048]{1,0:T(8,128)(2,1)} %refs_1_.1) | copy-start | bytes 1572868
  668.6 127.7 %copy-start.62 = (f32[128]{0:T(128)S(1)}, f32[128]{0:T(128)}, u32[]{:S(2)}) copy-start(f32[128]{0:T(128)} %get-tuple-element.227) | copy-start | bytes 1540
  804.6 6.4 copy-start.25
  804.6 6.4 copy-start.46
  804.6 7.0 copy-start.64
  811.1 2.4 copy-start.8
  811.1 3.7 copy-start.37
  811.6 18.9 %copy-start.31 = (bf16[16,128,128]{2,1,0:T(8,128)(2,1)}, bf16[16,128,128]{2,1,0:T(8,128)(2,1)S(1)}, u32[]{:S(2)}) copy-start(bf16[16,128,128]{2,1,0:T(8,128)(2,1)S(1)} %convolution_convert_fusion.5) | copy-start | bytes 1572868
  812.2 3.6 copy-start.4
  812.2 3.6 copy-start.6
  812.2 3.6 copy-start.51
  812.2 3.6 copy-start.53
  813.5 3.3 copy-start.61
  814.8 2.5 copy-start.29
  814.8 2.5 copy-start.43
  830.5 5.7 copy-start.60
  842.6 6.8 copy-start.32
  849.4 11.5 copy-start.56
  849.4 22.7 %copy-start.59 = (f32[128]{0:T(128)S(1)}, f32[128]{0:T(128)}, u32[]{:S(2)}) copy-start(f32[128]{0:T(128)} %get-tuple-element.221) | copy-start | bytes 1540
  862.7 17.1 %collective-permute-start.9 = (bf16[1,512,512]{2,1,0:T(8,128)(2,1)}, bf16[1,512,512]{2,1,0:T(8,128)(2,1)}, u32[]{:S(2)}, u32[]{:S(2)}) collective-permute-start(bf16[1,512,512]{2,1,0:T(8,128)(2,1)} %pad_maximum_fusion.16), channel_id=1, source_target_pairs={{0,8},{8,16},{16,24},{24,0},{1,9},{9,17},{17,25},{25,1},{2,10},{10... | collective-permute-start | bytes 1572872 | tf_op jit(solution)/shard_map/ppermute | solution.py:963
  864.9 35.4 %collective-permute-start.10 = (bf16[1,512,512]{2,1,0:T(8,128)(2,1)}, bf16[1,512,512]{2,1,0:T(8,128)(2,1)}, u32[]{:S(2)}, u32[]{:S(2)}) collective-permute-start(bf16[1,512,512]{2,1,0:T(8,128)(2,1)} %pad_maximum_fusion.17), channel_id=1, source_target_pairs={{0,16},{8,24},{16,0},{24,8},{1,17},{9,25},{17,1},{25,9},{2,18},{10... | collective-permute-start | bytes 1572872 | tf_op jit(solution)/shard_map/ppermute | solution.py:963
  866.1 34.2 %collective-permute-start.11 = (bf16[1,512,512]{2,1,0:T(8,128)(2,1)}, bf16[1,512,512]{2,1,0:T(8,128)(2,1)}, u32[]{:S(2)}, u32[]{:S(2)}) collective-permute-start(bf16[1,512,512]{2,1,0:T(8,128)(2,1)} %pad_maximum_fusion.18), channel_id=1, source_target_pairs={{0,24},{8,0},{16,8},{24,16},{1,25},{9,1},{17,9},{25,17},{2,26},{10... | collective-permute-start | bytes 1572872 | tf_op jit(solution)/shard_map/ppermute | solution.py:963
  900.4 278.9 %copy-start.2 = (f32[128,2048]{1,0:T(8,128)S(1)}, f32[128,2048]{1,0:T(8,128)}, u32[]{:S(2)}) copy-start(f32[128,2048]{1,0:T(8,128)} %get-tuple-element.236) | copy-start | bytes 3145732
  1194.7 11.9 copy-start.36
  1194.7 12.7 %copy-start.35 = (f32[64,2048]{1,0:T(8,128)S(1)}, f32[64,2048]{1,0:T(8,128)}, u32[]{:S(2)}) copy-start(f32[64,2048]{1,0:T(8,128)} %get-tuple-element.266) | copy-start | bytes 1572868
  1194.7 13.5 %copy-start.34 = (f32[64,2048]{1,0:T(8,128)S(1)}, f32[64,2048]{1,0:T(8,128)}, u32[]{:S(2)}) copy-start(f32[64,2048]{1,0:T(8,128)} %get-tuple-element.267) | copy-start | bytes 1572868
  1194.7 14.3 %copy-start.33 = (f32[64,2048]{1,0:T(8,128)S(1)}, f32[64,2048]{1,0:T(8,128)}, u32[]{:S(2)}) copy-start(f32[64,2048]{1,0:T(8,128)} %get-tuple-element.268) | copy-start | bytes 1572868
  1194.7 15.0 %copy-start.30 = (f32[64,128]{1,0:T(8,128)S(1)}, f32[64,128]{1,0:T(8,128)}, u32[]{:S(2)}) copy-start(f32[64,128]{1,0:T(8,128)} %get-tuple-element.144) | copy-start | bytes 98308
  (14 other events, 23.4 us)

commit v6 on v5

--- a/solution.py
+++ b/solution.py
@@ -70,6 +70,13 @@
         square = [chip, chip + 1 - 2 * (chip % 2), chip + 2 - 4 * (chip // 2), 3 - chip]
         return lambda k: square[k], lambda k: square[k]
     return lambda k: (chip + k) % chips, lambda k: (chip + chips - k) % chips
+
+
+def partners(z, n_dp):
+    if n_dp == 4:
+        pairs = [z, (z + 2) % 4, 3 - z, z + 1 - 2 * (z % 2)]
+        return lambda k: pairs[k], lambda k: pairs[k]
+    return lambda k: (z + k) % n_dp, lambda k: (z + n_dp - k) % n_dp
 
 
 def greet(n_dp, n_expert):
@@ -102,10 +109,11 @@
 
 def exchange(n_dp, pairs, send, receive, local):
     z, j, chip, core = place_of()
+    to_plane, unused = partners(z, n_dp)
     copies = []
     for i, (source, target) in enumerate(pairs):
         for k in range(1, n_dp):
-            to = (z + k) % n_dp
+            to = to_plane(k)
             copies.append(
                 remote(source(to), target(z), send.at[i, k], receive.at[i, k], (to, j))
             )
@@ -124,7 +132,7 @@
     return []
 
 
-def gather_kernel(n_dp, n_expert, n_items, places, cuts, puts, n_cut, n_out, *refs):
+def gather_kernel(n_dp, n_expert, n_items, places, cuts, puts, finish, n_cut, n_out, *refs):
     z, j, chip, core = place_of()
     chips = n_expert // 2
     square = chips == 4
@@ -255,6 +263,8 @@
                 remote(
                     block, block, send_a.at[i, plane, k], recv_a.at[i, plane, k], mate
                 ).wait_recv()
+        pltpu.make_async_copy(sources[i], slot(i, z, j), local.at[i]).wait()
+    finish(targets, cut_in, cut_out)
     for i in range(n_items):
         for plane in range(n_dp):
             block = slot(i, plane, j)
@@ -273,20 +283,32 @@
             def _():
                 along(i, plane, block, 1, -1).wait_send()
 
-        pltpu.make_async_copy(sources[i], slot(i, z, j), local.at[i]).wait()
     for copy in copies:
         copy.wait()
 
 
 def gather_call(
-    n_dp, n_expert, items, shapes, places, cut_in, cut_shapes, cuts, aliases, number, puts=nothing
+    n_dp,
+    n_expert,
+    items,
+    shapes,
+    places,
+    cut_in,
+    cut_shapes,
+    cuts,
+    aliases,
+    number,
+    puts=nothing,
+    finish=lambda items, ins, outs: None,
 ):
     chips = n_expert // 2
     n, m = len(items), len(cut_shapes)
     dma = pltpu.SemaphoreType.DMA
     anywhere = pl.BlockSpec(memory_space=pl.ANY)
     return pl.pallas_call(
-        functools.partial(gather_kernel, n_dp, n_expert, n, places, cuts, puts, len(cut_in), m),
+        functools.partial(
+            gather_kernel, n_dp, n_expert, n, places, cuts, puts, finish, len(cut_in), m
+        ),
         out_shape=[*shapes, *cut_shapes],
         in_specs=[anywhere] * (n + len(cut_in)),
         out_specs=[anywhere] * (n + m),
@@ -304,7 +326,9 @@
             dma((4 * n_dp,)),
         ],
         input_output_aliases=aliases,
-        compiler_params=pltpu.CompilerParams(collective_id=number, has_side_effects=True),
+        compiler_params=pltpu.CompilerParams(
+            collective_id=number, has_side_effects=True, vmem_limit_bytes=BIG
+        ),
     )(*items, *cut_in)
 
 
@@ -665,7 +689,7 @@
         grows_ref[e] = picked[e * size : (e + 1) * size]
 
 
-def expert_kernel(steps, half, n_weights, n_into, names_ref, x_ref, g_ref, gates_ref, *refs):
+def expert_kernel(steps, half, n_weights, n_into, n_pack, names_ref, x_ref, g_ref, gates_ref, *refs):
     weights, refs = refs[:n_weights], refs[n_weights:]
     down_ref, refs = refs[0], refs[1 + n_into :]
     (
@@ -675,6 +699,7 @@
         dgate_ref,
         dup_ref,
         ddown_ref,
+        *pack_refs,
         sum_gate,
         sum_up,
     ) = refs
@@ -758,6 +783,17 @@
             dgate_ref[0, span, :] = sum_gate[span, :].astype(bf16)
             dup_ref[0, span, :] = sum_up[span, :].astype(bf16)
 
+    if n_pack:
+
+        @pl.when((step == steps - 1) & (pl.program_id(0) < n_pack))
+        def _():
+            pack_ref = pack_refs[0]
+            depth = pack_ref.shape[2]
+            for plane in range(pack_ref.shape[0]):
+                here = pl.ds(plane * depth, depth)
+                pack_ref[plane, 0, :, :part] = dgate_ref[0, here, :]
+                pack_ref[plane, 0, :, part:] = dup_ref[0, here, :]
+
 
 def place_kernel(number, slots_ref, y_ref, dx_ref, probs_ref, out_ref, back_ref):
     pick = jnp.concatenate(picks(slots_ref, number), axis=0).astype(jnp.bfloat16)
@@ -773,13 +809,22 @@
     back_ref[:, width:] = dot(pick, part, (0, 0)).astype(jnp.bfloat16)
 
 
-def pick_call(number, experts_all, slots, x_all, g_all, router):
-    pairs, _, pair = slots.shape
+def pick_shapes(number, pairs):
     bf16 = jnp.bfloat16
     size = 2 * CAP
-    rows = pl.BlockSpec((number, size, D), lambda p: (0, p, 0))
+    return [
+        jax.ShapeDtypeStruct((number, pairs * size, D), bf16),
+        jax.ShapeDtypeStruct((number, pairs * size, D), bf16),
+        jax.ShapeDtypeStruct((number, pairs * size, 128), jnp.float32),
+    ]
+
+
+def pick_rows(number, experts_all, slots, x_all, g_all, router, rows, grows, gates):
+    pairs, _, pair = slots.shape
+    size = 2 * CAP
     tokens = pl.BlockSpec((pair, D), lambda p: (p, 0))
-    return pl.pallas_call(
+    picked = pl.BlockSpec((number, size, D), lambda p: (0, p, 0))
+    pltpu.emit_pipeline(
         functools.partial(pick_kernel, number, experts_all),
         grid=(pairs,),
         in_specs=[
@@ -788,17 +833,11 @@
             tokens,
             pl.BlockSpec(router.shape, lambda p: (0, 0)),
         ],
-        out_specs=[rows, rows, pl.BlockSpec((number, size, 128), lambda p: (0, p, 0))],
-        out_shape=[
-            jax.ShapeDtypeStruct((number, pairs * size, D), bf16),
-            jax.ShapeDtypeStruct((number, pairs * size, D), bf16),
-            jax.ShapeDtypeStruct((number, pairs * size, 128), jnp.float32),
-        ],
-        compiler_params=pltpu.CompilerParams(vmem_limit_bytes=BIG),
-    )(slots, x_all, g_all, router)
-
-
-def expert_call(names, half, low, number, rows, grows, gates, weights, down, into=()):
+        out_specs=[picked, picked, pl.BlockSpec((number, size, 128), lambda p: (0, p, 0))],
+    )(slots, x_all, g_all, router, rows, grows, gates)
+
+
+def expert_call(names, half, low, number, rows, grows, gates, weights, down, into=(), pack=()):
     total, depth, _ = rows.shape
     part = down.shape[1]
     size = depth
@@ -817,9 +856,18 @@
     def from_whole(*shape):
         return pl.BlockSpec((1, *shape), lambda e, r: (e + low, 0, 0))
 
+    packed = [
+        pl.BlockSpec(
+            (planes, 1, D // planes, 2 * part),
+            lambda e, r, n=n: (0, lax.min(e, n - 1), 0, 0),
+        )
+        for n, planes in ([pack] if pack else [])
+    ]
     keep = (D, part) if steps > 1 else (16, 128)
     return pl.pallas_call(
-        functools.partial(expert_kernel, steps, half, len(weights), len(into)),
+        functools.partial(
+            expert_kernel, steps, half, len(weights), len(into), pack[0] if pack else 0
+        ),
         grid=(number, steps),
         in_specs=[
             pl.BlockSpec(memory_space=pltpu.SMEM),
@@ -837,6 +885,7 @@
             whole(D, part),
             whole(D, part),
             from_whole(part, D),
+            *packed,
         ],
         out_shape=[
             jax.ShapeDtypeStruct((total, depth, D), bf16),
@@ -845,6 +894,10 @@
             jax.ShapeDtypeStruct((number, D, part), bf16),
             jax.ShapeDtypeStruct((number, D, part), bf16),
             jax.ShapeDtypeStruct((total, part, D), f32),
+            *[
+                jax.ShapeDtypeStruct((planes, n, D // planes, 2 * part), bf16)
+                for n, planes in ([pack] if pack else [])
+            ],
         ],
         input_output_aliases={
             5 + len(weights) + i: out for i, out in zip(range(len(into)), (0, 1, 2, 5))
@@ -878,6 +931,25 @@
         ],
         compiler_params=pltpu.CompilerParams(vmem_limit_bytes=BIG),
     )(slots, y, dx, probs)
+
+
+def widen_kernel(*refs):
+    half = len(refs) // 2
+    for source, target in zip(refs[:half], refs[half:]):
+        target[...] = source[...].astype(jnp.float32)
+
+
+def widen(values):
+    number, rows, columns = values[0].shape
+    block = pl.BlockSpec((1, rows, columns), lambda e: (e, 0, 0))
+    return pl.pallas_call(
+        widen_kernel,
+        grid=(number,),
+        in_specs=[block] * len(values),
+        out_specs=[block] * len(values),
+        out_shape=[jax.ShapeDtypeStruct(one.shape, jnp.float32) for one in values],
+        compiler_params=pltpu.CompilerParams(vmem_limit_bytes=BIG),
+    )(*values)
 
 
 def shards(
@@ -931,7 +1003,7 @@
     late = number - number // 4
     back_beside = number // 8
     back_third = back_beside + number // 4
-    back_late = back_third + number // 8
+    back_late = back_third + number // 4
     me = lax.axis_index("dp")
     cut_shape = jax.ShapeDtypeStruct((number, n_dp * depth, part), bf16)
 
@@ -957,44 +1029,36 @@
 
         return cuts
 
-    def permuted(pieces, after):
-        *pieces, unused = lax.optimization_barrier((*pieces, after))
-        return [pieces[0]] + [
-            lax.ppermute(pieces[k], "dp", [(i, (i + k) % n_dp) for i in range(n_dp)])
-            for k in range(1, n_dp)
-        ]
-
-    def weight_pieces(low, high, after):
-        return permuted(
-            [
-                jnp.concatenate(
-                    [
-                        lax.dynamic_slice_in_dim(one[low:high], (me + k) % n_dp * part, part, 2)
-                        for one in (w_gate, w_up)
-                    ],
-                    axis=2,
-                )
-                for k in range(n_dp)
-            ],
-            after,
-        )
-
-    def grad_pieces(gate, up, low, high, after):
-        return permuted(
-            [
-                jnp.concatenate(
-                    [
-                        lax.dynamic_slice_in_dim(one[low:high], (me + k) % n_dp * depth, depth, 1)
-                        for one in (gate, up)
-                    ],
-                    axis=2,
-                )
-                for k in range(n_dp)
-            ],
-            after,
-        )
-
-    weights_all, extras_all, gate_early, up_early = gather_call(
+    to_plane, from_plane = partners(me, n_dp)
+
+    def permuted(pieces, chained=False):
+        got = []
+        for k, piece in enumerate(pieces, 1):
+            if chained and got:
+                piece, last = lax.optimization_barrier((piece, got.pop()))
+                got.append(last)
+            paths = [(i, partners(i, n_dp)[0](k)) for i in range(n_dp)]
+            got.append(lax.ppermute(piece, "dp", paths))
+        return got
+
+    def cut_pieces(low, high, first_k, ins, outs):
+        to, unused = partners(lax.axis_index("dp"), n_dp)
+        pairs = []
+        for k, piece in enumerate(outs, first_k):
+            for n in range(2):
+                source = ins[n].at[pl.ds(low, high - low), :, columns_at(to(k))]
+                pairs.append((source, piece.at[:, :, pl.ds(n * part, part)]))
+        return pairs
+
+    def piece_shapes(size, first_k):
+        shape = jax.ShapeDtypeStruct((size, depth, 2 * part), bf16)
+        return [shape] * (n_dp - first_k if size else 0)
+
+    soon_shapes = piece_shapes(beside - early, 1)
+    late_shapes = piece_shapes(number - late, 0)
+    n_soon = len(soon_shapes)
+
+    weights_all, extras_all, gate_early, up_early, *pieces = gather_call(
         n_dp,
         n_expert,
         [weights, extras],
@@ -1009,11 +1073,14 @@
             row_block(count),
         ],
         [w_gate, w_up],
-        [cut_shape, cut_shape],
+        [cut_shape, cut_shape, *soon_shapes, *late_shapes],
         recut(0, early),
         {},
         0,
-    )
+        lambda ins, outs: cut_pieces(early, beside, 1, ins, outs[2 : 2 + n_soon])
+        + cut_pieces(late, number, 0, ins, outs[2 + n_soon :]),
+    )
+    soon_pieces, late_pieces = pieces[:n_soon], pieces[n_soon:]
     query_weight, key_weight, value_weight, out_weight = (weights_all[i] for i in range(4))
     small_all = (
         extras_all[:, width:].reshape(groups, count, width)[:, :rows_each].reshape(-1, width)
@@ -1051,35 +1118,6 @@
     mlp_low = mlp_normed.astype(bf16)
     router = jax.nn.softmax(product(mlp_low, router_weight, "td,de->te"), axis=-1)
 
-    pieces = []
-    if beside > early:
-        pieces = weight_pieces(early, beside, extras_all)
-        mlp_low, *pieces = lax.optimization_barrier((mlp_low, *pieces))
-
-    def put_weights(ins, outs):
-        chosen = pl.ds(early, beside - early)
-        pairs = []
-        for k, piece in enumerate(ins[4:]):
-            here = rows_at((lax.axis_index("dp") + n_dp - k) % n_dp)
-            for n in range(2):
-                columns = piece.at[:, :, pl.ds(n * part, part)]
-                pairs.append((columns, outs[n].at[chosen, here]))
-        return pairs
-
-    mlp_all, cotangent_all, gate_cut, up_cut = gather_call(
-        n_dp,
-        n_expert,
-        [mlp_low, cotangent],
-        [jax.ShapeDtypeStruct((groups * count, D), bf16)] * 2,
-        [row_block(count)] * 2,
-        [w_gate, w_up, gate_early, up_early, *pieces],
-        [cut_shape, cut_shape],
-        recut(beside, late),
-        {4: 2, 5: 3},
-        1,
-        put_weights,
-    )
-    late_pieces = weight_pieces(late, number, mlp_all)
     first = lax.axis_index("expert") * number
     hit = lax.dynamic_slice_in_dim(hits_all, first, number, 1).reshape(groups, count, number)
     before = jnp.tril(jnp.ones((count, count), bf16), -1)
@@ -1092,7 +1130,44 @@
     router_own = jnp.pad(
         jnp.roll(router_weight, -first, axis=1), ((0, 0), (0, width - experts_all))
     )
-    rows, grows, gates = pick_call(number, experts_all, slots, mlp_all, cotangent_all, router_own)
+    if n_soon:
+        mlp_low, *soon_pieces = lax.optimization_barrier((mlp_low, *permuted(soon_pieces)))
+
+    def put_weights(ins, outs):
+        chosen = pl.ds(early, beside - early)
+        unused, heard = partners(lax.axis_index("dp"), n_dp)
+        pairs = []
+        if beside > early:
+            own = lax.axis_index("dp")
+            for n in range(2):
+                source = ins[n].at[chosen, :, columns_at(own)]
+                pairs.append((source, outs[n].at[chosen, rows_at(own)]))
+        for k, piece in enumerate(ins[6:], 1):
+            for n in range(2):
+                columns = piece.at[:, :, pl.ds(n * part, part)]
+                pairs.append((columns, outs[n].at[chosen, rows_at(heard(k))]))
+        return pairs
+
+    def pick_all(items, ins, outs):
+        pick_rows(number, experts_all, ins[4], *items, ins[5], *outs[2:])
+
+    unused, unused, gate_cut, up_cut, rows, grows, gates = gather_call(
+        n_dp,
+        n_expert,
+        [mlp_low, cotangent],
+        [jax.ShapeDtypeStruct((groups * count, D), bf16)] * 2,
+        [row_block(count)] * 2,
+        [w_gate, w_up, gate_early, up_early, slots, router_own, *soon_pieces],
+        [cut_shape, cut_shape, *pick_shapes(number, groups // 2)],
+        recut(beside, late),
+        {4: 2, 5: 3},
+        1,
+        put_weights,
+        pick_all,
+    )
+    *late_pieces, rows = lax.optimization_barrier((*late_pieces, rows))
+    late_pieces = [late_pieces[0], *permuted(late_pieces[1:])]
+    packing = back_beside > 0 and depth == 512
     *outs, gate_soon, up_soon, down_soon = expert_call(
         first[None],
         experts_all,
@@ -1103,8 +1178,11 @@
         gates,
         [gate_cut, up_cut],
         w_down,
-    )
-    offsets = [(me + n_dp - k) % n_dp * depth for k in range(n_dp)]
+        pack=(back_beside, n_dp) if packing else (),
+    )
+    if packing:
+        *outs, gate_soon, up_soon, down_soon, packed = [*outs, gate_soon, up_soon, down_soon]
+    offsets = [from_plane(k) * depth for k in range(n_dp)]
     weighted, grad_rows, grad_gates, gate_rest, up_rest, grad_down_part = expert_call(
         jnp.stack([first + late, *offsets]),
         experts_all,
@@ -1128,35 +1206,62 @@
 
         return [pair(0), pair(1)]
 
-    def put_grads(low, high, pieces, outs):
+    def put_grads(low, high, ins, pieces, outs):
+        own = lax.axis_index("dp")
+        unused, heard = partners(own, n_dp)
+        chosen = pl.ds(low, high - low)
         pairs = []
-        for k, piece in enumerate(pieces):
-            here = columns_at((lax.axis_index("dp") + n_dp - k) % n_dp)
+        if high > low:
+            for n in range(2):
+                source = ins[n].at[chosen, rows_at(own)]
+                pairs.append((source, outs[n].at[chosen, :, columns_at(own)]))
+        for k, piece in enumerate(pieces, 1):
             for n in range(2):
                 columns = piece.at[:, :, pl.ds(n * part, part)]
-                pairs.append((columns, outs[n].at[pl.ds(low, high - low), :, here]))
+                pairs.append((columns, outs[n].at[chosen, :, columns_at(heard(k))]))
+        return pairs
+
+    def cut_grads(low, high, ins, outs):
+        to, unused = partners(lax.axis_index("dp"), n_dp)
+        pairs = []
+        for k, piece in enumerate(outs, 1):
+            for n in range(2):
+                source = ins[n].at[pl.ds(low, high - low), rows_at(to(k))]
+                pairs.append((source, piece.at[:, :, pl.ds(n * part, part)]))
         return pairs
 
     pieces = []
     if back_beside:
-        pieces = grad_pieces(gate_soon, up_soon, 0, back_beside, gate_soon)
-        part_back, *pieces = lax.optimization_barrier((part_back, *pieces))
+        for k in range(1, n_dp):
+            if packing:
+                piece = lax.dynamic_index_in_dim(packed, to_plane(k), 0, False)
+            else:
+                piece = jnp.concatenate(
+                    [
+                        lax.dynamic_slice_in_dim(
+                            one[:back_beside], to_plane(k) * depth, depth, 1
+                        )
+                        for one in (gate_soon, up_soon)
+                    ],
+                    axis=2,
+                )
+            pieces.append(piece)
+        part_back, *pieces = lax.optimization_barrier((part_back, *permuted(pieces)))
     way_shapes = [jax.ShapeDtypeStruct((number, depth, ff), bf16)] * 2
-    (back,), (gate_third, up_third) = scatter_all(
+    (back,), (gate_third, up_third, *pieces) = scatter_all(
         n_dp,
         n_expert,
         [part_back.reshape(n_dp, n_expert, count, D + width)],
         [gate_soon, up_soon, *pieces],
-        way_shapes,
+        way_shapes + piece_shapes(back_late - back_third, 1),
         lambda ins, outs: ways(back_beside, back_third, 0, ins, outs),
         8,
         (),
-        lambda ins, outs: put_grads(0, back_beside, ins[2:], outs),
-    )
-    pieces = []
-    if back_late > back_third:
-        pieces = grad_pieces(gate_soon, up_soon, back_third, back_late, back)
-        part_out, *pieces = lax.optimization_barrier((part_out, *pieces))
+        lambda ins, outs: put_grads(0, back_beside, ins, ins[2:], outs)
+        + cut_grads(back_third, back_late, ins, outs[2:]),
+    )
+    if pieces:
+        part_out, *pieces = lax.optimization_barrier((part_out, *permuted(pieces, True)))
 
     grad_final = cotangent.astype(jnp.float32)
     grad_mlp = back[:, :D]
@@ -1236,14 +1341,13 @@
         + ways(0, number - late, late, ins[4:6], outs),
         16,
         ((0, 0), (1, 1)),
-        lambda ins, outs: put_grads(back_third, back_late, ins[6:], outs),
+        lambda ins, outs: put_grads(back_third, back_late, ins[2:4], ins[6:], outs),
     )
     grad_out_part, grad_value_part, grad_key_part, grad_query_part, small_part, summed = sums
     output = (middle + summed).astype(bf16)
     grad_router_part = small_part[:, :experts_all]
     gain_parts = [small_part[:, experts_all + i] for i in range(4)]
-    grad_gate_part = gate_back.astype(jnp.float32)
-    grad_up_part = up_back.astype(jnp.float32)
+    grad_gate_part, grad_up_part = widen([gate_back, up_back])
     return (
         output,
         grad_inputs,

time: 1220 us -> 1410 us (1.16)
  Pallas kernels: 968 us -> 1160 us
  other arithmetic: 64.6 us -> 21.1 us
  waiting for transfers between devices: 25.6 us -> 55.3 us
  starting transfers between devices: 17.7 us -> 38.1 us
    pallas_call x2, Pallas kernels: 413 us -> 534 us  [gather_call(): pl.pallas_call(functools.partial(gather_kernel, n_dp, n_expert, n, places...]
    pallas_call x2, Pallas kernels: 403 us -> 487 us  [scatter_call(): pl.pallas_call(functools.partial(scatter_kernel, n_dp, n_expert, n, len(c...]
    ppermute x12, waiting for transfers between devices: 25.6 us -> 55.3 us  [permuted(): got.append(lax.ppermute(piece, 'dp', paths))]
    convert_element_type x2 -> x0, other arithmetic: 23.6 us -> none  [the longest x1 11.8 us: shards(): grad_up_part = up_back.astype(jnp.float32)]
    ppermute x12, starting transfers between devices: 17.7 us -> 38.1 us  [permuted(): got.append(lax.ppermute(piece, 'dp', paths))]
    pallas_call x1, Pallas kernels: 38.1 us -> 18.2 us  [widen(): pl.pallas_call(widen_kernel, grid=(number,), in_specs=[block] * len(value...]
    concatenate x16 -> x0, other arithmetic: 19 us -> none  [the longest x8 12.3 us: weight_pieces(): jnp.concatenate([lax.dynamic_slice_in_dim(one[low:high], (me + k) % n_dp...]
  transfers between devices with their start and end apart: 12 -> 12, of which waited for: 2 -> 4; matrix products, arithmetic and copies ran while one was open for 7% -> 7% of each run, Pallas kernels for 13% -> 8%
where the time goes in v6:
time: 1410 us; the launch traced here: 1390 us
  Pallas kernels  1160 us (82%)
  matrix products  81.7 us (6%)
  waiting for transfers between devices  55.3 us (4%)
  local copies, waits for them, and re-layouts  38.6 us (3%)
  starting transfers between devices  38.1 us (3%)
  other arithmetic  21.1 us (1%)
    pallas_call x2, Pallas kernels, gather_call(): pl.pallas_call(functools.partial(gather_kernel, n_dp, n_expert, n, places...  534 us
    pallas_call x2, Pallas kernels, scatter_call(): pl.pallas_call(functools.partial(scatter_kernel, n_dp, n_expert, n, len(c...  487 us
    dot_general x21, matrix products, product(): return jnp.einsum(form, left, right, preferred_element_type=jnp.float32)  79.3 us
    pallas_call x2, Pallas kernels, expert_call(): pl.pallas_call(functools.partial(expert_kernel, steps, half, len(weights)...  79.2 us
    ppermute x12, waiting for transfers between devices, permuted(): got.append(lax.ppermute(piece, 'dp', paths))  55.3 us
    pallas_call x1, Pallas kernels, place_call(): pl.pallas_call(functools.partial(place_kernel, number), grid=(pairs,), in...  38.3 us
    ppermute x12, starting transfers between devices, permuted(): got.append(lax.ppermute(piece, 'dp', paths))  38.1 us
  transfers between devices with their start and end apart: 12, of which 4 were waited for; matrix products, arithmetic and copies ran while one was open for 7% of the time, Pallas kernels for 8%

profile of v6, /device:TPU:0, one launch (start us, length us, event | category | flops | bytes accessed | tf_op | source)
XLA Modules:
  0.0 1393.5 jit_solution(8340445671092665581)
XLA Ops:
  4.8 0.8 concatenate.39
  6.2 2.3 pad_maximum_fusion.refs_0_
  8.5 313.0 %shard_map.272 = (bf16[4,2048,2048]{2,1,0:T(8,128)(2,1)}, bf16[4096,256]{1,0:T(8,128)(2,1)}, bf16[8,2048,256]{2,1,0:T(8,128)(2,1)}, bf16[8,2048,256]{2,1,0:T(8,1...) custom-call(bf16[4,64,2048]{2,1,0:T(8,128)(2,1)} %pad_maximum_fusion, ...), custom_call_target="tpu_custom_call" | custom-call | tf_op jit(solution)/shard_map/pallas_call | solution.py:308
  321.6 1.0 collective-permute-start.1
  322.7 2.4 collective-permute-start.2
  325.1 1.3 slice.87
  326.7 2.0 slice_reduce_fusion
  329.4 4.8 multiply_reduce_fusion.6
  334.1 5.1 multiply_reduce_fusion.7
  339.3 5.9 fusion.48
  345.2 2.3 slice.101
  347.8 1.3 fusion.111
  349.5 1.6 fusion.110
  351.8 4.2 subtract_convert_fusion.3
  356.0 2.4 fusion.112
  358.5 1.8 convolution_convert_fusion.6
  361.1 5.0 multiply_reduce_fusion.5
  366.1 1.6 constant_dynamic-slice_fusion
  369.8 0.9 pad.9.refs_7_
  370.7 1.0 multiply_convert_fusion.1.refs_0_
  371.6 220.9 %shard_map.273 = (bf16[4096,2048]{1,0:T(8,128)(2,1)}, bf16[4096,2048]{1,0:T(8,128)(2,1)}, bf16[8,2048,256]{2,1,0:T(8,128)(2,1)}, bf16[8,2048,256]{2,1,0:T(8,128)...) custom-call(bf16[128,2048]{1,0:T(8,128)(2,1)} %multiply_convert_fusi, ...), custom_call_target="tpu_custom_call", output_to_operand_aliasing={{2}: (4, {}), {3}: (5, {})} | custom-call | tf_op jit(solution)/shard_map/pallas_call | solution.py:308
  592.7 0.9 collective-permute-start.4
  593.6 2.5 collective-permute-start.5
  596.1 55.3 %shard_map.274 = (bf16[8,768,2048]{2,1,0:T(8,128)(2,1)}, bf16[8,768,2048]{2,1,0:T(8,128)(2,1)}, bf16[8,768,128]{2,1,0:T(8,128)(2,1)}, bf16[6,2048,256]{2,1,0:T(8...) custom-call(s32[1]{0:T(128)} %bitcast.32.names_ref, ...), custom_call_target="tpu_custom_call" | custom-call | tf_op jit(solution)/shard_map/pallas_call | solution.py:867
  651.4 2.4 dynamic-slice_bitcast_fusion
  653.9 1.0 collective-permute-start.6
  654.9 1.4 collective-permute-start.7
  656.2 17.0 %collective-permute-done.3.refs_1_ = bf16[2,512,512]{2,1,0:T(8,128)(2,1)} collective-permute-done((bf16[2,512,512]{2,1,0:T(8,128)(2,1)}, bf16[2,512,512]{2,1,0:T(8,128)(2,1)}, u32[]{:S(2)}, u32[]{:S(2)}) %collective-permute-start.3) | collective-permute-done | bytes 1048608 | tf_op jit(solution)/shard_map/ppermute | solution.py:1041
  674.6 23.9 %shard_map.275 = (bf16[8,768,2048]{2,1,0:T(8,128)(2,1)}, bf16[8,768,2048]{2,1,0:T(8,128)(2,1)}, bf16[8,768,128]{2,1,0:T(8,128)(2,1)}, bf16[2,2048,256]{2,1,0:T(8...) custom-call(s32[5]{0:T(128)} %stack.43.names_ref, ...), custom_call_target="tpu_custom_call", output_to_operand_aliasing={{0}: (9, {}), {1}: (10, {}), {2}: (11, {}), {5}: (12, {})} | custom-call | tf_op jit(solution)/shard_map/pallas_call | solution.py:867
  698.5 38.3 %shard_map.276 = (bf16[4096,2048]{1,0:T(8,128)(2,1)}, bf16[4096,2176]{1,0:T(8,128)(2,1)}) custom-call(s32[16,8,256]{2,1,0:T(8,128)} %select_bitcast_fusion.refs_6_.slots_ref, bf16[8,768,2048]{2,1,0:T(8,128)(2,1)} %get-tuple-element.111.y_ref, bf16[8,768,2048]{2,1,0:T(8,128)(2,1)} %get-tuple-element.112.dx_ref, bf16[8,768,128]{2,1,0:T(8,128)(2,1)} %get-tuple-element.113.probs_ref), custom_call_target="tpu_custom_call" | custom-call | tf_op jit(solution)/shard_map/pallas_call | solution.py:915
  736.8 221.2 %shard_map.277 = (f32[128,2176]{1,0:T(8,128)}, bf16[8,512,1024]{2,1,0:T(8,128)(2,1)}, bf16[8,512,1024]{2,1,0:T(8,128)(2,1)}, bf16[2,512,512]{2,1,0:T(8,128)(2,1)...) custom-call(bf16[4,8,128,2176]{3,2,1,0:T(8,128)(2,1)} %bitcast.170, ...), custom_call_target="tpu_custom_call" | custom-call | tf_op jit(solution)/shard_map/pallas_call | solution.py:591
  957.9 1.1 multiply_reduce_fusion.8
  959.1 2.0 multiply_reduce_fusion
  961.1 1.5 subtract_add_fusion
  962.7 6.4 fusion.45
  971.5 0.9 multiply_subtract_fusion
  972.4 1.0 fusion.62
  973.9 6.3 fusion.5
  980.2 5.7 convolution_convert_fusion.1
  985.9 5.1 collective-permute-start.9
  991.6 5.8 convolution_convert_fusion
  997.4 6.4 fusion.28
  1003.8 30.5 %collective-permute-done.9.refs_12_ = bf16[2,512,512]{2,1,0:T(8,128)(2,1)S(1)} collective-permute-done((bf16[2,512,512]{2,1,0:T(8,128)(2,1)S(1)}, bf16[2,512,512]{2,1,0:T(8,128)(2,1)S(1)}, u32[]{:S(2)}, u32[]{:S(2)}) %collective-permute-start.9) | collective-permute-done | bytes 1048608 | tf_op jit(solution)/shard_map/ppermute | solution.py:1041
  1034.3 3.0 collective-permute-start.10
  1037.3 5.8 convolution_convert_fusion.2
  1043.1 1.3 convolution_convert_fusion.4
  1044.4 7.4 fusion.60
  1051.7 7.6 collective-permute-done.10.refs_13_
  1059.4 20.5 %collective-permute-start.11 = (bf16[2,512,512]{2,1,0:T(8,128)(2,1)}, bf16[2,512,512]{2,1,0:T(8,128)(2,1)}, u32[]{:S(2)}, u32[]{:S(2)}) collective-permute-start(bf16[2,512,512]{2,1,0:T(8,128)(2,1)} %get-tuple-element.130), channel_id=1, source_target_pairs={{0,8},{8,0},{16,24},{24,16},{1,9},{9,1},{17,25},{25,17},{2,10},{10... | collective-permute-start | bytes 3145736 | tf_op jit(solution)/shard_map/ppermute | solution.py:1041
  1079.9 1.0 concatenate.52
  1080.9 1.0 copy.119
  1081.9 1.8 concatenate.53
  1083.7 1.8 concatenate.54
  1085.5 1.8 concatenate.55
  1087.3 1.1 broadcast_in_dim.52
  1088.5 4.2 concatenate.51.refs_4_
  1092.7 6.9 convolution_convert_fusion.3
  1099.5 1.4 fusion.59
  1101.1 266.1 %shard_map.278 = (f32[64,2048]{1,0:T(8,128)}, f32[64,2048]{1,0:T(8,128)}, f32[64,2048]{1,0:T(8,128)}, f32[64,2048]{1,0:T(8,128)}, f32[64,128]{1,0:T(8,128)}, /*i...) custom-call(bf16[4,8,64,2048]{3,2,1,0:T(8,128)(2,1)} %bitcast.169, ...), custom_call_target="tpu_custom_call", output_to_operand_aliasing={{6}: (6, {}), {7}: (7, {})} | custom-call | tf_op jit(solution)/shard_map/pallas_call | solution.py:591
  1367.2 2.1 add_convert_fusion
  1369.4 1.7 slice_reduce_fusion.4
  1371.1 18.2 %shard_map.279 = (f32[8,512,1024]{2,1,0:T(8,128)}, f32[8,512,1024]{2,1,0:T(8,128)}) custom-call(bf16[8,512,1024]{2,1,0:T(8,128)(2,1)} %get-tuple-element.145.refs_0_, bf16[8,512,1024]{2,1,0:T(8,128)(2,1)} %get-tuple-element.146.refs_1_), custom_call_target="tpu_custom_call" | custom-call | tf_op jit(solution)/shard_map/pallas_call | solution.py:945
  1389.3 0.8 copy.189
  1390.1 0.8 copy.190
  (122 shorter events, 17.2 us)
Async XLA Ops:
  321.5 7.1 copy-start
  321.5 50.1 %collective-permute-start = (bf16[1,512,512]{2,1,0:T(8,128)(2,1)}, bf16[1,512,512]{2,1,0:T(8,128)(2,1)}, u32[]{:S(2)}, u32[]{:S(2)}) collective-permute-start(bf16[1,512,512]{2,1,0:T(8,128)(2,1)} %get-tuple-element.88), channel_id=1, source_target_pairs={{0,16},{8,24},{16,0},{24,8},{1,17},{9,25},{17,1},{25,9},{2,18},{10... | collective-permute-start | bytes 1572872 | tf_op jit(solution)/shard_map/ppermute | solution.py:1041
  321.6 50.0 %collective-permute-start.1 = (bf16[1,512,512]{2,1,0:T(8,128)(2,1)}, bf16[1,512,512]{2,1,0:T(8,128)(2,1)}, u32[]{:S(2)}, u32[]{:S(2)}) collective-permute-start(bf16[1,512,512]{2,1,0:T(8,128)(2,1)} %get-tuple-element.89), channel_id=1, source_target_pairs={{0,24},{8,16},{16,8},{24,0},{1,25},{9,17},{17,9},{25,1},{2,26},{10... | collective-permute-start | bytes 1572872 | tf_op jit(solution)/shard_map/ppermute | solution.py:1041
  322.7 49.0 %collective-permute-start.2 = (bf16[1,512,512]{2,1,0:T(8,128)(2,1)}, bf16[1,512,512]{2,1,0:T(8,128)(2,1)}, u32[]{:S(2)}, u32[]{:S(2)}) collective-permute-start(bf16[1,512,512]{2,1,0:T(8,128)(2,1)} %get-tuple-element.90), channel_id=1, source_target_pairs={{0,8},{8,0},{16,24},{24,16},{1,9},{9,1},{17,25},{25,17},{2,10},{10... | collective-permute-start | bytes 1572872 | tf_op jit(solution)/shard_map/ppermute | solution.py:1041
  326.4 346.9 %copy-start.7 = (bf16[32,64,128]{2,1,0:T(8,128)(2,1)}, bf16[32,64,128]{2,1,0:T(8,128)(2,1)S(1)}, u32[]{:S(2)}) copy-start(bf16[32,64,128]{2,1,0:T(8,128)(2,1)S(1)} %slice.116) | copy-start | bytes 1572868
  334.1 13.3 copy-start.3
  339.3 9.9 copy-start.1
  347.5 3.7 copy-start.26
  356.0 4.2 copy-start.8
  356.0 4.2 copy-start.10
  358.5 7.6 copy-start.18
  360.3 0.8 copy-start.14
  592.6 80.7 %collective-permute-start.3 = (bf16[2,512,512]{2,1,0:T(8,128)(2,1)}, bf16[2,512,512]{2,1,0:T(8,128)(2,1)}, u32[]{:S(2)}, u32[]{:S(2)}) collective-permute-start(bf16[2,512,512]{2,1,0:T(8,128)(2,1)} %get-tuple-element.102), channel_id=1, source_target_pairs={{0,16},{8,24},{16,0},{24,8},{1,17},{9,25},{17,1},{25,9},{2,18},{10... | collective-permute-start | bytes 3145736 | tf_op jit(solution)/shard_map/ppermute | solution.py:1041
  592.7 81.9 %collective-permute-start.4 = (bf16[2,512,512]{2,1,0:T(8,128)(2,1)}, bf16[2,512,512]{2,1,0:T(8,128)(2,1)}, u32[]{:S(2)}, u32[]{:S(2)}) collective-permute-start(bf16[2,512,512]{2,1,0:T(8,128)(2,1)} %get-tuple-element.103), channel_id=1, source_target_pairs={{0,24},{8,16},{16,8},{24,0},{1,25},{9,17},{17,9},{25,1},{2,26},{10... | collective-permute-start | bytes 3145736 | tf_op jit(solution)/shard_map/ppermute | solution.py:1041
  593.6 81.0 %collective-permute-start.5 = (bf16[2,512,512]{2,1,0:T(8,128)(2,1)}, bf16[2,512,512]{2,1,0:T(8,128)(2,1)}, u32[]{:S(2)}, u32[]{:S(2)}) collective-permute-start(bf16[2,512,512]{2,1,0:T(8,128)(2,1)} %get-tuple-element.104), channel_id=1, source_target_pairs={{0,8},{8,0},{16,24},{24,16},{1,9},{9,1},{17,25},{25,17},{2,10},{10... | collective-permute-start | bytes 3145736 | tf_op jit(solution)/shard_map/ppermute | solution.py:1041
  596.1 77.2 %copy-start.5 = (bf16[128,2048]{1,0:T(8,128)(2,1)S(1)}, bf16[128,2048]{1,0:T(8,128)(2,1)}, u32[]{:S(2)}) copy-start(bf16[128,2048]{1,0:T(8,128)(2,1)} %multiply_convert_fusion.1.refs_0_) | copy-start | bytes 1572868
  653.9 82.9 %collective-permute-start.6 = (bf16[1,512,512]{2,1,0:T(8,128)(2,1)}, bf16[1,512,512]{2,1,0:T(8,128)(2,1)}, u32[]{:S(2)}, u32[]{:S(2)}) collective-permute-start(bf16[1,512,512]{2,1,0:T(8,128)(2,1)} %get-tuple-element.174), channel_id=1, source_target_pairs={{0,16},{8,24},{16,0},{24,8},{1,17},{9,25},{17,1},{25,9},{2,18},{10... | collective-permute-start | bytes 1572872 | tf_op jit(solution)/shard_map/ppermute | solution.py:1041
  654.9 81.9 %collective-permute-start.7 = (bf16[1,512,512]{2,1,0:T(8,128)(2,1)}, bf16[1,512,512]{2,1,0:T(8,128)(2,1)}, u32[]{:S(2)}, u32[]{:S(2)}) collective-permute-start(bf16[1,512,512]{2,1,0:T(8,128)(2,1)} %get-tuple-element.173), channel_id=1, source_target_pairs={{0,24},{8,16},{16,8},{24,0},{1,25},{9,17},{17,9},{25,1},{2,26},{10... | collective-permute-start | bytes 1572872 | tf_op jit(solution)/shard_map/ppermute | solution.py:1041
  673.3 63.5 %collective-permute-start.8 = (bf16[1,512,512]{2,1,0:T(8,128)(2,1)S(1)}, bf16[1,512,512]{2,1,0:T(8,128)(2,1)}, u32[]{:S(2)}, u32[]{:S(2)}) collective-permute-start(bf16[1,512,512]{2,1,0:T(8,128)(2,1)S(1)} %get-tuple-element.172), channel_id=1, source_target_pairs={{0,8},{8,0},{16,24},{24,16},{1,9},{9,1},{17,25},{25,17},{2,10},{10... | collective-permute-start | bytes 1572872 | tf_op jit(solution)/shard_map/ppermute | solution.py:1041
  961.1 8.0 copy-start.19
  961.1 8.0 copy-start.29
  962.6 7.2 copy-start.12
  962.6 7.2 copy-start.13
  962.7 7.7 copy-start.9
  962.7 7.7 copy-start.11
  970.4 2.0 copy-start.2
  970.4 2.0 copy-start.4
  980.2 5.7 copy-start.28
  985.9 48.4 %collective-permute-start.9 = (bf16[2,512,512]{2,1,0:T(8,128)(2,1)S(1)}, bf16[2,512,512]{2,1,0:T(8,128)(2,1)S(1)}, u32[]{:S(2)}, u32[]{:S(2)}) collective-permute-start(bf16[2,512,512]{2,1,0:T(8,128)(2,1)S(1)} %copy-done.28), channel_id=1, source_target_pairs={{0,16},{8,24},{16,0},{24,8},{1,17},{9,25},{17,1},{25,9},{2,18},{10... | collective-permute-start | bytes 3145736 | tf_op jit(solution)/shard_map/ppermute | solution.py:1041
  997.4 36.9 %copy-start.27 = (bf16[2,512,512]{2,1,0:T(8,128)(2,1)S(1)}, bf16[2,512,512]{2,1,0:T(8,128)(2,1)}, u32[]{:S(2)}) copy-start(bf16[2,512,512]{2,1,0:T(8,128)(2,1)} %get-tuple-element.128) | copy-start | bytes 3145732
  1003.8 39.3 %copy-start.6 = (bf16[128,2048]{1,0:T(8,128)(2,1)S(1)}, bf16[128,2048]{1,0:T(8,128)(2,1)}, u32[]{:S(2)}) copy-start(bf16[128,2048]{1,0:T(8,128)(2,1)} %multiply_convert_fusion.1.refs_0_) | copy-start | bytes 1572868
  1034.3 17.4 %copy-start.15 = (bf16[2,512,512]{2,1,0:T(8,128)(2,1)}, bf16[2,512,512]{2,1,0:T(8,128)(2,1)S(1)}, u32[]{:S(2)}) copy-start(bf16[2,512,512]{2,1,0:T(8,128)(2,1)S(1)} %collective-permute-done.9.refs_12_) | copy-start | bytes 3145732
  1034.3 25.0 %collective-permute-start.10 = (bf16[2,512,512]{2,1,0:T(8,128)(2,1)S(1)}, bf16[2,512,512]{2,1,0:T(8,128)(2,1)S(1)}, u32[]{:S(2)}, u32[]{:S(2)}) collective-permute-start(bf16[2,512,512]{2,1,0:T(8,128)(2,1)S(1)} %copy-done.27), channel_id=1, source_target_pairs={{0,24},{8,16},{16,8},{24,0},{1,25},{9,17},{17,9},{25,1},{2,26},{10... | collective-permute-start | bytes 3145736 | tf_op jit(solution)/shard_map/ppermute | solution.py:1041
  1059.4 20.5 %copy-start.16 = (bf16[2,512,512]{2,1,0:T(8,128)(2,1)}, bf16[2,512,512]{2,1,0:T(8,128)(2,1)S(1)}, u32[]{:S(2)}) copy-start(bf16[2,512,512]{2,1,0:T(8,128)(2,1)S(1)} %collective-permute-done.10.refs_13_) | copy-start | bytes 3145732
  1059.4 41.7 %collective-permute-start.11 = (bf16[2,512,512]{2,1,0:T(8,128)(2,1)}, bf16[2,512,512]{2,1,0:T(8,128)(2,1)}, u32[]{:S(2)}, u32[]{:S(2)}) collective-permute-start(bf16[2,512,512]{2,1,0:T(8,128)(2,1)} %get-tuple-element.130), channel_id=1, source_target_pairs={{0,8},{8,0},{16,24},{24,16},{1,9},{9,1},{17,25},{25,17},{2,10},{10... | collective-permute-start | bytes 3145736 | tf_op jit(solution)/shard_map/ppermute | solution.py:1041
  1088.5 11.0 copy-start.25
  1092.7 6.9 copy-start.17
  1371.1 18.2 %copy-start.24 = (f32[64,2048]{1,0:T(8,128)S(1)}, f32[64,2048]{1,0:T(8,128)}, u32[]{:S(2)}) copy-start(f32[64,2048]{1,0:T(8,128)} %get-tuple-element.230) | copy-start | bytes 1572868
  1371.1 19.0 %copy-start.23 = (f32[64,2048]{1,0:T(8,128)S(1)}, f32[64,2048]{1,0:T(8,128)}, u32[]{:S(2)}) copy-start(f32[64,2048]{1,0:T(8,128)} %get-tuple-element.231) | copy-start | bytes 1572868
  1371.1 19.8 %copy-start.22 = (f32[64,2048]{1,0:T(8,128)S(1)}, f32[64,2048]{1,0:T(8,128)}, u32[]{:S(2)}) copy-start(f32[64,2048]{1,0:T(8,128)} %get-tuple-element.232) | copy-start | bytes 1572868
  1371.1 20.6 %copy-start.21 = (f32[64,2048]{1,0:T(8,128)S(1)}, f32[64,2048]{1,0:T(8,128)}, u32[]{:S(2)}) copy-start(f32[64,2048]{1,0:T(8,128)} %get-tuple-element.233) | copy-start | bytes 1572868
  1371.1 21.4 %copy-start.20 = (f32[64,128]{1,0:T(8,128)S(1)}, f32[64,128]{1,0:T(8,128)}, u32[]{:S(2)}) copy-start(f32[64,128]{1,0:T(8,128)} %get-tuple-element.144) | copy-start | bytes 98308

commit v7 on v6

--- a/solution.py
+++ b/solution.py
@@ -107,7 +107,7 @@
     )
 
 
-def exchange(n_dp, pairs, send, receive, local):
+def exchange(n_dp, pairs, send, receive):
     z, j, chip, core = place_of()
     to_plane, unused = partners(z, n_dp)
     copies = []
@@ -117,22 +117,28 @@
             copies.append(
                 remote(source(to), target(z), send.at[i, k], receive.at[i, k], (to, j))
             )
-        copies.append(pltpu.make_async_copy(source(z), target(z), local.at[i]))
     return copies
 
 
-def moves(pairs, local):
-    return [
-        pltpu.make_async_copy(source, target, local.at[i])
+def moves(pairs, stages, local):
+    bring = [
+        pltpu.make_async_copy(source, stages[i], local.at[i, 0])
         for i, (source, target) in enumerate(pairs)
     ]
+    put = [
+        pltpu.make_async_copy(stages[i], target, local.at[i, 1])
+        for i, (source, target) in enumerate(pairs)
+    ]
+    return bring, put
 
 
 def nothing(ins, outs):
     return []
 
 
-def gather_kernel(n_dp, n_expert, n_items, places, cuts, puts, finish, n_cut, n_out, *refs):
+def gather_kernel(
+    n_dp, n_expert, n_items, places, cuts, puts, finish, n_cut, n_out, n_stages, *refs
+):
     z, j, chip, core = place_of()
     chips = n_expert // 2
     square = chips == 4
@@ -152,8 +158,8 @@
         local,
         send_x,
         recv_x,
-        local_x,
         local_y,
+        *stages,
     ) = refs[at + n_items + n_out :]
     greet(n_dp, n_expert)
     mate = (z, chip * 2 + 1 - core)
@@ -223,10 +229,17 @@
 
     for d in range(1, n_dp):
         at_distance(d, relay)
-    copies = exchange(n_dp, cuts(cut_in, cut_out), send_x, recv_x, local_x)
-    copies += moves(puts(cut_in, cut_out), local_y)
+    pairs = cuts(cut_in, cut_out)
+    copies = exchange(n_dp, pairs, send_x, recv_x)
     for copy in copies:
         copy.start()
+    own = [(source(z), target(z)) for source, target in pairs]
+    bring, put = moves(own + puts(cut_in, cut_out), stages, local_y)
+    for copy in bring:
+        copy.start()
+    for one, other in zip(bring, put):
+        one.wait()
+        other.start()
 
     def arrive(i, plane, k):
         column = from_chip(k) * 2 + core
@@ -283,7 +296,7 @@
             def _():
                 along(i, plane, block, 1, -1).wait_send()
 
-    for copy in copies:
+    for copy in copies + put:
         copy.wait()
 
 
@@ -298,6 +311,7 @@
     cuts,
     aliases,
     number,
+    stages,
     puts=nothing,
     finish=lambda items, ins, outs: None,
 ):
@@ -307,7 +321,17 @@
     anywhere = pl.BlockSpec(memory_space=pl.ANY)
     return pl.pallas_call(
         functools.partial(
-            gather_kernel, n_dp, n_expert, n, places, cuts, puts, finish, len(cut_in), m
+            gather_kernel,
+            n_dp,
+            n_expert,
+            n,
+            places,
+            cuts,
+            puts,
+            finish,
+            len(cut_in),
+            m,
+            len(stages),
         ),
         out_shape=[*shapes, *cut_shapes],
         in_specs=[anywhere] * (n + len(cut_in)),
@@ -322,8 +346,8 @@
             dma((n,)),
             dma((4, n_dp)),
             dma((4, n_dp)),
-            dma((4,)),
-            dma((4 * n_dp,)),
+            dma((max(len(stages), 1), 2)),
+            *[pltpu.VMEM(stage, jnp.bfloat16) for stage in stages],
         ],
         input_output_aliases=aliases,
         compiler_params=pltpu.CompilerParams(
@@ -332,7 +356,9 @@
     )(*items, *cut_in)
 
 
-def scatter_kernel(n_dp, n_expert, n_items, n_cut, n_out, cuts, puts, rings, n_rings, *refs):
+def scatter_kernel(
+    n_dp, n_expert, n_items, n_cut, n_out, cuts, puts, rings, n_rings, *refs
+):
     z, j, chip, core = place_of()
     chips = n_expert // 2
     square = chips == 4
@@ -359,8 +385,8 @@
         local,
         send_x,
         recv_x,
-        local_x,
         local_y,
+        *stages,
     ) = refs
     greet(n_dp, n_expert)
     mate = (z, chip * 2 + 1 - core)
@@ -466,9 +492,13 @@
         if ahead[rings[i]] < 2:
             load(i, k, at).start()
             ahead[rings[i]] += 1
-    copies = exchange(n_dp, cuts(cut_in, cut_out), send_x, recv_x, local_x)
-    copies += moves(puts(cut_in, cut_out), local_y)
+    pairs = cuts(cut_in, cut_out)
+    copies = exchange(n_dp, pairs, send_x, recv_x)
     for copy in copies:
+        copy.start()
+    own = [(source(z), target(z)) for source, target in pairs]
+    bring, put = moves(own + puts(cut_in, cut_out), stages, local_y)
+    for copy in bring:
         copy.start()
 
     for n, (i, k, at) in enumerate(loads):
@@ -489,6 +519,9 @@
             send_near(i, 1, low, 0).start()
         else:
             send_near(i, 2, high, 1).start()
+    for one, other in zip(bring, put):
+        one.wait()
+        other.start()
     if square:
         for i in range(n_items):
             send_over(i, 2, high).wait_recv()
@@ -571,12 +604,12 @@
                     mate,
                 ).wait_send()
 
-    for copy in copies:
+    for copy in copies + put:
         copy.wait()
 
 
 def scatter_call(
-    n_dp, n_expert, items, cut_in, cut_shapes, cuts, number, aliases, puts=nothing
+    n_dp, n_expert, items, cut_in, cut_shapes, cuts, number, aliases, stages, puts=nothing
 ):
     chips = n_expert // 2
     square = chips == 4
@@ -612,8 +645,8 @@
             dma((len(kinds), 2)),
             dma((4, n_dp)),
             dma((4, n_dp)),
-            dma((4,)),
-            dma((4 * n_dp,)),
+            dma((max(len(stages), 1), 2)),
+            *[pltpu.VMEM(stage, jnp.bfloat16) for stage in stages],
         ],
         input_output_aliases=aliases,
         compiler_params=pltpu.CompilerParams(
@@ -623,13 +656,14 @@
 
 
 def scatter_all(
-    n_dp, n_expert, items, cut_in, cut_shapes, cuts, number, aliases=(), puts=nothing
+    n_dp, n_expert, items, cut_in, cut_shapes, cuts, number, aliases, stages, puts=nothing
 ):
     chips = n_expert // 2
     blocks = (2 * chips - 1 if chips != 4 else 7) * n_dp + n_dp + 3
     need = sum(blocks * item.shape[2] * item.shape[3] * 2 for item in items)
     kinds = {item.shape[2:] for item in items}
     need += sum(2 * n_dp * kind[0] * kind[1] * 2 for kind in kinds)
+    need += sum(stage[0] * stage[1] * stage[2] * 2 for stage in stages)
     pieces = -(-need // (61 * 1024 * 1024))
     tiles = [item.shape[3] // 128 for item in items]
     results = [[] for item in items]
@@ -647,6 +681,7 @@
             cuts if first else nothing,
             number + piece,
             {len(used) + a: len(used) + b for a, b in aliases} if first else {},
+            stages if first else [],
             puts if first else nothing,
         )
         for i, out in zip(used, outs):
@@ -939,17 +974,58 @@
         target[...] = source[...].astype(jnp.float32)
 
 
-def widen(values):
+def widen(low, values):
     number, rows, columns = values[0].shape
-    block = pl.BlockSpec((1, rows, columns), lambda e: (e, 0, 0))
+    block = pl.BlockSpec((1, rows, columns), lambda e: (e + low, 0, 0))
     return pl.pallas_call(
         widen_kernel,
-        grid=(number,),
+        grid=(number - low,),
         in_specs=[block] * len(values),
         out_specs=[block] * len(values),
         out_shape=[jax.ShapeDtypeStruct(one.shape, jnp.float32) for one in values],
         compiler_params=pltpu.CompilerParams(vmem_limit_bytes=BIG),
     )(*values)
+
+
+def widen_pieces_kernel(n_pieces, offsets_ref, *refs):
+    pieces, refs = refs[:n_pieces], refs[n_pieces + 2 :]
+    targets, wide, sems = refs[:2], refs[2], refs[3]
+    part = wide.shape[4]
+    copies = []
+    for k, piece in enumerate(pieces):
+        columns = pl.ds(pl.multiple_of(offsets_ref[k], part), part)
+        for n in range(2):
+            wide[k, n] = piece[:, :, n * part : (n + 1) * part].astype(jnp.float32)
+            copy = pltpu.make_async_copy(
+                wide.at[k, n], targets[n].at[pl.ds(0, piece.shape[0]), :, columns], sems.at[k, n]
+            )
+            copy.start()
+            copies.append(copy)
+    for copy in copies:
+        copy.wait()
+
+
+def widen_pieces(offsets, pieces, into):
+    size, rows, columns = pieces[0].shape
+    anywhere = pl.BlockSpec(memory_space=pl.ANY)
+    count = len(pieces)
+    return pl.pallas_call(
+        functools.partial(widen_pieces_kernel, count),
+        in_specs=[
+            pl.BlockSpec(memory_space=pltpu.SMEM),
+            *[pl.BlockSpec(memory_space=pltpu.VMEM)] * count,
+            anywhere,
+            anywhere,
+        ],
+        out_specs=[anywhere, anywhere],
+        out_shape=[jax.ShapeDtypeStruct(one.shape, one.dtype) for one in into],
+        scratch_shapes=[
+            pltpu.VMEM((count, 2, size, rows, columns // 2), jnp.float32),
+            pltpu.SemaphoreType.DMA((count, 2)),
+        ],
+        input_output_aliases={1 + count: 0, 2 + count: 1},
+        compiler_params=pltpu.CompilerParams(vmem_limit_bytes=BIG),
+    )(offsets, *pieces, *into)
 
 
 def shards(
@@ -1002,8 +1078,7 @@
     beside = early + number // 8
     late = number - number // 4
     back_beside = number // 8
-    back_third = back_beside + number // 4
-    back_late = back_third + number // 4
+    back_third = back_beside + number * 3 // 8
     me = lax.axis_index("dp")
     cut_shape = jax.ShapeDtypeStruct((number, n_dp * depth, part), bf16)
 
@@ -1053,6 +1128,9 @@
     def piece_shapes(size, first_k):
         shape = jax.ShapeDtypeStruct((size, depth, 2 * part), bf16)
         return [shape] * (n_dp - first_k if size else 0)
+
+    def stages(*sizes):
+        return [(size, depth, part) for size in sizes]
 
     soon_shapes = piece_shapes(beside - early, 1)
     late_shapes = piece_shapes(number - late, 0)
@@ -1077,6 +1155,11 @@
         recut(0, early),
         {},
         0,
+        stages(
+            *[early] * 2,
+            *[beside - early] * (2 * n_soon),
+            *[number - late] * (2 * n_dp),
+        ),
         lambda ins, outs: cut_pieces(early, beside, 1, ins, outs[2 : 2 + n_soon])
         + cut_pieces(late, number, 0, ins, outs[2 + n_soon :]),
     )
@@ -1162,6 +1245,7 @@
         recut(beside, late),
         {4: 2, 5: 3},
         1,
+        stages(*[late - beside] * 2, *[beside - early] * (2 * n_dp if n_soon else 0)),
         put_weights,
         pick_all,
     )
@@ -1205,30 +1289,6 @@
             )
 
         return [pair(0), pair(1)]
-
-    def put_grads(low, high, ins, pieces, outs):
-        own = lax.axis_index("dp")
-        unused, heard = partners(own, n_dp)
-        chosen = pl.ds(low, high - low)
-        pairs = []
-        if high > low:
-            for n in range(2):
-                source = ins[n].at[chosen, rows_at(own)]
-                pairs.append((source, outs[n].at[chosen, :, columns_at(own)]))
-        for k, piece in enumerate(pieces, 1):
-            for n in range(2):
-                columns = piece.at[:, :, pl.ds(n * part, part)]
-                pairs.append((columns, outs[n].at[chosen, :, columns_at(heard(k))]))
-        return pairs
-
-    def cut_grads(low, high, ins, outs):
-        to, unused = partners(lax.axis_index("dp"), n_dp)
-        pairs = []
-        for k, piece in enumerate(outs, 1):
-            for n in range(2):
-                source = ins[n].at[pl.ds(low, high - low), rows_at(to(k))]
-                pairs.append((source, piece.at[:, :, pl.ds(n * part, part)]))
-        return pairs
 
     pieces = []
     if back_beside:
@@ -1246,22 +1306,19 @@
                     axis=2,
                 )
             pieces.append(piece)
-        part_back, *pieces = lax.optimization_barrier((part_back, *permuted(pieces)))
+        pieces = permuted(pieces)
     way_shapes = [jax.ShapeDtypeStruct((number, depth, ff), bf16)] * 2
-    (back,), (gate_third, up_third, *pieces) = scatter_all(
+    (back,), (gate_third, up_third) = scatter_all(
         n_dp,
         n_expert,
         [part_back.reshape(n_dp, n_expert, count, D + width)],
-        [gate_soon, up_soon, *pieces],
-        way_shapes + piece_shapes(back_late - back_third, 1),
+        [gate_soon, up_soon],
+        way_shapes,
         lambda ins, outs: ways(back_beside, back_third, 0, ins, outs),
         8,
         (),
-        lambda ins, outs: put_grads(0, back_beside, ins, ins[2:], outs)
-        + cut_grads(back_third, back_late, ins, outs[2:]),
-    )
-    if pieces:
-        part_out, *pieces = lax.optimization_barrier((part_out, *permuted(pieces, True)))
+        stages(*[back_third - back_beside] * 2),
+    )
 
     grad_final = cotangent.astype(jnp.float32)
     grad_mlp = back[:, :D]
@@ -1335,19 +1392,30 @@
             )
         ]
         + [part_out.reshape(n_dp, n_expert, count, D)],
-        [gate_third, up_third, gate_soon, up_soon, gate_rest, up_rest, *pieces],
+        [gate_third, up_third, gate_soon, up_soon, gate_rest, up_rest],
         way_shapes,
-        lambda ins, outs: ways(back_late, late, 0, ins[2:4], outs)
+        lambda ins, outs: ways(back_third, late, 0, ins[2:4], outs)
         + ways(0, number - late, late, ins[4:6], outs),
         16,
         ((0, 0), (1, 1)),
-        lambda ins, outs: put_grads(back_third, back_late, ins[2:4], ins[6:], outs),
+        stages(*[late - back_third] * 2, *[number - late] * 2),
     )
     grad_out_part, grad_value_part, grad_key_part, grad_query_part, small_part, summed = sums
     output = (middle + summed).astype(bf16)
     grad_router_part = small_part[:, :experts_all]
     gain_parts = [small_part[:, experts_all + i] for i in range(4)]
-    grad_gate_part, grad_up_part = widen([gate_back, up_back])
+    widened = widen(back_beside, [gate_back, up_back])
+    if back_beside:
+        own = jnp.concatenate(
+            [
+                lax.dynamic_slice_in_dim(one[:back_beside], me * depth, depth, 1)
+                for one in (gate_soon, up_soon)
+            ],
+            axis=2,
+        )
+        offsets = jnp.stack([from_plane(k) * part for k in range(n_dp)])
+        widened = widen_pieces(offsets, [own, *pieces], widened)
+    grad_gate_part, grad_up_part = widened
     return (
         output,
         grad_inputs,

time: 1410 us -> 1290 us (0.915)
  Pallas kernels: 1160 us -> 1100 us
  waiting for transfers between devices: 55.3 us -> 0.02 us
  local copies, waits for them, and re-layouts: 38.6 us -> 65.3 us
  starting transfers between devices: 38.1 us -> 12.8 us
    pallas_call x2, Pallas kernels: 534 us -> 386 us  [gather_call(): pl.pallas_call(functools.partial(gather_kernel, n_dp, n_expert, n, places...]
    pallas_call x2 -> x3, Pallas kernels: 487 us -> 572 us  [scatter_call(): pl.pallas_call(functools.partial(scatter_kernel, n_dp, n_expert, n, len(c...]
    ppermute x12 -> x9, waiting for transfers between devices: 55.3 us -> 0.02 us  [permuted(): got.append(lax.ppermute(piece, 'dp', paths))]
    slice x0 -> x6, local copies, waits for them, and re-layouts: none -> 29.7 us  [the longest x4 27.2 us: scatter_all(): items[i][..., ends[i][0]:ends[i][1]]]
    ppermute x12 -> x9, starting transfers between devices: 38.1 us -> 12.8 us  [permuted(): got.append(lax.ppermute(piece, 'dp', paths))]
  transfers between devices with their start and end apart: 12 -> 9, of which waited for: 4 -> 0; matrix products, arithmetic and copies ran while one was open for 7% -> 13% of each run, Pallas kernels for 8% -> 55%
where the time goes in v7:
time: 1290 us; the launch traced here: 1280 us
  Pallas kernels  1100 us (85%)
  matrix products  74.4 us (6%)
  local copies, waits for them, and re-layouts  65.3 us (5%)
  other arithmetic  31.5 us (2%)
    pallas_call x3, Pallas kernels, scatter_call(): pl.pallas_call(functools.partial(scatter_kernel, n_dp, n_expert, n, len(c...  572 us
    pallas_call x2, Pallas kernels, gather_call(): pl.pallas_call(functools.partial(gather_kernel, n_dp, n_expert, n, places...  386 us
    pallas_call x2, Pallas kernels, expert_call(): pl.pallas_call(functools.partial(expert_kernel, steps, half, len(weights)...  79.1 us
    dot_general x21, matrix products, product(): return jnp.einsum(form, left, right, preferred_element_type=jnp.float32)  72.1 us
    pallas_call x1, Pallas kernels, place_call(): pl.pallas_call(functools.partial(place_kernel, number), grid=(pairs,), in...  38.3 us
    slice x4, local copies, waits for them, and re-layouts, scatter_all(): items[i][..., ends[i][0]:ends[i][1]]  27.2 us
  transfers between devices with their start and end apart: 9, of which 0 were waited for; matrix products, arithmetic and copies ran while one was open for 13% of the time, Pallas kernels for 55%

profile of v7, /device:TPU:0, one launch (start us, length us, event | category | flops | bytes accessed | tf_op | source)
XLA Modules:
  0.0 1281.5 jit_solution(1441152082301941447)
XLA Ops:
  6.2 2.3 pad_maximum_fusion.refs_0_
  8.5 179.4 %shard_map.272 = (bf16[4,2048,2048]{2,1,0:T(8,128)(2,1)}, bf16[4096,256]{1,0:T(8,128)(2,1)}, bf16[8,2048,256]{2,1,0:T(8,128)(2,1)}, bf16[8,2048,256]{2,1,0:T(8,1...) custom-call(bf16[4,64,2048]{2,1,0:T(8,128)(2,1)} %pad_maximum_fusion, ...), custom_call_target="tpu_custom_call" | custom-call | tf_op jit(solution)/shard_map/pallas_call | solution.py:322
  188.1 3.4 collective-permute-start.2
  191.5 1.3 slice.123
  193.8 2.0 slice_reduce_fusion
  196.5 4.8 multiply_reduce_fusion.6
  201.3 5.1 multiply_reduce_fusion.7
  206.5 5.9 fusion.48
  212.4 2.3 slice.137
  215.0 1.3 fusion.117
  216.7 1.3 fusion.116
  218.7 4.2 subtract_convert_fusion.3
  222.8 2.4 fusion.118
  225.2 1.8 convolution_convert_fusion.6
  227.8 5.0 multiply_reduce_fusion.5
  232.8 2.0 constant_dynamic-slice_fusion.2
  235.1 1.8 dynamic-slice_maximum_fusion
  238.9 1.0 multiply_convert_fusion.1.refs_0_
  240.0 207.0 %shard_map.273 = (bf16[4096,2048]{1,0:T(8,128)(2,1)}, bf16[4096,2048]{1,0:T(8,128)(2,1)}, bf16[8,2048,256]{2,1,0:T(8,128)(2,1)}, bf16[8,2048,256]{2,1,0:T(8,128)...) custom-call(bf16[128,2048]{1,0:T(8,128)(2,1)} %multiply_convert_fusi, ...), custom_call_target="tpu_custom_call", output_to_operand_aliasing={{2}: (4, {}), {3}: (5, {})} | custom-call | tf_op jit(solution)/shard_map/pallas_call | solution.py:322
  447.0 2.6 collective-permute-start.3
  449.6 2.3 collective-permute-start.4
  453.8 55.2 %shard_map.274 = (bf16[8,768,2048]{2,1,0:T(8,128)(2,1)}, bf16[8,768,2048]{2,1,0:T(8,128)(2,1)}, bf16[8,768,128]{2,1,0:T(8,128)(2,1)}, bf16[6,2048,256]{2,1,0:T(8...) custom-call(s32[1]{0:T(128)} %bitcast.32.names_ref, ...), custom_call_target="tpu_custom_call" | custom-call | tf_op jit(solution)/shard_map/pallas_call | solution.py:902
  509.1 1.3 slice.162
  510.4 1.3 slice.163
  511.7 2.6 dynamic-slice_bitcast_fusion
  514.2 2.1 collective-permute-start.6
  516.3 2.3 collective-permute-start.7
  519.5 23.8 %shard_map.275 = (bf16[8,768,2048]{2,1,0:T(8,128)(2,1)}, bf16[8,768,2048]{2,1,0:T(8,128)(2,1)}, bf16[8,768,128]{2,1,0:T(8,128)(2,1)}, bf16[2,2048,256]{2,1,0:T(8...) custom-call(s32[5]{0:T(128)} %stack.58.names_ref, ...), custom_call_target="tpu_custom_call", output_to_operand_aliasing={{0}: (9, {}), {1}: (10, {}), {2}: (11, {}), {5}: (12, {})} | custom-call | tf_op jit(solution)/shard_map/pallas_call | solution.py:902
  543.3 38.3 %shard_map.276 = (bf16[4096,2048]{1,0:T(8,128)(2,1)}, bf16[4096,2176]{1,0:T(8,128)(2,1)}) custom-call(s32[16,8,256]{2,1,0:T(8,128)} %select_bitcast_fusion.refs_6_.slots_ref, bf16[8,768,2048]{2,1,0:T(8,128)(2,1)} %get-tuple-element.103.y_ref, bf16[8,768,2048]{2,1,0:T(8,128)(2,1)} %get-tuple-element.104.dx_ref, bf16[8,768,128]{2,1,0:T(8,128)(2,1)} %get-tuple-element.105.probs_ref), custom_call_target="tpu_custom_call" | custom-call | tf_op jit(solution)/shard_map/pallas_call | solution.py:950
  581.7 208.3 %shard_map.277 = (f32[128,2176]{1,0:T(8,128)}, bf16[8,512,1024]{2,1,0:T(8,128)(2,1)}, bf16[8,512,1024]{2,1,0:T(8,128)(2,1)}) custom-call(bf16[4,8,128,2176]{3,2,1,0:T(8,128)(2,1)} %bitcast.174, bf16[6,2048,256]{2,1,0:T(8,128)(2,1)} %get-tuple-element.107.refs_1_.refs_7_, bf16[6,2048,256]{2,1,0:T(8,128)(2,1)} %get-tuple-element.108.refs_2_.refs_8_), custom_call_target="tpu_custom_call" | custom-call | tf_op jit(solution)/shard_map/pallas_call | solution.py:624
  789.9 1.1 multiply_reduce_fusion.8
  791.1 2.0 multiply_reduce_fusion
  793.1 1.8 subtract_add_fusion
  795.0 6.4 fusion.45
  803.2 5.5 convolution_convert_fusion.3
  809.3 1.0 multiply_subtract_fusion
  810.3 1.0 fusion.62
  811.9 2.5 convolution_convert_fusion.1
  814.4 6.7 fusion.5
  821.1 1.3 convolution_convert_fusion.4
  823.0 2.5 convolution_convert_fusion
  825.4 3.9 fusion.112
  829.3 4.6 fusion.113
  834.0 6.0 convolution_convert_fusion.2
  840.0 6.3 fusion.111
  846.3 6.3 fusion.28
  852.7 7.4 fusion.60
  860.1 1.0 concatenate.76
  861.4 1.8 concatenate.77
  863.2 1.8 concatenate.78
  865.0 1.8 concatenate.79
  866.8 12.3 fusion.114
  880.0 4.2 concatenate.69.refs_4_
  884.3 141.0 %shard_map.279 = (f32[64,1024]{1,0:T(8,128)}, f32[64,1024]{1,0:T(8,128)}, f32[64,1024]{1,0:T(8,128)}, f32[64,1024]{1,0:T(8,128)}, f32[64,128]{1,0:T(8,128)}, /*index=5*/f32[128,1024]{1,0:T(8,128)}) custom-call(bf16[4,8,64,1024]{3,2,1,0:T(8,128)(2,1)} %get-tuple-element.208.refs_0_, bf16[4,8,64,1024]{3,2,1,0:T(8,128)(2,1)} %get-tuple-element.159.refs_1_, ...), custom_call_target="tpu_custom_call" | custom-call | tf_op jit(solution)/shard_map/pallas_call | solution.py:624
  1025.3 1.7 slice_reduce_fusion.4
  1027.0 223.1 %shard_map.278 = (f32[64,1024]{1,0:T(8,128)}, f32[64,1024]{1,0:T(8,128)}, f32[64,1024]{1,0:T(8,128)}, f32[64,1024]{1,0:T(8,128)}, f32[128,1024]{1,0:T(8,128)}, /...) custom-call(bf16[4,8,64,1024]{3,2,1,0:T(8,128)(2,1)} %get-tuple-element., ...), custom_call_target="tpu_custom_call", output_to_operand_aliasing={{5}: (5, {}), {6}: (6, {})} | custom-call | tf_op jit(solution)/shard_map/pallas_call | solution.py:624
  1250.1 16.1 %shard_map.280 = (f32[8,512,1024]{2,1,0:T(8,128)}, f32[8,512,1024]{2,1,0:T(8,128)}) custom-call(bf16[8,512,1024]{2,1,0:T(8,128)(2,1)} %get-tuple-element.127.refs_0_, bf16[8,512,1024]{2,1,0:T(8,128)(2,1)} %get-tuple-element.128.refs_1_), custom_call_target="tpu_custom_call" | custom-call | tf_op jit(solution)/shard_map/pallas_call | solution.py:980
  1266.2 1.9 pad_maximum_fusion.6
  1268.0 1.9 pad_maximum_fusion.5
  1269.9 1.9 pad_maximum_fusion.4
  1271.7 1.8 pad_maximum_fusion.3
  1273.5 2.1 fusion.65
  1275.6 1.4 fusion.59
  1277.1 3.6 shard_map.281
  (126 shorter events, 20.2 us)
Async XLA Ops:
  187.9 7.9 copy-start
  187.9 52.0 %collective-permute-start = (bf16[1,512,512]{2,1,0:T(8,128)(2,1)}, bf16[1,512,512]{2,1,0:T(8,128)(2,1)}, u32[]{:S(2)}, u32[]{:S(2)}) collective-permute-start(bf16[1,512,512]{2,1,0:T(8,128)(2,1)} %get-tuple-element.80), channel_id=1, source_target_pairs={{0,16},{8,24},{16,0},{24,8},{1,17},{9,25},{17,1},{25,9},{2,18},{10... | collective-permute-start | bytes 1572872 | tf_op jit(solution)/shard_map/ppermute | solution.py:1116
  188.0 51.9 %collective-permute-start.1 = (bf16[1,512,512]{2,1,0:T(8,128)(2,1)}, bf16[1,512,512]{2,1,0:T(8,128)(2,1)}, u32[]{:S(2)}, u32[]{:S(2)}) collective-permute-start(bf16[1,512,512]{2,1,0:T(8,128)(2,1)} %get-tuple-element.81), channel_id=1, source_target_pairs={{0,24},{8,16},{16,8},{24,0},{1,25},{9,17},{17,9},{25,1},{2,26},{10... | collective-permute-start | bytes 1572872 | tf_op jit(solution)/shard_map/ppermute | solution.py:1116
  188.1 51.8 %collective-permute-start.2 = (bf16[1,512,512]{2,1,0:T(8,128)(2,1)}, bf16[1,512,512]{2,1,0:T(8,128)(2,1)}, u32[]{:S(2)}, u32[]{:S(2)}) collective-permute-start(bf16[1,512,512]{2,1,0:T(8,128)(2,1)} %get-tuple-element.82), channel_id=1, source_target_pairs={{0,8},{8,0},{16,24},{24,16},{1,9},{9,1},{17,25},{25,17},{2,10},{10... | collective-permute-start | bytes 1572872 | tf_op jit(solution)/shard_map/ppermute | solution.py:1116
  192.8 0.8 copy-start.9
  201.3 13.3 %copy-start.5 = (f32[128,2048]{1,0:T(8,128)}, f32[128,2048]{1,0:T(8,128)S(1)}, u32[]{:S(2)}) copy-start(f32[128,2048]{1,0:T(8,128)S(1)} %get-tuple-element.195) | copy-start | bytes 3145732
  206.5 9.9 copy-start.3
  214.6 3.4 copy-start.23
  225.2 7.6 copy-start.18
  227.0 0.8 copy-start.15
  232.8 558.3 %copy-start.1 = (f32[128,2048]{1,0:T(8,128)}, f32[128,2048]{1,0:T(8,128)S(1)}, u32[]{:S(2)}) copy-start(f32[128,2048]{1,0:T(8,128)S(1)} %get-tuple-element.199) | copy-start | bytes 3145732
  239.9 211.9 %copy-start.7 = (bf16[128,2048]{1,0:T(8,128)(2,1)S(1)}, bf16[128,2048]{1,0:T(8,128)(2,1)}, u32[]{:S(2)}) copy-start(bf16[128,2048]{1,0:T(8,128)(2,1)} %multiply_convert_fusion.1.refs_0_) | copy-start | bytes 1572868
  239.9 211.9 %copy-start.10 = (bf16[32,64,128]{2,1,0:T(8,128)(2,1)S(1)}, bf16[32,64,128]{2,1,0:T(8,128)(2,1)}, u32[]{:S(2)}) copy-start(bf16[32,64,128]{2,1,0:T(8,128)(2,1)} %copy-done.9) | copy-start | bytes 1572868
  447.0 72.5 %collective-permute-start.3 = (bf16[2,512,512]{2,1,0:T(8,128)(2,1)}, bf16[2,512,512]{2,1,0:T(8,128)(2,1)}, u32[]{:S(2)}, u32[]{:S(2)}) collective-permute-start(bf16[2,512,512]{2,1,0:T(8,128)(2,1)} %get-tuple-element.94), channel_id=1, source_target_pairs={{0,16},{8,24},{16,0},{24,8},{1,17},{9,25},{17,1},{25,9},{2,18},{10... | collective-permute-start | bytes 3145736 | tf_op jit(solution)/shard_map/ppermute | solution.py:1116
  449.6 69.9 %collective-permute-start.4 = (bf16[2,512,512]{2,1,0:T(8,128)(2,1)}, bf16[2,512,512]{2,1,0:T(8,128)(2,1)}, u32[]{:S(2)}, u32[]{:S(2)}) collective-permute-start(bf16[2,512,512]{2,1,0:T(8,128)(2,1)} %get-tuple-element.95), channel_id=1, source_target_pairs={{0,24},{8,16},{16,8},{24,0},{1,25},{9,17},{17,9},{25,1},{2,26},{10... | collective-permute-start | bytes 3145736 | tf_op jit(solution)/shard_map/ppermute | solution.py:1116
  451.9 67.6 %collective-permute-start.5 = (bf16[2,512,512]{2,1,0:T(8,128)(2,1)}, bf16[2,512,512]{2,1,0:T(8,128)(2,1)}, u32[]{:S(2)}, u32[]{:S(2)}) collective-permute-start(bf16[2,512,512]{2,1,0:T(8,128)(2,1)} %get-tuple-element.96), channel_id=1, source_target_pairs={{0,8},{8,0},{16,24},{24,16},{1,9},{9,1},{17,25},{25,17},{2,10},{10... | collective-permute-start | bytes 3145736 | tf_op jit(solution)/shard_map/ppermute | solution.py:1116
  514.2 762.9 %collective-permute-start.6 = (bf16[1,512,512]{2,1,0:T(8,128)(2,1)}, bf16[1,512,512]{2,1,0:T(8,128)(2,1)}, u32[]{:S(2)}, u32[]{:S(2)}) collective-permute-start(bf16[1,512,512]{2,1,0:T(8,128)(2,1)} %get-tuple-element.168), channel_id=1, source_target_pairs={{0,16},{8,24},{16,0},{24,8},{1,17},{9,25},{17,1},{25,9},{2,18},{10... | collective-permute-start | bytes 1572872 | tf_op jit(solution)/shard_map/ppermute | solution.py:1116
  516.3 760.7 %collective-permute-start.7 = (bf16[1,512,512]{2,1,0:T(8,128)(2,1)}, bf16[1,512,512]{2,1,0:T(8,128)(2,1)}, u32[]{:S(2)}, u32[]{:S(2)}) collective-permute-start(bf16[1,512,512]{2,1,0:T(8,128)(2,1)} %get-tuple-element.167), channel_id=1, source_target_pairs={{0,24},{8,16},{16,8},{24,0},{1,25},{9,17},{17,9},{25,1},{2,26},{10... | collective-permute-start | bytes 1572872 | tf_op jit(solution)/shard_map/ppermute | solution.py:1116
  519.5 757.6 %collective-permute-start.8 = (bf16[1,512,512]{2,1,0:T(8,128)(2,1)}, bf16[1,512,512]{2,1,0:T(8,128)(2,1)}, u32[]{:S(2)}, u32[]{:S(2)}) collective-permute-start(bf16[1,512,512]{2,1,0:T(8,128)(2,1)} %get-tuple-element.166), channel_id=1, source_target_pairs={{0,8},{8,0},{16,24},{24,16},{1,9},{9,1},{17,25},{25,17},{2,10},{10... | collective-permute-start | bytes 1572872 | tf_op jit(solution)/shard_map/ppermute | solution.py:1116
  793.1 8.3 copy-start.19
  793.1 8.3 copy-start.24
  795.0 7.2 copy-start.13
  795.0 7.2 copy-start.14
  795.0 7.7 copy-start.11
  795.0 7.7 copy-start.12
  801.4 1.8 copy-start.16
  808.8 1.6 copy-start.4
  808.8 1.6 copy-start.6
  814.3 6.8 copy-start.8
  829.3 10.7 slice-start
  829.3 10.7 slice-start.1
  829.3 10.7 slice-start.2
  834.0 6.0 slice-start.3
  1250.1 21.7 %copy-start.21 = (f32[64,1024]{1,0:T(8,128)S(1)}, f32[64,1024]{1,0:T(8,128)}, u32[]{:S(2)}) copy-start(f32[64,1024]{1,0:T(8,128)} %get-tuple-element.118) | copy-start | bytes 786436
  1250.1 23.5 %copy-start.2 = (f32[128,2048]{1,0:T(8,128)S(1)}, f32[128,2048]{1,0:T(8,128)}, u32[]{:S(2)}) copy-start(f32[128,2048]{1,0:T(8,128)} %copy-done.1) | copy-start | bytes 3145732
  1250.1 25.6 %copy-start.17 = (f32[128,2048]{1,0:T(8,128)S(1)}, f32[128,2048]{1,0:T(8,128)}, u32[]{:S(2)}) copy-start(f32[128,2048]{1,0:T(8,128)} %get-tuple-element.205) | copy-start | bytes 3145732
  1250.1 25.5 %copy-start.22 = (f32[128]{0:T(128)S(1)}, f32[128]{0:T(128)}, u32[]{:S(2)}) copy-start(f32[128]{0:T(128)} %get-tuple-element.184) | copy-start | bytes 1540
  1277.1 3.7 copy-start.20

commit v8 on v7

--- a/solution.py
+++ b/solution.py
@@ -121,6 +121,14 @@
 
 
 def moves(pairs, stages, local):
+    if not stages:
+        copies = [
+            pltpu.make_async_copy(source, target, local.at[i, 0])
+            for i, (source, target) in enumerate(pairs)
+        ]
+        for copy in copies:
+            copy.start()
+        return [], copies
     bring = [
         pltpu.make_async_copy(source, stages[i], local.at[i, 0])
         for i, (source, target) in enumerate(pairs)
@@ -346,7 +354,7 @@
             dma((n,)),
             dma((4, n_dp)),
             dma((4, n_dp)),
-            dma((max(len(stages), 1), 2)),
+            dma((max(len(stages), 4), 2)),
             *[pltpu.VMEM(stage, jnp.bfloat16) for stage in stages],
         ],
         input_output_aliases=aliases,
@@ -645,7 +653,7 @@
             dma((len(kinds), 2)),
             dma((4, n_dp)),
             dma((4, n_dp)),
-            dma((max(len(stages), 1), 2)),
+            dma((max(len(stages), 4), 2)),
             *[pltpu.VMEM(stage, jnp.bfloat16) for stage in stages],
         ],
         input_output_aliases=aliases,
@@ -974,12 +982,17 @@
         target[...] = source[...].astype(jnp.float32)
 
 
-def widen(low, values):
+def widen(spans, values):
     number, rows, columns = values[0].shape
-    block = pl.BlockSpec((1, rows, columns), lambda e: (e + low, 0, 0))
+    (low, high), (again, end) = spans
+
+    def chosen(e):
+        return (jnp.where(e < high - low, e + low, e - (high - low) + again), 0, 0)
+
+    block = pl.BlockSpec((1, rows, columns), chosen)
     return pl.pallas_call(
         widen_kernel,
-        grid=(number - low,),
+        grid=(high - low + end - again,),
         in_specs=[block] * len(values),
         out_specs=[block] * len(values),
         out_shape=[jax.ShapeDtypeStruct(one.shape, jnp.float32) for one in values],
@@ -987,7 +1000,7 @@
     )(*values)
 
 
-def widen_pieces_kernel(n_pieces, offsets_ref, *refs):
+def widen_pieces_kernel(low, n_pieces, offsets_ref, *refs):
     pieces, refs = refs[:n_pieces], refs[n_pieces + 2 :]
     targets, wide, sems = refs[:2], refs[2], refs[3]
     part = wide.shape[4]
@@ -997,7 +1010,7 @@
         for n in range(2):
             wide[k, n] = piece[:, :, n * part : (n + 1) * part].astype(jnp.float32)
             copy = pltpu.make_async_copy(
-                wide.at[k, n], targets[n].at[pl.ds(0, piece.shape[0]), :, columns], sems.at[k, n]
+                wide.at[k, n], targets[n].at[pl.ds(low, piece.shape[0]), :, columns], sems.at[k, n]
             )
             copy.start()
             copies.append(copy)
@@ -1005,12 +1018,12 @@
         copy.wait()
 
 
-def widen_pieces(offsets, pieces, into):
+def widen_pieces(offsets, low, pieces, into):
     size, rows, columns = pieces[0].shape
     anywhere = pl.BlockSpec(memory_space=pl.ANY)
     count = len(pieces)
     return pl.pallas_call(
-        functools.partial(widen_pieces_kernel, count),
+        functools.partial(widen_pieces_kernel, low, count),
         in_specs=[
             pl.BlockSpec(memory_space=pltpu.SMEM),
             *[pl.BlockSpec(memory_space=pltpu.VMEM)] * count,
@@ -1078,7 +1091,8 @@
     beside = early + number // 8
     late = number - number // 4
     back_beside = number // 8
-    back_third = back_beside + number * 3 // 8
+    back_third = back_beside + number // 4
+    back_late = back_third + number // 4
     me = lax.axis_index("dp")
     cut_shape = jax.ShapeDtypeStruct((number, n_dp * depth, part), bf16)
 
@@ -1290,6 +1304,15 @@
 
         return [pair(0), pair(1)]
 
+    def cut_grads(low, high, ins, outs):
+        to, unused = partners(lax.axis_index("dp"), n_dp)
+        pairs = []
+        for k, piece in enumerate(outs, 1):
+            for n in range(2):
+                source = ins[n].at[pl.ds(low, high - low), rows_at(to(k))]
+                pairs.append((source, piece.at[:, :, pl.ds(n * part, part)]))
+        return pairs
+
     pieces = []
     if back_beside:
         for k in range(1, n_dp):
@@ -1308,113 +1331,123 @@
             pieces.append(piece)
         pieces = permuted(pieces)
     way_shapes = [jax.ShapeDtypeStruct((number, depth, ff), bf16)] * 2
-    (back,), (gate_third, up_third) = scatter_all(
+    piece_shape = jax.ShapeDtypeStruct((back_late - back_third, depth, 2 * part), bf16)
+    (back,), (gate_third, up_third, *later_pieces) = scatter_all(
         n_dp,
         n_expert,
         [part_back.reshape(n_dp, n_expert, count, D + width)],
         [gate_soon, up_soon],
-        way_shapes,
+        way_shapes + [piece_shape] * (n_dp - 1),
         lambda ins, outs: ways(back_beside, back_third, 0, ins, outs),
         8,
         (),
-        stages(*[back_third - back_beside] * 2),
+        stages(
+            *[back_third - back_beside] * 2, *[back_late - back_third] * (2 * (n_dp - 1))
+        ),
+        lambda ins, outs: cut_grads(back_third, back_late, ins, outs[2:]),
     )
-
-    grad_final = cotangent.astype(jnp.float32)
-    grad_mlp = back[:, :D]
-    grad_router_probs = back[:, D : D + experts_all] + back[:, D + experts_all :]
-    grad_logits = router * (
-        grad_router_probs - jnp.sum(router * grad_router_probs, axis=1, keepdims=True)
-    )
-    grad_logits_low = grad_logits.astype(bf16)
-    grad_router_full = product(mlp_low, grad_logits_low, "td,te->de")
-    grad_mlp = grad_mlp + product(grad_logits_low, router_weight, "te,de->td")
-    grad_middle_part, grad_mlp_gain = rms_backward(middle, mlp_inverse, mlp_gain, grad_mlp)
-    grad_middle = grad_final + grad_middle_part
-    grad_branch_low = grad_middle.astype(bf16)
-    grad_out_full = product(attended_low, grad_branch_low, "td,te->de")
-    grad_attended = (
-        product(grad_branch_low, out_weight, "te,de->td").astype(bf16).reshape(count, HEADS, HD)
-    )
-    grad_weights = product(grad_attended, value_heads, "qhd,khd->hqk")
-    grad_scores = probs * (grad_weights - jnp.sum(probs * grad_weights, axis=-1, keepdims=True))
-    grad_scores_low = grad_scores.astype(bf16)
-    grad_query_turn = product(grad_scores_low, key_low, "hqk,khd->qhd").reshape(count, D) * scale
-    grad_key_turn = product(grad_scores_low, query_low, "hqk,qhd->khd").reshape(count, D) * scale
-    grad_value_low = (
-        product(probs_low, grad_attended, "hqk,qhd->khd").reshape(count, D).astype(bf16)
-    )
-    grad_query_raw, grad_query_gain = rms_backward(
-        query_raw, query_inverse, query_gain, rotate(grad_query_turn, cosine, -sine)
-    )
-    grad_key_raw, grad_key_gain = rms_backward(
-        key_raw, key_inverse, key_gain, rotate(grad_key_turn, cosine, -sine)
-    )
-    grad_query_low = grad_query_raw.astype(bf16)
-    grad_key_low = grad_key_raw.astype(bf16)
-    grad_query_full = product(normed_low, grad_query_low, "td,te->de")
-    grad_key_full = product(normed_low, grad_key_low, "td,te->de")
-    grad_value_full = product(normed_low, grad_value_low, "td,te->de")
-    grad_normed = (
-        product(grad_query_low, query_weight, "te,de->td")
-        + product(grad_key_low, key_weight, "te,de->td")
-        + product(grad_value_low, value_weight, "te,de->td")
-    )
-    grad_inputs_part, grad_attn_gain = rms_backward(inputs, attn_inverse, attn_gain, grad_normed)
-    grad_inputs = grad_middle + grad_inputs_part
-
-    small_grads = jnp.concatenate(
-        [
-            grad_router_full,
-            grad_attn_gain[:, None],
-            grad_query_gain[:, None],
-            grad_key_gain[:, None],
-            grad_mlp_gain[:, None],
-            jnp.zeros((D, width - experts_all - 4), jnp.float32),
-        ],
-        axis=1,
-    )
+    later_pieces = permuted(later_pieces)
+
+    def attention_back(back):
+        grad_final = cotangent.astype(jnp.float32)
+        grad_mlp = back[:, :D]
+        grad_router_probs = back[:, D : D + experts_all] + back[:, D + experts_all :]
+        grad_logits = router * (
+            grad_router_probs - jnp.sum(router * grad_router_probs, axis=1, keepdims=True)
+        )
+        grad_logits_low = grad_logits.astype(bf16)
+        grad_router_full = product(mlp_low, grad_logits_low, "td,te->de")
+        grad_mlp = grad_mlp + product(grad_logits_low, router_weight, "te,de->td")
+        grad_middle_part, grad_mlp_gain = rms_backward(middle, mlp_inverse, mlp_gain, grad_mlp)
+        grad_middle = grad_final + grad_middle_part
+        grad_branch_low = grad_middle.astype(bf16)
+        grad_out_full = product(attended_low, grad_branch_low, "td,te->de")
+        grad_attended = (
+            product(grad_branch_low, out_weight, "te,de->td").astype(bf16).reshape(count, HEADS, HD)
+        )
+        grad_weights = product(grad_attended, value_heads, "qhd,khd->hqk")
+        grad_scores = probs * (grad_weights - jnp.sum(probs * grad_weights, axis=-1, keepdims=True))
+        grad_scores_low = grad_scores.astype(bf16)
+        grad_query_turn = product(grad_scores_low, key_low, "hqk,khd->qhd").reshape(count, D) * scale
+        grad_key_turn = product(grad_scores_low, query_low, "hqk,qhd->khd").reshape(count, D) * scale
+        grad_value_low = (
+            product(probs_low, grad_attended, "hqk,qhd->khd").reshape(count, D).astype(bf16)
+        )
+        grad_query_raw, grad_query_gain = rms_backward(
+            query_raw, query_inverse, query_gain, rotate(grad_query_turn, cosine, -sine)
+        )
+        grad_key_raw, grad_key_gain = rms_backward(
+            key_raw, key_inverse, key_gain, rotate(grad_key_turn, cosine, -sine)
+        )
+        grad_query_low = grad_query_raw.astype(bf16)
+        grad_key_low = grad_key_raw.astype(bf16)
+        grad_query_full = product(normed_low, grad_query_low, "td,te->de")
+        grad_key_full = product(normed_low, grad_key_low, "td,te->de")
+        grad_value_full = product(normed_low, grad_value_low, "td,te->de")
+        grad_normed = (
+            product(grad_query_low, query_weight, "te,de->td")
+            + product(grad_key_low, key_weight, "te,de->td")
+            + product(grad_value_low, value_weight, "te,de->td")
+        )
+        grad_inputs_part, grad_attn_gain = rms_backward(inputs, attn_inverse, attn_gain, grad_normed)
+        grad_inputs = grad_middle + grad_inputs_part
+
+        small_grads = jnp.concatenate(
+            [
+                grad_router_full,
+                grad_attn_gain[:, None],
+                grad_query_gain[:, None],
+                grad_key_gain[:, None],
+                grad_mlp_gain[:, None],
+                jnp.zeros((D, width - experts_all - 4), jnp.float32),
+            ],
+            axis=1,
+        )
+        grads = (grad_out_full, grad_value_full, grad_key_full, grad_query_full, small_grads)
+        return grad_inputs, *[one.astype(bf16) for one in grads]
+
+    def unreached(back):
+        shapes = [(count, D)] + [(D, D)] * 4 + [(D, width)]
+        kinds = [jnp.float32] + [bf16] * 5
+        return tuple(jnp.zeros(shape, kind) for shape, kind in zip(shapes, kinds))
+
+    grad_inputs, *weight_grads = lax.cond(lengths[0, 0] > 0, attention_back, unreached, back)
 
     def blocks_of(value):
-        return value.astype(bf16).reshape(n_dp, n_expert, rows_each, -1)
+        return value.reshape(n_dp, n_expert, rows_each, -1)
 
     sums, (gate_back, up_back) = scatter_all(
         n_dp,
         n_expert,
-        [
-            blocks_of(value)
-            for value in (
-                grad_out_full,
-                grad_value_full,
-                grad_key_full,
-                grad_query_full,
-                small_grads,
-            )
-        ]
+        [blocks_of(value) for value in weight_grads]
         + [part_out.reshape(n_dp, n_expert, count, D)],
         [gate_third, up_third, gate_soon, up_soon, gate_rest, up_rest],
         way_shapes,
-        lambda ins, outs: ways(back_third, late, 0, ins[2:4], outs)
+        lambda ins, outs: ways(back_late, late, 0, ins[2:4], outs)
         + ways(0, number - late, late, ins[4:6], outs),
         16,
         ((0, 0), (1, 1)),
-        stages(*[late - back_third] * 2, *[number - late] * 2),
+        [],
     )
     grad_out_part, grad_value_part, grad_key_part, grad_query_part, small_part, summed = sums
     output = (middle + summed).astype(bf16)
     grad_router_part = small_part[:, :experts_all]
     gain_parts = [small_part[:, experts_all + i] for i in range(4)]
-    widened = widen(back_beside, [gate_back, up_back])
-    if back_beside:
-        own = jnp.concatenate(
-            [
-                lax.dynamic_slice_in_dim(one[:back_beside], me * depth, depth, 1)
-                for one in (gate_soon, up_soon)
-            ],
-            axis=2,
-        )
-        offsets = jnp.stack([from_plane(k) * part for k in range(n_dp)])
-        widened = widen_pieces(offsets, [own, *pieces], widened)
+    widened = widen([(back_beside, back_third), (back_late, number)], [gate_back, up_back])
+    offsets = jnp.stack([from_plane(k) * part for k in range(n_dp)])
+    for low, high, others in (
+        (0, back_beside, pieces),
+        (back_third, back_late, later_pieces),
+    ):
+        if high > low:
+            own = jnp.concatenate(
+                [
+                    lax.dynamic_slice_in_dim(one[low:high], me * depth, depth, 1)
+                    for one in (gate_soon, up_soon)
+                ],
+                axis=2,
+            )
+            widened = widen_pieces(offsets, low, [own, *others], widened)
     grad_gate_part, grad_up_part = widened
     return (
         output,

time: 1290 us -> 1180 us (0.915)
  Pallas kernels: 1100 us -> 945 us
  local copies, waits for them, and re-layouts: 65.3 us -> 80.7 us
    pallas_call x3 -> x2, Pallas kernels: 572 us -> 420 us  [scatter_call(): pl.pallas_call(functools.partial(scatter_kernel, n_dp, n_expert, n, len(c...]
    squeeze x0 -> x1, local copies, waits for them, and re-layouts: none -> 23.5 us  [shards(): weights_all[i]]
    slice x6 -> x4, local copies, waits for them, and re-layouts: 29.7 us -> 7.04 us  [shards(): one[low:high]]
  transfers between devices with their start and end apart: 9 -> 12, of which waited for: 0 -> 2; matrix products, arithmetic and copies ran while one was open for 13% -> 16% of each run, Pallas kernels for 55% -> 47%
where the time goes in v8:
time: 1180 us; the launch traced here: 1170 us
  Pallas kernels  945 us (80%)
  matrix products  85.1 us (7%)
  local copies, waits for them, and re-layouts  80.7 us (7%)
  other arithmetic  32.9 us (3%)
  starting transfers between devices  16.1 us (1%)
    pallas_call x2, Pallas kernels, scatter_call(): pl.pallas_call(functools.partial(scatter_kernel, n_dp, n_expert, n, len(c...  420 us
    pallas_call x2, Pallas kernels, gather_call(): pl.pallas_call(functools.partial(gather_kernel, n_dp, n_expert, n, places...  386 us
    dot_general x21, matrix products, product(): return jnp.einsum(form, left, right, preferred_element_type=jnp.float32)  83.6 us
    pallas_call x2, Pallas kernels, expert_call(): pl.pallas_call(functools.partial(expert_kernel, steps, half, len(weights)...  79.3 us
    pallas_call x1, Pallas kernels, place_call(): pl.pallas_call(functools.partial(place_kernel, number), grid=(pairs,), in...  38.3 us
  transfers between devices with their start and end apart: 12, of which 2 were waited for; matrix products, arithmetic and copies ran while one was open for 16% of the time, Pallas kernels for 47%

profile of v8, /device:TPU:0, one launch (start us, length us, event | category | flops | bytes accessed | tf_op | source)
XLA Modules:
  0.0 1167.2 jit_solution(2467071345597151571)
XLA Ops:
  6.2 2.3 pad_maximum_fusion.2.refs_0_
  8.5 179.4 %shard_map.272 = (bf16[4,2048,2048]{2,1,0:T(8,128)(2,1)}, bf16[4096,256]{1,0:T(8,128)(2,1)}, bf16[8,2048,256]{2,1,0:T(8,128)(2,1)}, bf16[8,2048,256]{2,1,0:T(8,1...) custom-call(bf16[4,64,2048]{2,1,0:T(8,128)(2,1)} %pad_maximum_fusion, ...), custom_call_target="tpu_custom_call" | custom-call | tf_op jit(solution)/shard_map/pallas_call | solution.py:330
  188.1 3.4 collective-permute-start.2
  193.0 3.0 slice_reduce_fusion.4
  196.4 4.9 multiply_reduce_fusion.10
  201.3 6.0 multiply_reduce_fusion.9
  207.4 5.4 convolution_convert_fusion.7
  212.8 2.4 slice.117
  215.2 23.5 %slice_bitcast_fusion.3 = (bf16[2048,2048]{1,0:T(8,128)(2,1)}, bf16[2048,2048]{1,0:T(8,128)(2,1)}, bf16[2048,2048]{1,0:T(8,128)(2,1)}, bf16[2048,2048]{1,0:T(8,128)(2,1)}) fusion(bf16[4,2048,2048]{2,1,0:T(8,128)(2,1)} %get-tuple-element.176), kind=kLoop, calls=%fused_computation.74 | loop fusion | bytes 67108864 | tf_op jit(solution)/shard_map/squeeze | solution.py:1181
  239.2 1.3 fusion.40
  240.7 1.6 fusion.41
  243.0 3.2 subtract_convert_fusion.2
  246.9 1.5 fusion.42
  248.4 2.4 fusion.39
  250.8 1.6 convolution_convert_fusion.8
  252.4 4.9 multiply_reduce_fusion.8
  257.4 1.6 constant_dynamic-slice_fusion.4
  262.1 206.8 %shard_map.273 = (bf16[4096,2048]{1,0:T(8,128)(2,1)}, bf16[4096,2048]{1,0:T(8,128)(2,1)}, bf16[8,2048,256]{2,1,0:T(8,128)(2,1)}, bf16[8,2048,256]{2,1,0:T(8,128)...) custom-call(bf16[128,2048]{1,0:T(8,128)(2,1)S(1)} %multiply_convert_, ...), custom_call_target="tpu_custom_call", output_to_operand_aliasing={{2}: (4, {}), {3}: (5, {})} | custom-call | tf_op jit(solution)/shard_map/pallas_call | solution.py:330
  468.9 2.7 collective-permute-start.3
  471.6 2.2 collective-permute-start.4
  474.2 55.8 %shard_map.274 = (bf16[8,768,2048]{2,1,0:T(8,128)(2,1)}, bf16[8,768,2048]{2,1,0:T(8,128)(2,1)}, bf16[8,768,128]{2,1,0:T(8,128)(2,1)}, bf16[6,2048,256]{2,1,0:T(8...) custom-call(s32[1]{0:T(128)} %bitcast.62.names_ref, ...), custom_call_target="tpu_custom_call" | custom-call | tf_op jit(solution)/shard_map/pallas_call | solution.py:910
  530.0 2.5 dynamic-slice_bitcast_fusion
  532.6 1.6 collective-permute-start.10
  538.7 1.7 slice.126
  544.2 2.3 slice.127
  546.5 4.9 collective-permute-done.5.refs_3_
  551.4 23.5 %shard_map.275 = (bf16[8,768,2048]{2,1,0:T(8,128)(2,1)}, bf16[8,768,2048]{2,1,0:T(8,128)(2,1)}, bf16[8,768,128]{2,1,0:T(8,128)(2,1)}, bf16[2,2048,256]{2,1,0:T(8...) custom-call(s32[5]{0:T(128)} %stack.58.names_ref, ...), custom_call_target="tpu_custom_call", output_to_operand_aliasing={{0}: (9, {}), {1}: (10, {}), {2}: (11, {}), {5}: (12, {})} | custom-call | tf_op jit(solution)/shard_map/pallas_call | solution.py:910
  574.9 38.3 %shard_map.276 = (bf16[4096,2048]{1,0:T(8,128)(2,1)}, bf16[4096,2176]{1,0:T(8,128)(2,1)}) custom-call(s32[16,8,256]{2,1,0:T(8,128)} %select_bitcast_fusion.refs_6_.slots_ref, bf16[8,768,2048]{2,1,0:T(8,128)(2,1)} %get-tuple-element.204.y_ref, bf16[8,768,2048]{2,1,0:T(8,128)(2,1)} %get-tuple-element.205.dx_ref, bf16[8,768,128]{2,1,0:T(8,128)(2,1)} %get-tuple-element.206.probs_ref), custom_call_target="tpu_custom_call" | custom-call | tf_op jit(solution)/shard_map/pallas_call | solution.py:958
  613.2 156.4 %shard_map.277 = (f32[128,2176]{1,0:T(8,128)}, bf16[8,512,1024]{2,1,0:T(8,128)(2,1)}, bf16[8,512,1024]{2,1,0:T(8,128)(2,1)}, bf16[2,512,512]{2,1,0:T(8,128)(2,1)...) custom-call(bf16[4,8,128,2176]{3,2,1,0:T(8,128)(2,1)} %bitcast.188, ...), custom_call_target="tpu_custom_call" | custom-call | tf_op jit(solution)/shard_map/pallas_call | solution.py:632
  770.3 3.0 collective-permute-start.7
  774.3 1.7 slice.125
  777.0 2.1 pad_maximum_fusion.3.refs_0_
  779.1 97.6 %conditional.1 = (f32[128,2048]{1,0:T(8,128)}, bf16[4,8,64,2048]{3,2,1,0:T(8,128)(2,1)}, bf16[4,8,64,2048]{3,2,1,0:T(8,128)(2,1)}, bf16[4,8,64,2048]{3,2,1,0:T(8...) conditional(s32[]{:T(128)} %bitcast.49, () %tuple.28, ...), branch_computations={%region_12.13_spmd, %region_13.24_spmd} | conditional | flops 8961121280 | bytes 184194992 | solution.py:1414
  780.8 1.9 multiply_reduce_fusion
  782.7 1.4 subtract_add_fusion.1
  784.1 7.1 convolution_convert_fusion.4
  791.2 1.3 copy.146
  792.5 1.9 multiply_reduce_fusion.5
  794.4 1.4 multiply_convert_fusion
  795.8 1.5 fusion.1
  797.4 1.4 fusion.2
  801.6 2.5 copy.123
  804.1 2.6 copy.126
  806.7 1.6 copy.125
  808.2 1.6 copy.122
  809.8 2.8 fusion.4
  812.7 2.0 subtract_convert_fusion
  814.7 2.1 subtract_convert_fusion.1
  817.6 6.5 fusion.44
  824.1 3.8 convolution_add_fusion.2
  829.3 1.6 copy.128
  830.8 8.0 multiply_reduce_fusion.1
  840.2 1.3 concatenate.33
  841.5 1.9 constant_dynamic-update-slice_fusion.4
  846.8 3.0 copy.140
  849.8 6.8 convolution_convert_fusion.2
  856.7 7.3 convolution_convert_fusion.1
  864.0 1.3 subtract_add_fusion
  865.3 5.6 convolution_convert_fusion.3
  870.9 5.6 convolution_convert_fusion
  876.6 263.8 %shard_map.278 = (f32[64,2048]{1,0:T(8,128)}, f32[64,2048]{1,0:T(8,128)}, f32[64,2048]{1,0:T(8,128)}, f32[64,2048]{1,0:T(8,128)}, f32[64,128]{1,0:T(8,128)}, /*i...) custom-call(bf16[4,8,64,2048]{3,2,1,0:T(8,128)(2,1)} %get-tuple-elem, ...), custom_call_target="tpu_custom_call", output_to_operand_aliasing={{6}: (6, {}), {7}: (7, {})} | custom-call | tf_op jit(solution)/shard_map/pallas_call | solution.py:632
  1140.4 11.5 shard_map.279
  1152.0 3.7 shard_map.280
  1157.4 5.8 shard_map.281
  (172 shorter events, 40.8 us)
Async XLA Ops:
  187.9 8.1 copy-start.10
  187.9 74.2 %collective-permute-start = (bf16[1,512,512]{2,1,0:T(8,128)(2,1)}, bf16[1,512,512]{2,1,0:T(8,128)(2,1)}, u32[]{:S(2)}, u32[]{:S(2)}) collective-permute-start(bf16[1,512,512]{2,1,0:T(8,128)(2,1)} %get-tuple-element.181), channel_id=1, source_target_pairs={{0,16},{8,24},{16,0},{24,8},{1,17},{9,25},{17,1},{25,9},{2,18},{10... | collective-permute-start | bytes 1572872 | tf_op jit(solution)/shard_map/ppermute | solution.py:1130
  188.0 74.1 %collective-permute-start.1 = (bf16[1,512,512]{2,1,0:T(8,128)(2,1)}, bf16[1,512,512]{2,1,0:T(8,128)(2,1)}, u32[]{:S(2)}, u32[]{:S(2)}) collective-permute-start(bf16[1,512,512]{2,1,0:T(8,128)(2,1)} %get-tuple-element.182), channel_id=1, source_target_pairs={{0,24},{8,16},{16,8},{24,0},{1,25},{9,17},{17,9},{25,1},{2,26},{10... | collective-permute-start | bytes 1572872 | tf_op jit(solution)/shard_map/ppermute | solution.py:1130
  188.1 74.0 %collective-permute-start.2 = (bf16[1,512,512]{2,1,0:T(8,128)(2,1)}, bf16[1,512,512]{2,1,0:T(8,128)(2,1)}, u32[]{:S(2)}, u32[]{:S(2)}) collective-permute-start(bf16[1,512,512]{2,1,0:T(8,128)(2,1)} %get-tuple-element.183), channel_id=1, source_target_pairs={{0,8},{8,0},{16,24},{24,16},{1,9},{9,1},{17,25},{25,17},{2,10},{10... | collective-permute-start | bytes 1572872 | tf_op jit(solution)/shard_map/ppermute | solution.py:1130
  196.2 11.2 copy-start.29
  196.4 11.0 copy-start.3
  201.3 37.4 %copy-start.15 = (f32[128,2048]{1,0:T(8,128)}, f32[128,2048]{1,0:T(8,128)S(1)}, u32[]{:S(2)}) copy-start(f32[128,2048]{1,0:T(8,128)S(1)} %get-tuple-element.409) | copy-start | bytes 3145732
  215.2 23.6 %copy-start.16 = (f32[128,2048]{1,0:T(8,128)S(1)}, f32[128,2048]{1,0:T(8,128)}, u32[]{:S(2)}) copy-start(f32[128,2048]{1,0:T(8,128)} %get-tuple-element.407) | copy-start | bytes 3145732
  238.8 3.6 copy-start.31
  246.6 4.2 copy-start.21
  246.9 5.5 copy-start.22
  250.8 1.6 copy-start.8
  252.4 5.0 copy-start.18
  262.1 211.8 %copy-start.1 = (bf16[128,2048]{1,0:T(8,128)(2,1)}, bf16[128,2048]{1,0:T(8,128)(2,1)S(1)}, u32[]{:S(2)}) copy-start(bf16[128,2048]{1,0:T(8,128)(2,1)S(1)} %multiply_convert_fusion.2.refs_0_) | copy-start | bytes 1572868
  468.9 74.2 %collective-permute-start.3 = (bf16[2,512,512]{2,1,0:T(8,128)(2,1)}, bf16[2,512,512]{2,1,0:T(8,128)(2,1)}, u32[]{:S(2)}, u32[]{:S(2)}) collective-permute-start(bf16[2,512,512]{2,1,0:T(8,128)(2,1)} %get-tuple-element.195), channel_id=1, source_target_pairs={{0,16},{8,24},{16,0},{24,8},{1,17},{9,25},{17,1},{25,9},{2,18},{10... | collective-permute-start | bytes 3145736 | tf_op jit(solution)/shard_map/ppermute | solution.py:1130
  471.6 74.9 %collective-permute-start.4 = (bf16[2,512,512]{2,1,0:T(8,128)(2,1)}, bf16[2,512,512]{2,1,0:T(8,128)(2,1)}, u32[]{:S(2)}, u32[]{:S(2)}) collective-permute-start(bf16[2,512,512]{2,1,0:T(8,128)(2,1)} %get-tuple-element.196), channel_id=1, source_target_pairs={{0,24},{8,16},{16,8},{24,0},{1,25},{9,17},{17,9},{25,1},{2,26},{10... | collective-permute-start | bytes 3145736 | tf_op jit(solution)/shard_map/ppermute | solution.py:1130
  473.8 77.6 %collective-permute-start.5 = (bf16[2,512,512]{2,1,0:T(8,128)(2,1)}, bf16[2,512,512]{2,1,0:T(8,128)(2,1)}, u32[]{:S(2)}, u32[]{:S(2)}) collective-permute-start(bf16[2,512,512]{2,1,0:T(8,128)(2,1)} %get-tuple-element.197), channel_id=1, source_target_pairs={{0,8},{8,0},{16,24},{24,16},{1,9},{9,1},{17,25},{25,17},{2,10},{10... | collective-permute-start | bytes 3145736 | tf_op jit(solution)/shard_map/ppermute | solution.py:1130
  474.2 60.6 %copy-start.11 = (bf16[128,2048]{1,0:T(8,128)(2,1)S(1)}, bf16[128,2048]{1,0:T(8,128)(2,1)}, u32[]{:S(2)}) copy-start(bf16[128,2048]{1,0:T(8,128)(2,1)} %param.19) | copy-start | bytes 1572868
  474.2 61.6 %copy-start.20 = (bf16[128,2048]{1,0:T(8,128)(2,1)S(1)}, bf16[128,2048]{1,0:T(8,128)(2,1)}, u32[]{:S(2)}) copy-start(bf16[128,2048]{1,0:T(8,128)(2,1)} %convolution_convert_fusion.7) | copy-start | bytes 1572868
  532.6 240.8 %collective-permute-start.10 = (bf16[1,512,512]{2,1,0:T(8,128)(2,1)}, bf16[1,512,512]{2,1,0:T(8,128)(2,1)}, u32[]{:S(2)}, u32[]{:S(2)}) collective-permute-start(bf16[1,512,512]{2,1,0:T(8,128)(2,1)} %get-tuple-element.392), channel_id=1, source_target_pairs={{0,24},{8,16},{16,8},{24,0},{1,25},{9,17},{17,9},{25,1},{2,26},{10... | collective-permute-start | bytes 1572872 | tf_op jit(solution)/shard_map/ppermute | solution.py:1130
  540.5 611.5 %collective-permute-start.11 = (bf16[1,512,512]{2,1,0:T(8,128)(2,1)}, bf16[1,512,512]{2,1,0:T(8,128)(2,1)}, u32[]{:S(2)}, u32[]{:S(2)}) collective-permute-start(bf16[1,512,512]{2,1,0:T(8,128)(2,1)} %get-tuple-element.391), channel_id=1, source_target_pairs={{0,8},{8,0},{16,24},{24,16},{1,9},{9,1},{17,25},{25,17},{2,10},{10... | collective-permute-start | bytes 1572872 | tf_op jit(solution)/shard_map/ppermute | solution.py:1130
  543.0 608.9 %collective-permute-start.9 = (bf16[1,512,512]{2,1,0:T(8,128)(2,1)}, bf16[1,512,512]{2,1,0:T(8,128)(2,1)}, u32[]{:S(2)}, u32[]{:S(2)}) collective-permute-start(bf16[1,512,512]{2,1,0:T(8,128)(2,1)} %get-tuple-element.393), channel_id=1, source_target_pairs={{0,16},{8,24},{16,0},{24,8},{1,17},{9,25},{17,1},{25,9},{2,18},{10... | collective-permute-start | bytes 1572872 | tf_op jit(solution)/shard_map/ppermute | solution.py:1130
  769.6 9.5 copy-start.17
  769.6 9.5 copy-start.30
  769.6 387.7 %collective-permute-start.6 = (bf16[2,512,512]{2,1,0:T(8,128)(2,1)}, bf16[2,512,512]{2,1,0:T(8,128)(2,1)}, u32[]{:S(2)}, u32[]{:S(2)}) collective-permute-start(bf16[2,512,512]{2,1,0:T(8,128)(2,1)} %get-tuple-element.228), channel_id=1, source_target_pairs={{0,16},{8,24},{16,0},{24,8},{1,17},{9,25},{17,1},{25,9},{2,18},{10... | collective-permute-start | bytes 3145736 | tf_op jit(solution)/shard_map/ppermute | solution.py:1130
  770.3 387.0 %collective-permute-start.7 = (bf16[2,512,512]{2,1,0:T(8,128)(2,1)}, bf16[2,512,512]{2,1,0:T(8,128)(2,1)}, u32[]{:S(2)}, u32[]{:S(2)}) collective-permute-start(bf16[2,512,512]{2,1,0:T(8,128)(2,1)} %get-tuple-element.229), channel_id=1, source_target_pairs={{0,24},{8,16},{16,8},{24,0},{1,25},{9,17},{17,9},{25,1},{2,26},{10... | collective-permute-start | bytes 3145736 | tf_op jit(solution)/shard_map/ppermute | solution.py:1130
  773.3 384.0 %collective-permute-start.8 = (bf16[2,512,512]{2,1,0:T(8,128)(2,1)}, bf16[2,512,512]{2,1,0:T(8,128)(2,1)}, u32[]{:S(2)}, u32[]{:S(2)}) collective-permute-start(bf16[2,512,512]{2,1,0:T(8,128)(2,1)} %get-tuple-element.230), channel_id=1, source_target_pairs={{0,8},{8,0},{16,24},{24,16},{1,9},{9,1},{17,25},{25,17},{2,10},{10... | collective-permute-start | bytes 3145736 | tf_op jit(solution)/shard_map/ppermute | solution.py:1130
  792.5 9.1 copy-start.12
  812.6 11.5 slice-start
  814.7 13.3 %copy-start.7 = (bf16[128,2048]{0,1:T(8,128)(2,1)}, bf16[128,2048]{0,1:T(8,128)(2,1)S(1)}, u32[]{:S(2)}) copy-start(bf16[128,2048]{0,1:T(8,128)(2,1)S(1)} %subtract_convert_fusion) | copy-start | bytes 1572868 | tf_op jit(solution)/shard_map/cond
  816.8 0.8 copy-start.6
  817.6 6.5 slice-start.1
  817.6 10.4 copy-start.9
  817.6 10.4 copy-start.13
  828.0 11.0 copy-start.2
  840.2 16.5 %copy-start.4 = (bf16[128,2048]{1,0:T(8,128)(2,1)S(1)}, bf16[128,2048]{1,0:T(8,128)(2,1)}, u32[]{:S(2)}) copy-start(bf16[128,2048]{1,0:T(8,128)(2,1)} %get-tuple-element.93) | copy-start | bytes 1572868 | tf_op jit(solution)/shard_map/cond
  856.7 7.3 copy-start
  856.7 7.3 copy-start.14
  856.7 8.6 copy-start.5
  864.0 6.9 copy-start.19
  1151.9 3.7 copy-start.24
  1151.9 4.5 copy-start.23
  1157.4 5.8 copy-start.28
  1157.4 6.6 copy-start.27
  1157.4 7.4 copy-start.26
  1157.4 8.2 copy-start.25

commit v9 on v8

--- a/solution.py
+++ b/solution.py
@@ -365,7 +365,7 @@
 
 
 def scatter_kernel(
-    n_dp, n_expert, n_items, n_cut, n_out, cuts, puts, rings, n_rings, *refs
+    n_dp, n_expert, n_items, n_cut, n_out, cuts, puts, middle, rings, n_rings, *refs
 ):
     z, j, chip, core = place_of()
     chips = n_expert // 2
@@ -530,6 +530,7 @@
     for one, other in zip(bring, put):
         one.wait()
         other.start()
+    middle(cut_in, cut_out)
     if square:
         for i in range(n_items):
             send_over(i, 2, high).wait_recv()
@@ -617,7 +618,17 @@
 
 
 def scatter_call(
-    n_dp, n_expert, items, cut_in, cut_shapes, cuts, number, aliases, stages, puts=nothing
+    n_dp,
+    n_expert,
+    items,
+    cut_in,
+    cut_shapes,
+    cuts,
+    number,
+    aliases,
+    stages,
+    puts=nothing,
+    middle=nothing,
 ):
     chips = n_expert // 2
     square = chips == 4
@@ -631,7 +642,17 @@
     heard = 2 if square else chips - 1
     return pl.pallas_call(
         functools.partial(
-            scatter_kernel, n_dp, n_expert, n, len(cut_in), m, cuts, puts, rings, len(kinds)
+            scatter_kernel,
+            n_dp,
+            n_expert,
+            n,
+            len(cut_in),
+            m,
+            cuts,
+            puts,
+            middle,
+            rings,
+            len(kinds),
         ),
         out_shape=[*[jax.ShapeDtypeStruct(block, jnp.float32) for block in blocks], *cut_shapes],
         in_specs=[anywhere] * (n + len(cut_in)),
@@ -664,7 +685,17 @@
 
 
 def scatter_all(
-    n_dp, n_expert, items, cut_in, cut_shapes, cuts, number, aliases, stages, puts=nothing
+    n_dp,
+    n_expert,
+    items,
+    cut_in,
+    cut_shapes,
+    cuts,
+    number,
+    aliases,
+    stages,
+    puts=nothing,
+    middle=nothing,
 ):
     chips = n_expert // 2
     blocks = (2 * chips - 1 if chips != 4 else 7) * n_dp + n_dp + 3
@@ -691,6 +722,7 @@
             {len(used) + a: len(used) + b for a, b in aliases} if first else {},
             stages if first else [],
             puts if first else nothing,
+            middle if first else nothing,
         )
         for i, out in zip(used, outs):
             results[i].append(out)
@@ -838,18 +870,38 @@
                 pack_ref[plane, 0, :, part:] = dup_ref[0, here, :]
 
 
-def place_kernel(number, slots_ref, y_ref, dx_ref, probs_ref, out_ref, back_ref):
+def put_back(number, slots_ref, pairs):
     pick = jnp.concatenate(picks(slots_ref, number), axis=0).astype(jnp.bfloat16)
-    width = out_ref.shape[1]
     piece = 512
-    flat = number * 2 * CAP
-    for at in range(0, width, piece):
-        part = y_ref[:, :, at : at + piece].reshape(flat, piece)
-        out_ref[:, at : at + piece] = dot(pick, part, (0, 0)).astype(jnp.bfloat16)
-        part = dx_ref[:, :, at : at + piece].reshape(flat, piece)
-        back_ref[:, at : at + piece] = dot(pick, part, (0, 0)).astype(jnp.bfloat16)
-    part = probs_ref[...].reshape(flat, 128)
-    back_ref[:, width:] = dot(pick, part, (0, 0)).astype(jnp.bfloat16)
+    for source, target, first in pairs:
+        width = source.shape[2]
+        for at in range(0, width, piece):
+            size = min(piece, width)
+            part = source[:, :, at : at + size].reshape(-1, size)
+            target[:, first + at : first + at + size] = dot(pick, part, (0, 0)).astype(
+                jnp.bfloat16
+            )
+
+
+def place_back_kernel(number, slots_ref, dx_ref, probs_ref, back_ref):
+    put_back(number, slots_ref, [(dx_ref, back_ref, 0), (probs_ref, back_ref, dx_ref.shape[2])])
+
+
+def place_out_kernel(number, slots_ref, y_ref, out_ref):
+    put_back(number, slots_ref, [(y_ref, out_ref, 0)])
+
+
+def place_out(slots, y, out):
+    pairs, number, pair = slots.shape
+    pltpu.emit_pipeline(
+        functools.partial(place_out_kernel, number),
+        grid=(pairs,),
+        in_specs=[
+            pl.BlockSpec((1, number, pair), lambda p: (p, 0, 0)),
+            pl.BlockSpec((number, 2 * CAP, D), lambda p: (0, p, 0)),
+        ],
+        out_specs=[pl.BlockSpec((pair, D), lambda p: (p, 0))],
+    )(slots, y, out)
 
 
 def pick_shapes(number, pairs):
@@ -950,30 +1002,21 @@
     )(names, rows, grows, gates, *weights, down, *into)
 
 
-def place_call(number, slots, y, dx, probs):
-    pairs, _, pair = slots.shape
-    bf16 = jnp.bfloat16
+def place_back(slots, dx, probs):
+    pairs, number, pair = slots.shape
     size = 2 * CAP
-    rows = pl.BlockSpec((number, size, D), lambda p: (0, p, 0))
+
+    def rows(one):
+        return pl.BlockSpec((number, size, one.shape[2]), lambda p: (0, p, 0))
+
     return pl.pallas_call(
-        functools.partial(place_kernel, number),
+        functools.partial(place_back_kernel, number),
         grid=(pairs,),
-        in_specs=[
-            pl.BlockSpec((1, number, pair), lambda p: (p, 0, 0)),
-            rows,
-            rows,
-            pl.BlockSpec((number, size, 128), lambda p: (0, p, 0)),
-        ],
-        out_specs=[
-            pl.BlockSpec((pair, D), lambda p: (p, 0)),
-            pl.BlockSpec((pair, D + 128), lambda p: (p, 0)),
-        ],
-        out_shape=[
-            jax.ShapeDtypeStruct((pairs * pair, D), bf16),
-            jax.ShapeDtypeStruct((pairs * pair, D + 128), bf16),
-        ],
+        in_specs=[pl.BlockSpec((1, number, pair), lambda p: (p, 0, 0)), rows(dx), rows(probs)],
+        out_specs=pl.BlockSpec((pair, D + 128), lambda p: (p, 0)),
+        out_shape=jax.ShapeDtypeStruct((pairs * pair, D + 128), jnp.bfloat16),
         compiler_params=pltpu.CompilerParams(vmem_limit_bytes=BIG),
-    )(slots, y, dx, probs)
+    )(slots, dx, probs)
 
 
 def widen_kernel(*refs):
@@ -1091,7 +1134,7 @@
     beside = early + number // 8
     late = number - number // 4
     back_beside = number // 8
-    back_third = back_beside + number // 4
+    back_third = back_beside + max(number // 8, 1)
     back_late = back_third + number // 4
     me = lax.axis_index("dp")
     cut_shape = jax.ShapeDtypeStruct((number, n_dp * depth, part), bf16)
@@ -1293,7 +1336,7 @@
         w_down,
         [*outs, down_soon],
     )
-    part_out, part_back = place_call(number, slots, weighted, grad_rows, grad_gates)
+    part_back = place_back(slots, grad_rows, grad_gates)
 
     def ways(low, high, at, ins, outs):
         def pair(n):
@@ -1329,26 +1372,34 @@
                     axis=2,
                 )
             pieces.append(piece)
-        pieces = permuted(pieces)
+        ahead = lax.optimization_barrier((*pieces, *late_pieces[1:]))
+        pieces = permuted(ahead[: n_dp - 1])
+        part_back, *pieces = lax.optimization_barrier((part_back, *pieces))
     way_shapes = [jax.ShapeDtypeStruct((number, depth, ff), bf16)] * 2
     piece_shape = jax.ShapeDtypeStruct((back_late - back_third, depth, 2 * part), bf16)
-    (back,), (gate_third, up_third, *later_pieces) = scatter_all(
+    (back,), (gate_third, up_third, part_out, *later_pieces) = scatter_all(
         n_dp,
         n_expert,
         [part_back.reshape(n_dp, n_expert, count, D + width)],
-        [gate_soon, up_soon],
-        way_shapes + [piece_shape] * (n_dp - 1),
+        [gate_soon, up_soon, slots, weighted],
+        [
+            *way_shapes,
+            jax.ShapeDtypeStruct((groups * count, D), bf16),
+            *[piece_shape] * (n_dp - 1),
+        ],
         lambda ins, outs: ways(back_beside, back_third, 0, ins, outs),
         8,
         (),
         stages(
             *[back_third - back_beside] * 2, *[back_late - back_third] * (2 * (n_dp - 1))
         ),
-        lambda ins, outs: cut_grads(back_third, back_late, ins, outs[2:]),
+        lambda ins, outs: cut_grads(back_third, back_late, ins, outs[3:]),
+        lambda ins, outs: place_out(ins[2], ins[3], outs[2]),
     )
     later_pieces = permuted(later_pieces)
 
     def attention_back(back):
+        query_weight, key_weight, value_weight, out_weight = (weights_all[i] for i in range(4))
         grad_final = cotangent.astype(jnp.float32)
         grad_mlp = back[:, :D]
         grad_router_probs = back[:, D : D + experts_all] + back[:, D + experts_all :]

time: 1180 us -> 1150 us (0.975)
  Pallas kernels: 945 us -> 901 us
  local copies, waits for them, and re-layouts: 80.7 us -> 59.1 us
  starting transfers between devices: 16.1 us -> 36.9 us
    pallas_call x2, Pallas kernels: 420 us -> 391 us  [scatter_call(): pl.pallas_call(functools.partial(scatter_kernel, n_dp, n_expert, n, len(c...]
    squeeze x1 -> x0, local copies, waits for them, and re-layouts: 23.5 us -> none  [shards(): weights_all[i]]
    ppermute x12, starting transfers between devices: 16.1 us -> 36.9 us  [permuted(): got.append(lax.ppermute(piece, 'dp', paths))]
    pallas_call x1, Pallas kernels: 38.3 us -> 23.5 us  [place_back(): pl.pallas_call(functools.partial(place_back_kernel, number), grid=(pairs,...]
  transfers between devices with their start and end apart: 12 -> 12, of which waited for: 2 -> 2; matrix products, arithmetic and copies ran while one was open for 16% -> 15% of each run, Pallas kernels for 47% -> 34%
where the time goes in v9:
time: 1150 us; the launch traced here: 1130 us
  Pallas kernels  901 us (78%)
  matrix products  88.2 us (8%)
  local copies, waits for them, and re-layouts  59.1 us (5%)
  other arithmetic  38.4 us (3%)
  starting transfers between devices  36.9 us (3%)
    pallas_call x2, Pallas kernels, scatter_call(): pl.pallas_call(functools.partial(scatter_kernel, n_dp, n_expert, n, len(c...  391 us
    pallas_call x2, Pallas kernels, gather_call(): pl.pallas_call(functools.partial(gather_kernel, n_dp, n_expert, n, places...  386 us
    dot_general x21, matrix products, product(): return jnp.einsum(form, left, right, preferred_element_type=jnp.float32)  86.7 us
    pallas_call x2, Pallas kernels, expert_call(): pl.pallas_call(functools.partial(expert_kernel, steps, half, len(weights)...  78.9 us
    ppermute x12, starting transfers between devices, permuted(): got.append(lax.ppermute(piece, 'dp', paths))  36.9 us
    pallas_call x1, Pallas kernels, place_back(): pl.pallas_call(functools.partial(place_back_kernel, number), grid=(pairs,...  23.5 us
  transfers between devices with their start and end apart: 12, of which 2 were waited for; matrix products, arithmetic and copies ran while one was open for 15% of the time, Pallas kernels for 34%

profile of v9, /device:TPU:0, one launch (start us, length us, event | category | flops | bytes accessed | tf_op | source)
XLA Modules:
  0.0 1134.0 jit_solution(13490823484688106326)
XLA Ops:
  6.2 2.3 pad_maximum_fusion.2.refs_0_
  8.5 179.4 %shard_map.272 = (bf16[4,2048,2048]{2,1,0:T(8,128)(2,1)}, bf16[4096,256]{1,0:T(8,128)(2,1)}, bf16[8,2048,256]{2,1,0:T(8,128)(2,1)}, bf16[8,2048,256]{2,1,0:T(8,1...) custom-call(bf16[4,64,2048]{2,1,0:T(8,128)(2,1)} %pad_maximum_fusion, ...), custom_call_target="tpu_custom_call" | custom-call | tf_op jit(solution)/shard_map/pallas_call | solution.py:330
  188.1 3.4 collective-permute-start.2
  193.0 3.0 slice_reduce_fusion.4
  196.4 4.9 multiply_reduce_fusion.10
  201.4 6.0 multiply_reduce_fusion.9
  207.4 5.4 fusion.53
  212.8 2.3 slice.140
  215.2 1.5 multiply_bitcast_fusion
  218.3 1.6 fusion.78
  220.7 3.2 subtract_convert_fusion.2
  224.5 1.5 fusion.79
  226.0 2.4 fusion.76
  228.4 1.6 convolution_bitcast_fusion
  230.8 5.1 multiply_reduce_fusion.8
  236.0 1.6 constant_dynamic-slice_fusion.4
  240.7 206.8 %shard_map.273 = (bf16[4096,2048]{1,0:T(8,128)(2,1)}, bf16[4096,2048]{1,0:T(8,128)(2,1)}, bf16[8,2048,256]{2,1,0:T(8,128)(2,1)}, bf16[8,2048,256]{2,1,0:T(8,128)...) custom-call(bf16[128,2048]{1,0:T(8,128)(2,1)S(1)} %multiply_convert_, ...), custom_call_target="tpu_custom_call", output_to_operand_aliasing={{2}: (4, {}), {3}: (5, {})} | custom-call | tf_op jit(solution)/shard_map/pallas_call | solution.py:330
  447.5 2.7 collective-permute-start.3
  450.2 2.2 collective-permute-start.4
  452.4 55.3 %shard_map.274 = (bf16[8,768,2048]{2,1,0:T(8,128)(2,1)}, bf16[8,768,2048]{2,1,0:T(8,128)(2,1)}, bf16[8,768,128]{2,1,0:T(8,128)(2,1)}, bf16[6,2048,256]{2,1,0:T(8...) custom-call(s32[1]{0:T(128)} %bitcast.56.names_ref, ...), custom_call_target="tpu_custom_call" | custom-call | tf_op jit(solution)/shard_map/pallas_call | solution.py:962
  507.7 2.5 dynamic-slice_bitcast_fusion
  510.3 7.2 collective-permute-done.3.refs_1_
  518.9 22.3 %collective-permute-start.6 = (bf16[1,512,512]{2,1,0:T(8,128)(2,1)}, bf16[1,512,512]{2,1,0:T(8,128)(2,1)}, u32[]{:S(2)}, u32[]{:S(2)}) collective-permute-start(bf16[1,512,512]{2,1,0:T(8,128)(2,1)} %get-tuple-element.319), channel_id=1, source_target_pairs={{0,16},{8,24},{16,0},{24,8},{1,17},{9,25},{17,1},{25,9},{2,18},{10... | collective-permute-start | bytes 1572872 | tf_op jit(solution)/shard_map/ppermute | solution.py:1173
  541.2 1.6 collective-permute-start.7
  547.8 1.7 slice.149
  549.5 2.3 slice.150
  552.6 23.6 %shard_map.275 = (bf16[8,768,2048]{2,1,0:T(8,128)(2,1)}, bf16[8,768,2048]{2,1,0:T(8,128)(2,1)}, bf16[8,768,128]{2,1,0:T(8,128)(2,1)}, bf16[2,2048,256]{2,1,0:T(8...) custom-call(s32[5]{0:T(128)} %stack.58.names_ref, ...), custom_call_target="tpu_custom_call", output_to_operand_aliasing={{0}: (9, {}), {1}: (10, {}), {2}: (11, {}), {5}: (12, {})} | custom-call | tf_op jit(solution)/shard_map/pallas_call | solution.py:962
  576.2 23.5 %shard_map.276 = bf16[4096,2176]{1,0:T(8,128)(2,1)} custom-call(s32[16,8,256]{2,1,0:T(8,128)} %select_bitcast_fusion.refs_6_.slots_ref.refs_3_, bf16[8,768,2048]{2,1,0:T(8,128)(2,1)} %get-tuple-element.316.dx_ref, bf16[8,768,128]{2,1,0:T(8,128)(2,1)} %get-tuple-element.317.probs_ref), custom_call_target="tpu_custom_call" | custom-call | tf_op jit(solution)/shard_map/pallas_call | solution.py:1012
  599.8 125.3 %shard_map.277 = (f32[128,2176]{1,0:T(8,128)}, bf16[8,512,1024]{2,1,0:T(8,128)(2,1)}, bf16[8,512,1024]{2,1,0:T(8,128)(2,1)}, bf16[4096,2048]{1,0:T(8,128)(2,1)},...) custom-call(bf16[4,8,128,2176]{3,2,1,0:T(8,128)(2,1)} %bitcast.189, ...), custom_call_target="tpu_custom_call" | custom-call | tf_op jit(solution)/shard_map/pallas_call | solution.py:643
  725.1 2.0 collective-permute-start.10
  727.2 2.4 collective-permute-start.9
  730.5 1.7 slice.148
  733.1 2.1 pad_maximum_fusion.3.refs_0_
  735.3 106.2 %conditional.1 = (f32[128,2048]{1,0:T(8,128)}, bf16[4,8,64,2048]{3,2,1,0:T(8,128)(2,1)}, bf16[4,8,64,2048]{3,2,1,0:T(8,128)(2,1)}, bf16[4,8,64,2048]{3,2,1,0:T(8...) conditional(s32[]{:T(128)} %bitcast.43, () %tuple.33, ...), branch_computations={%region_10.11_spmd, %region_11.24_spmd} | conditional | flops 8961171456 | bytes 162147504 | solution.py:1465
  737.5 1.9 multiply_reduce_fusion
  739.4 1.4 subtract_add_fusion.1
  740.8 7.1 fusion.18
  749.2 1.9 multiply_reduce_fusion.5
  751.0 1.4 multiply_convert_fusion
  752.5 1.6 fusion.22
  754.0 1.4 fusion.23
  758.0 2.5 copy.121
  760.5 1.6 copy.120
  762.0 2.2 fusion.27
  764.2 2.7 subtract_convert_fusion.1
  766.9 2.3 pad_maximum_fusion.1
  769.2 2.5 copy.124
  771.7 1.6 copy.123
  773.3 2.2 fusion.25
  775.5 1.9 subtract_convert_fusion
  778.2 6.3 fusion.2
  784.6 7.4 fusion.12
  793.2 1.6 copy.126
  794.8 8.1 multiply_reduce_fusion.1
  805.6 1.9 constant_dynamic-update-slice_fusion.4
  810.9 3.0 copy.136
  814.0 6.6 convolution_convert_fusion
  820.6 5.6 convolution_convert_fusion.1
  827.5 5.8 convolution_convert_fusion.2
  834.5 6.8 convolution_convert_fusion.3
  841.5 265.8 %shard_map.278 = (f32[64,2048]{1,0:T(8,128)}, f32[64,2048]{1,0:T(8,128)}, f32[64,2048]{1,0:T(8,128)}, f32[64,2048]{1,0:T(8,128)}, f32[64,128]{1,0:T(8,128)}, /*i...) custom-call(bf16[4,8,64,2048]{3,2,1,0:T(8,128)(2,1)} %get-tuple-elem, ...), custom_call_target="tpu_custom_call", output_to_operand_aliasing={{6}: (6, {}), {7}: (7, {})} | custom-call | tf_op jit(solution)/shard_map/pallas_call | solution.py:643
  1107.3 11.5 %shard_map.279 = (f32[8,512,1024]{2,1,0:T(8,128)}, f32[8,512,1024]{2,1,0:T(8,128)}) custom-call(bf16[8,512,1024]{2,1,0:T(8,128)(2,1)} %get-tuple-element.350.refs_0_, bf16[8,512,1024]{2,1,0:T(8,128)(2,1)} %get-tuple-element.351.refs_1_), custom_call_target="tpu_custom_call" | custom-call | tf_op jit(solution)/shard_map/pallas_call | solution.py:1036
  1118.8 3.7 shard_map.280
  1124.2 5.8 shard_map.281
  (165 shorter events, 45.5 us)
Async XLA Ops:
  187.9 8.1 copy-start.6
  187.9 52.8 %collective-permute-start = (bf16[1,512,512]{2,1,0:T(8,128)(2,1)}, bf16[1,512,512]{2,1,0:T(8,128)(2,1)}, u32[]{:S(2)}, u32[]{:S(2)}) collective-permute-start(bf16[1,512,512]{2,1,0:T(8,128)(2,1)} %get-tuple-element.293), channel_id=1, source_target_pairs={{0,16},{8,24},{16,0},{24,8},{1,17},{9,25},{17,1},{25,9},{2,18},{10... | collective-permute-start | bytes 1572872 | tf_op jit(solution)/shard_map/ppermute | solution.py:1173
  188.0 52.7 %collective-permute-start.1 = (bf16[1,512,512]{2,1,0:T(8,128)(2,1)}, bf16[1,512,512]{2,1,0:T(8,128)(2,1)}, u32[]{:S(2)}, u32[]{:S(2)}) collective-permute-start(bf16[1,512,512]{2,1,0:T(8,128)(2,1)} %get-tuple-element.294), channel_id=1, source_target_pairs={{0,24},{8,16},{16,8},{24,0},{1,25},{9,17},{17,9},{25,1},{2,26},{10... | collective-permute-start | bytes 1572872 | tf_op jit(solution)/shard_map/ppermute | solution.py:1173
  188.1 52.6 %collective-permute-start.2 = (bf16[1,512,512]{2,1,0:T(8,128)(2,1)}, bf16[1,512,512]{2,1,0:T(8,128)(2,1)}, u32[]{:S(2)}, u32[]{:S(2)}) collective-permute-start(bf16[1,512,512]{2,1,0:T(8,128)(2,1)} %get-tuple-element.295), channel_id=1, source_target_pairs={{0,8},{8,0},{16,24},{24,16},{1,9},{9,1},{17,25},{25,17},{2,10},{10... | collective-permute-start | bytes 1572872 | tf_op jit(solution)/shard_map/ppermute | solution.py:1173
  196.2 11.2 copy-start.29
  196.4 11.0 copy-start.2
  201.4 13.8 %copy-start.9 = (f32[128,2048]{1,0:T(8,128)}, f32[128,2048]{1,0:T(8,128)S(1)}, u32[]{:S(2)}) copy-start(f32[128,2048]{1,0:T(8,128)S(1)} %get-tuple-element.507) | copy-start | bytes 3145732
  215.1 4.8 copy-start.31
  224.2 11.7 %copy-start.20 = (bf16[128,16,128]{2,0,1:T(8,128)(2,1)}, bf16[128,16,128]{2,0,1:T(8,128)(2,1)S(1)}, u32[]{:S(2)}) copy-start(bf16[128,16,128]{2,0,1:T(8,128)(2,1)S(1)} %pad_maximum_fusion.5) | copy-start | bytes 1572868
  224.5 11.4 %copy-start.21 = (bf16[128,16,128]{2,0,1:T(8,128)(2,1)}, bf16[128,16,128]{2,0,1:T(8,128)(2,1)S(1)}, u32[]{:S(2)}) copy-start(bf16[128,16,128]{2,0,1:T(8,128)(2,1)S(1)} %pad_maximum_fusion.4) | copy-start | bytes 1572868
  228.4 1.6 copy-start.4
  230.0 0.8 copy-start.17
  240.7 305.4 %copy-start = (bf16[128,2048]{1,0:T(8,128)(2,1)}, bf16[128,2048]{1,0:T(8,128)(2,1)S(1)}, u32[]{:S(2)}) copy-start(bf16[128,2048]{1,0:T(8,128)(2,1)S(1)} %multiply_convert_fusion.2.refs_0_) | copy-start | bytes 1572868
  447.5 70.0 %collective-permute-start.3 = (bf16[2,512,512]{2,1,0:T(8,128)(2,1)}, bf16[2,512,512]{2,1,0:T(8,128)(2,1)}, u32[]{:S(2)}, u32[]{:S(2)}) collective-permute-start(bf16[2,512,512]{2,1,0:T(8,128)(2,1)} %get-tuple-element.307), channel_id=1, source_target_pairs={{0,16},{8,24},{16,0},{24,8},{1,17},{9,25},{17,1},{25,9},{2,18},{10... | collective-permute-start | bytes 3145736 | tf_op jit(solution)/shard_map/ppermute | solution.py:1173
  450.2 67.3 %collective-permute-start.4 = (bf16[2,512,512]{2,1,0:T(8,128)(2,1)}, bf16[2,512,512]{2,1,0:T(8,128)(2,1)}, u32[]{:S(2)}, u32[]{:S(2)}) collective-permute-start(bf16[2,512,512]{2,1,0:T(8,128)(2,1)} %get-tuple-element.308), channel_id=1, source_target_pairs={{0,24},{8,16},{16,8},{24,0},{1,25},{9,17},{17,9},{25,1},{2,26},{10... | collective-permute-start | bytes 3145736 | tf_op jit(solution)/shard_map/ppermute | solution.py:1173
  452.4 66.4 %collective-permute-start.5 = (bf16[2,512,512]{2,1,0:T(8,128)(2,1)}, bf16[2,512,512]{2,1,0:T(8,128)(2,1)}, u32[]{:S(2)}, u32[]{:S(2)}) collective-permute-start(bf16[2,512,512]{2,1,0:T(8,128)(2,1)} %get-tuple-element.309), channel_id=1, source_target_pairs={{0,8},{8,0},{16,24},{24,16},{1,9},{9,1},{17,25},{25,17},{2,10},{10... | collective-permute-start | bytes 3145736 | tf_op jit(solution)/shard_map/ppermute | solution.py:1173
  452.4 92.1 %copy-start.19 = (bf16[128,2048]{1,0:T(8,128)(2,1)S(1)}, bf16[128,2048]{1,0:T(8,128)(2,1)}, u32[]{:S(2)}) copy-start(bf16[128,2048]{1,0:T(8,128)(2,1)} %fusion.53) | copy-start | bytes 1572868
  518.9 80.9 %collective-permute-start.6 = (bf16[1,512,512]{2,1,0:T(8,128)(2,1)}, bf16[1,512,512]{2,1,0:T(8,128)(2,1)}, u32[]{:S(2)}, u32[]{:S(2)}) collective-permute-start(bf16[1,512,512]{2,1,0:T(8,128)(2,1)} %get-tuple-element.319), channel_id=1, source_target_pairs={{0,16},{8,24},{16,0},{24,8},{1,17},{9,25},{17,1},{25,9},{2,18},{10... | collective-permute-start | bytes 1572872 | tf_op jit(solution)/shard_map/ppermute | solution.py:1173
  541.2 58.5 %collective-permute-start.7 = (bf16[1,512,512]{2,1,0:T(8,128)(2,1)}, bf16[1,512,512]{2,1,0:T(8,128)(2,1)}, u32[]{:S(2)}, u32[]{:S(2)}) collective-permute-start(bf16[1,512,512]{2,1,0:T(8,128)(2,1)} %get-tuple-element.320), channel_id=1, source_target_pairs={{0,24},{8,16},{16,8},{24,0},{1,25},{9,17},{17,9},{25,1},{2,26},{10... | collective-permute-start | bytes 1572872 | tf_op jit(solution)/shard_map/ppermute | solution.py:1173
  542.8 56.9 %collective-permute-start.8 = (bf16[1,512,512]{2,1,0:T(8,128)(2,1)}, bf16[1,512,512]{2,1,0:T(8,128)(2,1)}, u32[]{:S(2)}, u32[]{:S(2)}) collective-permute-start(bf16[1,512,512]{2,1,0:T(8,128)(2,1)} %get-tuple-element.321), channel_id=1, source_target_pairs={{0,8},{8,0},{16,24},{24,16},{1,9},{9,1},{17,25},{25,17},{2,10},{10... | collective-permute-start | bytes 1572872 | tf_op jit(solution)/shard_map/ppermute | solution.py:1173
  725.1 10.2 copy-start.1
  725.1 10.2 copy-start.11
  725.1 10.2 copy-start.30
  725.1 399.1 %collective-permute-start.10 = (bf16[2,512,512]{2,1,0:T(8,128)(2,1)}, bf16[2,512,512]{2,1,0:T(8,128)(2,1)}, u32[]{:S(2)}, u32[]{:S(2)}) collective-permute-start(bf16[2,512,512]{2,1,0:T(8,128)(2,1)} %get-tuple-element.345), channel_id=1, source_target_pairs={{0,24},{8,16},{16,8},{24,0},{1,25},{9,17},{17,9},{25,1},{2,26},{10... | collective-permute-start | bytes 3145736 | tf_op jit(solution)/shard_map/ppermute | solution.py:1173
  727.1 397.0 %collective-permute-start.11 = (bf16[2,512,512]{2,1,0:T(8,128)(2,1)}, bf16[2,512,512]{2,1,0:T(8,128)(2,1)}, u32[]{:S(2)}, u32[]{:S(2)}) collective-permute-start(bf16[2,512,512]{2,1,0:T(8,128)(2,1)} %get-tuple-element.346), channel_id=1, source_target_pairs={{0,8},{8,0},{16,24},{24,16},{1,9},{9,1},{17,25},{25,17},{2,10},{10... | collective-permute-start | bytes 3145736 | tf_op jit(solution)/shard_map/ppermute | solution.py:1173
  727.2 397.0 %collective-permute-start.9 = (bf16[2,512,512]{2,1,0:T(8,128)(2,1)}, bf16[2,512,512]{2,1,0:T(8,128)(2,1)}, u32[]{:S(2)}, u32[]{:S(2)}) collective-permute-start(bf16[2,512,512]{2,1,0:T(8,128)(2,1)} %get-tuple-element.344), channel_id=1, source_target_pairs={{0,16},{8,24},{16,0},{24,8},{1,17},{9,25},{17,1},{25,9},{2,18},{10... | collective-permute-start | bytes 3145736 | tf_op jit(solution)/shard_map/ppermute | solution.py:1173
  749.2 11.3 copy-start.7
  773.3 11.3 copy-start.13
  777.4 0.8 copy-start.14
  784.5 7.4 copy-start.5
  784.5 7.4 copy-start.8
  794.8 19.2 %copy-start.3 = (bf16[128,2048]{1,0:T(8,128)(2,1)S(1)}, bf16[128,2048]{1,0:T(8,128)(2,1)}, u32[]{:S(2)}) copy-start(bf16[128,2048]{1,0:T(8,128)(2,1)} %get-tuple-element.199) | copy-start | bytes 1572868 | tf_op jit(solution)/shard_map/cond
  804.2 16.3 %copy-start.15 = (bf16[128,2048]{0,1:T(8,128)(2,1)S(1)}, bf16[128,2048]{0,1:T(8,128)(2,1)}, u32[]{:S(2)}) copy-start(bf16[128,2048]{0,1:T(8,128)(2,1)} %copy-done.14) | copy-start | bytes 1572868 | tf_op jit(solution)/shard_map/cond
  820.6 5.6 copy-start.10
  820.6 5.6 copy-start.22
  820.6 6.9 copy-start.12
  826.2 7.1 copy-start.18
  833.3 8.0 copy-start.16
  1118.8 3.7 copy-start.24
  1118.8 4.5 copy-start.23
  1124.2 5.8 copy-start.28
  1124.2 6.6 copy-start.27
  1124.2 7.4 copy-start.26
  1124.2 8.2 copy-start.25

commit v10 on v9

--- a/solution.py
+++ b/solution.py
@@ -365,8 +365,9 @@
 
 
 def scatter_kernel(
-    n_dp, n_expert, n_items, n_cut, n_out, cuts, puts, middle, rings, n_rings, *refs
+    n_dp, n_expert, n_arrays, items, n_cut, n_out, cuts, puts, middle, rings, n_rings, *refs
 ):
+    n_items = len(items)
     z, j, chip, core = place_of()
     chips = n_expert // 2
     square = chips == 4
@@ -378,7 +379,7 @@
         del refs[:count]
         return taken
 
-    sources, cut_in, targets, cut_out = take(n_items), take(n_cut), take(n_items), take(n_out)
+    sources, cut_in, targets, cut_out = take(n_arrays), take(n_cut), take(n_arrays), take(n_out)
     ring, got_a, got_b, got_c = take(n_rings), take(n_items), take(n_items), take(n_items)
     transit = take(n_items)
     (
@@ -405,9 +406,13 @@
     def chip_of(k):
         return to_chip(k) if k else chip
 
+    def source(i, column):
+        array, first, rows = items[i]
+        return sources[array].at[:, column, pl.ds(first, rows)]
+
     def to_mate(i, k):
         return remote(
-            sources[i].at[:, chip_of(k) * 2 + 1 - core],
+            source(i, chip_of(k) * 2 + 1 - core),
             got_a[i].at[k],
             send_a.at[i, k],
             recv_a.at[i, k],
@@ -423,7 +428,7 @@
 
     def load(i, k, at):
         return pltpu.make_async_copy(
-            sources[i].at[:, chip_of(k) * 2 + core], ring[rings[i]].at[at], local.at[rings[i], at]
+            source(i, chip_of(k) * 2 + core), ring[rings[i]].at[at], local.at[rings[i], at]
         )
 
     def send_near(i, k, part, number):
@@ -509,37 +514,39 @@
     for copy in bring:
         copy.start()
 
-    for n, (i, k, at) in enumerate(loads):
-        load(i, k, at).wait()
-        to_mate(i, k).wait_recv()
-        grow(i, k, 0, n_dp, lambda plane, rows: ring[rings[i]][at, plane, rows])
-        later = [one for one in loads[n + 1 :] if rings[one[0]] == rings[i]]
-        if len(later) >= 2:
-            load(*later[1]).start()
-        if not k:
-            continue
+    def over_cores(i):
+        for n, (item, k, at) in enumerate(loads):
+            if item != i:
+                continue
+            load(i, k, at).wait()
+            to_mate(i, k).wait_recv()
+            grow(i, k, 0, n_dp, lambda plane, rows: ring[rings[i]][at, plane, rows])
+            later = [one for one in loads[n + 1 :] if rings[one[0]] == rings[i]]
+            if len(later) >= 2:
+                load(*later[1]).start()
+            if not k:
+                continue
+            if not square:
+                send_far(i, k).start()
+            elif k == 3:
+                send_over(i, 1, low).start()
+                send_over(i, 2, high).start()
+            elif k == 1:
+                send_near(i, 1, low, 0).start()
+            else:
+                send_near(i, 2, high, 1).start()
+
+    def pass_over(i):
         if not square:
-            send_far(i, k).start()
-        elif k == 3:
-            send_over(i, 1, low).start()
-            send_over(i, 2, high).start()
-        elif k == 1:
-            send_near(i, 1, low, 0).start()
-        else:
-            send_near(i, 2, high, 1).start()
-    for one, other in zip(bring, put):
-        one.wait()
-        other.start()
-    middle(cut_in, cut_out)
-    if square:
-        for i in range(n_items):
-            send_over(i, 2, high).wait_recv()
-            grow(i, 1, half, n_dp - half, lambda plane, rows: transit[i][1, plane, rows])
-            send_near(i, 1, high, 2).start()
-            send_over(i, 1, low).wait_recv()
-            grow(i, 2, 0, half, lambda plane, rows: transit[i][0, plane, rows])
-            send_near(i, 2, low, 3).start()
-    for i in range(n_items):
+            return
+        send_over(i, 2, high).wait_recv()
+        grow(i, 1, half, n_dp - half, lambda plane, rows: transit[i][1, plane, rows])
+        send_near(i, 1, high, 2).start()
+        send_over(i, 1, low).wait_recv()
+        grow(i, 2, 0, half, lambda plane, rows: transit[i][0, plane, rows])
+        send_near(i, 2, low, 3).start()
+
+    def over_chips(i):
         if square:
             send_near(i, 1, low, 0).wait_recv()
             send_near(i, 2, high, 1).wait_recv()
@@ -560,22 +567,31 @@
         for d in range(n_dp - 1, 0, -1):
             for way in (0, 1):
                 plane = z - d if way else z + d
-                arrives = z < n_dp - 1 if way else z > 0
-                slot = n_dp - z + plane if way else plane - z
-
-                @pl.when(plane >= 0 if way else plane < n_dp)
+
+                @pl.when(z == (n_dp - 1 if way else 0))
                 def _():
-                    @pl.when(arrives)
-                    def _():
-                        from_along(i, slot).wait_recv()
-                        grow(i, 0, plane, 1, lambda unused, at: got_c[i][slot, at])
-
                     along(i, plane, way).start()
 
-    for i in range(n_items):
+    def over_planes(i):
+        for d in range(n_dp - 2, 0, -1):
+            for way in (0, 1):
+                plane = z - d if way else z + d
+                slot = n_dp - d if way else d
+
+                @pl.when((plane >= 0) & (z < n_dp - 1) if way else (plane < n_dp) & (z > 0))
+                def _():
+                    from_along(i, slot).wait_recv()
+                    grow(i, 0, plane, 1, lambda unused, at: got_c[i][slot, at])
+                    along(i, plane, way).start()
+
+    def finish(i):
+        array, first, rows = items[i]
+
+        def here(at):
+            return pl.ds(pl.multiple_of(first + at.start, 16), 16)
 
         def own(unused, at, total):
-            targets[i][at] = total
+            targets[array][here(at)] = total
 
         add(i, 1, own, [lambda unused, at: got_a[i][0, z, at]])
         for slot, arrives in ((0, z > 0), (n_dp, z < n_dp - 1)):
@@ -587,9 +603,22 @@
                     i,
                     1,
                     own,
-                    [lambda unused, at: targets[i][at], lambda unused, at: got_c[i][slot, at]],
+                    [
+                        lambda unused, at: targets[array][here(at)],
+                        lambda unused, at: got_c[i][slot, at],
+                    ],
                 )
 
+    steps = (over_cores, pass_over, over_chips, over_planes, finish)
+    for n in range(n_items + len(steps) - 1):
+        for late, step in enumerate(steps):
+            if 0 <= n - late < n_items:
+                step(n - late)
+        if n == min(1, n_items - 1):
+            for one, other in zip(bring, put):
+                one.wait()
+                other.start()
+            middle(cut_in, cut_out)
     for i in range(n_items):
         for k in range(chips):
             to_mate(i, k).wait_send()
@@ -620,7 +649,8 @@
 def scatter_call(
     n_dp,
     n_expert,
-    items,
+    arrays,
+    splits,
     cut_in,
     cut_shapes,
     cuts,
@@ -632,10 +662,15 @@
 ):
     chips = n_expert // 2
     square = chips == 4
+    items = []
+    for array, (one, split) in enumerate(zip(arrays, splits)):
+        rows = one.shape[2] // split
+        items += [(array, first, rows) for first in range(0, one.shape[2], rows)]
     n, m = len(items), len(cut_shapes)
+    count = len(arrays)
     dma = pltpu.SemaphoreType.DMA
     anywhere = pl.BlockSpec(memory_space=pl.ANY)
-    blocks = [item.shape[2:] for item in items]
+    blocks = [(rows, arrays[array].shape[3]) for array, unused, rows in items]
     kinds = sorted(set(blocks))
     rings = [kinds.index(block) for block in blocks]
     bf16 = jnp.bfloat16
@@ -645,7 +680,8 @@
             scatter_kernel,
             n_dp,
             n_expert,
-            n,
+            count,
+            items,
             len(cut_in),
             m,
             cuts,
@@ -654,9 +690,12 @@
             rings,
             len(kinds),
         ),
-        out_shape=[*[jax.ShapeDtypeStruct(block, jnp.float32) for block in blocks], *cut_shapes],
-        in_specs=[anywhere] * (n + len(cut_in)),
-        out_specs=[pl.BlockSpec(memory_space=pltpu.VMEM)] * n + [anywhere] * m,
+        out_shape=[
+            *[jax.ShapeDtypeStruct(one.shape[2:], jnp.float32) for one in arrays],
+            *cut_shapes,
+        ],
+        in_specs=[anywhere] * (count + len(cut_in)),
+        out_specs=[pl.BlockSpec(memory_space=pltpu.VMEM)] * count + [anywhere] * m,
         scratch_shapes=[
             *[pltpu.VMEM((2, n_dp, *kind), bf16) for kind in kinds],
             *[pltpu.VMEM((chips, n_dp, *block), bf16) for block in blocks],
@@ -681,13 +720,14 @@
         compiler_params=pltpu.CompilerParams(
             collective_id=number, has_side_effects=True, vmem_limit_bytes=62 * 1024 * 1024
         ),
-    )(*items, *cut_in)
+    )(*arrays, *cut_in)
 
 
 def scatter_all(
     n_dp,
     n_expert,
     items,
+    splits,
     cut_in,
     cut_shapes,
     cuts,
@@ -700,7 +740,7 @@
     chips = n_expert // 2
     blocks = (2 * chips - 1 if chips != 4 else 7) * n_dp + n_dp + 3
     need = sum(blocks * item.shape[2] * item.shape[3] * 2 for item in items)
-    kinds = {item.shape[2:] for item in items}
+    kinds = {(item.shape[2] // split, item.shape[3]) for item, split in zip(items, splits)}
     need += sum(2 * n_dp * kind[0] * kind[1] * 2 for kind in kinds)
     need += sum(stage[0] * stage[1] * stage[2] * 2 for stage in stages)
     pieces = -(-need // (61 * 1024 * 1024))
@@ -715,6 +755,7 @@
             n_dp,
             n_expert,
             [items[i][..., ends[i][0] : ends[i][1]] if pieces > 1 else items[i] for i in used],
+            [splits[i] for i in used],
             cut_in if first else [],
             cut_shapes if first else [],
             cuts if first else nothing,
@@ -1134,7 +1175,7 @@
     beside = early + number // 8
     late = number - number // 4
     back_beside = number // 8
-    back_third = back_beside + max(number // 8, 1)
+    back_third = back_beside + max(number // 4, 1)
     back_late = back_third + number // 4
     me = lax.axis_index("dp")
     cut_shape = jax.ShapeDtypeStruct((number, n_dp * depth, part), bf16)
@@ -1381,6 +1422,7 @@
         n_dp,
         n_expert,
         [part_back.reshape(n_dp, n_expert, count, D + width)],
+        [4],
         [gate_soon, up_soon, slots, weighted],
         [
             *way_shapes,
@@ -1470,8 +1512,9 @@
     sums, (gate_back, up_back) = scatter_all(
         n_dp,
         n_expert,
-        [blocks_of(value) for value in weight_grads]
-        + [part_out.reshape(n_dp, n_expert, count, D)],
+        [part_out.reshape(n_dp, n_expert, count, D)]
+        + [blocks_of(value) for value in weight_grads],
+        [2] + [1] * len(weight_grads),
         [gate_third, up_third, gate_soon, up_soon, gate_rest, up_rest],
         way_shapes,
         lambda ins, outs: ways(back_late, late, 0, ins[2:4], outs)
@@ -1480,7 +1523,7 @@
         ((0, 0), (1, 1)),
         [],
     )
-    grad_out_part, grad_value_part, grad_key_part, grad_query_part, small_part, summed = sums
+    summed, grad_out_part, grad_value_part, grad_key_part, grad_query_part, small_part = sums
     output = (middle + summed).astype(bf16)
     grad_router_part = small_part[:, :experts_all]
     gain_parts = [small_part[:, experts_all + i] for i in range(4)]

time: 1150 us -> 1140 us (level)
  transfers between devices with their start and end apart: 12 -> 12, of which waited for: 2 -> 2; matrix products, arithmetic and copies ran while one was open for 15% -> 15% of each run, Pallas kernels for 34% -> 33%
where the time goes in v10:
time: 1140 us; the launch traced here: 1120 us
  Pallas kernels  890 us (78%)
  matrix products  88.2 us (8%)
  local copies, waits for them, and re-layouts  59.1 us (5%)
  other arithmetic  38.4 us (3%)
  starting transfers between devices  36.9 us (3%)
    pallas_call x2, Pallas kernels, gather_call(): pl.pallas_call(functools.partial(gather_kernel, n_dp, n_expert, n, places...  386 us
    pallas_call x2, Pallas kernels, scatter_call(): pl.pallas_call(functools.partial(scatter_kernel, n_dp, n_expert, count, i...  380 us
    dot_general x21, matrix products, product(): return jnp.einsum(form, left, right, preferred_element_type=jnp.float32)  86.7 us
    pallas_call x2, Pallas kernels, expert_call(): pl.pallas_call(functools.partial(expert_kernel, steps, half, len(weights)...  78.9 us
    ppermute x12, starting transfers between devices, permuted(): got.append(lax.ppermute(piece, 'dp', paths))  36.9 us
    pallas_call x1, Pallas kernels, place_back(): pl.pallas_call(functools.partial(place_back_kernel, number), grid=(pairs,...  23.5 us
  transfers between devices with their start and end apart: 12, of which 2 were waited for; matrix products, arithmetic and copies ran while one was open for 15% of the time, Pallas kernels for 33%

profile of v10, /device:TPU:0, one launch (start us, length us, event | category | flops | bytes accessed | tf_op | source)
XLA Modules:
  0.0 1123.2 jit_solution(14679372156707322792)
XLA Ops:
  6.2 2.3 pad_maximum_fusion.2.refs_0_
  8.5 179.4 %shard_map.272 = (bf16[4,2048,2048]{2,1,0:T(8,128)(2,1)}, bf16[4096,256]{1,0:T(8,128)(2,1)}, bf16[8,2048,256]{2,1,0:T(8,128)(2,1)}, bf16[8,2048,256]{2,1,0:T(8,1...) custom-call(bf16[4,64,2048]{2,1,0:T(8,128)(2,1)} %pad_maximum_fusion, ...), custom_call_target="tpu_custom_call" | custom-call | tf_op jit(solution)/shard_map/pallas_call | solution.py:330
  188.1 3.4 collective-permute-start.2
  193.0 3.0 slice_reduce_fusion.4
  196.4 4.9 multiply_reduce_fusion.10
  201.4 6.0 multiply_reduce_fusion.9
  207.4 5.4 fusion.53
  212.8 2.3 slice.139
  215.2 1.5 multiply_bitcast_fusion
  218.3 1.6 fusion.78
  220.7 3.2 subtract_convert_fusion.2
  224.5 1.5 fusion.79
  226.0 2.4 fusion.76
  228.4 1.6 convolution_bitcast_fusion
  230.8 5.1 multiply_reduce_fusion.8
  236.0 1.6 constant_dynamic-slice_fusion.4
  240.7 206.8 %shard_map.273 = (bf16[4096,2048]{1,0:T(8,128)(2,1)}, bf16[4096,2048]{1,0:T(8,128)(2,1)}, bf16[8,2048,256]{2,1,0:T(8,128)(2,1)}, bf16[8,2048,256]{2,1,0:T(8,128)...) custom-call(bf16[128,2048]{1,0:T(8,128)(2,1)S(1)} %multiply_convert_, ...), custom_call_target="tpu_custom_call", output_to_operand_aliasing={{2}: (4, {}), {3}: (5, {})} | custom-call | tf_op jit(solution)/shard_map/pallas_call | solution.py:330
  447.5 2.7 collective-permute-start.3
  450.2 2.2 collective-permute-start.4
  452.4 55.3 %shard_map.274 = (bf16[8,768,2048]{2,1,0:T(8,128)(2,1)}, bf16[8,768,2048]{2,1,0:T(8,128)(2,1)}, bf16[8,768,128]{2,1,0:T(8,128)(2,1)}, bf16[6,2048,256]{2,1,0:T(8...) custom-call(s32[1]{0:T(128)} %bitcast.55.names_ref, ...), custom_call_target="tpu_custom_call" | custom-call | tf_op jit(solution)/shard_map/pallas_call | solution.py:1003
  507.7 2.5 dynamic-slice_bitcast_fusion
  510.3 7.2 collective-permute-done.3.refs_1_
  518.9 22.3 %collective-permute-start.6 = (bf16[1,512,512]{2,1,0:T(8,128)(2,1)}, bf16[1,512,512]{2,1,0:T(8,128)(2,1)}, u32[]{:S(2)}, u32[]{:S(2)}) collective-permute-start(bf16[1,512,512]{2,1,0:T(8,128)(2,1)} %get-tuple-element.319), channel_id=1, source_target_pairs={{0,16},{8,24},{16,0},{24,8},{1,17},{9,25},{17,1},{25,9},{2,18},{10... | collective-permute-start | bytes 1572872 | tf_op jit(solution)/shard_map/ppermute | solution.py:1214
  541.2 1.6 collective-permute-start.7
  547.8 1.7 slice.149
  549.5 2.3 slice.150
  552.6 23.6 %shard_map.275 = (bf16[8,768,2048]{2,1,0:T(8,128)(2,1)}, bf16[8,768,2048]{2,1,0:T(8,128)(2,1)}, bf16[8,768,128]{2,1,0:T(8,128)(2,1)}, bf16[2,2048,256]{2,1,0:T(8...) custom-call(s32[5]{0:T(128)} %stack.58.names_ref, ...), custom_call_target="tpu_custom_call", output_to_operand_aliasing={{0}: (9, {}), {1}: (10, {}), {2}: (11, {}), {5}: (12, {})} | custom-call | tf_op jit(solution)/shard_map/pallas_call | solution.py:1003
  576.2 23.5 %shard_map.276 = bf16[4096,2176]{1,0:T(8,128)(2,1)} custom-call(s32[16,8,256]{2,1,0:T(8,128)} %select_bitcast_fusion.refs_6_.slots_ref.refs_3_, bf16[8,768,2048]{2,1,0:T(8,128)(2,1)} %get-tuple-element.316.dx_ref, bf16[8,768,128]{2,1,0:T(8,128)(2,1)} %get-tuple-element.317.probs_ref), custom_call_target="tpu_custom_call" | custom-call | tf_op jit(solution)/shard_map/pallas_call | solution.py:1053
  599.8 123.0 %shard_map.277 = (f32[128,2176]{1,0:T(8,128)}, bf16[8,512,1024]{2,1,0:T(8,128)(2,1)}, bf16[8,512,1024]{2,1,0:T(8,128)(2,1)}, bf16[4096,2048]{1,0:T(8,128)(2,1)},...) custom-call(bf16[4,8,128,2176]{3,2,1,0:T(8,128)(2,1)} %bitcast.189, ...), custom_call_target="tpu_custom_call" | custom-call | tf_op jit(solution)/shard_map/pallas_call | solution.py:678
  722.8 1.9 collective-permute-start.10
  724.7 2.5 collective-permute-start.9
  728.2 1.7 slice.148
  730.8 2.1 pad_maximum_fusion.3.refs_0_
  732.9 106.2 %conditional.1 = (f32[128,2048]{1,0:T(8,128)}, bf16[4,8,64,2048]{3,2,1,0:T(8,128)(2,1)}, bf16[4,8,64,2048]{3,2,1,0:T(8,128)(2,1)}, bf16[4,8,64,2048]{3,2,1,0:T(8...) conditional(s32[]{:T(128)} %bitcast.61, () %tuple.37, ...), branch_computations={%region_10.11_spmd, %region_11.24_spmd} | conditional | flops 8961171456 | bytes 162147504 | solution.py:1507
  735.1 1.9 multiply_reduce_fusion
  737.0 1.4 subtract_add_fusion.1
  738.4 7.1 fusion.18
  746.8 1.9 multiply_reduce_fusion.5
  748.7 1.4 multiply_convert_fusion
  750.1 1.6 fusion.22
  751.7 1.4 fusion.23
  755.6 2.5 copy.121
  758.1 1.6 copy.120
  759.7 2.2 fusion.27
  761.9 2.7 subtract_convert_fusion.1
  764.5 2.3 pad_maximum_fusion.1
  766.8 2.5 copy.124
  769.4 1.6 copy.123
  770.9 2.2 fusion.25
  773.2 1.9 subtract_convert_fusion
  775.9 6.3 fusion.2
  782.2 7.4 fusion.12
  790.9 1.6 copy.126
  792.4 8.1 multiply_reduce_fusion.1
  803.2 1.9 constant_dynamic-update-slice_fusion.4
  808.6 3.0 copy.136
  811.6 6.6 convolution_convert_fusion
  818.2 5.6 convolution_convert_fusion.1
  825.1 5.8 convolution_convert_fusion.2
  832.1 6.8 convolution_convert_fusion.3
  839.1 257.4 %shard_map.278 = (f32[128,2048]{1,0:T(8,128)}, f32[64,2048]{1,0:T(8,128)}, f32[64,2048]{1,0:T(8,128)}, f32[64,2048]{1,0:T(8,128)}, f32[64,2048]{1,0:T(8,128)}, /...) custom-call(bf16[4,8,128,2048]{3,2,1,0:T(8,128)(2,1)} %bitcast.190, ...), custom_call_target="tpu_custom_call", output_to_operand_aliasing={{6}: (6, {}), {7}: (7, {})} | custom-call | tf_op jit(solution)/shard_map/pallas_call | solution.py:678
  1096.5 11.5 %shard_map.279 = (f32[8,512,1024]{2,1,0:T(8,128)}, f32[8,512,1024]{2,1,0:T(8,128)}) custom-call(bf16[8,512,1024]{2,1,0:T(8,128)(2,1)} %get-tuple-element.350.refs_0_, bf16[8,512,1024]{2,1,0:T(8,128)(2,1)} %get-tuple-element.351.refs_1_), custom_call_target="tpu_custom_call" | custom-call | tf_op jit(solution)/shard_map/pallas_call | solution.py:1077
  1108.0 3.7 shard_map.280
  1113.4 5.8 shard_map.281
  (165 shorter events, 45.5 us)
Async XLA Ops:
  187.9 8.1 copy-start.6
  187.9 52.8 %collective-permute-start = (bf16[1,512,512]{2,1,0:T(8,128)(2,1)}, bf16[1,512,512]{2,1,0:T(8,128)(2,1)}, u32[]{:S(2)}, u32[]{:S(2)}) collective-permute-start(bf16[1,512,512]{2,1,0:T(8,128)(2,1)} %get-tuple-element.293), channel_id=1, source_target_pairs={{0,16},{8,24},{16,0},{24,8},{1,17},{9,25},{17,1},{25,9},{2,18},{10... | collective-permute-start | bytes 1572872 | tf_op jit(solution)/shard_map/ppermute | solution.py:1214
  188.0 52.7 %collective-permute-start.1 = (bf16[1,512,512]{2,1,0:T(8,128)(2,1)}, bf16[1,512,512]{2,1,0:T(8,128)(2,1)}, u32[]{:S(2)}, u32[]{:S(2)}) collective-permute-start(bf16[1,512,512]{2,1,0:T(8,128)(2,1)} %get-tuple-element.294), channel_id=1, source_target_pairs={{0,24},{8,16},{16,8},{24,0},{1,25},{9,17},{17,9},{25,1},{2,26},{10... | collective-permute-start | bytes 1572872 | tf_op jit(solution)/shard_map/ppermute | solution.py:1214
  188.1 52.6 %collective-permute-start.2 = (bf16[1,512,512]{2,1,0:T(8,128)(2,1)}, bf16[1,512,512]{2,1,0:T(8,128)(2,1)}, u32[]{:S(2)}, u32[]{:S(2)}) collective-permute-start(bf16[1,512,512]{2,1,0:T(8,128)(2,1)} %get-tuple-element.295), channel_id=1, source_target_pairs={{0,8},{8,0},{16,24},{24,16},{1,9},{9,1},{17,25},{25,17},{2,10},{10... | collective-permute-start | bytes 1572872 | tf_op jit(solution)/shard_map/ppermute | solution.py:1214
  196.2 11.2 copy-start.29
  196.4 11.0 copy-start.2
  201.4 13.8 %copy-start.9 = (f32[128,2048]{1,0:T(8,128)}, f32[128,2048]{1,0:T(8,128)S(1)}, u32[]{:S(2)}) copy-start(f32[128,2048]{1,0:T(8,128)S(1)} %get-tuple-element.507) | copy-start | bytes 3145732
  215.1 4.8 copy-start.31
  224.2 11.7 %copy-start.20 = (bf16[128,16,128]{2,0,1:T(8,128)(2,1)}, bf16[128,16,128]{2,0,1:T(8,128)(2,1)S(1)}, u32[]{:S(2)}) copy-start(bf16[128,16,128]{2,0,1:T(8,128)(2,1)S(1)} %pad_maximum_fusion.5) | copy-start | bytes 1572868
  224.5 11.4 %copy-start.21 = (bf16[128,16,128]{2,0,1:T(8,128)(2,1)}, bf16[128,16,128]{2,0,1:T(8,128)(2,1)S(1)}, u32[]{:S(2)}) copy-start(bf16[128,16,128]{2,0,1:T(8,128)(2,1)S(1)} %pad_maximum_fusion.4) | copy-start | bytes 1572868
  228.4 1.6 copy-start.4
  230.0 0.8 copy-start.17
  240.7 305.4 %copy-start = (bf16[128,2048]{1,0:T(8,128)(2,1)}, bf16[128,2048]{1,0:T(8,128)(2,1)S(1)}, u32[]{:S(2)}) copy-start(bf16[128,2048]{1,0:T(8,128)(2,1)S(1)} %multiply_convert_fusion.2.refs_0_) | copy-start | bytes 1572868
  447.5 70.0 %collective-permute-start.3 = (bf16[2,512,512]{2,1,0:T(8,128)(2,1)}, bf16[2,512,512]{2,1,0:T(8,128)(2,1)}, u32[]{:S(2)}, u32[]{:S(2)}) collective-permute-start(bf16[2,512,512]{2,1,0:T(8,128)(2,1)} %get-tuple-element.307), channel_id=1, source_target_pairs={{0,16},{8,24},{16,0},{24,8},{1,17},{9,25},{17,1},{25,9},{2,18},{10... | collective-permute-start | bytes 3145736 | tf_op jit(solution)/shard_map/ppermute | solution.py:1214
  450.2 67.3 %collective-permute-start.4 = (bf16[2,512,512]{2,1,0:T(8,128)(2,1)}, bf16[2,512,512]{2,1,0:T(8,128)(2,1)}, u32[]{:S(2)}, u32[]{:S(2)}) collective-permute-start(bf16[2,512,512]{2,1,0:T(8,128)(2,1)} %get-tuple-element.308), channel_id=1, source_target_pairs={{0,24},{8,16},{16,8},{24,0},{1,25},{9,17},{17,9},{25,1},{2,26},{10... | collective-permute-start | bytes 3145736 | tf_op jit(solution)/shard_map/ppermute | solution.py:1214
  452.4 66.4 %collective-permute-start.5 = (bf16[2,512,512]{2,1,0:T(8,128)(2,1)}, bf16[2,512,512]{2,1,0:T(8,128)(2,1)}, u32[]{:S(2)}, u32[]{:S(2)}) collective-permute-start(bf16[2,512,512]{2,1,0:T(8,128)(2,1)} %get-tuple-element.309), channel_id=1, source_target_pairs={{0,8},{8,0},{16,24},{24,16},{1,9},{9,1},{17,25},{25,17},{2,10},{10... | collective-permute-start | bytes 3145736 | tf_op jit(solution)/shard_map/ppermute | solution.py:1214
  452.4 92.1 %copy-start.19 = (bf16[128,2048]{1,0:T(8,128)(2,1)S(1)}, bf16[128,2048]{1,0:T(8,128)(2,1)}, u32[]{:S(2)}) copy-start(bf16[128,2048]{1,0:T(8,128)(2,1)} %fusion.53) | copy-start | bytes 1572868
  518.9 80.9 %collective-permute-start.6 = (bf16[1,512,512]{2,1,0:T(8,128)(2,1)}, bf16[1,512,512]{2,1,0:T(8,128)(2,1)}, u32[]{:S(2)}, u32[]{:S(2)}) collective-permute-start(bf16[1,512,512]{2,1,0:T(8,128)(2,1)} %get-tuple-element.319), channel_id=1, source_target_pairs={{0,16},{8,24},{16,0},{24,8},{1,17},{9,25},{17,1},{25,9},{2,18},{10... | collective-permute-start | bytes 1572872 | tf_op jit(solution)/shard_map/ppermute | solution.py:1214
  541.2 58.5 %collective-permute-start.7 = (bf16[1,512,512]{2,1,0:T(8,128)(2,1)}, bf16[1,512,512]{2,1,0:T(8,128)(2,1)}, u32[]{:S(2)}, u32[]{:S(2)}) collective-permute-start(bf16[1,512,512]{2,1,0:T(8,128)(2,1)} %get-tuple-element.320), channel_id=1, source_target_pairs={{0,24},{8,16},{16,8},{24,0},{1,25},{9,17},{17,9},{25,1},{2,26},{10... | collective-permute-start | bytes 1572872 | tf_op jit(solution)/shard_map/ppermute | solution.py:1214
  542.8 56.9 %collective-permute-start.8 = (bf16[1,512,512]{2,1,0:T(8,128)(2,1)}, bf16[1,512,512]{2,1,0:T(8,128)(2,1)}, u32[]{:S(2)}, u32[]{:S(2)}) collective-permute-start(bf16[1,512,512]{2,1,0:T(8,128)(2,1)} %get-tuple-element.321), channel_id=1, source_target_pairs={{0,8},{8,0},{16,24},{24,16},{1,9},{9,1},{17,25},{25,17},{2,10},{10... | collective-permute-start | bytes 1572872 | tf_op jit(solution)/shard_map/ppermute | solution.py:1214
  722.7 10.2 copy-start.1
  722.7 10.2 copy-start.11
  722.8 10.2 copy-start.30
  722.8 390.6 %collective-permute-start.10 = (bf16[2,512,512]{2,1,0:T(8,128)(2,1)}, bf16[2,512,512]{2,1,0:T(8,128)(2,1)}, u32[]{:S(2)}, u32[]{:S(2)}) collective-permute-start(bf16[2,512,512]{2,1,0:T(8,128)(2,1)} %get-tuple-element.345), channel_id=1, source_target_pairs={{0,24},{8,16},{16,8},{24,0},{1,25},{9,17},{17,9},{25,1},{2,26},{10... | collective-permute-start | bytes 3145736 | tf_op jit(solution)/shard_map/ppermute | solution.py:1214
  724.7 388.7 %collective-permute-start.11 = (bf16[2,512,512]{2,1,0:T(8,128)(2,1)}, bf16[2,512,512]{2,1,0:T(8,128)(2,1)}, u32[]{:S(2)}, u32[]{:S(2)}) collective-permute-start(bf16[2,512,512]{2,1,0:T(8,128)(2,1)} %get-tuple-element.346), channel_id=1, source_target_pairs={{0,8},{8,0},{16,24},{24,16},{1,9},{9,1},{17,25},{25,17},{2,10},{10... | collective-permute-start | bytes 3145736 | tf_op jit(solution)/shard_map/ppermute | solution.py:1214
  724.7 388.7 %collective-permute-start.9 = (bf16[2,512,512]{2,1,0:T(8,128)(2,1)}, bf16[2,512,512]{2,1,0:T(8,128)(2,1)}, u32[]{:S(2)}, u32[]{:S(2)}) collective-permute-start(bf16[2,512,512]{2,1,0:T(8,128)(2,1)} %get-tuple-element.344), channel_id=1, source_target_pairs={{0,16},{8,24},{16,0},{24,8},{1,17},{9,25},{17,1},{25,9},{2,18},{10... | collective-permute-start | bytes 3145736 | tf_op jit(solution)/shard_map/ppermute | solution.py:1214
  746.8 11.3 %copy-start.7 = (bf16[128,2048]{0,1:T(8,128)(2,1)}, bf16[128,2048]{0,1:T(8,128)(2,1)S(1)}, u32[]{:S(2)}) copy-start(bf16[128,2048]{0,1:T(8,128)(2,1)S(1)} %copy.142) | copy-start | bytes 1572868 | tf_op jit(solution)/shard_map/cond
  770.9 11.3 %copy-start.13 = (bf16[128,2048]{0,1:T(8,128)(2,1)S(1)}, bf16[128,2048]{0,1:T(8,128)(2,1)}, u32[]{:S(2)}) copy-start(bf16[128,2048]{0,1:T(8,128)(2,1)} %subtract_convert_fusion.1) | copy-start | bytes 1572868 | tf_op jit(solution)/shard_map/cond
  775.1 0.8 copy-start.14
  782.2 7.4 copy-start.5
  782.2 7.4 copy-start.8
  792.4 19.2 %copy-start.3 = (bf16[128,2048]{1,0:T(8,128)(2,1)S(1)}, bf16[128,2048]{1,0:T(8,128)(2,1)}, u32[]{:S(2)}) copy-start(bf16[128,2048]{1,0:T(8,128)(2,1)} %get-tuple-element.199) | copy-start | bytes 1572868 | tf_op jit(solution)/shard_map/cond
  801.9 16.3 %copy-start.15 = (bf16[128,2048]{0,1:T(8,128)(2,1)S(1)}, bf16[128,2048]{0,1:T(8,128)(2,1)}, u32[]{:S(2)}) copy-start(bf16[128,2048]{0,1:T(8,128)(2,1)} %copy-done.14) | copy-start | bytes 1572868 | tf_op jit(solution)/shard_map/cond
  818.2 5.6 copy-start.10
  818.2 5.6 copy-start.22
  818.2 6.9 copy-start.12
  823.8 7.1 copy-start.18
  830.9 8.0 copy-start.16
  1108.0 3.7 copy-start.24
  1108.0 4.5 copy-start.23
  1113.4 5.8 copy-start.28
  1113.4 6.6 copy-start.27
  1113.4 7.4 copy-start.26
  1113.4 8.2 copy-start.25

commit v11 on v10

--- a/solution.py
+++ b/solution.py
@@ -74,7 +74,7 @@
 
 def partners(z, n_dp):
     if n_dp == 4:
-        pairs = [z, (z + 2) % 4, 3 - z, z + 1 - 2 * (z % 2)]
+        pairs = [z, 3 - z, (z + 2) % 4, z + 1 - 2 * (z % 2)]
         return lambda k: pairs[k], lambda k: pairs[k]
     return lambda k: (z + k) % n_dp, lambda k: (z + n_dp - k) % n_dp
 
@@ -1175,7 +1175,7 @@
     beside = early + number // 8
     late = number - number // 4
     back_beside = number // 8
-    back_third = back_beside + max(number // 4, 1)
+    back_third = back_beside + max(number // 8, 1)
     back_late = back_third + number // 4
     me = lax.axis_index("dp")
     cut_shape = jax.ShapeDtypeStruct((number, n_dp * depth, part), bf16)
@@ -1422,7 +1422,7 @@
         n_dp,
         n_expert,
         [part_back.reshape(n_dp, n_expert, count, D + width)],
-        [4],
+        [8],
         [gate_soon, up_soon, slots, weighted],
         [
             *way_shapes,
@@ -1514,7 +1514,7 @@
         n_expert,
         [part_out.reshape(n_dp, n_expert, count, D)]
         + [blocks_of(value) for value in weight_grads],
-        [2] + [1] * len(weight_grads),
+        [4] + [2 if rows_each > 16 else 1] * (len(weight_grads) - 1) + [1],
         [gate_third, up_third, gate_soon, up_soon, gate_rest, up_rest],
         way_shapes,
         lambda ins, outs: ways(back_late, late, 0, ins[2:4], outs)

time: 1140 us -> 1210 us (1.061)
  Pallas kernels: 890 us -> 953 us
  waiting for transfers between devices: 8.61 us -> 28.7 us
    pallas_call x2, Pallas kernels: 380 us -> 462 us  [scatter_call(): pl.pallas_call(functools.partial(scatter_kernel, n_dp, n_expert, count, i...]
    pallas_call x2, Pallas kernels: 386 us -> 357 us  [gather_call(): pl.pallas_call(functools.partial(gather_kernel, n_dp, n_expert, n, places...]
    ppermute x12, waiting for transfers between devices: 8.61 us -> 28.7 us  [permuted(): got.append(lax.ppermute(piece, 'dp', paths))]
  transfers between devices with their start and end apart: 12 -> 12, of which waited for: 2 -> 1; matrix products, arithmetic and copies ran while one was open for 15% -> 14% of each run, Pallas kernels for 33% -> 40%
where the time goes in v11:
time: 1210 us; the launch traced here: 1200 us
  Pallas kernels  953 us (79%)
  matrix products  88.1 us (7%)
  local copies, waits for them, and re-layouts  59.1 us (5%)
  other arithmetic  38.4 us (3%)
  starting transfers between devices  29.3 us (2%)
  waiting for transfers between devices  28.7 us (2%)
    pallas_call x2, Pallas kernels, scatter_call(): pl.pallas_call(functools.partial(scatter_kernel, n_dp, n_expert, count, i...  462 us
    pallas_call x2, Pallas kernels, gather_call(): pl.pallas_call(functools.partial(gather_kernel, n_dp, n_expert, n, places...  357 us
    pallas_call x2, Pallas kernels, expert_call(): pl.pallas_call(functools.partial(expert_kernel, steps, half, len(weights)...  88.9 us
    dot_general x21, matrix products, product(): return jnp.einsum(form, left, right, preferred_element_type=jnp.float32)  86.6 us
    ppermute x12, starting transfers between devices, permuted(): got.append(lax.ppermute(piece, 'dp', paths))  29.3 us
    ppermute x12, waiting for transfers between devices, permuted(): got.append(lax.ppermute(piece, 'dp', paths))  28.7 us
  transfers between devices with their start and end apart: 12, of which 1 were waited for; matrix products, arithmetic and copies ran while one was open for 14% of the time, Pallas kernels for 40%

profile of v11, /device:TPU:0, one launch (start us, length us, event | category | flops | bytes accessed | tf_op | source)
XLA Modules:
  0.0 1198.5 jit_solution(9967383503149934229)
XLA Ops:
  6.2 2.3 pad_maximum_fusion.2.refs_0_
  8.5 167.3 %shard_map.272 = (bf16[4,2048,2048]{2,1,0:T(8,128)(2,1)}, bf16[4096,256]{1,0:T(8,128)(2,1)}, bf16[8,2048,256]{2,1,0:T(8,128)(2,1)}, bf16[8,2048,256]{2,1,0:T(8,1...) custom-call(bf16[4,64,2048]{2,1,0:T(8,128)(2,1)} %pad_maximum_fusion, ...), custom_call_target="tpu_custom_call" | custom-call | tf_op jit(solution)/shard_map/pallas_call | solution.py:330
  176.0 4.3 collective-permute-start.2
  181.8 3.0 slice_reduce_fusion.4
  185.2 4.9 multiply_reduce_fusion.10
  190.1 6.0 multiply_reduce_fusion.9
  196.2 5.4 fusion.53
  201.6 2.3 slice.139
  203.9 1.5 multiply_bitcast_fusion
  207.1 1.6 fusion.78
  209.4 3.2 subtract_convert_fusion.2
  213.3 1.5 fusion.79
  214.8 2.4 fusion.76
  217.2 1.6 convolution_bitcast_fusion
  219.6 5.0 multiply_reduce_fusion.8
  224.7 1.6 constant_dynamic-slice_fusion.4
  229.4 190.0 %shard_map.273 = (bf16[4096,2048]{1,0:T(8,128)(2,1)}, bf16[4096,2048]{1,0:T(8,128)(2,1)}, bf16[8,2048,256]{2,1,0:T(8,128)(2,1)}, bf16[8,2048,256]{2,1,0:T(8,128)...) custom-call(bf16[128,2048]{1,0:T(8,128)(2,1)S(1)} %multiply_convert_, ...), custom_call_target="tpu_custom_call", output_to_operand_aliasing={{2}: (4, {}), {3}: (5, {})} | custom-call | tf_op jit(solution)/shard_map/pallas_call | solution.py:330
  419.4 1.6 collective-permute-start.3
  421.0 2.4 collective-permute-start.4
  423.9 55.3 %shard_map.274 = (bf16[8,768,2048]{2,1,0:T(8,128)(2,1)}, bf16[8,768,2048]{2,1,0:T(8,128)(2,1)}, bf16[8,768,128]{2,1,0:T(8,128)(2,1)}, bf16[6,2048,256]{2,1,0:T(8...) custom-call(s32[1]{0:T(128)} %bitcast.55.names_ref, ...), custom_call_target="tpu_custom_call" | custom-call | tf_op jit(solution)/shard_map/pallas_call | solution.py:1003
  479.2 2.5 dynamic-slice_bitcast_fusion
  481.7 28.7 %collective-permute-done.4.refs_2_ = bf16[2,512,512]{2,1,0:T(8,128)(2,1)} collective-permute-done((bf16[2,512,512]{2,1,0:T(8,128)(2,1)}, bf16[2,512,512]{2,1,0:T(8,128)(2,1)}, u32[]{:S(2)}, u32[]{:S(2)}) %collective-permute-start.4) | collective-permute-done | bytes 1048608 | tf_op jit(solution)/shard_map/ppermute | solution.py:1214
  510.4 15.4 %collective-permute-start.6 = (bf16[1,512,512]{2,1,0:T(8,128)(2,1)}, bf16[1,512,512]{2,1,0:T(8,128)(2,1)}, u32[]{:S(2)}, u32[]{:S(2)}) collective-permute-start(bf16[1,512,512]{2,1,0:T(8,128)(2,1)} %get-tuple-element.319), channel_id=1, source_target_pairs={{0,24},{8,16},{16,8},{24,0},{1,25},{9,17},{17,9},{25,1},{2,26},{10... | collective-permute-start | bytes 1572872 | tf_op jit(solution)/shard_map/ppermute | solution.py:1214
  531.3 1.7 slice.149
  533.0 2.3 slice.150
  536.1 33.6 %shard_map.275 = (bf16[8,768,2048]{2,1,0:T(8,128)(2,1)}, bf16[8,768,2048]{2,1,0:T(8,128)(2,1)}, bf16[8,768,128]{2,1,0:T(8,128)(2,1)}, bf16[2,2048,256]{2,1,0:T(8...) custom-call(s32[5]{0:T(128)} %stack.58.names_ref, ...), custom_call_target="tpu_custom_call", output_to_operand_aliasing={{0}: (9, {}), {1}: (10, {}), {2}: (11, {}), {5}: (12, {})} | custom-call | tf_op jit(solution)/shard_map/pallas_call | solution.py:1003
  569.8 23.5 %shard_map.276 = bf16[4096,2176]{1,0:T(8,128)(2,1)} custom-call(s32[16,8,256]{2,1,0:T(8,128)} %select_bitcast_fusion.refs_6_.slots_ref.refs_3_, bf16[8,768,2048]{2,1,0:T(8,128)(2,1)} %get-tuple-element.316.dx_ref, bf16[8,768,128]{2,1,0:T(8,128)(2,1)} %get-tuple-element.317.probs_ref), custom_call_target="tpu_custom_call" | custom-call | tf_op jit(solution)/shard_map/pallas_call | solution.py:1053
  593.3 109.8 %shard_map.277 = (f32[128,2176]{1,0:T(8,128)}, bf16[8,512,1024]{2,1,0:T(8,128)(2,1)}, bf16[8,512,1024]{2,1,0:T(8,128)(2,1)}, bf16[4096,2048]{1,0:T(8,128)(2,1)},...) custom-call(bf16[4,8,128,2176]{3,2,1,0:T(8,128)(2,1)} %bitcast.189, ...), custom_call_target="tpu_custom_call" | custom-call | tf_op jit(solution)/shard_map/pallas_call | solution.py:678
  703.5 2.5 collective-permute-start.11
  706.1 1.6 collective-permute-start.9
  708.6 1.7 slice.148
  711.2 2.1 pad_maximum_fusion.3.refs_0_
  713.3 106.2 %conditional.1 = (f32[128,2048]{1,0:T(8,128)}, bf16[4,8,64,2048]{3,2,1,0:T(8,128)(2,1)}, bf16[4,8,64,2048]{3,2,1,0:T(8,128)(2,1)}, bf16[4,8,64,2048]{3,2,1,0:T(8...) conditional(s32[]{:T(128)} %bitcast.61, () %tuple.37, ...), branch_computations={%region_10.11_spmd, %region_11.24_spmd} | conditional | flops 8961171456 | bytes 162147504 | solution.py:1507
  715.6 1.9 multiply_reduce_fusion
  717.4 1.4 subtract_add_fusion.1
  718.8 7.1 fusion.18
  727.2 1.9 multiply_reduce_fusion.5
  729.1 1.4 multiply_convert_fusion
  730.5 1.6 fusion.22
  732.1 1.4 fusion.23
  736.0 2.5 copy.121
  738.5 1.6 copy.120
  740.1 2.2 fusion.27
  742.3 2.7 subtract_convert_fusion.1
  745.0 2.3 pad_maximum_fusion.1
  747.2 2.5 copy.124
  749.8 1.6 copy.123
  751.3 2.2 fusion.25
  753.6 1.9 subtract_convert_fusion
  756.3 6.3 fusion.2
  762.6 7.4 fusion.12
  771.3 1.6 copy.126
  772.8 8.1 multiply_reduce_fusion.1
  782.3 1.3 concatenate.36
  783.6 1.9 constant_dynamic-update-slice_fusion.4
  789.0 3.0 copy.136
  792.0 6.6 convolution_convert_fusion
  798.6 5.6 convolution_convert_fusion.1
  805.5 5.8 convolution_convert_fusion.2
  812.5 6.8 convolution_convert_fusion.3
  819.5 352.2 %shard_map.278 = (f32[128,2048]{1,0:T(8,128)}, f32[64,2048]{1,0:T(8,128)}, f32[64,2048]{1,0:T(8,128)}, f32[64,2048]{1,0:T(8,128)}, f32[64,2048]{1,0:T(8,128)}, /...) custom-call(bf16[4,8,128,2048]{3,2,1,0:T(8,128)(2,1)} %bitcast.190, ...), custom_call_target="tpu_custom_call", output_to_operand_aliasing={{6}: (6, {}), {7}: (7, {})} | custom-call | tf_op jit(solution)/shard_map/pallas_call | solution.py:678
  1171.7 11.5 shard_map.279
  1183.2 3.7 shard_map.280
  1188.6 5.8 shard_map.281
  (165 shorter events, 44.2 us)
Async XLA Ops:
  175.8 9.0 copy-start.6
  175.8 53.6 %collective-permute-start = (bf16[1,512,512]{2,1,0:T(8,128)(2,1)}, bf16[1,512,512]{2,1,0:T(8,128)(2,1)}, u32[]{:S(2)}, u32[]{:S(2)}) collective-permute-start(bf16[1,512,512]{2,1,0:T(8,128)(2,1)} %get-tuple-element.293), channel_id=1, source_target_pairs={{0,24},{8,16},{16,8},{24,0},{1,25},{9,17},{17,9},{25,1},{2,26},{10... | collective-permute-start | bytes 1572872 | tf_op jit(solution)/shard_map/ppermute | solution.py:1214
  175.9 53.5 %collective-permute-start.1 = (bf16[1,512,512]{2,1,0:T(8,128)(2,1)}, bf16[1,512,512]{2,1,0:T(8,128)(2,1)}, u32[]{:S(2)}, u32[]{:S(2)}) collective-permute-start(bf16[1,512,512]{2,1,0:T(8,128)(2,1)} %get-tuple-element.294), channel_id=1, source_target_pairs={{0,16},{8,24},{16,0},{24,8},{1,17},{9,25},{17,1},{25,9},{2,18},{10... | collective-permute-start | bytes 1572872 | tf_op jit(solution)/shard_map/ppermute | solution.py:1214
  176.0 53.5 %collective-permute-start.2 = (bf16[1,512,512]{2,1,0:T(8,128)(2,1)}, bf16[1,512,512]{2,1,0:T(8,128)(2,1)}, u32[]{:S(2)}, u32[]{:S(2)}) collective-permute-start(bf16[1,512,512]{2,1,0:T(8,128)(2,1)} %get-tuple-element.295), channel_id=1, source_target_pairs={{0,8},{8,0},{16,24},{24,16},{1,9},{9,1},{17,25},{25,17},{2,10},{10... | collective-permute-start | bytes 1572872 | tf_op jit(solution)/shard_map/ppermute | solution.py:1214
  185.0 11.2 copy-start.29
  185.2 10.9 copy-start.2
  190.1 13.8 %copy-start.9 = (f32[128,2048]{1,0:T(8,128)}, f32[128,2048]{1,0:T(8,128)S(1)}, u32[]{:S(2)}) copy-start(f32[128,2048]{1,0:T(8,128)S(1)} %get-tuple-element.507) | copy-start | bytes 3145732
  203.9 4.8 copy-start.31
  213.0 11.7 copy-start.20
  213.3 11.4 copy-start.21
  217.2 1.6 copy-start.4
  218.8 0.8 copy-start.17
  229.4 300.2 %copy-start = (bf16[128,2048]{1,0:T(8,128)(2,1)}, bf16[128,2048]{1,0:T(8,128)(2,1)S(1)}, u32[]{:S(2)}) copy-start(bf16[128,2048]{1,0:T(8,128)(2,1)S(1)} %multiply_convert_fusion.2.refs_0_) | copy-start | bytes 1572868
  419.4 62.3 %collective-permute-start.3 = (bf16[2,512,512]{2,1,0:T(8,128)(2,1)}, bf16[2,512,512]{2,1,0:T(8,128)(2,1)}, u32[]{:S(2)}, u32[]{:S(2)}) collective-permute-start(bf16[2,512,512]{2,1,0:T(8,128)(2,1)} %get-tuple-element.307), channel_id=1, source_target_pairs={{0,24},{8,16},{16,8},{24,0},{1,25},{9,17},{17,9},{25,1},{2,26},{10... | collective-permute-start | bytes 3145736 | tf_op jit(solution)/shard_map/ppermute | solution.py:1214
  421.0 89.4 %collective-permute-start.4 = (bf16[2,512,512]{2,1,0:T(8,128)(2,1)}, bf16[2,512,512]{2,1,0:T(8,128)(2,1)}, u32[]{:S(2)}, u32[]{:S(2)}) collective-permute-start(bf16[2,512,512]{2,1,0:T(8,128)(2,1)} %get-tuple-element.308), channel_id=1, source_target_pairs={{0,16},{8,24},{16,0},{24,8},{1,17},{9,25},{17,1},{25,9},{2,18},{10... | collective-permute-start | bytes 3145736 | tf_op jit(solution)/shard_map/ppermute | solution.py:1214
  423.4 87.0 %collective-permute-start.5 = (bf16[2,512,512]{2,1,0:T(8,128)(2,1)}, bf16[2,512,512]{2,1,0:T(8,128)(2,1)}, u32[]{:S(2)}, u32[]{:S(2)}) collective-permute-start(bf16[2,512,512]{2,1,0:T(8,128)(2,1)} %get-tuple-element.309), channel_id=1, source_target_pairs={{0,8},{8,0},{16,24},{24,16},{1,9},{9,1},{17,25},{25,17},{2,10},{10... | collective-permute-start | bytes 3145736 | tf_op jit(solution)/shard_map/ppermute | solution.py:1214
  423.9 104.2 %copy-start.19 = (bf16[128,2048]{1,0:T(8,128)(2,1)S(1)}, bf16[128,2048]{1,0:T(8,128)(2,1)}, u32[]{:S(2)}) copy-start(bf16[128,2048]{1,0:T(8,128)(2,1)} %fusion.53) | copy-start | bytes 1572868
  510.4 82.9 %collective-permute-start.6 = (bf16[1,512,512]{2,1,0:T(8,128)(2,1)}, bf16[1,512,512]{2,1,0:T(8,128)(2,1)}, u32[]{:S(2)}, u32[]{:S(2)}) collective-permute-start(bf16[1,512,512]{2,1,0:T(8,128)(2,1)} %get-tuple-element.319), channel_id=1, source_target_pairs={{0,24},{8,16},{16,8},{24,0},{1,25},{9,17},{17,9},{25,1},{2,26},{10... | collective-permute-start | bytes 1572872 | tf_op jit(solution)/shard_map/ppermute | solution.py:1214
  525.8 67.5 %collective-permute-start.7 = (bf16[1,512,512]{2,1,0:T(8,128)(2,1)}, bf16[1,512,512]{2,1,0:T(8,128)(2,1)}, u32[]{:S(2)}, u32[]{:S(2)}) collective-permute-start(bf16[1,512,512]{2,1,0:T(8,128)(2,1)} %get-tuple-element.320), channel_id=1, source_target_pairs={{0,16},{8,24},{16,0},{24,8},{1,17},{9,25},{17,1},{25,9},{2,18},{10... | collective-permute-start | bytes 1572872 | tf_op jit(solution)/shard_map/ppermute | solution.py:1214
  525.8 67.5 %collective-permute-start.8 = (bf16[1,512,512]{2,1,0:T(8,128)(2,1)}, bf16[1,512,512]{2,1,0:T(8,128)(2,1)}, u32[]{:S(2)}, u32[]{:S(2)}) collective-permute-start(bf16[1,512,512]{2,1,0:T(8,128)(2,1)} %get-tuple-element.321), channel_id=1, source_target_pairs={{0,8},{8,0},{16,24},{24,16},{1,9},{9,1},{17,25},{25,17},{2,10},{10... | collective-permute-start | bytes 1572872 | tf_op jit(solution)/shard_map/ppermute | solution.py:1214
  703.1 10.2 copy-start.1
  703.1 10.2 copy-start.11
  703.2 10.2 copy-start.30
  703.2 485.4 %collective-permute-start.10 = (bf16[2,512,512]{2,1,0:T(8,128)(2,1)}, bf16[2,512,512]{2,1,0:T(8,128)(2,1)}, u32[]{:S(2)}, u32[]{:S(2)}) collective-permute-start(bf16[2,512,512]{2,1,0:T(8,128)(2,1)} %get-tuple-element.345), channel_id=1, source_target_pairs={{0,16},{8,24},{16,0},{24,8},{1,17},{9,25},{17,1},{25,9},{2,18},{10... | collective-permute-start | bytes 3145736 | tf_op jit(solution)/shard_map/ppermute | solution.py:1214
  703.5 485.1 %collective-permute-start.11 = (bf16[2,512,512]{2,1,0:T(8,128)(2,1)}, bf16[2,512,512]{2,1,0:T(8,128)(2,1)}, u32[]{:S(2)}, u32[]{:S(2)}) collective-permute-start(bf16[2,512,512]{2,1,0:T(8,128)(2,1)} %get-tuple-element.346), channel_id=1, source_target_pairs={{0,8},{8,0},{16,24},{24,16},{1,9},{9,1},{17,25},{25,17},{2,10},{10... | collective-permute-start | bytes 3145736 | tf_op jit(solution)/shard_map/ppermute | solution.py:1214
  706.1 482.5 %collective-permute-start.9 = (bf16[2,512,512]{2,1,0:T(8,128)(2,1)}, bf16[2,512,512]{2,1,0:T(8,128)(2,1)}, u32[]{:S(2)}, u32[]{:S(2)}) collective-permute-start(bf16[2,512,512]{2,1,0:T(8,128)(2,1)} %get-tuple-element.344), channel_id=1, source_target_pairs={{0,24},{8,16},{16,8},{24,0},{1,25},{9,17},{17,9},{25,1},{2,26},{10... | collective-permute-start | bytes 3145736 | tf_op jit(solution)/shard_map/ppermute | solution.py:1214
  727.2 11.3 copy-start.7
  751.3 11.3 copy-start.13
  755.5 0.8 copy-start.14
  762.6 7.4 copy-start.5
  762.6 7.4 copy-start.8
  772.8 19.2 %copy-start.3 = (bf16[128,2048]{1,0:T(8,128)(2,1)S(1)}, bf16[128,2048]{1,0:T(8,128)(2,1)}, u32[]{:S(2)}) copy-start(bf16[128,2048]{1,0:T(8,128)(2,1)} %get-tuple-element.199) | copy-start | bytes 1572868 | tf_op jit(solution)/shard_map/cond
  782.3 16.3 %copy-start.15 = (bf16[128,2048]{0,1:T(8,128)(2,1)S(1)}, bf16[128,2048]{0,1:T(8,128)(2,1)}, u32[]{:S(2)}) copy-start(bf16[128,2048]{0,1:T(8,128)(2,1)} %copy-done.14) | copy-start | bytes 1572868 | tf_op jit(solution)/shard_map/cond
  798.6 5.6 copy-start.10
  798.6 5.6 copy-start.22
  798.6 6.9 copy-start.12
  804.2 7.1 copy-start.18
  811.3 8.0 copy-start.16
  1183.2 3.7 copy-start.24
  1183.2 4.5 copy-start.23
  1188.6 5.8 copy-start.28
  1188.6 6.6 copy-start.27
  1188.6 7.4 copy-start.26
  1188.6 8.2 copy-start.25

commit v12 on v10

--- a/solution.py
+++ b/solution.py
@@ -74,7 +74,7 @@
 
 def partners(z, n_dp):
     if n_dp == 4:
-        pairs = [z, (z + 2) % 4, 3 - z, z + 1 - 2 * (z % 2)]
+        pairs = [z, 3 - z, (z + 2) % 4, z + 1 - 2 * (z % 2)]
         return lambda k: pairs[k], lambda k: pairs[k]
     return lambda k: (z + k) % n_dp, lambda k: (z + n_dp - k) % n_dp
 
@@ -507,8 +507,6 @@
             ahead[rings[i]] += 1
     pairs = cuts(cut_in, cut_out)
     copies = exchange(n_dp, pairs, send_x, recv_x)
-    for copy in copies:
-        copy.start()
     own = [(source(z), target(z)) for source, target in pairs]
     bring, put = moves(own + puts(cut_in, cut_out), stages, local_y)
     for copy in bring:
@@ -610,7 +608,10 @@
                 )
 
     steps = (over_cores, pass_over, over_chips, over_planes, finish)
+    share = -(-len(copies) // n_items)
     for n in range(n_items + len(steps) - 1):
+        for copy in copies[n * share : (n + 1) * share]:
+            copy.start()
         for late, step in enumerate(steps):
             if 0 <= n - late < n_items:
                 step(n - late)
@@ -711,9 +712,9 @@
             dma((n, 3)),
             dma((n, 3)),
             dma((len(kinds), 2)),
-            dma((4, n_dp)),
-            dma((4, n_dp)),
-            dma((max(len(stages), 4), 2)),
+            dma((16, n_dp)),
+            dma((16, n_dp)),
+            dma((max(len(stages), 16), 2)),
             *[pltpu.VMEM(stage, jnp.bfloat16) for stage in stages],
         ],
         input_output_aliases=aliases,
@@ -1380,13 +1381,13 @@
     part_back = place_back(slots, grad_rows, grad_gates)
 
     def ways(low, high, at, ins, outs):
-        def pair(n):
+        def pair(e, n):
             return (
-                lambda to: ins[n].at[pl.ds(low, high - low), rows_at(to)],
-                lambda here: outs[n].at[pl.ds(low + at, high - low), :, columns_at(here)],
+                lambda to: ins[n].at[pl.ds(e, 1), rows_at(to)],
+                lambda here: outs[n].at[pl.ds(e + at, 1), :, columns_at(here)],
             )
 
-        return [pair(0), pair(1)]
+        return [pair(e, n) for e in range(low, high) for n in range(2)]
 
     def cut_grads(low, high, ins, outs):
         to, unused = partners(lax.axis_index("dp"), n_dp)
@@ -1433,7 +1434,8 @@
         8,
         (),
         stages(
-            *[back_third - back_beside] * 2, *[back_late - back_third] * (2 * (n_dp - 1))
+            *[1] * (2 * (back_third - back_beside)),
+            *[back_late - back_third] * (2 * (n_dp - 1)),
         ),
         lambda ins, outs: cut_grads(back_third, back_late, ins, outs[3:]),
         lambda ins, outs: place_out(ins[2], ins[3], outs[2]),
@@ -1514,7 +1516,7 @@
         n_expert,
         [part_out.reshape(n_dp, n_expert, count, D)]
         + [blocks_of(value) for value in weight_grads],
-        [2] + [1] * len(weight_grads),
+        [2, 1, 1, 1, 2 if rows_each > 16 else 1, 1],
         [gate_third, up_third, gate_soon, up_soon, gate_rest, up_rest],
         way_shapes,
         lambda ins, outs: ways(back_late, late, 0, ins[2:4], outs)

time: 1140 us -> 1100 us (0.965)
  Pallas kernels: 890 us -> 839 us
  waiting for transfers between devices: 8.61 us -> 28.7 us
    pallas_call x2, Pallas kernels: 386 us -> 357 us  [gather_call(): pl.pallas_call(functools.partial(gather_kernel, n_dp, n_expert, n, places...]
    pallas_call x2, Pallas kernels: 380 us -> 359 us  [scatter_call(): pl.pallas_call(functools.partial(scatter_kernel, n_dp, n_expert, count, i...]
    ppermute x12, waiting for transfers between devices: 8.61 us -> 28.7 us  [permuted(): got.append(lax.ppermute(piece, 'dp', paths))]
  transfers between devices with their start and end apart: 12 -> 12, of which waited for: 2 -> 1; matrix products, arithmetic and copies ran while one was open for 15% -> 16% of each run, Pallas kernels for 33% -> 32%
where the time goes in v12:
time: 1100 us; the launch traced here: 1090 us
  Pallas kernels  839 us (76%)
  matrix products  88.2 us (8%)
  local copies, waits for them, and re-layouts  59.1 us (5%)
  other arithmetic  38.4 us (3%)
  starting transfers between devices  29.3 us (3%)
  waiting for transfers between devices  28.7 us (3%)
    pallas_call x2, Pallas kernels, scatter_call(): pl.pallas_call(functools.partial(scatter_kernel, n_dp, n_expert, count, i...  359 us
    pallas_call x2, Pallas kernels, gather_call(): pl.pallas_call(functools.partial(gather_kernel, n_dp, n_expert, n, places...  357 us
    dot_general x21, matrix products, product(): return jnp.einsum(form, left, right, preferred_element_type=jnp.float32)  86.7 us
    pallas_call x2, Pallas kernels, expert_call(): pl.pallas_call(functools.partial(expert_kernel, steps, half, len(weights)...  78.9 us
    ppermute x12, starting transfers between devices, permuted(): got.append(lax.ppermute(piece, 'dp', paths))  29.3 us
    ppermute x12, waiting for transfers between devices, permuted(): got.append(lax.ppermute(piece, 'dp', paths))  28.7 us
    pallas_call x1, Pallas kernels, place_back(): pl.pallas_call(functools.partial(place_back_kernel, number), grid=(pairs,...  23.5 us
  transfers between devices with their start and end apart: 12, of which 1 were waited for; matrix products, arithmetic and copies ran while one was open for 16% of the time, Pallas kernels for 32%

profile of v12, /device:TPU:0, one launch (start us, length us, event | category | flops | bytes accessed | tf_op | source)
XLA Modules:
  0.0 1085.0 jit_solution(6572599745525904004)
XLA Ops:
  6.2 2.3 pad_maximum_fusion.2.refs_0_
  8.5 167.3 %shard_map.272 = (bf16[4,2048,2048]{2,1,0:T(8,128)(2,1)}, bf16[4096,256]{1,0:T(8,128)(2,1)}, bf16[8,2048,256]{2,1,0:T(8,128)(2,1)}, bf16[8,2048,256]{2,1,0:T(8,1...) custom-call(bf16[4,64,2048]{2,1,0:T(8,128)(2,1)} %pad_maximum_fusion, ...), custom_call_target="tpu_custom_call" | custom-call | tf_op jit(solution)/shard_map/pallas_call | solution.py:330
  176.0 4.3 collective-permute-start.2
  181.8 3.0 slice_reduce_fusion.4
  185.2 4.9 multiply_reduce_fusion.10
  190.1 6.0 multiply_reduce_fusion.9
  196.2 5.4 fusion.53
  201.6 2.3 slice.139
  203.9 1.5 multiply_bitcast_fusion
  207.1 1.6 fusion.78
  209.4 3.2 subtract_convert_fusion.2
  213.3 1.5 fusion.79
  214.8 2.4 fusion.76
  217.2 1.6 convolution_bitcast_fusion
  219.6 5.1 multiply_reduce_fusion.8
  224.7 1.6 constant_dynamic-slice_fusion.4
  229.5 190.0 %shard_map.273 = (bf16[4096,2048]{1,0:T(8,128)(2,1)}, bf16[4096,2048]{1,0:T(8,128)(2,1)}, bf16[8,2048,256]{2,1,0:T(8,128)(2,1)}, bf16[8,2048,256]{2,1,0:T(8,128)...) custom-call(bf16[128,2048]{1,0:T(8,128)(2,1)S(1)} %multiply_convert_, ...), custom_call_target="tpu_custom_call", output_to_operand_aliasing={{2}: (4, {}), {3}: (5, {})} | custom-call | tf_op jit(solution)/shard_map/pallas_call | solution.py:330
  419.5 1.6 collective-permute-start.3
  421.1 2.4 collective-permute-start.4
  423.9 55.3 %shard_map.274 = (bf16[8,768,2048]{2,1,0:T(8,128)(2,1)}, bf16[8,768,2048]{2,1,0:T(8,128)(2,1)}, bf16[8,768,128]{2,1,0:T(8,128)(2,1)}, bf16[6,2048,256]{2,1,0:T(8...) custom-call(s32[1]{0:T(128)} %bitcast.55.names_ref, ...), custom_call_target="tpu_custom_call" | custom-call | tf_op jit(solution)/shard_map/pallas_call | solution.py:1004
  479.2 2.5 dynamic-slice_bitcast_fusion
  481.8 28.7 %collective-permute-done.4.refs_2_ = bf16[2,512,512]{2,1,0:T(8,128)(2,1)} collective-permute-done((bf16[2,512,512]{2,1,0:T(8,128)(2,1)}, bf16[2,512,512]{2,1,0:T(8,128)(2,1)}, u32[]{:S(2)}, u32[]{:S(2)}) %collective-permute-start.4) | collective-permute-done | bytes 1048608 | tf_op jit(solution)/shard_map/ppermute | solution.py:1215
  510.5 15.4 %collective-permute-start.6 = (bf16[1,512,512]{2,1,0:T(8,128)(2,1)}, bf16[1,512,512]{2,1,0:T(8,128)(2,1)}, u32[]{:S(2)}, u32[]{:S(2)}) collective-permute-start(bf16[1,512,512]{2,1,0:T(8,128)(2,1)} %get-tuple-element.319), channel_id=1, source_target_pairs={{0,24},{8,16},{16,8},{24,0},{1,25},{9,17},{17,9},{25,1},{2,26},{10... | collective-permute-start | bytes 1572872 | tf_op jit(solution)/shard_map/ppermute | solution.py:1215
  531.4 1.7 slice.149
  533.1 2.3 slice.150
  536.2 23.6 %shard_map.275 = (bf16[8,768,2048]{2,1,0:T(8,128)(2,1)}, bf16[8,768,2048]{2,1,0:T(8,128)(2,1)}, bf16[8,768,128]{2,1,0:T(8,128)(2,1)}, bf16[2,2048,256]{2,1,0:T(8...) custom-call(s32[5]{0:T(128)} %stack.58.names_ref, ...), custom_call_target="tpu_custom_call", output_to_operand_aliasing={{0}: (9, {}), {1}: (10, {}), {2}: (11, {}), {5}: (12, {})} | custom-call | tf_op jit(solution)/shard_map/pallas_call | solution.py:1004
  559.8 23.5 %shard_map.276 = bf16[4096,2176]{1,0:T(8,128)(2,1)} custom-call(s32[16,8,256]{2,1,0:T(8,128)} %select_bitcast_fusion.refs_6_.slots_ref.refs_3_, bf16[8,768,2048]{2,1,0:T(8,128)(2,1)} %get-tuple-element.316.dx_ref, bf16[8,768,128]{2,1,0:T(8,128)(2,1)} %get-tuple-element.317.probs_ref), custom_call_target="tpu_custom_call" | custom-call | tf_op jit(solution)/shard_map/pallas_call | solution.py:1054
  583.3 124.7 %shard_map.277 = (f32[128,2176]{1,0:T(8,128)}, bf16[8,512,1024]{2,1,0:T(8,128)(2,1)}, bf16[8,512,1024]{2,1,0:T(8,128)(2,1)}, bf16[4096,2048]{1,0:T(8,128)(2,1)},...) custom-call(bf16[4,8,128,2176]{3,2,1,0:T(8,128)(2,1)} %bitcast.189, ...), custom_call_target="tpu_custom_call" | custom-call | tf_op jit(solution)/shard_map/pallas_call | solution.py:679
  708.2 1.4 collective-permute-start.11
  709.5 3.0 collective-permute-start.9
  713.5 1.7 slice.148
  716.1 2.1 pad_maximum_fusion.3.refs_0_
  718.2 106.2 %conditional.1 = (f32[128,2048]{1,0:T(8,128)}, bf16[4,8,64,2048]{3,2,1,0:T(8,128)(2,1)}, bf16[4,8,64,2048]{3,2,1,0:T(8,128)(2,1)}, bf16[4,8,64,2048]{3,2,1,0:T(8...) conditional(s32[]{:T(128)} %bitcast.61, () %tuple.37, ...), branch_computations={%region_10.11_spmd, %region_11.24_spmd} | conditional | flops 8961171456 | bytes 162147504 | solution.py:1509
  720.5 1.9 multiply_reduce_fusion
  722.3 1.4 subtract_add_fusion.1
  723.7 7.1 fusion.18
  732.1 1.9 multiply_reduce_fusion.5
  734.0 1.4 multiply_convert_fusion
  735.4 1.6 fusion.22
  737.0 1.4 fusion.23
  740.9 2.5 copy.121
  743.4 1.6 copy.120
  745.0 2.2 fusion.27
  747.2 2.7 subtract_convert_fusion.1
  749.9 2.3 pad_maximum_fusion.1
  752.1 2.5 copy.124
  754.7 1.6 copy.123
  756.2 2.2 fusion.25
  758.5 1.9 subtract_convert_fusion
  761.2 6.3 fusion.2
  767.5 7.4 fusion.12
  776.2 1.6 copy.126
  777.8 8.1 multiply_reduce_fusion.1
  787.2 1.3 concatenate.36
  788.5 1.9 constant_dynamic-update-slice_fusion.4
  793.9 3.0 copy.136
  796.9 6.6 convolution_convert_fusion
  803.5 5.6 convolution_convert_fusion.1
  810.5 5.8 convolution_convert_fusion.2
  817.4 6.8 convolution_convert_fusion.3
  824.4 233.8 %shard_map.278 = (f32[128,2048]{1,0:T(8,128)}, f32[64,2048]{1,0:T(8,128)}, f32[64,2048]{1,0:T(8,128)}, f32[64,2048]{1,0:T(8,128)}, f32[64,2048]{1,0:T(8,128)}, /...) custom-call(bf16[4,8,128,2048]{3,2,1,0:T(8,128)(2,1)} %bitcast.190, ...), custom_call_target="tpu_custom_call", output_to_operand_aliasing={{6}: (6, {}), {7}: (7, {})} | custom-call | tf_op jit(solution)/shard_map/pallas_call | solution.py:679
  1058.3 11.5 %shard_map.279 = (f32[8,512,1024]{2,1,0:T(8,128)}, f32[8,512,1024]{2,1,0:T(8,128)}) custom-call(bf16[8,512,1024]{2,1,0:T(8,128)(2,1)} %get-tuple-element.350.refs_0_, bf16[8,512,1024]{2,1,0:T(8,128)(2,1)} %get-tuple-element.351.refs_1_), custom_call_target="tpu_custom_call" | custom-call | tf_op jit(solution)/shard_map/pallas_call | solution.py:1078
  1069.8 3.7 shard_map.280
  1075.2 5.8 shard_map.281
  (165 shorter events, 43.9 us)
Async XLA Ops:
  175.8 9.0 copy-start.6
  175.8 53.7 %collective-permute-start = (bf16[1,512,512]{2,1,0:T(8,128)(2,1)}, bf16[1,512,512]{2,1,0:T(8,128)(2,1)}, u32[]{:S(2)}, u32[]{:S(2)}) collective-permute-start(bf16[1,512,512]{2,1,0:T(8,128)(2,1)} %get-tuple-element.293), channel_id=1, source_target_pairs={{0,24},{8,16},{16,8},{24,0},{1,25},{9,17},{17,9},{25,1},{2,26},{10... | collective-permute-start | bytes 1572872 | tf_op jit(solution)/shard_map/ppermute | solution.py:1215
  175.9 53.6 %collective-permute-start.1 = (bf16[1,512,512]{2,1,0:T(8,128)(2,1)}, bf16[1,512,512]{2,1,0:T(8,128)(2,1)}, u32[]{:S(2)}, u32[]{:S(2)}) collective-permute-start(bf16[1,512,512]{2,1,0:T(8,128)(2,1)} %get-tuple-element.294), channel_id=1, source_target_pairs={{0,16},{8,24},{16,0},{24,8},{1,17},{9,25},{17,1},{25,9},{2,18},{10... | collective-permute-start | bytes 1572872 | tf_op jit(solution)/shard_map/ppermute | solution.py:1215
  176.0 53.5 %collective-permute-start.2 = (bf16[1,512,512]{2,1,0:T(8,128)(2,1)}, bf16[1,512,512]{2,1,0:T(8,128)(2,1)}, u32[]{:S(2)}, u32[]{:S(2)}) collective-permute-start(bf16[1,512,512]{2,1,0:T(8,128)(2,1)} %get-tuple-element.295), channel_id=1, source_target_pairs={{0,8},{8,0},{16,24},{24,16},{1,9},{9,1},{17,25},{25,17},{2,10},{10... | collective-permute-start | bytes 1572872 | tf_op jit(solution)/shard_map/ppermute | solution.py:1215
  185.0 11.2 %copy-start.29 = (f32[128]{0:T(128)}, f32[128]{0:T(128)S(1)}, u32[]{:S(2)}) copy-start(f32[128]{0:T(128)S(1)} %multiply_reduce_fusion.11) | copy-start | bytes 1540
  185.2 10.9 %copy-start.2 = (bf16[128,2048]{1,0:T(8,128)(2,1)}, bf16[128,2048]{1,0:T(8,128)(2,1)S(1)}, u32[]{:S(2)}) copy-start(bf16[128,2048]{1,0:T(8,128)(2,1)S(1)} %multiply_convert_fusion.3) | copy-start | bytes 1572868
  190.1 13.8 %copy-start.9 = (f32[128,2048]{1,0:T(8,128)}, f32[128,2048]{1,0:T(8,128)S(1)}, u32[]{:S(2)}) copy-start(f32[128,2048]{1,0:T(8,128)S(1)} %get-tuple-element.507) | copy-start | bytes 3145732
  203.9 4.8 copy-start.31
  213.0 11.7 %copy-start.20 = (bf16[128,16,128]{2,0,1:T(8,128)(2,1)}, bf16[128,16,128]{2,0,1:T(8,128)(2,1)S(1)}, u32[]{:S(2)}) copy-start(bf16[128,16,128]{2,0,1:T(8,128)(2,1)S(1)} %pad_maximum_fusion.5) | copy-start | bytes 1572868
  213.3 11.4 %copy-start.21 = (bf16[128,16,128]{2,0,1:T(8,128)(2,1)}, bf16[128,16,128]{2,0,1:T(8,128)(2,1)S(1)}, u32[]{:S(2)}) copy-start(bf16[128,16,128]{2,0,1:T(8,128)(2,1)S(1)} %pad_maximum_fusion.4) | copy-start | bytes 1572868
  217.2 1.6 copy-start.4
  218.8 0.8 copy-start.17
  229.5 300.2 %copy-start = (bf16[128,2048]{1,0:T(8,128)(2,1)}, bf16[128,2048]{1,0:T(8,128)(2,1)S(1)}, u32[]{:S(2)}) copy-start(bf16[128,2048]{1,0:T(8,128)(2,1)S(1)} %multiply_convert_fusion.2.refs_0_) | copy-start | bytes 1572868
  419.5 62.3 %collective-permute-start.3 = (bf16[2,512,512]{2,1,0:T(8,128)(2,1)}, bf16[2,512,512]{2,1,0:T(8,128)(2,1)}, u32[]{:S(2)}, u32[]{:S(2)}) collective-permute-start(bf16[2,512,512]{2,1,0:T(8,128)(2,1)} %get-tuple-element.307), channel_id=1, source_target_pairs={{0,24},{8,16},{16,8},{24,0},{1,25},{9,17},{17,9},{25,1},{2,26},{10... | collective-permute-start | bytes 3145736 | tf_op jit(solution)/shard_map/ppermute | solution.py:1215
  421.1 89.4 %collective-permute-start.4 = (bf16[2,512,512]{2,1,0:T(8,128)(2,1)}, bf16[2,512,512]{2,1,0:T(8,128)(2,1)}, u32[]{:S(2)}, u32[]{:S(2)}) collective-permute-start(bf16[2,512,512]{2,1,0:T(8,128)(2,1)} %get-tuple-element.308), channel_id=1, source_target_pairs={{0,16},{8,24},{16,0},{24,8},{1,17},{9,25},{17,1},{25,9},{2,18},{10... | collective-permute-start | bytes 3145736 | tf_op jit(solution)/shard_map/ppermute | solution.py:1215
  423.5 87.0 %collective-permute-start.5 = (bf16[2,512,512]{2,1,0:T(8,128)(2,1)}, bf16[2,512,512]{2,1,0:T(8,128)(2,1)}, u32[]{:S(2)}, u32[]{:S(2)}) collective-permute-start(bf16[2,512,512]{2,1,0:T(8,128)(2,1)} %get-tuple-element.309), channel_id=1, source_target_pairs={{0,8},{8,0},{16,24},{24,16},{1,9},{9,1},{17,25},{25,17},{2,10},{10... | collective-permute-start | bytes 3145736 | tf_op jit(solution)/shard_map/ppermute | solution.py:1215
  423.9 104.2 %copy-start.19 = (bf16[128,2048]{1,0:T(8,128)(2,1)S(1)}, bf16[128,2048]{1,0:T(8,128)(2,1)}, u32[]{:S(2)}) copy-start(bf16[128,2048]{1,0:T(8,128)(2,1)} %fusion.53) | copy-start | bytes 1572868
  510.5 72.8 %collective-permute-start.6 = (bf16[1,512,512]{2,1,0:T(8,128)(2,1)}, bf16[1,512,512]{2,1,0:T(8,128)(2,1)}, u32[]{:S(2)}, u32[]{:S(2)}) collective-permute-start(bf16[1,512,512]{2,1,0:T(8,128)(2,1)} %get-tuple-element.319), channel_id=1, source_target_pairs={{0,24},{8,16},{16,8},{24,0},{1,25},{9,17},{17,9},{25,1},{2,26},{10... | collective-permute-start | bytes 1572872 | tf_op jit(solution)/shard_map/ppermute | solution.py:1215
  525.8 57.5 %collective-permute-start.7 = (bf16[1,512,512]{2,1,0:T(8,128)(2,1)}, bf16[1,512,512]{2,1,0:T(8,128)(2,1)}, u32[]{:S(2)}, u32[]{:S(2)}) collective-permute-start(bf16[1,512,512]{2,1,0:T(8,128)(2,1)} %get-tuple-element.320), channel_id=1, source_target_pairs={{0,16},{8,24},{16,0},{24,8},{1,17},{9,25},{17,1},{25,9},{2,18},{10... | collective-permute-start | bytes 1572872 | tf_op jit(solution)/shard_map/ppermute | solution.py:1215
  525.8 57.5 %collective-permute-start.8 = (bf16[1,512,512]{2,1,0:T(8,128)(2,1)}, bf16[1,512,512]{2,1,0:T(8,128)(2,1)}, u32[]{:S(2)}, u32[]{:S(2)}) collective-permute-start(bf16[1,512,512]{2,1,0:T(8,128)(2,1)} %get-tuple-element.321), channel_id=1, source_target_pairs={{0,8},{8,0},{16,24},{24,16},{1,9},{9,1},{17,25},{25,17},{2,10},{10... | collective-permute-start | bytes 1572872 | tf_op jit(solution)/shard_map/ppermute | solution.py:1215
  708.0 10.2 copy-start.1
  708.0 10.2 copy-start.11
  708.1 10.2 copy-start.30
  708.1 367.1 %collective-permute-start.10 = (bf16[2,512,512]{2,1,0:T(8,128)(2,1)}, bf16[2,512,512]{2,1,0:T(8,128)(2,1)}, u32[]{:S(2)}, u32[]{:S(2)}) collective-permute-start(bf16[2,512,512]{2,1,0:T(8,128)(2,1)} %get-tuple-element.345), channel_id=1, source_target_pairs={{0,16},{8,24},{16,0},{24,8},{1,17},{9,25},{17,1},{25,9},{2,18},{10... | collective-permute-start | bytes 3145736 | tf_op jit(solution)/shard_map/ppermute | solution.py:1215
  708.2 367.0 %collective-permute-start.11 = (bf16[2,512,512]{2,1,0:T(8,128)(2,1)}, bf16[2,512,512]{2,1,0:T(8,128)(2,1)}, u32[]{:S(2)}, u32[]{:S(2)}) collective-permute-start(bf16[2,512,512]{2,1,0:T(8,128)(2,1)} %get-tuple-element.346), channel_id=1, source_target_pairs={{0,8},{8,0},{16,24},{24,16},{1,9},{9,1},{17,25},{25,17},{2,10},{10... | collective-permute-start | bytes 3145736 | tf_op jit(solution)/shard_map/ppermute | solution.py:1215
  709.5 365.6 %collective-permute-start.9 = (bf16[2,512,512]{2,1,0:T(8,128)(2,1)}, bf16[2,512,512]{2,1,0:T(8,128)(2,1)}, u32[]{:S(2)}, u32[]{:S(2)}) collective-permute-start(bf16[2,512,512]{2,1,0:T(8,128)(2,1)} %get-tuple-element.344), channel_id=1, source_target_pairs={{0,24},{8,16},{16,8},{24,0},{1,25},{9,17},{17,9},{25,1},{2,26},{10... | collective-permute-start | bytes 3145736 | tf_op jit(solution)/shard_map/ppermute | solution.py:1215
  732.1 11.3 %copy-start.7 = (bf16[128,2048]{0,1:T(8,128)(2,1)}, bf16[128,2048]{0,1:T(8,128)(2,1)S(1)}, u32[]{:S(2)}) copy-start(bf16[128,2048]{0,1:T(8,128)(2,1)S(1)} %copy.142) | copy-start | bytes 1572868 | tf_op jit(solution)/shard_map/cond
  756.2 11.3 %copy-start.13 = (bf16[128,2048]{0,1:T(8,128)(2,1)S(1)}, bf16[128,2048]{0,1:T(8,128)(2,1)}, u32[]{:S(2)}) copy-start(bf16[128,2048]{0,1:T(8,128)(2,1)} %subtract_convert_fusion.1) | copy-start | bytes 1572868 | tf_op jit(solution)/shard_map/cond
  760.4 0.8 copy-start.14
  767.5 7.4 copy-start.5
  767.5 7.4 copy-start.8
  777.8 19.2 %copy-start.3 = (bf16[128,2048]{1,0:T(8,128)(2,1)S(1)}, bf16[128,2048]{1,0:T(8,128)(2,1)}, u32[]{:S(2)}) copy-start(bf16[128,2048]{1,0:T(8,128)(2,1)} %get-tuple-element.199) | copy-start | bytes 1572868 | tf_op jit(solution)/shard_map/cond
  787.2 16.3 %copy-start.15 = (bf16[128,2048]{0,1:T(8,128)(2,1)S(1)}, bf16[128,2048]{0,1:T(8,128)(2,1)}, u32[]{:S(2)}) copy-start(bf16[128,2048]{0,1:T(8,128)(2,1)} %copy-done.14) | copy-start | bytes 1572868 | tf_op jit(solution)/shard_map/cond
  803.5 5.6 copy-start.10
  803.5 5.6 copy-start.22
  803.5 6.9 copy-start.12
  809.1 7.1 copy-start.18
  816.2 8.0 copy-start.16
  1069.8 3.7 copy-start.24
  1069.8 4.5 copy-start.23
  1075.2 5.8 copy-start.28
  1075.2 6.6 copy-start.27
  1075.2 7.4 copy-start.26
  1075.2 8.2 copy-start.25

commit v13 on v12

--- a/solution.py
+++ b/solution.py
@@ -1061,6 +1061,60 @@
     )(slots, dx, probs)
 
 
+def through_kernel(count, *refs):
+    lefts, weight_ref, out_ref = refs[:count], refs[count], refs[count + 1]
+    for i in range(count):
+
+        @pl.when(pl.program_id(1) == i)
+        def _():
+            part = dot(lefts[i][...], weight_ref[0], (1, 1))
+            if i:
+                part = part + out_ref[...]
+            out_ref[...] = part
+
+
+def through(lefts, weights, first):
+    count, (rows, depth) = len(lefts), lefts[0].shape
+    piece = 512
+    return pl.pallas_call(
+        functools.partial(through_kernel, count),
+        grid=(depth // piece, count),
+        in_specs=[
+            *[pl.BlockSpec((rows, depth), lambda c, i: (0, 0))] * count,
+            pl.BlockSpec((1, piece, depth), lambda c, i: (i + first, c, 0)),
+        ],
+        out_specs=pl.BlockSpec((rows, piece), lambda c, i: (0, c)),
+        out_shape=jax.ShapeDtypeStruct((rows, depth), jnp.float32),
+        compiler_params=pltpu.CompilerParams(vmem_limit_bytes=BIG),
+    )(*lefts, weights)
+
+
+def outer_kernel(which, n_left, *refs):
+    lefts, rights = refs[:n_left], refs[n_left : n_left + len(which)]
+    piece = 512
+    for left, right, out_ref in zip(which, rights, refs[n_left + len(which) :]):
+        for at in range(0, out_ref.shape[1], piece):
+            out_ref[:, at : at + piece] = dot(
+                lefts[left][...], right[:, at : at + piece], (0, 0)
+            ).astype(out_ref.dtype)
+
+
+def outer(lefts, rights, which):
+    rows, depth = lefts[0].shape
+    piece = 256
+    return pl.pallas_call(
+        functools.partial(outer_kernel, which, len(lefts)),
+        grid=(depth // piece,),
+        in_specs=[
+            *[pl.BlockSpec((rows, piece), lambda c: (0, c))] * len(lefts),
+            *[pl.BlockSpec((rows, depth), lambda c: (0, 0))] * len(rights),
+        ],
+        out_specs=[pl.BlockSpec((piece, depth), lambda c: (c, 0))] * len(rights),
+        out_shape=[jax.ShapeDtypeStruct((depth, depth), jnp.bfloat16)] * len(rights),
+        compiler_params=pltpu.CompilerParams(vmem_limit_bytes=BIG),
+    )(*lefts, *rights)
+
+
 def widen_kernel(*refs):
     half = len(refs) // 2
     for source, target in zip(refs[:half], refs[half:]):
@@ -1443,7 +1497,6 @@
     later_pieces = permuted(later_pieces)
 
     def attention_back(back):
-        query_weight, key_weight, value_weight, out_weight = (weights_all[i] for i in range(4))
         grad_final = cotangent.astype(jnp.float32)
         grad_mlp = back[:, :D]
         grad_router_probs = back[:, D : D + experts_all] + back[:, D + experts_all :]
@@ -1451,14 +1504,15 @@
             grad_router_probs - jnp.sum(router * grad_router_probs, axis=1, keepdims=True)
         )
         grad_logits_low = grad_logits.astype(bf16)
-        grad_router_full = product(mlp_low, grad_logits_low, "td,te->de")
+        grad_router_full = product(
+            mlp_low, jnp.pad(grad_logits_low, ((0, 0), (0, width - experts_all))), "td,te->de"
+        )
         grad_mlp = grad_mlp + product(grad_logits_low, router_weight, "te,de->td")
         grad_middle_part, grad_mlp_gain = rms_backward(middle, mlp_inverse, mlp_gain, grad_mlp)
         grad_middle = grad_final + grad_middle_part
         grad_branch_low = grad_middle.astype(bf16)
-        grad_out_full = product(attended_low, grad_branch_low, "td,te->de")
         grad_attended = (
-            product(grad_branch_low, out_weight, "te,de->td").astype(bf16).reshape(count, HEADS, HD)
+            through([grad_branch_low], weights_all, 3).astype(bf16).reshape(count, HEADS, HD)
         )
         grad_weights = product(grad_attended, value_heads, "qhd,khd->hqk")
         grad_scores = probs * (grad_weights - jnp.sum(probs * grad_weights, axis=-1, keepdims=True))
@@ -1476,47 +1530,41 @@
         )
         grad_query_low = grad_query_raw.astype(bf16)
         grad_key_low = grad_key_raw.astype(bf16)
-        grad_query_full = product(normed_low, grad_query_low, "td,te->de")
-        grad_key_full = product(normed_low, grad_key_low, "td,te->de")
-        grad_value_full = product(normed_low, grad_value_low, "td,te->de")
-        grad_normed = (
-            product(grad_query_low, query_weight, "te,de->td")
-            + product(grad_key_low, key_weight, "te,de->td")
-            + product(grad_value_low, value_weight, "te,de->td")
-        )
+        full_grads = outer(
+            [attended_low, normed_low],
+            [grad_branch_low, grad_value_low, grad_key_low, grad_query_low],
+            (0, 1, 1, 1),
+        )
+        grad_normed = through([grad_query_low, grad_key_low, grad_value_low], weights_all, 0)
         grad_inputs_part, grad_attn_gain = rms_backward(inputs, attn_inverse, attn_gain, grad_normed)
         grad_inputs = grad_middle + grad_inputs_part
 
-        small_grads = jnp.concatenate(
-            [
-                grad_router_full,
-                grad_attn_gain[:, None],
-                grad_query_gain[:, None],
-                grad_key_gain[:, None],
-                grad_mlp_gain[:, None],
-                jnp.zeros((D, width - experts_all - 4), jnp.float32),
-            ],
-            axis=1,
-        )
-        grads = (grad_out_full, grad_value_full, grad_key_full, grad_query_full, small_grads)
-        return grad_inputs, *[one.astype(bf16) for one in grads]
+        gain_grads = jnp.stack([grad_attn_gain, grad_query_gain, grad_key_gain, grad_mlp_gain])
+        gain_grads = jnp.transpose(gain_grads.reshape(4, groups, rows_each), (1, 0, 2))
+        gain_grads = jnp.pad(gain_grads, ((0, 0), (0, 12), (0, width - rows_each)))
+        return (
+            grad_inputs,
+            *full_grads,
+            grad_router_full.astype(bf16),
+            gain_grads.astype(bf16).reshape(groups * 16, width),
+        )
 
     def unreached(back):
-        shapes = [(count, D)] + [(D, D)] * 4 + [(D, width)]
-        kinds = [jnp.float32] + [bf16] * 5
+        shapes = [(count, D)] + [(D, D)] * 4 + [(D, width), (groups * 16, width)]
+        kinds = [jnp.float32] + [bf16] * 6
         return tuple(jnp.zeros(shape, kind) for shape, kind in zip(shapes, kinds))
 
     grad_inputs, *weight_grads = lax.cond(lengths[0, 0] > 0, attention_back, unreached, back)
 
     def blocks_of(value):
-        return value.reshape(n_dp, n_expert, rows_each, -1)
+        return value.reshape(n_dp, n_expert, -1, value.shape[1])
 
     sums, (gate_back, up_back) = scatter_all(
         n_dp,
         n_expert,
         [part_out.reshape(n_dp, n_expert, count, D)]
         + [blocks_of(value) for value in weight_grads],
-        [2, 1, 1, 1, 2 if rows_each > 16 else 1, 1],
+        [2, 1, 1, 1, 2 if rows_each > 16 else 1, 1, 1],
         [gate_third, up_third, gate_soon, up_soon, gate_rest, up_rest],
         way_shapes,
         lambda ins, outs: ways(back_late, late, 0, ins[2:4], outs)
@@ -1525,10 +1573,10 @@
         ((0, 0), (1, 1)),
         [],
     )
-    summed, grad_out_part, grad_value_part, grad_key_part, grad_query_part, small_part = sums
+    summed, grad_out_part, grad_value_part, grad_key_part, grad_query_part, router_part, small = sums
     output = (middle + summed).astype(bf16)
-    grad_router_part = small_part[:, :experts_all]
-    gain_parts = [small_part[:, experts_all + i] for i in range(4)]
+    grad_router_part = router_part[:, :experts_all]
+    gain_parts = [small[i, :rows_each] for i in range(4)]
     widened = widen([(back_beside, back_third), (back_late, number)], [gate_back, up_back])
     offsets = jnp.stack([from_plane(k) * part for k in range(n_dp)])
     for low, high, others in (

time: 1100 us -> 1110 us (level)
  Pallas kernels: 839 us -> 908 us
  matrix products: 88.2 us -> 31.8 us
    dot_general x21 -> x13, matrix products: 86.7 us -> 30.3 us  [product(): return jnp.einsum(form, left, right, preferred_element_type=jnp.float32)]
    pallas_call x0 -> x3, Pallas kernels: none -> 38.2 us  [the longest x2 24.5 us: through(): pl.pallas_call(functools.partial(through_kernel, count), grid=(depth // p...]
    pallas_call x2, Pallas kernels: 359 us -> 389 us  [scatter_call(): pl.pallas_call(functools.partial(scatter_kernel, n_dp, n_expert, count, i...]
  transfers between devices with their start and end apart: 12 -> 12, of which waited for: 1 -> 1; matrix products, arithmetic and copies ran while one was open for 16% -> 10% of each run, Pallas kernels for 32% -> 38%
where the time goes in v13:
time: 1110 us; the launch traced here: 1090 us
  Pallas kernels  908 us (82%)
  local copies, waits for them, and re-layouts  52.7 us (5%)
  other arithmetic  41 us (4%)
  matrix products  31.8 us (3%)
  starting transfers between devices  29.3 us (3%)
  waiting for transfers between devices  28.4 us (3%)
    pallas_call x2, Pallas kernels, scatter_call(): pl.pallas_call(functools.partial(scatter_kernel, n_dp, n_expert, count, i...  389 us
    pallas_call x2, Pallas kernels, gather_call(): pl.pallas_call(functools.partial(gather_kernel, n_dp, n_expert, n, places...  357 us
    pallas_call x2, Pallas kernels, expert_call(): pl.pallas_call(functools.partial(expert_kernel, steps, half, len(weights)...  79 us
    dot_general x13, matrix products, product(): return jnp.einsum(form, left, right, preferred_element_type=jnp.float32)  30.3 us
    ppermute x12, starting transfers between devices, permuted(): got.append(lax.ppermute(piece, 'dp', paths))  29.3 us
    ppermute x12, waiting for transfers between devices, permuted(): got.append(lax.ppermute(piece, 'dp', paths))  28.4 us
    pallas_call x2, Pallas kernels, through(): pl.pallas_call(functools.partial(through_kernel, count), grid=(depth // p...  24.5 us
    pallas_call x1, Pallas kernels, place_back(): pl.pallas_call(functools.partial(place_back_kernel, number), grid=(pairs,...  23.5 us
  transfers between devices with their start and end apart: 12, of which 1 were waited for; matrix products, arithmetic and copies ran while one was open for 10% of the time, Pallas kernels for 38%

profile of v13, /device:TPU:0, one launch (start us, length us, event | category | flops | bytes accessed | tf_op | source)
XLA Modules:
  0.0 1093.2 jit_solution(2452203872296868544)
XLA Ops:
  6.2 2.3 pad_maximum_fusion.2.refs_0_
  8.5 167.3 %shard_map.272 = (bf16[4,2048,2048]{2,1,0:T(8,128)(2,1)}, bf16[4096,256]{1,0:T(8,128)(2,1)}, bf16[8,2048,256]{2,1,0:T(8,128)(2,1)}, bf16[8,2048,256]{2,1,0:T(8,1...) custom-call(bf16[4,64,2048]{2,1,0:T(8,128)(2,1)} %pad_maximum_fusion, ...), custom_call_target="tpu_custom_call" | custom-call | tf_op jit(solution)/shard_map/pallas_call | solution.py:330
  176.0 4.3 collective-permute-start.2
  180.3 1.3 slice.102
  181.8 3.0 slice_reduce_fusion
  185.2 4.9 multiply_reduce_fusion.12
  190.2 5.1 multiply_reduce_fusion.11
  195.3 5.8 fusion.28
  201.1 2.3 slice.116
  203.9 1.3 fusion.53
  205.4 1.6 fusion.54
  207.7 3.2 subtract_convert_fusion.2
  211.6 1.5 fusion.55
  213.1 2.4 fusion.52
  215.5 1.6 convolution_convert_fusion.2
  217.9 5.1 multiply_reduce_fusion.10
  223.0 1.6 constant_dynamic-slice_fusion.4
  227.8 190.0 %shard_map.273 = (bf16[4096,2048]{1,0:T(8,128)(2,1)}, bf16[4096,2048]{1,0:T(8,128)(2,1)}, bf16[8,2048,256]{2,1,0:T(8,128)(2,1)}, bf16[8,2048,256]{2,1,0:T(8,128)...) custom-call(bf16[128,2048]{1,0:T(8,128)(2,1)S(1)} %multiply_convert_, ...), custom_call_target="tpu_custom_call", output_to_operand_aliasing={{2}: (4, {}), {3}: (5, {})} | custom-call | tf_op jit(solution)/shard_map/pallas_call | solution.py:330
  417.8 1.6 collective-permute-start.3
  419.3 2.4 collective-permute-start.4
  422.6 55.3 %shard_map.274 = (bf16[8,768,2048]{2,1,0:T(8,128)(2,1)}, bf16[8,768,2048]{2,1,0:T(8,128)(2,1)}, bf16[8,768,128]{2,1,0:T(8,128)(2,1)}, bf16[6,2048,256]{2,1,0:T(8...) custom-call(s32[1]{0:T(128)} %bitcast.60.names_ref, ...), custom_call_target="tpu_custom_call" | custom-call | tf_op jit(solution)/shard_map/pallas_call | solution.py:1004
  477.9 2.4 dynamic-slice_bitcast_fusion
  480.4 28.4 %collective-permute-done.4.refs_2_ = bf16[2,512,512]{2,1,0:T(8,128)(2,1)} collective-permute-done((bf16[2,512,512]{2,1,0:T(8,128)(2,1)}, bf16[2,512,512]{2,1,0:T(8,128)(2,1)}, u32[]{:S(2)}, u32[]{:S(2)}) %collective-permute-start.4) | collective-permute-done | bytes 1048608 | tf_op jit(solution)/shard_map/ppermute | solution.py:1269
  508.7 15.4 %collective-permute-start.6 = (bf16[1,512,512]{2,1,0:T(8,128)(2,1)}, bf16[1,512,512]{2,1,0:T(8,128)(2,1)}, u32[]{:S(2)}, u32[]{:S(2)}) collective-permute-start(bf16[1,512,512]{2,1,0:T(8,128)(2,1)} %get-tuple-element.211), channel_id=1, source_target_pairs={{0,24},{8,16},{16,8},{24,0},{1,25},{9,17},{17,9},{25,1},{2,26},{10... | collective-permute-start | bytes 1572872 | tf_op jit(solution)/shard_map/ppermute | solution.py:1269
  528.0 1.3 slice.128
  529.3 1.7 slice.126
  531.0 2.3 slice.127
  533.3 1.7 slice.125
  536.7 23.7 %shard_map.275 = (bf16[8,768,2048]{2,1,0:T(8,128)(2,1)}, bf16[8,768,2048]{2,1,0:T(8,128)(2,1)}, bf16[8,768,128]{2,1,0:T(8,128)(2,1)}, bf16[2,2048,256]{2,1,0:T(8...) custom-call(s32[5]{0:T(128)} %stack.73.names_ref, ...), custom_call_target="tpu_custom_call", output_to_operand_aliasing={{0}: (9, {}), {1}: (10, {}), {2}: (11, {}), {5}: (12, {})} | custom-call | tf_op jit(solution)/shard_map/pallas_call | solution.py:1004
  560.4 23.5 %shard_map.276 = bf16[4096,2176]{1,0:T(8,128)(2,1)} custom-call(s32[16,8,256]{2,1,0:T(8,128)} %select_bitcast_fusion.refs_6_.slots_ref.refs_3_, bf16[8,768,2048]{2,1,0:T(8,128)(2,1)} %get-tuple-element.208.dx_ref, bf16[8,768,128]{2,1,0:T(8,128)(2,1)} %get-tuple-element.209.probs_ref), custom_call_target="tpu_custom_call" | custom-call | tf_op jit(solution)/shard_map/pallas_call | solution.py:1054
  584.0 124.7 %shard_map.277 = (f32[128,2176]{1,0:T(8,128)}, bf16[8,512,1024]{2,1,0:T(8,128)(2,1)}, bf16[8,512,1024]{2,1,0:T(8,128)(2,1)}, bf16[4096,2048]{1,0:T(8,128)(2,1)},...) custom-call(bf16[4,8,128,2176]{3,2,1,0:T(8,128)(2,1)} %bitcast.160, ...), custom_call_target="tpu_custom_call" | custom-call | tf_op jit(solution)/shard_map/pallas_call | solution.py:679
  708.7 1.4 collective-permute-start.11
  710.1 3.0 collective-permute-start.9
  714.9 2.3 pad_maximum_fusion.3.refs_0_
  717.2 83.9 %conditional.1 = (f32[128,2048]{1,0:T(8,128)}, bf16[4,8,64,2048]{3,2,1,0:T(8,128)(2,1)}, bf16[4,8,64,2048]{3,2,1,0:T(8,128)(2,1)}, bf16[4,8,64,2048]{3,2,1,0:T(8...) conditional(s32[]{:T(128)} %bitcast.66, () %tuple.36, ...), branch_computations={%region_12.13_spmd, %region_13.24_spmd} | conditional | flops 387291904 | bytes 72241856 | solution.py:1557
  717.5 1.1 multiply_reduce_fusion.9
  719.7 1.6 copy.127
  721.2 1.8 multiply_reduce_fusion
  723.0 2.6 fusion.51
  725.6 6.8 branch_1_fun.3
  732.4 1.3 convert_element_type.76
  734.0 1.3 multiply_reduce_fusion.7
  735.6 1.6 fusion.1
  737.1 1.5 fusion.2
  738.9 1.3 multiply_subtract_fusion
  741.2 2.6 copy.145
  743.9 2.3 pad_maximum_fusion
  746.2 2.5 copy.144
  748.7 1.6 copy.132
  750.3 1.6 copy.130
  751.8 2.5 multiply_reduce_fusion.1
  754.3 2.6 subtract_convert_fusion.refs_1_.refs_4_
  757.0 2.3 subtract_convert_fusion.1.refs_0_.refs_5_
  760.7 2.1 copy.135.refs_0_
  762.8 13.7 %branch_1_fun.5 = (bf16[2048,2048]{1,0:T(8,128)(2,1)}, bf16[2048,2048]{1,0:T(8,128)(2,1)}, bf16[2048,2048]{1,0:T(8,128)(2,1)}, bf16[2048,2048]{1,0:T(8,128)(2,1)}) custom-call(bf16[128,2048]{1,0:T(8,128)(2,1)} %copy.135.refs_0_, bf16[128,2048]{1,0:T(8,128)(2,1)} %get-tuple-element.85.refs_1_, bf16[128,2048]{1,0:T(8,128)(2,1)} %get-tuple-element.366.refs_0_.refs_2_, ...), custom_call_target="tpu_custom_call" | custom-call | tf_op jit(solution)/shard_map/cond/branch_1_fun/pallas_call | solution.py:1105
  776.5 17.6 %branch_1_fun.4 = f32[128,2048]{1,0:T(8,128)} custom-call(bf16[128,2048]{1,0:T(8,128)(2,1)} %subtract_convert_fusion.1.refs_0_.refs_5_, bf16[128,2048]{1,0:T(8,128)(2,1)} %subtract_convert_fusion.refs_1_.refs_4_, bf16[128,2048]{1,0:T(8,128)(2,1)} %copy.146.refs_2_.refs_3_, bf16[4,2048,2048]{2,1,0:T(8,128)(2,1)} %get-tuple-element.70.refs_1_.refs_3_), custom_call_target="tpu_custom_call" | custom-call | tf_op jit(solution)/shard_map/cond/branch_1_fun/pallas_call | solution.py:1079
  794.2 1.6 copy.134
  795.7 1.5 multiply_reduce_fusion.3
  797.7 2.8 subtract_add_fusion
  801.1 264.6 %shard_map.278 = (f32[128,2048]{1,0:T(8,128)}, f32[64,2048]{1,0:T(8,128)}, f32[64,2048]{1,0:T(8,128)}, f32[64,2048]{1,0:T(8,128)}, f32[64,2048]{1,0:T(8,128)}, /...) custom-call(bf16[4,8,128,2048]{3,2,1,0:T(8,128)(2,1)} %bitcast.161, ...), custom_call_target="tpu_custom_call", output_to_operand_aliasing={{7}: (7, {}), {8}: (8, {})} | custom-call | tf_op jit(solution)/shard_map/pallas_call | solution.py:679
  1065.7 11.5 %shard_map.279 = (f32[8,512,1024]{2,1,0:T(8,128)}, f32[8,512,1024]{2,1,0:T(8,128)}) custom-call(bf16[8,512,1024]{2,1,0:T(8,128)(2,1)} %get-tuple-element.244.refs_0_, bf16[8,512,1024]{2,1,0:T(8,128)(2,1)} %get-tuple-element.245.refs_1_), custom_call_target="tpu_custom_call" | custom-call | tf_op jit(solution)/shard_map/pallas_call | solution.py:1132
  1077.2 3.7 shard_map.280
  1080.9 1.3 slice_bitcast_fusion
  1083.2 5.8 shard_map.281
  (146 shorter events, 30.7 us)
Async XLA Ops:
  175.8 9.0 copy-start.9
  175.8 52.0 %collective-permute-start = (bf16[1,512,512]{2,1,0:T(8,128)(2,1)}, bf16[1,512,512]{2,1,0:T(8,128)(2,1)}, u32[]{:S(2)}, u32[]{:S(2)}) collective-permute-start(bf16[1,512,512]{2,1,0:T(8,128)(2,1)} %get-tuple-element.185), channel_id=1, source_target_pairs={{0,24},{8,16},{16,8},{24,0},{1,25},{9,17},{17,9},{25,1},{2,26},{10... | collective-permute-start | bytes 1572872 | tf_op jit(solution)/shard_map/ppermute | solution.py:1269
  175.9 51.9 %collective-permute-start.1 = (bf16[1,512,512]{2,1,0:T(8,128)(2,1)}, bf16[1,512,512]{2,1,0:T(8,128)(2,1)}, u32[]{:S(2)}, u32[]{:S(2)}) collective-permute-start(bf16[1,512,512]{2,1,0:T(8,128)(2,1)} %get-tuple-element.186), channel_id=1, source_target_pairs={{0,16},{8,24},{16,0},{24,8},{1,17},{9,25},{17,1},{25,9},{2,18},{10... | collective-permute-start | bytes 1572872 | tf_op jit(solution)/shard_map/ppermute | solution.py:1269
  176.0 51.8 %collective-permute-start.2 = (bf16[1,512,512]{2,1,0:T(8,128)(2,1)}, bf16[1,512,512]{2,1,0:T(8,128)(2,1)}, u32[]{:S(2)}, u32[]{:S(2)}) collective-permute-start(bf16[1,512,512]{2,1,0:T(8,128)(2,1)} %get-tuple-element.187), channel_id=1, source_target_pairs={{0,8},{8,0},{16,24},{24,16},{1,9},{9,1},{17,25},{25,17},{2,10},{10... | collective-permute-start | bytes 1572872 | tf_op jit(solution)/shard_map/ppermute | solution.py:1269
  185.0 10.2 copy-start.21
  185.2 10.1 copy-start.14
  190.2 13.2 %copy-start.2 = (f32[128,2048]{1,0:T(8,128)}, f32[128,2048]{1,0:T(8,128)S(1)}, u32[]{:S(2)}) copy-start(f32[128,2048]{1,0:T(8,128)S(1)} %get-tuple-element.409) | copy-start | bytes 3145732
  195.3 8.4 copy-start.4
  203.4 3.6 copy-start.23
  211.2 11.7 %copy-start.12 = (bf16[128,16,128]{2,0,1:T(8,128)(2,1)}, bf16[128,16,128]{2,0,1:T(8,128)(2,1)S(1)}, u32[]{:S(2)}) copy-start(bf16[128,16,128]{2,0,1:T(8,128)(2,1)S(1)} %pad_maximum_fusion.5) | copy-start | bytes 1572868
  211.6 11.4 %copy-start.13 = (bf16[128,16,128]{2,0,1:T(8,128)(2,1)}, bf16[128,16,128]{2,0,1:T(8,128)(2,1)S(1)}, u32[]{:S(2)}) copy-start(bf16[128,16,128]{2,0,1:T(8,128)(2,1)S(1)} %pad_maximum_fusion.4) | copy-start | bytes 1572868
  215.4 1.6 copy-start.7
  217.0 0.8 copy-start.10
  227.8 194.5 %copy-start.5 = (bf16[128,2048]{1,0:T(8,128)(2,1)}, bf16[128,2048]{1,0:T(8,128)(2,1)S(1)}, u32[]{:S(2)}) copy-start(bf16[128,2048]{1,0:T(8,128)(2,1)S(1)} %multiply_convert_fusion.2.refs_0_) | copy-start | bytes 1572868
  417.8 62.6 %collective-permute-start.3 = (bf16[2,512,512]{2,1,0:T(8,128)(2,1)}, bf16[2,512,512]{2,1,0:T(8,128)(2,1)}, u32[]{:S(2)}, u32[]{:S(2)}) collective-permute-start(bf16[2,512,512]{2,1,0:T(8,128)(2,1)} %get-tuple-element.199), channel_id=1, source_target_pairs={{0,24},{8,16},{16,8},{24,0},{1,25},{9,17},{17,9},{25,1},{2,26},{10... | collective-permute-start | bytes 3145736 | tf_op jit(solution)/shard_map/ppermute | solution.py:1269
  419.3 89.4 %collective-permute-start.4 = (bf16[2,512,512]{2,1,0:T(8,128)(2,1)}, bf16[2,512,512]{2,1,0:T(8,128)(2,1)}, u32[]{:S(2)}, u32[]{:S(2)}) collective-permute-start(bf16[2,512,512]{2,1,0:T(8,128)(2,1)} %get-tuple-element.200), channel_id=1, source_target_pairs={{0,16},{8,24},{16,0},{24,8},{1,17},{9,25},{17,1},{25,9},{2,18},{10... | collective-permute-start | bytes 3145736 | tf_op jit(solution)/shard_map/ppermute | solution.py:1269
  421.8 87.0 %collective-permute-start.5 = (bf16[2,512,512]{2,1,0:T(8,128)(2,1)}, bf16[2,512,512]{2,1,0:T(8,128)(2,1)}, u32[]{:S(2)}, u32[]{:S(2)}) collective-permute-start(bf16[2,512,512]{2,1,0:T(8,128)(2,1)} %get-tuple-element.201), channel_id=1, source_target_pairs={{0,8},{8,0},{16,24},{24,16},{1,9},{9,1},{17,25},{25,17},{2,10},{10... | collective-permute-start | bytes 3145736 | tf_op jit(solution)/shard_map/ppermute | solution.py:1269
  422.6 103.3 %copy-start.11 = (bf16[128,2048]{1,0:T(8,128)(2,1)S(1)}, bf16[128,2048]{1,0:T(8,128)(2,1)}, u32[]{:S(2)}) copy-start(bf16[128,2048]{1,0:T(8,128)(2,1)} %fusion.28) | copy-start | bytes 1572868
  508.7 75.2 %collective-permute-start.6 = (bf16[1,512,512]{2,1,0:T(8,128)(2,1)}, bf16[1,512,512]{2,1,0:T(8,128)(2,1)}, u32[]{:S(2)}, u32[]{:S(2)}) collective-permute-start(bf16[1,512,512]{2,1,0:T(8,128)(2,1)} %get-tuple-element.211), channel_id=1, source_target_pairs={{0,24},{8,16},{16,8},{24,0},{1,25},{9,17},{17,9},{25,1},{2,26},{10... | collective-permute-start | bytes 1572872 | tf_op jit(solution)/shard_map/ppermute | solution.py:1269
  524.1 59.8 %collective-permute-start.7 = (bf16[1,512,512]{2,1,0:T(8,128)(2,1)}, bf16[1,512,512]{2,1,0:T(8,128)(2,1)}, u32[]{:S(2)}, u32[]{:S(2)}) collective-permute-start(bf16[1,512,512]{2,1,0:T(8,128)(2,1)} %get-tuple-element.212), channel_id=1, source_target_pairs={{0,16},{8,24},{16,0},{24,8},{1,17},{9,25},{17,1},{25,9},{2,18},{10... | collective-permute-start | bytes 1572872 | tf_op jit(solution)/shard_map/ppermute | solution.py:1269
  524.1 59.8 %collective-permute-start.8 = (bf16[1,512,512]{2,1,0:T(8,128)(2,1)S(1)}, bf16[1,512,512]{2,1,0:T(8,128)(2,1)}, u32[]{:S(2)}, u32[]{:S(2)}) collective-permute-start(bf16[1,512,512]{2,1,0:T(8,128)(2,1)S(1)} %get-tuple-element.213), channel_id=1, source_target_pairs={{0,8},{8,0},{16,24},{24,16},{1,9},{9,1},{17,25},{25,17},{2,10},{10... | collective-permute-start | bytes 1572872 | tf_op jit(solution)/shard_map/ppermute | solution.py:1269
  583.9 133.2 %copy-start.22 = (f32[128]{0:T(128)S(1)}, f32[128]{0:T(128)}, u32[]{:S(2)}) copy-start(f32[128]{0:T(128)} %copy-done.21) | copy-start | bytes 1540
  708.6 374.5 %collective-permute-start.10 = (bf16[2,512,512]{2,1,0:T(8,128)(2,1)}, bf16[2,512,512]{2,1,0:T(8,128)(2,1)}, u32[]{:S(2)}, u32[]{:S(2)}) collective-permute-start(bf16[2,512,512]{2,1,0:T(8,128)(2,1)} %get-tuple-element.239), channel_id=1, source_target_pairs={{0,16},{8,24},{16,0},{24,8},{1,17},{9,25},{17,1},{25,9},{2,18},{10... | collective-permute-start | bytes 3145736 | tf_op jit(solution)/shard_map/ppermute | solution.py:1269
  708.7 374.4 %collective-permute-start.11 = (bf16[2,512,512]{2,1,0:T(8,128)(2,1)}, bf16[2,512,512]{2,1,0:T(8,128)(2,1)}, u32[]{:S(2)}, u32[]{:S(2)}) collective-permute-start(bf16[2,512,512]{2,1,0:T(8,128)(2,1)} %get-tuple-element.240), channel_id=1, source_target_pairs={{0,8},{8,0},{16,24},{24,16},{1,9},{9,1},{17,25},{25,17},{2,10},{10... | collective-permute-start | bytes 3145736 | tf_op jit(solution)/shard_map/ppermute | solution.py:1269
  710.1 373.1 %collective-permute-start.9 = (bf16[2,512,512]{2,1,0:T(8,128)(2,1)}, bf16[2,512,512]{2,1,0:T(8,128)(2,1)}, u32[]{:S(2)}, u32[]{:S(2)}) collective-permute-start(bf16[2,512,512]{2,1,0:T(8,128)(2,1)} %get-tuple-element.238), channel_id=1, source_target_pairs={{0,24},{8,16},{16,8},{24,0},{1,25},{9,17},{17,9},{25,1},{2,26},{10... | collective-permute-start | bytes 3145736 | tf_op jit(solution)/shard_map/ppermute | solution.py:1269
  725.6 8.4 copy-start
  737.1 14.7 %copy-start.3 = (f32[128,2048]{1,0:T(8,128)S(1)}, f32[128,2048]{1,0:T(8,128)}, u32[]{:S(2)}) copy-start(f32[128,2048]{1,0:T(8,128)} %get-tuple-element.76) | copy-start | bytes 3145732 | tf_op jit(solution)/shard_map/cond
  743.9 15.4 %copy-start.8 = (bf16[16,128,128]{1,2,0:T(8,128)(2,1)S(1)}, bf16[16,128,128]{1,2,0:T(8,128)(2,1)}, u32[]{:S(2)}) copy-start(bf16[16,128,128]{1,2,0:T(8,128)(2,1)} %get-tuple-element.343) | copy-start | bytes 1572868 | tf_op jit(solution)/shard_map/cond
  776.5 19.2 %copy-start.1 = (f32[128,2048]{1,0:T(8,128)S(1)}, f32[128,2048]{1,0:T(8,128)}, u32[]{:S(2)}) copy-start(f32[128,2048]{1,0:T(8,128)} %get-tuple-element.83) | copy-start | bytes 3145732 | tf_op jit(solution)/shard_map/cond
  776.5 24.0 %copy-start.6 = (bf16[128,2048]{1,0:T(8,128)(2,1)S(1)}, bf16[128,2048]{1,0:T(8,128)(2,1)}, u32[]{:S(2)}) copy-start(bf16[128,2048]{1,0:T(8,128)(2,1)} %get-tuple-element.90) | copy-start | bytes 1572868 | tf_op jit(solution)/shard_map/cond
  1077.2 5.1 copy-start.15
  1083.2 5.8 copy-start.19
  1083.2 6.6 copy-start.18
  1083.2 7.4 copy-start.17
  1083.2 8.2 copy-start.16
  1083.2 9.0 copy-start.20

commit v14 on v13

--- a/solution.py
+++ b/solution.py
@@ -607,12 +607,19 @@
                     ],
                 )
 
-    steps = (over_cores, pass_over, over_chips, over_planes, finish)
+    behind = min(4, n_items // 2)
+    steps = (
+        (0, over_cores),
+        (1, pass_over),
+        (2, over_chips),
+        (2 + behind, over_planes),
+        (3 + behind, finish),
+    )
     share = -(-len(copies) // n_items)
-    for n in range(n_items + len(steps) - 1):
+    for n in range(n_items + 3 + behind):
         for copy in copies[n * share : (n + 1) * share]:
             copy.start()
-        for late, step in enumerate(steps):
+        for late, step in steps:
             if 0 <= n - late < n_items:
                 step(n - late)
         if n == min(1, n_items - 1):
@@ -1089,6 +1096,26 @@
     )(*lefts, weights)
 
 
+def project_kernel(left_ref, weight_ref, out_ref):
+    out_ref[0] = dot(left_ref[...], weight_ref[0], (1, 0))
+
+
+def project(left, weights, first, count):
+    rows, depth = left.shape
+    piece = 512
+    return pl.pallas_call(
+        project_kernel,
+        grid=(count, depth // piece),
+        in_specs=[
+            pl.BlockSpec((rows, depth), lambda i, c: (0, 0)),
+            pl.BlockSpec((1, depth, piece), lambda i, c: (i + first, 0, c)),
+        ],
+        out_specs=pl.BlockSpec((1, rows, piece), lambda i, c: (i, 0, c)),
+        out_shape=jax.ShapeDtypeStruct((count, rows, depth), jnp.float32),
+        compiler_params=pltpu.CompilerParams(vmem_limit_bytes=BIG),
+    )(left, weights)
+
+
 def outer_kernel(which, n_left, *refs):
     lefts, rights = refs[:n_left], refs[n_left : n_left + len(which)]
     piece = 512
@@ -1317,7 +1344,6 @@
         + cut_pieces(late, number, 0, ins, outs[2 + n_soon :]),
     )
     soon_pieces, late_pieces = pieces[:n_soon], pieces[n_soon:]
-    query_weight, key_weight, value_weight, out_weight = (weights_all[i] for i in range(4))
     small_all = (
         extras_all[:, width:].reshape(groups, count, width)[:, :rows_each].reshape(-1, width)
     )
@@ -1335,9 +1361,8 @@
     scale = HD ** (-0.5)
     normed, attn_inverse = rms_forward(inputs, attn_gain)
     normed_low = normed.astype(bf16)
-    query_raw = product(normed_low, query_weight, "td,de->te")
-    key_raw = product(normed_low, key_weight, "td,de->te")
-    value_low = product(normed_low, value_weight, "td,de->te").astype(bf16)
+    query_raw, key_raw, value_raw = project(normed_low, weights_all, 0, 3)
+    value_low = value_raw.astype(bf16)
     query_normed, query_inverse = rms_forward(query_raw, query_gain)
     key_normed, key_inverse = rms_forward(key_raw, key_gain)
     query_low = rotate(query_normed, cosine, sine).astype(bf16).reshape(count, HEADS, HD)
@@ -1349,7 +1374,7 @@
     probs = jax.nn.softmax(scores, axis=-1)
     probs_low = probs.astype(bf16)
     attended_low = product(probs_low, value_heads, "hqk,khd->qhd").reshape(count, D).astype(bf16)
-    middle = inputs + product(attended_low, out_weight, "td,de->te")
+    middle = inputs + project(attended_low, weights_all, 3, 1)[0]
     mlp_normed, mlp_inverse = rms_forward(middle, mlp_gain)
     mlp_low = mlp_normed.astype(bf16)
     router = jax.nn.softmax(product(mlp_low, router_weight, "td,de->te"), axis=-1)
@@ -1446,7 +1471,7 @@
     def cut_grads(low, high, ins, outs):
         to, unused = partners(lax.axis_index("dp"), n_dp)
         pairs = []
-        for k, piece in enumerate(outs, 1):
+        for k, piece in enumerate(outs):
             for n in range(2):
                 source = ins[n].at[pl.ds(low, high - low), rows_at(to(k))]
                 pairs.append((source, piece.at[:, :, pl.ds(n * part, part)]))
@@ -1454,7 +1479,7 @@
 
     pieces = []
     if back_beside:
-        for k in range(1, n_dp):
+        for k in range(n_dp):
             if packing:
                 piece = lax.dynamic_index_in_dim(packed, to_plane(k), 0, False)
             else:
@@ -1468,8 +1493,8 @@
                     axis=2,
                 )
             pieces.append(piece)
-        ahead = lax.optimization_barrier((*pieces, *late_pieces[1:]))
-        pieces = permuted(ahead[: n_dp - 1])
+        ahead = lax.optimization_barrier((*pieces[1:], *late_pieces[1:]))
+        pieces = [pieces[0], *permuted(ahead[: n_dp - 1])]
         part_back, *pieces = lax.optimization_barrier((part_back, *pieces))
     way_shapes = [jax.ShapeDtypeStruct((number, depth, ff), bf16)] * 2
     piece_shape = jax.ShapeDtypeStruct((back_late - back_third, depth, 2 * part), bf16)
@@ -1482,19 +1507,19 @@
         [
             *way_shapes,
             jax.ShapeDtypeStruct((groups * count, D), bf16),
-            *[piece_shape] * (n_dp - 1),
+            *[piece_shape] * n_dp,
         ],
         lambda ins, outs: ways(back_beside, back_third, 0, ins, outs),
         8,
         (),
         stages(
             *[1] * (2 * (back_third - back_beside)),
-            *[back_late - back_third] * (2 * (n_dp - 1)),
+            *[back_late - back_third] * (2 * n_dp),
         ),
         lambda ins, outs: cut_grads(back_third, back_late, ins, outs[3:]),
         lambda ins, outs: place_out(ins[2], ins[3], outs[2]),
     )
-    later_pieces = permuted(later_pieces)
+    later_pieces = [later_pieces[0], *permuted(later_pieces[1:])]
 
     def attention_back(back):
         grad_final = cotangent.astype(jnp.float32)
@@ -1584,14 +1609,7 @@
         (back_third, back_late, later_pieces),
     ):
         if high > low:
-            own = jnp.concatenate(
-                [
-                    lax.dynamic_slice_in_dim(one[low:high], me * depth, depth, 1)
-                    for one in (gate_soon, up_soon)
-                ],
-                axis=2,
-            )
-            widened = widen_pieces(offsets, low, [own, *others], widened)
+            widened = widen_pieces(offsets, low, others, widened)
     grad_gate_part, grad_up_part = widened
     return (
         output,

time: 1110 us -> 1130 us (1.018)
  Pallas kernels: 908 us -> 963 us
  matrix products: 31.8 us -> 8.5 us
    pallas_call x2, Pallas kernels: 389 us -> 423 us  [scatter_call(): pl.pallas_call(functools.partial(scatter_kernel, n_dp, n_expert, count, i...]
    dot_general x13 -> x9, matrix products: 30.3 us -> 6.98 us  [product(): return jnp.einsum(form, left, right, preferred_element_type=jnp.float32)]
    pallas_call x0 -> x2, Pallas kernels: none -> 21 us  [project(): pl.pallas_call(project_kernel, grid=(count, depth // piece), in_specs=[pl...]
  transfers between devices with their start and end apart: 12 -> 12, of which waited for: 1 -> 1; matrix products, arithmetic and copies ran while one was open for 10% -> 7% of each run, Pallas kernels for 38% -> 43%
where the time goes in v14:
time: 1130 us; the launch traced here: 1120 us
  Pallas kernels  963 us (85%)
  local copies, waits for them, and re-layouts  45.5 us (4%)
  other arithmetic  41 us (4%)
  starting transfers between devices  29.3 us (3%)
  waiting for transfers between devices  28.1 us (2%)
    pallas_call x2, Pallas kernels, scatter_call(): pl.pallas_call(functools.partial(scatter_kernel, n_dp, n_expert, count, i...  423 us
    pallas_call x2, Pallas kernels, gather_call(): pl.pallas_call(functools.partial(gather_kernel, n_dp, n_expert, n, places...  357 us
    pallas_call x2, Pallas kernels, expert_call(): pl.pallas_call(functools.partial(expert_kernel, steps, half, len(weights)...  79.5 us
    ppermute x12, starting transfers between devices, permuted(): got.append(lax.ppermute(piece, 'dp', paths))  29.3 us
    ppermute x12, waiting for transfers between devices, permuted(): got.append(lax.ppermute(piece, 'dp', paths))  28.1 us
    pallas_call x2, Pallas kernels, through(): pl.pallas_call(functools.partial(through_kernel, count), grid=(depth // p...  24.5 us
    pallas_call x1, Pallas kernels, place_back(): pl.pallas_call(functools.partial(place_back_kernel, number), grid=(pairs,...  23.5 us
  transfers between devices with their start and end apart: 12, of which 1 were waited for; matrix products, arithmetic and copies ran while one was open for 7% of the time, Pallas kernels for 43%

profile of v14, /device:TPU:0, one launch (start us, length us, event | category | flops | bytes accessed | tf_op | source)
XLA Modules:
  0.0 1117.7 jit_solution(9581216110513161132)
XLA Ops:
  6.2 2.3 pad_maximum_fusion.2.refs_0_
  8.5 167.3 %shard_map.272 = (bf16[4,2048,2048]{2,1,0:T(8,128)(2,1)}, bf16[4096,256]{1,0:T(8,128)(2,1)}, bf16[8,2048,256]{2,1,0:T(8,128)(2,1)}, bf16[8,2048,256]{2,1,0:T(8,1...) custom-call(bf16[4,64,2048]{2,1,0:T(8,128)(2,1)} %pad_maximum_fusion, ...), custom_call_target="tpu_custom_call" | custom-call | tf_op jit(solution)/shard_map/pallas_call | solution.py:330
  176.0 4.3 collective-permute-start.2
  180.3 1.3 slice.78
  181.8 3.0 slice_reduce_fusion
  185.2 15.2 %shard_map.273 = f32[3,128,2048]{2,1,0:T(8,128)} custom-call(bf16[128,2048]{1,0:T(8,128)(2,1)S(1)} %multiply_convert_fusion.3.left_ref, bf16[4,2048,2048]{2,1,0:T(8,128)(2,1)} %get-tuple-element.182.weight_ref), custom_call_target="tpu_custom_call" | custom-call | tf_op jit(solution)/shard_map/pallas_call | solution.py:1106
  200.5 1.8 multiply_reduce_fusion.11
  202.2 3.4 slice_bitcast_fusion
  205.7 2.1 fusion.19
  207.8 2.3 slice.88
  210.1 1.2 copy.147
  211.2 1.2 copy.148
  212.7 1.1 copy.146
  214.2 1.6 fusion.18
  215.8 1.6 fusion.17
  218.8 1.5 fusion.37
  220.3 2.4 fusion.36
  224.5 5.7 shard_map.274
  230.2 1.4 multiply_reduce_fusion.10
  231.7 1.6 constant_dynamic-slice_fusion
  236.4 189.9 %shard_map.275 = (bf16[4096,2048]{1,0:T(8,128)(2,1)}, bf16[4096,2048]{1,0:T(8,128)(2,1)}, bf16[8,2048,256]{2,1,0:T(8,128)(2,1)}, bf16[8,2048,256]{2,1,0:T(8,128)...) custom-call(bf16[128,2048]{1,0:T(8,128)(2,1)S(1)} %multiply_convert_, ...), custom_call_target="tpu_custom_call", output_to_operand_aliasing={{2}: (4, {}), {3}: (5, {})} | custom-call | tf_op jit(solution)/shard_map/pallas_call | solution.py:330
  426.4 1.6 collective-permute-start.3
  428.0 2.4 collective-permute-start.4
  430.8 55.8 %shard_map.276 = (bf16[8,768,2048]{2,1,0:T(8,128)(2,1)}, bf16[8,768,2048]{2,1,0:T(8,128)(2,1)}, bf16[8,768,128]{2,1,0:T(8,128)(2,1)}, bf16[6,2048,256]{2,1,0:T(8...) custom-call(s32[1]{0:T(128)} %bitcast.59.names_ref, ...), custom_call_target="tpu_custom_call" | custom-call | tf_op jit(solution)/shard_map/pallas_call | solution.py:1011
  486.6 2.7 dynamic-slice_bitcast_fusion
  489.3 28.0 %collective-permute-done.4.refs_2_ = bf16[2,512,512]{2,1,0:T(8,128)(2,1)} collective-permute-done((bf16[2,512,512]{2,1,0:T(8,128)(2,1)}, bf16[2,512,512]{2,1,0:T(8,128)(2,1)}, u32[]{:S(2)}, u32[]{:S(2)}) %collective-permute-start.4) | collective-permute-done | bytes 1048608 | tf_op jit(solution)/shard_map/ppermute | solution.py:1296
  517.4 15.4 %collective-permute-start.6 = (bf16[1,512,512]{2,1,0:T(8,128)(2,1)}, bf16[1,512,512]{2,1,0:T(8,128)(2,1)}, u32[]{:S(2)}, u32[]{:S(2)}) collective-permute-start(bf16[1,512,512]{2,1,0:T(8,128)(2,1)} %get-tuple-element.213), channel_id=1, source_target_pairs={{0,24},{8,16},{16,8},{24,0},{1,25},{9,17},{17,9},{25,1},{2,26},{10... | collective-permute-start | bytes 1572872 | tf_op jit(solution)/shard_map/ppermute | solution.py:1296
  533.3 1.1 convert_element_type.99
  535.5 23.7 %shard_map.277 = (bf16[8,768,2048]{2,1,0:T(8,128)(2,1)}, bf16[8,768,2048]{2,1,0:T(8,128)(2,1)}, bf16[8,768,128]{2,1,0:T(8,128)(2,1)}, bf16[2,2048,256]{2,1,0:T(8...) custom-call(s32[5]{0:T(128)} %stack.73.names_ref, ...), custom_call_target="tpu_custom_call", output_to_operand_aliasing={{0}: (9, {}), {1}: (10, {}), {2}: (11, {}), {5}: (12, {})} | custom-call | tf_op jit(solution)/shard_map/pallas_call | solution.py:1011
  559.2 23.5 %shard_map.278 = bf16[4096,2176]{1,0:T(8,128)(2,1)} custom-call(s32[16,8,256]{2,1,0:T(8,128)} %select_bitcast_fusion.refs_6_.slots_ref.refs_3_, bf16[8,768,2048]{2,1,0:T(8,128)(2,1)} %get-tuple-element.210.dx_ref, bf16[8,768,128]{2,1,0:T(8,128)(2,1)} %get-tuple-element.211.probs_ref), custom_call_target="tpu_custom_call" | custom-call | tf_op jit(solution)/shard_map/pallas_call | solution.py:1061
  582.7 125.0 %shard_map.279 = (f32[128,2176]{1,0:T(8,128)}, bf16[8,512,1024]{2,1,0:T(8,128)(2,1)}, bf16[8,512,1024]{2,1,0:T(8,128)(2,1)}, bf16[4096,2048]{1,0:T(8,128)(2,1)},...) custom-call(bf16[4,8,128,2176]{3,2,1,0:T(8,128)(2,1)} %bitcast.146, ...), custom_call_target="tpu_custom_call" | custom-call | tf_op jit(solution)/shard_map/pallas_call | solution.py:686
  708.5 3.6 collective-permute-start.9
  712.8 79.5 %conditional.1 = (f32[128,2048]{1,0:T(8,128)}, bf16[4,8,64,2048]{3,2,1,0:T(8,128)(2,1)}, bf16[4,8,64,2048]{3,2,1,0:T(8,128)(2,1)}, bf16[4,8,64,2048]{3,2,1,0:T(8...) conditional(s32[]{:T(128)} %bitcast.66, () %tuple.36, ...), branch_computations={%region_12.13_spmd, %region_13.24_spmd} | conditional | flops 387291904 | bytes 77484864 | solution.py:1582
  713.2 1.1 multiply_reduce_fusion.9
  714.3 1.1 multiply_convert_fusion.1
  715.3 1.6 copy.122
  716.9 1.8 multiply_reduce_fusion
  718.7 2.6 fusion.35
  721.3 6.9 branch_1_fun.3
  728.1 2.1 convert_element_type.74
  730.2 1.3 copy.145
  732.1 1.6 fusion.1
  733.6 1.4 fusion.2
  735.3 1.1 multiply_subtract_fusion
  736.5 1.3 copy.139
  737.8 2.1 pad_maximum_fusion
  739.9 1.6 copy.138
  741.6 1.6 copy.127
  743.1 1.6 copy.125
  744.7 2.5 multiply_reduce_fusion.1
  747.3 2.6 subtract_convert_fusion.refs_1_.refs_4_
  749.9 2.3 subtract_convert_fusion.1.refs_0_.refs_5_
  752.7 1.0 copy.140.refs_2_.refs_3_
  753.7 13.7 %branch_1_fun.5 = (bf16[2048,2048]{1,0:T(8,128)(2,1)}, bf16[2048,2048]{1,0:T(8,128)(2,1)}, bf16[2048,2048]{1,0:T(8,128)(2,1)}, bf16[2048,2048]{1,0:T(8,128)(2,1)}) custom-call(bf16[128,2048]{1,0:T(8,128)(2,1)S(1)} %copy-done.6, bf16[128,2048]{1,0:T(8,128)(2,1)S(1)} %copy-done.8, bf16[128,2048]{1,0:T(8,128)(2,1)} %get-tuple-element.372.refs_0_.refs_2_, ...), custom_call_target="tpu_custom_call" | custom-call | tf_op jit(solution)/shard_map/cond/branch_1_fun/pallas_call | solution.py:1132
  767.4 17.6 %branch_1_fun.4 = f32[128,2048]{1,0:T(8,128)} custom-call(bf16[128,2048]{1,0:T(8,128)(2,1)} %subtract_convert_fusion.1.refs_0_.refs_5_, bf16[128,2048]{1,0:T(8,128)(2,1)} %subtract_convert_fusion.refs_1_.refs_4_, bf16[128,2048]{1,0:T(8,128)(2,1)} %copy.140.refs_2_.refs_3_, bf16[4,2048,2048]{2,1,0:T(8,128)(2,1)} %get-tuple-element.70.refs_1_.refs_3_), custom_call_target="tpu_custom_call" | custom-call | tf_op jit(solution)/shard_map/cond/branch_1_fun/pallas_call | solution.py:1086
  785.1 1.6 copy.129
  786.7 1.5 multiply_reduce_fusion.3
  788.6 2.8 subtract_add_fusion
  792.3 298.0 %shard_map.280 = (f32[128,2048]{1,0:T(8,128)}, f32[64,2048]{1,0:T(8,128)}, f32[64,2048]{1,0:T(8,128)}, f32[64,2048]{1,0:T(8,128)}, f32[64,2048]{1,0:T(8,128)}, /...) custom-call(bf16[4,8,128,2048]{3,2,1,0:T(8,128)(2,1)} %bitcast.147, ...), custom_call_target="tpu_custom_call", output_to_operand_aliasing={{7}: (7, {}), {8}: (8, {})} | custom-call | tf_op jit(solution)/shard_map/pallas_call | solution.py:686
  1090.4 11.5 %shard_map.281 = (f32[8,512,1024]{2,1,0:T(8,128)}, f32[8,512,1024]{2,1,0:T(8,128)}) custom-call(bf16[8,512,1024]{2,1,0:T(8,128)(2,1)} %get-tuple-element.248.refs_0_, bf16[8,512,1024]{2,1,0:T(8,128)(2,1)} %get-tuple-element.249.refs_1_), custom_call_target="tpu_custom_call" | custom-call | tf_op jit(solution)/shard_map/pallas_call | solution.py:1159
  1101.8 3.7 shard_map.282
  1105.6 1.3 slice_bitcast_fusion.4
  1106.9 0.9 add_convert_fusion
  1107.9 5.8 shard_map.283
  (140 shorter events, 23.1 us)
Async XLA Ops:
  175.8 9.0 copy-start.4
  175.8 60.6 %collective-permute-start = (bf16[1,512,512]{2,1,0:T(8,128)(2,1)}, bf16[1,512,512]{2,1,0:T(8,128)(2,1)}, u32[]{:S(2)}, u32[]{:S(2)}) collective-permute-start(bf16[1,512,512]{2,1,0:T(8,128)(2,1)} %get-tuple-element.187), channel_id=1, source_target_pairs={{0,24},{8,16},{16,8},{24,0},{1,25},{9,17},{17,9},{25,1},{2,26},{10... | collective-permute-start | bytes 1572872 | tf_op jit(solution)/shard_map/ppermute | solution.py:1296
  175.9 60.5 %collective-permute-start.1 = (bf16[1,512,512]{2,1,0:T(8,128)(2,1)}, bf16[1,512,512]{2,1,0:T(8,128)(2,1)}, u32[]{:S(2)}, u32[]{:S(2)}) collective-permute-start(bf16[1,512,512]{2,1,0:T(8,128)(2,1)} %get-tuple-element.188), channel_id=1, source_target_pairs={{0,16},{8,24},{16,0},{24,8},{1,17},{9,25},{17,1},{25,9},{2,18},{10... | collective-permute-start | bytes 1572872 | tf_op jit(solution)/shard_map/ppermute | solution.py:1296
  176.0 60.4 %collective-permute-start.2 = (bf16[1,512,512]{2,1,0:T(8,128)(2,1)}, bf16[1,512,512]{2,1,0:T(8,128)(2,1)}, u32[]{:S(2)}, u32[]{:S(2)}) collective-permute-start(bf16[1,512,512]{2,1,0:T(8,128)(2,1)} %get-tuple-element.189), channel_id=1, source_target_pairs={{0,8},{8,0},{16,24},{24,16},{1,9},{9,1},{17,25},{25,17},{2,10},{10... | collective-permute-start | bytes 1572872 | tf_op jit(solution)/shard_map/ppermute | solution.py:1296
  185.0 15.4 %copy-start.23 = (f32[128]{0:T(128)}, f32[128]{0:T(128)S(1)}, u32[]{:S(2)}) copy-start(f32[128]{0:T(128)S(1)} %add_rsqrt_fusion.3) | copy-start | bytes 1540
  185.2 15.2 %copy-start.7 = (bf16[128,2048]{1,0:T(8,128)(2,1)}, bf16[128,2048]{1,0:T(8,128)(2,1)S(1)}, u32[]{:S(2)}) copy-start(bf16[128,2048]{1,0:T(8,128)(2,1)S(1)} %multiply_convert_fusion.3.left_ref) | copy-start | bytes 1572868
  200.5 11.9 %copy-start.25 = (s32[1,3]{1,0:T(1,128)S(1)}, s32[1,3]{1,0:T(1,128)}, u32[]{:S(2)}) copy-start(s32[1,3]{1,0:T(1,128)} %param.21) | copy-start | bytes 40
  213.9 8.7 copy-start.11
  218.4 1.8 copy-start.15
  218.7 3.9 copy-start.16
  222.6 0.8 copy-start.9
  223.7 0.8 copy-start.5
  236.4 298.7 %copy-start.2 = (bf16[128,2048]{1,0:T(8,128)(2,1)}, bf16[128,2048]{1,0:T(8,128)(2,1)S(1)}, u32[]{:S(2)}) copy-start(bf16[128,2048]{1,0:T(8,128)(2,1)S(1)} %multiply_convert_fusion.2.refs_0_) | copy-start | bytes 1572868
  426.4 63.0 %collective-permute-start.3 = (bf16[2,512,512]{2,1,0:T(8,128)(2,1)}, bf16[2,512,512]{2,1,0:T(8,128)(2,1)}, u32[]{:S(2)}, u32[]{:S(2)}) collective-permute-start(bf16[2,512,512]{2,1,0:T(8,128)(2,1)} %get-tuple-element.201), channel_id=1, source_target_pairs={{0,24},{8,16},{16,8},{24,0},{1,25},{9,17},{17,9},{25,1},{2,26},{10... | collective-permute-start | bytes 3145736 | tf_op jit(solution)/shard_map/ppermute | solution.py:1296
  428.0 89.4 %collective-permute-start.4 = (bf16[2,512,512]{2,1,0:T(8,128)(2,1)}, bf16[2,512,512]{2,1,0:T(8,128)(2,1)}, u32[]{:S(2)}, u32[]{:S(2)}) collective-permute-start(bf16[2,512,512]{2,1,0:T(8,128)(2,1)} %get-tuple-element.202), channel_id=1, source_target_pairs={{0,16},{8,24},{16,0},{24,8},{1,17},{9,25},{17,1},{25,9},{2,18},{10... | collective-permute-start | bytes 3145736 | tf_op jit(solution)/shard_map/ppermute | solution.py:1296
  430.4 87.0 %collective-permute-start.5 = (bf16[2,512,512]{2,1,0:T(8,128)(2,1)}, bf16[2,512,512]{2,1,0:T(8,128)(2,1)}, u32[]{:S(2)}, u32[]{:S(2)}) collective-permute-start(bf16[2,512,512]{2,1,0:T(8,128)(2,1)} %get-tuple-element.203), channel_id=1, source_target_pairs={{0,8},{8,0},{16,24},{24,16},{1,9},{9,1},{17,25},{25,17},{2,10},{10... | collective-permute-start | bytes 3145736 | tf_op jit(solution)/shard_map/ppermute | solution.py:1296
  517.4 65.3 %collective-permute-start.6 = (bf16[1,512,512]{2,1,0:T(8,128)(2,1)}, bf16[1,512,512]{2,1,0:T(8,128)(2,1)}, u32[]{:S(2)}, u32[]{:S(2)}) collective-permute-start(bf16[1,512,512]{2,1,0:T(8,128)(2,1)} %get-tuple-element.213), channel_id=1, source_target_pairs={{0,24},{8,16},{16,8},{24,0},{1,25},{9,17},{17,9},{25,1},{2,26},{10... | collective-permute-start | bytes 1572872 | tf_op jit(solution)/shard_map/ppermute | solution.py:1296
  532.7 50.0 %collective-permute-start.7 = (bf16[1,512,512]{2,1,0:T(8,128)(2,1)}, bf16[1,512,512]{2,1,0:T(8,128)(2,1)}, u32[]{:S(2)}, u32[]{:S(2)}) collective-permute-start(bf16[1,512,512]{2,1,0:T(8,128)(2,1)} %get-tuple-element.214), channel_id=1, source_target_pairs={{0,16},{8,24},{16,0},{24,8},{1,17},{9,25},{17,1},{25,9},{2,18},{10... | collective-permute-start | bytes 1572872 | tf_op jit(solution)/shard_map/ppermute | solution.py:1296
  532.7 50.0 %collective-permute-start.8 = (bf16[1,512,512]{2,1,0:T(8,128)(2,1)S(1)}, bf16[1,512,512]{2,1,0:T(8,128)(2,1)}, u32[]{:S(2)}, u32[]{:S(2)}) collective-permute-start(bf16[1,512,512]{2,1,0:T(8,128)(2,1)S(1)} %get-tuple-element.215), channel_id=1, source_target_pairs={{0,8},{8,0},{16,24},{24,16},{1,9},{9,1},{17,25},{25,17},{2,10},{10... | collective-permute-start | bytes 1572872 | tf_op jit(solution)/shard_map/ppermute | solution.py:1296
  582.7 130.1 %copy-start.24 = (f32[128]{0:T(128)S(1)}, f32[128]{0:T(128)}, u32[]{:S(2)}) copy-start(f32[128]{0:T(128)} %copy-done.23) | copy-start | bytes 1540
  707.7 400.1 %collective-permute-start.10 = (bf16[2,512,512]{2,1,0:T(8,128)(2,1)}, bf16[2,512,512]{2,1,0:T(8,128)(2,1)}, u32[]{:S(2)}, u32[]{:S(2)}) collective-permute-start(bf16[2,512,512]{2,1,0:T(8,128)(2,1)} %get-tuple-element.242), channel_id=1, source_target_pairs={{0,16},{8,24},{16,0},{24,8},{1,17},{9,25},{17,1},{25,9},{2,18},{10... | collective-permute-start | bytes 3145736 | tf_op jit(solution)/shard_map/ppermute | solution.py:1296
  707.8 400.0 %collective-permute-start.11 = (bf16[2,512,512]{2,1,0:T(8,128)(2,1)}, bf16[2,512,512]{2,1,0:T(8,128)(2,1)}, u32[]{:S(2)}, u32[]{:S(2)}) collective-permute-start(bf16[2,512,512]{2,1,0:T(8,128)(2,1)} %get-tuple-element.243), channel_id=1, source_target_pairs={{0,8},{8,0},{16,24},{24,16},{1,9},{9,1},{17,25},{25,17},{2,10},{10... | collective-permute-start | bytes 3145736 | tf_op jit(solution)/shard_map/ppermute | solution.py:1296
  708.5 399.3 %collective-permute-start.9 = (bf16[2,512,512]{2,1,0:T(8,128)(2,1)}, bf16[2,512,512]{2,1,0:T(8,128)(2,1)}, u32[]{:S(2)}, u32[]{:S(2)}) collective-permute-start(bf16[2,512,512]{2,1,0:T(8,128)(2,1)} %get-tuple-element.241), channel_id=1, source_target_pairs={{0,24},{8,16},{16,8},{24,0},{1,25},{9,17},{17,9},{25,1},{2,26},{10... | collective-permute-start | bytes 3145736 | tf_op jit(solution)/shard_map/ppermute | solution.py:1296
  721.3 10.3 copy-start
  721.3 10.3 copy-start.12
  731.5 6.3 copy-start.13
  739.9 13.8 %copy-start.6 = (bf16[128,2048]{1,0:T(8,128)(2,1)S(1)}, bf16[128,2048]{1,0:T(8,128)(2,1)}, u32[]{:S(2)}) copy-start(bf16[128,2048]{1,0:T(8,128)(2,1)} %get-tuple-element.84.refs_0_) | copy-start | bytes 1572868 | tf_op jit(solution)/shard_map/cond
  739.9 13.8 %copy-start.8 = (bf16[128,2048]{1,0:T(8,128)(2,1)S(1)}, bf16[128,2048]{1,0:T(8,128)(2,1)}, u32[]{:S(2)}) copy-start(bf16[128,2048]{1,0:T(8,128)(2,1)} %get-tuple-element.85.refs_1_) | copy-start | bytes 1572868 | tf_op jit(solution)/shard_map/cond
  744.7 7.5 copy-start.10
  744.7 7.5 copy-start.14
  767.4 19.2 %copy-start.1 = (f32[128,2048]{1,0:T(8,128)S(1)}, f32[128,2048]{1,0:T(8,128)}, u32[]{:S(2)}) copy-start(f32[128,2048]{1,0:T(8,128)} %get-tuple-element.83) | copy-start | bytes 3145732 | tf_op jit(solution)/shard_map/cond
  767.4 24.0 %copy-start.3 = (bf16[128,2048]{1,0:T(8,128)(2,1)S(1)}, bf16[128,2048]{1,0:T(8,128)(2,1)}, u32[]{:S(2)}) copy-start(bf16[128,2048]{1,0:T(8,128)(2,1)} %get-tuple-element.90) | copy-start | bytes 1572868 | tf_op jit(solution)/shard_map/cond
  1101.8 5.1 copy-start.17
  1107.8 5.8 copy-start.21
  1107.8 6.6 copy-start.20
  1107.9 7.4 copy-start.19
  1107.9 8.2 copy-start.18
  1107.9 9.0 copy-start.22

commit v15 on v14

--- a/solution.py
+++ b/solution.py
@@ -607,17 +607,14 @@
                     ],
                 )
 
-    behind = min(4, n_items // 2)
-    steps = (
-        (0, over_cores),
-        (1, pass_over),
-        (2, over_chips),
-        (2 + behind, over_planes),
-        (3 + behind, finish),
-    )
-    share = -(-len(copies) // n_items)
-    for n in range(n_items + 3 + behind):
-        for copy in copies[n * share : (n + 1) * share]:
+    steps = ((0, over_cores), (1, pass_over), (2, over_chips), (3, over_planes), (4, finish))
+    if n_items >= 6:
+        quotas = [-(-len(copies) * part // 9) for part in (2, 2, 2, 1, 1, 1)]
+    else:
+        quotas = [-(-len(copies) // n_items)] * n_items
+    quotas += [0] * (n_items + len(steps) - len(quotas))
+    for n in range(n_items + len(steps) - 1):
+        for copy in copies[sum(quotas[:n]) : sum(quotas[: n + 1])]:
             copy.start()
         for late, step in steps:
             if 0 <= n - late < n_items:
@@ -1096,26 +1093,6 @@
     )(*lefts, weights)
 
 
-def project_kernel(left_ref, weight_ref, out_ref):
-    out_ref[0] = dot(left_ref[...], weight_ref[0], (1, 0))
-
-
-def project(left, weights, first, count):
-    rows, depth = left.shape
-    piece = 512
-    return pl.pallas_call(
-        project_kernel,
-        grid=(count, depth // piece),
-        in_specs=[
-            pl.BlockSpec((rows, depth), lambda i, c: (0, 0)),
-            pl.BlockSpec((1, depth, piece), lambda i, c: (i + first, 0, c)),
-        ],
-        out_specs=pl.BlockSpec((1, rows, piece), lambda i, c: (i, 0, c)),
-        out_shape=jax.ShapeDtypeStruct((count, rows, depth), jnp.float32),
-        compiler_params=pltpu.CompilerParams(vmem_limit_bytes=BIG),
-    )(left, weights)
-
-
 def outer_kernel(which, n_left, *refs):
     lefts, rights = refs[:n_left], refs[n_left : n_left + len(which)]
     piece = 512
@@ -1143,27 +1120,22 @@
 
 
 def widen_kernel(*refs):
-    half = len(refs) // 2
-    for source, target in zip(refs[:half], refs[half:]):
+    for source, target in zip(refs[:2], refs[-2:]):
         target[...] = source[...].astype(jnp.float32)
 
 
-def widen(spans, values):
+def widen(low, high, values, into=()):
     number, rows, columns = values[0].shape
-    (low, high), (again, end) = spans
-
-    def chosen(e):
-        return (jnp.where(e < high - low, e + low, e - (high - low) + again), 0, 0)
-
-    block = pl.BlockSpec((1, rows, columns), chosen)
+    block = pl.BlockSpec((1, rows, columns), lambda e: (e + low, 0, 0))
     return pl.pallas_call(
         widen_kernel,
-        grid=(high - low + end - again,),
-        in_specs=[block] * len(values),
-        out_specs=[block] * len(values),
+        grid=(high - low,),
+        in_specs=[block] * 2 + [pl.BlockSpec(memory_space=pl.ANY)] * len(into),
+        out_specs=[block] * 2,
         out_shape=[jax.ShapeDtypeStruct(one.shape, jnp.float32) for one in values],
+        input_output_aliases={2 + i: i for i in range(len(into))},
         compiler_params=pltpu.CompilerParams(vmem_limit_bytes=BIG),
-    )(*values)
+    )(*values, *into)
 
 
 def widen_pieces_kernel(low, n_pieces, offsets_ref, *refs):
@@ -1361,8 +1333,9 @@
     scale = HD ** (-0.5)
     normed, attn_inverse = rms_forward(inputs, attn_gain)
     normed_low = normed.astype(bf16)
-    query_raw, key_raw, value_raw = project(normed_low, weights_all, 0, 3)
-    value_low = value_raw.astype(bf16)
+    query_raw = product(normed_low, weights_all[0], "td,de->te")
+    key_raw = product(normed_low, weights_all[1], "td,de->te")
+    value_low = product(normed_low, weights_all[2], "td,de->te").astype(bf16)
     query_normed, query_inverse = rms_forward(query_raw, query_gain)
     key_normed, key_inverse = rms_forward(key_raw, key_gain)
     query_low = rotate(query_normed, cosine, sine).astype(bf16).reshape(count, HEADS, HD)
@@ -1374,7 +1347,7 @@
     probs = jax.nn.softmax(scores, axis=-1)
     probs_low = probs.astype(bf16)
     attended_low = product(probs_low, value_heads, "hqk,khd->qhd").reshape(count, D).astype(bf16)
-    middle = inputs + project(attended_low, weights_all, 3, 1)[0]
+    middle = inputs + product(attended_low, weights_all[3], "td,de->te")
     mlp_normed, mlp_inverse = rms_forward(middle, mlp_gain)
     mlp_low = mlp_normed.astype(bf16)
     router = jax.nn.softmax(product(mlp_low, router_weight, "td,de->te"), axis=-1)
@@ -1521,6 +1494,12 @@
     )
     later_pieces = [later_pieces[0], *permuted(later_pieces[1:])]
 
+    offsets = jnp.stack([from_plane(k) * part for k in range(n_dp)])
+    widened = widen(back_beside, back_third, [gate_third, up_third])
+    if back_beside:
+        widened = widen_pieces(offsets, 0, pieces, widened)
+    part_out, *widened = lax.optimization_barrier((part_out, *widened))
+
     def attention_back(back):
         grad_final = cotangent.astype(jnp.float32)
         grad_mlp = back[:, :D]
@@ -1590,26 +1569,21 @@
         [part_out.reshape(n_dp, n_expert, count, D)]
         + [blocks_of(value) for value in weight_grads],
         [2, 1, 1, 1, 2 if rows_each > 16 else 1, 1, 1],
-        [gate_third, up_third, gate_soon, up_soon, gate_rest, up_rest],
+        [gate_soon, up_soon, gate_rest, up_rest],
         way_shapes,
-        lambda ins, outs: ways(back_late, late, 0, ins[2:4], outs)
-        + ways(0, number - late, late, ins[4:6], outs),
+        lambda ins, outs: ways(back_late, late, 0, ins[:2], outs)
+        + ways(0, number - late, late, ins[2:], outs),
         16,
-        ((0, 0), (1, 1)),
+        (),
         [],
     )
     summed, grad_out_part, grad_value_part, grad_key_part, grad_query_part, router_part, small = sums
     output = (middle + summed).astype(bf16)
     grad_router_part = router_part[:, :experts_all]
     gain_parts = [small[i, :rows_each] for i in range(4)]
-    widened = widen([(back_beside, back_third), (back_late, number)], [gate_back, up_back])
-    offsets = jnp.stack([from_plane(k) * part for k in range(n_dp)])
-    for low, high, others in (
-        (0, back_beside, pieces),
-        (back_third, back_late, later_pieces),
-    ):
-        if high > low:
-            widened = widen_pieces(offsets, low, others, widened)
+    widened = widen(back_late, number, [gate_back, up_back], widened)
+    if back_late > back_third:
+        widened = widen_pieces(offsets, back_third, later_pieces, widened)
     grad_gate_part, grad_up_part = widened
     return (
         output,

time: 1130 us -> 1080 us (0.956)
  Pallas kernels: 963 us -> 891 us
  matrix products: 8.5 us -> 32.1 us
    pallas_call x2, Pallas kernels: 423 us -> 362 us  [scatter_call(): pl.pallas_call(functools.partial(scatter_kernel, n_dp, n_expert, count, i...]
    dot_general x9 -> x13, matrix products: 6.98 us -> 30.5 us  [product(): return jnp.einsum(form, left, right, preferred_element_type=jnp.float32)]
    pallas_call x3 -> x2, Pallas kernels: 32.4 us -> 12.4 us  [widen(): pl.pallas_call(widen_kernel, grid=(high - low,), in_specs=[block] * 2 + [...]
  transfers between devices with their start and end apart: 12 -> 12, of which waited for: 1 -> 1; matrix products, arithmetic and copies ran while one was open for 7% -> 10% of each run, Pallas kernels for 43% -> 38%
where the time goes in v15:
time: 1080 us; the launch traced here: 1070 us
  Pallas kernels  891 us (82%)
  local copies, waits for them, and re-layouts  45.5 us (4%)
  other arithmetic  38.7 us (4%)
  matrix products  32.1 us (3%)
  starting transfers between devices  29.3 us (3%)
  waiting for transfers between devices  28.4 us (3%)
    pallas_call x2, Pallas kernels, scatter_call(): pl.pallas_call(functools.partial(scatter_kernel, n_dp, n_expert, count, i...  362 us
    pallas_call x2, Pallas kernels, gather_call(): pl.pallas_call(functools.partial(gather_kernel, n_dp, n_expert, n, places...  357 us
    pallas_call x2, Pallas kernels, expert_call(): pl.pallas_call(functools.partial(expert_kernel, steps, half, len(weights)...  88.6 us
    dot_general x13, matrix products, product(): return jnp.einsum(form, left, right, preferred_element_type=jnp.float32)  30.5 us
    ppermute x12, starting transfers between devices, permuted(): got.append(lax.ppermute(piece, 'dp', paths))  29.3 us
    ppermute x12, waiting for transfers between devices, permuted(): got.append(lax.ppermute(piece, 'dp', paths))  28.4 us
    pallas_call x2, Pallas kernels, through(): pl.pallas_call(functools.partial(through_kernel, count), grid=(depth // p...  24.4 us
    pallas_call x1, Pallas kernels, place_back(): pl.pallas_call(functools.partial(place_back_kernel, number), grid=(pairs,...  23.5 us
  transfers between devices with their start and end apart: 12, of which 1 were waited for; matrix products, arithmetic and copies ran while one was open for 10% of the time, Pallas kernels for 38%

profile of v15, /device:TPU:0, one launch (start us, length us, event | category | flops | bytes accessed | tf_op | source)
XLA Modules:
  0.0 1066.8 jit_solution(1760145152828985523)
XLA Ops:
  6.2 2.3 pad_maximum_fusion.2.refs_0_
  8.5 167.3 %shard_map.272 = (bf16[4,2048,2048]{2,1,0:T(8,128)(2,1)}, bf16[4096,256]{1,0:T(8,128)(2,1)}, bf16[8,2048,256]{2,1,0:T(8,128)(2,1)}, bf16[8,2048,256]{2,1,0:T(8,1...) custom-call(bf16[4,64,2048]{2,1,0:T(8,128)(2,1)} %pad_maximum_fusion, ...), custom_call_target="tpu_custom_call" | custom-call | tf_op jit(solution)/shard_map/pallas_call | solution.py:330
  176.0 4.3 collective-permute-start.2
  180.3 1.3 slice.90
  181.8 3.0 slice_reduce_fusion
  185.3 4.9 multiply_reduce_fusion.12
  190.2 5.1 multiply_reduce_fusion.11
  195.3 5.8 fusion.28
  201.1 2.3 slice.104
  203.9 1.3 fusion.53
  205.4 1.6 fusion.54
  207.7 3.2 subtract_convert_fusion.2
  211.6 1.5 fusion.55
  213.1 2.4 fusion.52
  215.5 1.6 convolution_convert_fusion.2
  217.1 5.2 multiply_reduce_fusion.10
  222.3 1.6 constant_dynamic-slice_fusion
  227.1 190.0 %shard_map.273 = (bf16[4096,2048]{1,0:T(8,128)(2,1)}, bf16[4096,2048]{1,0:T(8,128)(2,1)}, bf16[8,2048,256]{2,1,0:T(8,128)(2,1)}, bf16[8,2048,256]{2,1,0:T(8,128)...) custom-call(bf16[128,2048]{1,0:T(8,128)(2,1)S(1)} %multiply_convert_, ...), custom_call_target="tpu_custom_call", output_to_operand_aliasing={{2}: (4, {}), {3}: (5, {})} | custom-call | tf_op jit(solution)/shard_map/pallas_call | solution.py:330
  417.1 1.6 collective-permute-start.3
  418.7 2.4 collective-permute-start.4
  421.6 55.3 %shard_map.274 = (bf16[8,768,2048]{2,1,0:T(8,128)(2,1)}, bf16[8,768,2048]{2,1,0:T(8,128)(2,1)}, bf16[8,768,128]{2,1,0:T(8,128)(2,1)}, bf16[6,2048,256]{2,1,0:T(8...) custom-call(s32[1]{0:T(128)} %bitcast.60.names_ref, ...), custom_call_target="tpu_custom_call" | custom-call | tf_op jit(solution)/shard_map/pallas_call | solution.py:1008
  476.9 2.9 dynamic-slice_bitcast_fusion
  479.8 28.3 %collective-permute-done.4.refs_2_ = bf16[2,512,512]{2,1,0:T(8,128)(2,1)} collective-permute-done((bf16[2,512,512]{2,1,0:T(8,128)(2,1)}, bf16[2,512,512]{2,1,0:T(8,128)(2,1)}, u32[]{:S(2)}, u32[]{:S(2)}) %collective-permute-start.4) | collective-permute-done | bytes 1048608 | tf_op jit(solution)/shard_map/ppermute | solution.py:1268
  508.1 15.4 %collective-permute-start.6 = (bf16[1,512,512]{2,1,0:T(8,128)(2,1)}, bf16[1,512,512]{2,1,0:T(8,128)(2,1)}, u32[]{:S(2)}, u32[]{:S(2)}) collective-permute-start(bf16[1,512,512]{2,1,0:T(8,128)(2,1)} %get-tuple-element.218), channel_id=1, source_target_pairs={{0,24},{8,16},{16,8},{24,0},{1,25},{9,17},{17,9},{25,1},{2,26},{10... | collective-permute-start | bytes 1572872 | tf_op jit(solution)/shard_map/ppermute | solution.py:1268
  524.1 1.1 convert_element_type.101
  525.2 1.9 copy.158
  528.2 33.3 %shard_map.275 = (bf16[8,768,2048]{2,1,0:T(8,128)(2,1)}, bf16[8,768,2048]{2,1,0:T(8,128)(2,1)}, bf16[8,768,128]{2,1,0:T(8,128)(2,1)}, bf16[2,2048,256]{2,1,0:T(8...) custom-call(s32[5]{0:T(128)} %stack.73.names_ref, ...), custom_call_target="tpu_custom_call", output_to_operand_aliasing={{0}: (9, {}), {1}: (10, {}), {2}: (11, {}), {5}: (12, {})} | custom-call | tf_op jit(solution)/shard_map/pallas_call | solution.py:1008
  561.5 23.5 %shard_map.276 = bf16[4096,2176]{1,0:T(8,128)(2,1)} custom-call(s32[16,8,256]{2,1,0:T(8,128)} %select_bitcast_fusion.refs_6_.slots_ref.refs_3_, bf16[8,768,2048]{2,1,0:T(8,128)(2,1)} %get-tuple-element.215.dx_ref, bf16[8,768,128]{2,1,0:T(8,128)(2,1)} %get-tuple-element.216.probs_ref), custom_call_target="tpu_custom_call" | custom-call | tf_op jit(solution)/shard_map/pallas_call | solution.py:1058
  585.0 124.7 %shard_map.277 = (f32[128,2176]{1,0:T(8,128)}, bf16[8,512,1024]{2,1,0:T(8,128)(2,1)}, bf16[8,512,1024]{2,1,0:T(8,128)(2,1)}, bf16[4096,2048]{1,0:T(8,128)(2,1)},...) custom-call(bf16[4,8,128,2176]{3,2,1,0:T(8,128)(2,1)} %bitcast.162, ...), custom_call_target="tpu_custom_call" | custom-call | tf_op jit(solution)/shard_map/pallas_call | solution.py:683
  709.8 1.4 collective-permute-start.11
  711.2 3.0 collective-permute-start.9
  714.8 5.1 shard_map.278
  719.8 3.7 shard_map.279
  723.6 86.7 %conditional.1 = (f32[128,2048]{1,0:T(8,128)}, bf16[4,8,64,2048]{3,2,1,0:T(8,128)(2,1)}, bf16[4,8,64,2048]{3,2,1,0:T(8,128)(2,1)}, bf16[4,8,64,2048]{3,2,1,0:T(8...) conditional(s32[]{:T(128)} %bitcast.71, () %tuple.38, ...), branch_computations={%region_12.13_spmd, %region_13.24_spmd} | conditional | flops 387291904 | bytes 72241888 | solution.py:1561
  724.0 1.1 multiply_reduce_fusion.9
  726.1 1.6 copy.127
  727.7 1.8 multiply_reduce_fusion
  729.4 2.6 fusion.51
  732.0 6.7 branch_1_fun.3
  738.8 2.1 convert_element_type.76
  740.9 1.3 copy.154
  742.2 1.5 multiply_reduce_fusion.7
  744.0 1.6 fusion.1
  745.5 1.5 fusion.2
  747.3 1.3 multiply_subtract_fusion
  748.6 1.1 pad_maximum_fusion.1
  749.6 2.5 copy.145
  752.2 2.4 pad_maximum_fusion
  754.5 2.5 copy.144
  757.1 1.6 copy.132
  758.6 1.6 copy.130
  760.2 2.5 multiply_reduce_fusion.1
  762.7 2.6 subtract_convert_fusion.refs_1_.refs_4_
  765.3 2.3 subtract_convert_fusion.1.refs_0_.refs_5_
  769.2 2.0 copy.135.refs_0_
  771.2 13.8 %branch_1_fun.5 = (bf16[2048,2048]{1,0:T(8,128)(2,1)}, bf16[2048,2048]{1,0:T(8,128)(2,1)}, bf16[2048,2048]{1,0:T(8,128)(2,1)}, bf16[2048,2048]{1,0:T(8,128)(2,1)}) custom-call(bf16[128,2048]{1,0:T(8,128)(2,1)} %copy.135.refs_0_, bf16[128,2048]{1,0:T(8,128)(2,1)} %get-tuple-element.85.refs_1_, bf16[128,2048]{1,0:T(8,128)(2,1)} %get-tuple-element.380.refs_0_.refs_2_, ...), custom_call_target="tpu_custom_call" | custom-call | tf_op jit(solution)/shard_map/cond/branch_1_fun/pallas_call | solution.py:1109
  785.0 17.6 %branch_1_fun.4 = f32[128,2048]{1,0:T(8,128)} custom-call(bf16[128,2048]{1,0:T(8,128)(2,1)} %subtract_convert_fusion.1.refs_0_.refs_5_, bf16[128,2048]{1,0:T(8,128)(2,1)} %subtract_convert_fusion.refs_1_.refs_4_, bf16[128,2048]{1,0:T(8,128)(2,1)} %copy.146.refs_2_.refs_3_, bf16[4,2048,2048]{2,1,0:T(8,128)(2,1)} %get-tuple-element.70.refs_1_.refs_3_), custom_call_target="tpu_custom_call" | custom-call | tf_op jit(solution)/shard_map/cond/branch_1_fun/pallas_call | solution.py:1083
  802.6 1.6 copy.134
  804.2 1.5 multiply_reduce_fusion.3
  806.1 2.8 subtract_add_fusion
  810.3 236.9 %shard_map.280 = (f32[128,2048]{1,0:T(8,128)}, f32[64,2048]{1,0:T(8,128)}, f32[64,2048]{1,0:T(8,128)}, f32[64,2048]{1,0:T(8,128)}, f32[64,2048]{1,0:T(8,128)}, /...) custom-call(bf16[4,8,128,2048]{3,2,1,0:T(8,128)(2,1)} %bitcast.163, ...), custom_call_target="tpu_custom_call" | custom-call | tf_op jit(solution)/shard_map/pallas_call | solution.py:683
  1047.2 7.3 shard_map.281
  1054.5 1.4 slice_bitcast_fusion
  1056.8 5.8 shard_map.282
  (151 shorter events, 23.8 us)
Async XLA Ops:
  175.8 9.1 copy-start.9
  175.8 51.3 %collective-permute-start = (bf16[1,512,512]{2,1,0:T(8,128)(2,1)}, bf16[1,512,512]{2,1,0:T(8,128)(2,1)}, u32[]{:S(2)}, u32[]{:S(2)}) collective-permute-start(bf16[1,512,512]{2,1,0:T(8,128)(2,1)} %get-tuple-element.192), channel_id=1, source_target_pairs={{0,24},{8,16},{16,8},{24,0},{1,25},{9,17},{17,9},{25,1},{2,26},{10... | collective-permute-start | bytes 1572872 | tf_op jit(solution)/shard_map/ppermute | solution.py:1268
  175.9 51.2 %collective-permute-start.1 = (bf16[1,512,512]{2,1,0:T(8,128)(2,1)}, bf16[1,512,512]{2,1,0:T(8,128)(2,1)}, u32[]{:S(2)}, u32[]{:S(2)}) collective-permute-start(bf16[1,512,512]{2,1,0:T(8,128)(2,1)} %get-tuple-element.193), channel_id=1, source_target_pairs={{0,16},{8,24},{16,0},{24,8},{1,17},{9,25},{17,1},{25,9},{2,18},{10... | collective-permute-start | bytes 1572872 | tf_op jit(solution)/shard_map/ppermute | solution.py:1268
  176.0 51.1 %collective-permute-start.2 = (bf16[1,512,512]{2,1,0:T(8,128)(2,1)}, bf16[1,512,512]{2,1,0:T(8,128)(2,1)}, u32[]{:S(2)}, u32[]{:S(2)}) collective-permute-start(bf16[1,512,512]{2,1,0:T(8,128)(2,1)} %get-tuple-element.194), channel_id=1, source_target_pairs={{0,8},{8,0},{16,24},{24,16},{1,9},{9,1},{17,25},{25,17},{2,10},{10... | collective-permute-start | bytes 1572872 | tf_op jit(solution)/shard_map/ppermute | solution.py:1268
  185.0 10.2 copy-start.28
  185.3 10.1 copy-start.17
  190.2 13.3 %copy-start.2 = (f32[128,2048]{1,0:T(8,128)}, f32[128,2048]{1,0:T(8,128)S(1)}, u32[]{:S(2)}) copy-start(f32[128,2048]{1,0:T(8,128)S(1)} %get-tuple-element.424) | copy-start | bytes 3145732
  195.3 8.4 copy-start.4
  203.4 3.6 copy-start.24
  203.4 3.6 copy-start.26
  203.5 3.6 copy-start.30
  207.1 10.0 copy-start.10
  211.3 4.2 copy-start.15
  211.6 5.5 copy-start.16
  215.5 1.6 copy-start.7
  217.1 5.2 copy-start.14
  227.1 300.7 %copy-start.5 = (bf16[128,2048]{1,0:T(8,128)(2,1)}, bf16[128,2048]{1,0:T(8,128)(2,1)S(1)}, u32[]{:S(2)}) copy-start(bf16[128,2048]{1,0:T(8,128)(2,1)S(1)} %multiply_convert_fusion.2.refs_0_) | copy-start | bytes 1572868
  417.1 62.7 %collective-permute-start.3 = (bf16[2,512,512]{2,1,0:T(8,128)(2,1)}, bf16[2,512,512]{2,1,0:T(8,128)(2,1)}, u32[]{:S(2)}, u32[]{:S(2)}) collective-permute-start(bf16[2,512,512]{2,1,0:T(8,128)(2,1)} %get-tuple-element.206), channel_id=1, source_target_pairs={{0,24},{8,16},{16,8},{24,0},{1,25},{9,17},{17,9},{25,1},{2,26},{10... | collective-permute-start | bytes 3145736 | tf_op jit(solution)/shard_map/ppermute | solution.py:1268
  418.7 89.4 %collective-permute-start.4 = (bf16[2,512,512]{2,1,0:T(8,128)(2,1)}, bf16[2,512,512]{2,1,0:T(8,128)(2,1)}, u32[]{:S(2)}, u32[]{:S(2)}) collective-permute-start(bf16[2,512,512]{2,1,0:T(8,128)(2,1)} %get-tuple-element.207), channel_id=1, source_target_pairs={{0,16},{8,24},{16,0},{24,8},{1,17},{9,25},{17,1},{25,9},{2,18},{10... | collective-permute-start | bytes 3145736 | tf_op jit(solution)/shard_map/ppermute | solution.py:1268
  421.1 87.0 %collective-permute-start.5 = (bf16[2,512,512]{2,1,0:T(8,128)(2,1)}, bf16[2,512,512]{2,1,0:T(8,128)(2,1)}, u32[]{:S(2)}, u32[]{:S(2)}) collective-permute-start(bf16[2,512,512]{2,1,0:T(8,128)(2,1)} %get-tuple-element.208), channel_id=1, source_target_pairs={{0,8},{8,0},{16,24},{24,16},{1,9},{9,1},{17,25},{25,17},{2,10},{10... | collective-permute-start | bytes 3145736 | tf_op jit(solution)/shard_map/ppermute | solution.py:1268
  421.6 102.5 %copy-start.11 = (bf16[128,2048]{1,0:T(8,128)(2,1)S(1)}, bf16[128,2048]{1,0:T(8,128)(2,1)}, u32[]{:S(2)}) copy-start(bf16[128,2048]{1,0:T(8,128)(2,1)} %param.19) | copy-start | bytes 1572868
  508.1 76.9 %collective-permute-start.6 = (bf16[1,512,512]{2,1,0:T(8,128)(2,1)}, bf16[1,512,512]{2,1,0:T(8,128)(2,1)}, u32[]{:S(2)}, u32[]{:S(2)}) collective-permute-start(bf16[1,512,512]{2,1,0:T(8,128)(2,1)} %get-tuple-element.218), channel_id=1, source_target_pairs={{0,24},{8,16},{16,8},{24,0},{1,25},{9,17},{17,9},{25,1},{2,26},{10... | collective-permute-start | bytes 1572872 | tf_op jit(solution)/shard_map/ppermute | solution.py:1268
  523.5 61.5 %collective-permute-start.7 = (bf16[1,512,512]{2,1,0:T(8,128)(2,1)}, bf16[1,512,512]{2,1,0:T(8,128)(2,1)}, u32[]{:S(2)}, u32[]{:S(2)}) collective-permute-start(bf16[1,512,512]{2,1,0:T(8,128)(2,1)} %get-tuple-element.219), channel_id=1, source_target_pairs={{0,16},{8,24},{16,0},{24,8},{1,17},{9,25},{17,1},{25,9},{2,18},{10... | collective-permute-start | bytes 1572872 | tf_op jit(solution)/shard_map/ppermute | solution.py:1268
  523.5 61.5 %collective-permute-start.8 = (bf16[1,512,512]{2,1,0:T(8,128)(2,1)}, bf16[1,512,512]{2,1,0:T(8,128)(2,1)}, u32[]{:S(2)}, u32[]{:S(2)}) collective-permute-start(bf16[1,512,512]{2,1,0:T(8,128)(2,1)} %get-tuple-element.220), channel_id=1, source_target_pairs={{0,8},{8,0},{16,24},{24,16},{1,9},{9,1},{17,25},{25,17},{2,10},{10... | collective-permute-start | bytes 1572872 | tf_op jit(solution)/shard_map/ppermute | solution.py:1268
  709.7 347.1 %collective-permute-start.10 = (bf16[2,512,512]{2,1,0:T(8,128)(2,1)}, bf16[2,512,512]{2,1,0:T(8,128)(2,1)}, u32[]{:S(2)}, u32[]{:S(2)}) collective-permute-start(bf16[2,512,512]{2,1,0:T(8,128)(2,1)} %get-tuple-element.256), channel_id=1, source_target_pairs={{0,16},{8,24},{16,0},{24,8},{1,17},{9,25},{17,1},{25,9},{2,18},{10... | collective-permute-start | bytes 3145736 | tf_op jit(solution)/shard_map/ppermute | solution.py:1268
  709.8 347.0 %collective-permute-start.11 = (bf16[2,512,512]{2,1,0:T(8,128)(2,1)}, bf16[2,512,512]{2,1,0:T(8,128)(2,1)}, u32[]{:S(2)}, u32[]{:S(2)}) collective-permute-start(bf16[2,512,512]{2,1,0:T(8,128)(2,1)} %get-tuple-element.257), channel_id=1, source_target_pairs={{0,8},{8,0},{16,24},{24,16},{1,9},{9,1},{17,25},{25,17},{2,10},{10... | collective-permute-start | bytes 3145736 | tf_op jit(solution)/shard_map/ppermute | solution.py:1268
  711.2 345.6 %collective-permute-start.9 = (bf16[2,512,512]{2,1,0:T(8,128)(2,1)}, bf16[2,512,512]{2,1,0:T(8,128)(2,1)}, u32[]{:S(2)}, u32[]{:S(2)}) collective-permute-start(bf16[2,512,512]{2,1,0:T(8,128)(2,1)} %get-tuple-element.255), channel_id=1, source_target_pairs={{0,24},{8,16},{16,8},{24,0},{1,25},{9,17},{17,9},{25,1},{2,26},{10... | collective-permute-start | bytes 3145736 | tf_op jit(solution)/shard_map/ppermute | solution.py:1268
  719.8 3.7 copy-start
  719.8 3.8 copy-start.25
  719.8 3.8 copy-start.27
  719.8 3.8 copy-start.29
  742.2 7.4 copy-start.12
  745.5 14.7 %copy-start.3 = (f32[128,2048]{1,0:T(8,128)S(1)}, f32[128,2048]{1,0:T(8,128)}, u32[]{:S(2)}) copy-start(f32[128,2048]{1,0:T(8,128)} %get-tuple-element.76) | copy-start | bytes 3145732 | tf_op jit(solution)/shard_map/cond
  752.2 15.5 %copy-start.8 = (bf16[16,128,128]{1,2,0:T(8,128)(2,1)S(1)}, bf16[16,128,128]{1,2,0:T(8,128)(2,1)}, u32[]{:S(2)}) copy-start(bf16[16,128,128]{1,2,0:T(8,128)(2,1)} %get-tuple-element.357) | copy-start | bytes 1572868 | tf_op jit(solution)/shard_map/cond
  760.2 7.4 copy-start.13
  785.0 19.2 %copy-start.1 = (f32[128,2048]{1,0:T(8,128)S(1)}, f32[128,2048]{1,0:T(8,128)}, u32[]{:S(2)}) copy-start(f32[128,2048]{1,0:T(8,128)} %get-tuple-element.83) | copy-start | bytes 3145732 | tf_op jit(solution)/shard_map/cond
  785.0 24.0 %copy-start.6 = (bf16[128,2048]{1,0:T(8,128)(2,1)S(1)}, bf16[128,2048]{1,0:T(8,128)(2,1)}, u32[]{:S(2)}) copy-start(bf16[128,2048]{1,0:T(8,128)(2,1)} %get-tuple-element.90) | copy-start | bytes 1572868 | tf_op jit(solution)/shard_map/cond
  1047.2 8.7 copy-start.18
  1056.8 5.8 copy-start.22
  1056.8 6.6 copy-start.21
  1056.8 7.4 copy-start.20
  1056.8 8.2 copy-start.19
  1056.8 9.0 copy-start.23

commit v16 on v15

--- a/solution.py
+++ b/solution.py
@@ -1065,6 +1065,77 @@
     )(slots, dx, probs)
 
 
+def core_back_kernel(
+    scale,
+    q_ref,
+    k_ref,
+    v_ref,
+    grad_ref,
+    probs_ref,
+    cos_ref,
+    sin_ref,
+    q_raw_ref,
+    k_raw_ref,
+    q_inverse_ref,
+    k_inverse_ref,
+    q_gain_ref,
+    k_gain_ref,
+    grad_q_ref,
+    grad_k_ref,
+    grad_v_ref,
+    grad_q_gain_ref,
+    grad_k_gain_ref,
+    q_turned,
+    k_turned,
+):
+    bf16 = jnp.bfloat16
+    cosine, sine = cos_ref[...], sin_ref[...]
+    for head in range(HEADS):
+        at = slice(head * HD, (head + 1) * HD)
+        probs, grad = probs_ref[head], grad_ref[:, at]
+        weights = dot(grad, v_ref[:, at], (1, 1))
+        scores = probs * (weights - jnp.sum(probs * weights, axis=1, keepdims=True))
+        scores = scores.astype(bf16)
+        grad_v_ref[:, at] = dot(probs.astype(bf16), grad, (0, 0)).astype(bf16)
+        for other_ref, side, turned in ((k_ref, 1, q_turned), (q_ref, 0, k_turned)):
+            rope = dot(scores, other_ref[:, at], (side, 0)) * scale
+            turned[:, at] = rope * cosine + pltpu.roll(rope, HD // 2, 1) * sine
+    for turned, raw_ref, inverse_ref, gain_ref, out_ref, out_gain_ref in (
+        (q_turned, q_raw_ref, q_inverse_ref, q_gain_ref, grad_q_ref, grad_q_gain_ref),
+        (k_turned, k_raw_ref, k_inverse_ref, k_gain_ref, grad_k_ref, grad_k_gain_ref),
+    ):
+        grad, raw, inverse = turned[...], raw_ref[...], inverse_ref[...]
+        scaled = grad * gain_ref[...]
+        inner = jnp.mean(scaled * raw, axis=1, keepdims=True)
+        out_ref[...] = (inverse * scaled - raw * (inverse * inverse * inverse) * inner).astype(bf16)
+        out_gain_ref[...] = jnp.sum(grad * raw * inverse, axis=0, keepdims=True)
+
+
+def core_back(scale, q, k, v, grad, probs, cosine, sine, q_raw, k_raw, q_inverse, k_inverse, gains):
+    count, depth = q.shape
+    low = jax.ShapeDtypeStruct((count, depth), jnp.bfloat16)
+    gain = jax.ShapeDtypeStruct((1, depth), jnp.float32)
+    return pl.pallas_call(
+        functools.partial(core_back_kernel, scale),
+        out_shape=[low, low, low, gain, gain],
+        scratch_shapes=[pltpu.VMEM((count, depth), jnp.float32)] * 2,
+        compiler_params=pltpu.CompilerParams(vmem_limit_bytes=BIG),
+    )(
+        q,
+        k,
+        v,
+        grad,
+        probs,
+        jnp.concatenate([cosine, cosine], axis=1),
+        jnp.concatenate([sine, -sine], axis=1),
+        q_raw,
+        k_raw,
+        q_inverse,
+        k_inverse,
+        *[one[None] for one in gains],
+    )
+
+
 def through_kernel(count, *refs):
     lefts, weight_ref, out_ref = refs[:count], refs[count], refs[count + 1]
     for i in range(count):
@@ -1515,25 +1586,22 @@
         grad_middle_part, grad_mlp_gain = rms_backward(middle, mlp_inverse, mlp_gain, grad_mlp)
         grad_middle = grad_final + grad_middle_part
         grad_branch_low = grad_middle.astype(bf16)
-        grad_attended = (
-            through([grad_branch_low], weights_all, 3).astype(bf16).reshape(count, HEADS, HD)
+        grad_attended = through([grad_branch_low], weights_all, 3).astype(bf16)
+        grad_query_low, grad_key_low, grad_value_low, grad_query_gain, grad_key_gain = core_back(
+            scale,
+            query_low.reshape(count, D),
+            key_low.reshape(count, D),
+            value_low,
+            grad_attended,
+            probs,
+            cosine[:, 0],
+            sine[:, 0],
+            query_raw,
+            key_raw,
+            query_inverse,
+            key_inverse,
+            (query_gain, key_gain),
         )
-        grad_weights = product(grad_attended, value_heads, "qhd,khd->hqk")
-        grad_scores = probs * (grad_weights - jnp.sum(probs * grad_weights, axis=-1, keepdims=True))
-        grad_scores_low = grad_scores.astype(bf16)
-        grad_query_turn = product(grad_scores_low, key_low, "hqk,khd->qhd").reshape(count, D) * scale
-        grad_key_turn = product(grad_scores_low, query_low, "hqk,qhd->khd").reshape(count, D) * scale
-        grad_value_low = (
-            product(probs_low, grad_attended, "hqk,qhd->khd").reshape(count, D).astype(bf16)
-        )
-        grad_query_raw, grad_query_gain = rms_backward(
-            query_raw, query_inverse, query_gain, rotate(grad_query_turn, cosine, -sine)
-        )
-        grad_key_raw, grad_key_gain = rms_backward(
-            key_raw, key_inverse, key_gain, rotate(grad_key_turn, cosine, -sine)
-        )
-        grad_query_low = grad_query_raw.astype(bf16)
-        grad_key_low = grad_key_raw.astype(bf16)
         full_grads = outer(
             [attended_low, normed_low],
             [grad_branch_low, grad_value_low, grad_key_low, grad_query_low],
@@ -1543,7 +1611,9 @@
         grad_inputs_part, grad_attn_gain = rms_backward(inputs, attn_inverse, attn_gain, grad_normed)
         grad_inputs = grad_middle + grad_inputs_part
 
-        gain_grads = jnp.stack([grad_attn_gain, grad_query_gain, grad_key_gain, grad_mlp_gain])
+        gain_grads = jnp.stack(
+            [grad_attn_gain, grad_query_gain[0], grad_key_gain[0], grad_mlp_gain]
+        )
         gain_grads = jnp.transpose(gain_grads.reshape(4, groups, rows_each), (1, 0, 2))
         gain_grads = jnp.pad(gain_grads, ((0, 0), (0, 12), (0, width - rows_each)))
         return (

time: 1080 us -> 1070 us (level)
  other arithmetic: 38.7 us -> 27.5 us
    dot_general x13 -> x9, matrix products: 30.5 us -> 25.8 us  [product(): return jnp.einsum(form, left, right, preferred_element_type=jnp.float32)]
  transfers between devices with their start and end apart: 12 -> 12, of which waited for: 1 -> 1; matrix products, arithmetic and copies ran while one was open for 10% -> 8% of each run, Pallas kernels for 38% -> 39%
where the time goes in v16:
time: 1070 us; the launch traced here: 1060 us
  Pallas kernels  900 us (84%)
  local copies, waits for them, and re-layouts  44.4 us (4%)
  starting transfers between devices  29.3 us (3%)
  waiting for transfers between devices  28.3 us (3%)
  other arithmetic  27.5 us (3%)
  matrix products  27.3 us (3%)
    pallas_call x2, Pallas kernels, scatter_call(): pl.pallas_call(functools.partial(scatter_kernel, n_dp, n_expert, count, i...  361 us
    pallas_call x2, Pallas kernels, gather_call(): pl.pallas_call(functools.partial(gather_kernel, n_dp, n_expert, n, places...  357 us
    pallas_call x2, Pallas kernels, expert_call(): pl.pallas_call(functools.partial(expert_kernel, steps, half, len(weights)...  88.7 us
    ppermute x12, starting transfers between devices, permuted(): got.append(lax.ppermute(piece, 'dp', paths))  29.3 us
    ppermute x12, waiting for transfers between devices, permuted(): got.append(lax.ppermute(piece, 'dp', paths))  28.3 us
    dot_general x9, matrix products, product(): return jnp.einsum(form, left, right, preferred_element_type=jnp.float32)  25.8 us
    pallas_call x2, Pallas kernels, through(): pl.pallas_call(functools.partial(through_kernel, count), grid=(depth // p...  24.4 us
    pallas_call x1, Pallas kernels, place_back(): pl.pallas_call(functools.partial(place_back_kernel, number), grid=(pairs,...  23.5 us
  transfers between devices with their start and end apart: 12, of which 1 were waited for; matrix products, arithmetic and copies ran while one was open for 8% of the time, Pallas kernels for 39%

profile of v16, /device:TPU:0, one launch (start us, length us, event | category | flops | bytes accessed | tf_op | source)
XLA Modules:
  0.0 1058.3 jit_solution(15448370286492511035)
XLA Ops:
  4.8 0.8 concatenate.24
  6.2 2.3 pad_maximum_fusion.2.refs_0_
  8.5 167.3 %shard_map.272 = (bf16[4,2048,2048]{2,1,0:T(8,128)(2,1)}, bf16[4096,256]{1,0:T(8,128)(2,1)}, bf16[8,2048,256]{2,1,0:T(8,128)(2,1)}, bf16[8,2048,256]{2,1,0:T(8,1...) custom-call(bf16[4,64,2048]{2,1,0:T(8,128)(2,1)} %pad_maximum_fusion, ...), custom_call_target="tpu_custom_call" | custom-call | tf_op jit(solution)/shard_map/pallas_call | solution.py:330
  176.0 4.3 collective-permute-start.2
  180.3 1.3 slice.78
  181.8 3.0 slice_reduce_fusion
  185.2 5.8 multiply_reduce_fusion.7
  191.0 5.7 multiply_reduce_fusion.6
  196.7 4.6 fusion.21
  201.4 2.4 slice.92
  203.9 1.8 multiply_bitcast_fusion
  205.9 1.6 fusion.44
  207.7 1.3 fusion.45
  209.4 1.0 copy.121
  210.7 3.2 multiply_subtract_fusion
  214.6 1.5 fusion.46
  216.1 1.3 broadcast_divide_fusion.1
  217.4 1.7 convolution_convert_fusion.1
  220.0 5.0 multiply_reduce_fusion.5
  225.0 1.6 constant_dynamic-slice_fusion
  228.7 0.9 pad.18.refs_7_
  229.8 190.0 %shard_map.273 = (bf16[4096,2048]{1,0:T(8,128)(2,1)}, bf16[4096,2048]{1,0:T(8,128)(2,1)}, bf16[8,2048,256]{2,1,0:T(8,128)(2,1)}, bf16[8,2048,256]{2,1,0:T(8,128)...) custom-call(bf16[128,2048]{1,0:T(8,128)(2,1)S(1)} %multiply_convert_, ...), custom_call_target="tpu_custom_call", output_to_operand_aliasing={{2}: (4, {}), {3}: (5, {})} | custom-call | tf_op jit(solution)/shard_map/pallas_call | solution.py:330
  419.8 1.6 collective-permute-start.3
  421.3 2.4 collective-permute-start.4
  424.2 55.3 %shard_map.274 = (bf16[8,768,2048]{2,1,0:T(8,128)(2,1)}, bf16[8,768,2048]{2,1,0:T(8,128)(2,1)}, bf16[8,768,128]{2,1,0:T(8,128)(2,1)}, bf16[6,2048,256]{2,1,0:T(8...) custom-call(s32[1]{0:T(128)} %bitcast.50.names_ref, ...), custom_call_target="tpu_custom_call" | custom-call | tf_op jit(solution)/shard_map/pallas_call | solution.py:1008
  479.5 2.9 dynamic-slice_bitcast_fusion
  482.4 28.3 %collective-permute-done.4.refs_2_ = bf16[2,512,512]{2,1,0:T(8,128)(2,1)} collective-permute-done((bf16[2,512,512]{2,1,0:T(8,128)(2,1)}, bf16[2,512,512]{2,1,0:T(8,128)(2,1)}, u32[]{:S(2)}, u32[]{:S(2)}) %collective-permute-start.4) | collective-permute-done | bytes 1048608 | tf_op jit(solution)/shard_map/ppermute | solution.py:1339
  510.7 15.4 %collective-permute-start.6 = (bf16[1,512,512]{2,1,0:T(8,128)(2,1)}, bf16[1,512,512]{2,1,0:T(8,128)(2,1)}, u32[]{:S(2)}, u32[]{:S(2)}) collective-permute-start(bf16[1,512,512]{2,1,0:T(8,128)(2,1)} %get-tuple-element.220), channel_id=1, source_target_pairs={{0,24},{8,16},{16,8},{24,0},{1,25},{9,17},{17,9},{25,1},{2,26},{10... | collective-permute-start | bytes 1572872 | tf_op jit(solution)/shard_map/ppermute | solution.py:1339
  526.7 1.1 convert_element_type.95
  528.7 33.4 %shard_map.275 = (bf16[8,768,2048]{2,1,0:T(8,128)(2,1)}, bf16[8,768,2048]{2,1,0:T(8,128)(2,1)}, bf16[8,768,128]{2,1,0:T(8,128)(2,1)}, bf16[2,2048,256]{2,1,0:T(8...) custom-call(s32[5]{0:T(128)} %stack.71.names_ref, ...), custom_call_target="tpu_custom_call", output_to_operand_aliasing={{0}: (9, {}), {1}: (10, {}), {2}: (11, {}), {5}: (12, {})} | custom-call | tf_op jit(solution)/shard_map/pallas_call | solution.py:1008
  562.1 23.5 %shard_map.276 = bf16[4096,2176]{1,0:T(8,128)(2,1)} custom-call(s32[16,8,256]{2,1,0:T(8,128)} %select_bitcast_fusion.refs_6_.slots_ref.refs_3_, bf16[8,768,2048]{2,1,0:T(8,128)(2,1)} %get-tuple-element.217.dx_ref, bf16[8,768,128]{2,1,0:T(8,128)(2,1)} %get-tuple-element.218.probs_ref), custom_call_target="tpu_custom_call" | custom-call | tf_op jit(solution)/shard_map/pallas_call | solution.py:1058
  585.6 124.6 %shard_map.277 = (f32[128,2176]{1,0:T(8,128)}, bf16[8,512,1024]{2,1,0:T(8,128)(2,1)}, bf16[8,512,1024]{2,1,0:T(8,128)(2,1)}, bf16[4096,2048]{1,0:T(8,128)(2,1)},...) custom-call(bf16[4,8,128,2176]{3,2,1,0:T(8,128)(2,1)} %bitcast.137, ...), custom_call_target="tpu_custom_call" | custom-call | tf_op jit(solution)/shard_map/pallas_call | solution.py:683
  710.3 1.6 collective-permute-start.11
  711.9 2.8 collective-permute-start.9
  715.4 5.1 shard_map.278
  720.5 3.7 shard_map.279
  724.2 77.5 %conditional.1 = (f32[128,2048]{1,0:T(8,128)}, bf16[4,8,64,2048]{3,2,1,0:T(8,128)(2,1)}, bf16[4,8,64,2048]{3,2,1,0:T(8,128)(2,1)}, bf16[4,8,64,2048]{3,2,1,0:T(8...) conditional(s32[]{:T(128)} %bitcast.61, () %tuple.38, ...), branch_computations={%region_12.13_spmd, %region_13.19_spmd} | conditional | flops 108413184 | bytes 35258440 | solution.py:1631
  724.6 1.1 multiply_reduce_fusion.4
  725.7 1.0 multiply_convert_fusion
  726.7 1.6 copy.110
  728.3 1.8 multiply_reduce_fusion
  730.1 2.6 fusion.43
  732.7 6.8 branch_1_fun.4
  739.5 2.1 convert_element_type.72.grad_ref
  742.3 1.2 copy_bitcast_fusion
  743.5 2.6 copy.115.probs_ref
  747.6 2.1 copy.111
  749.8 2.1 copy.112
  751.9 8.6 branch_1_fun.5
  760.5 2.1 copy.117.refs_0_
  762.6 13.8 %branch_1_fun.7 = (bf16[2048,2048]{1,0:T(8,128)(2,1)}, bf16[2048,2048]{1,0:T(8,128)(2,1)}, bf16[2048,2048]{1,0:T(8,128)(2,1)}, bf16[2048,2048]{1,0:T(8,128)(2,1)}) custom-call(bf16[128,2048]{1,0:T(8,128)(2,1)} %copy.117.refs_0_, bf16[128,2048]{1,0:T(8,128)(2,1)} %get-tuple-element.85.refs_1_, bf16[128,2048]{1,0:T(8,128)(2,1)} %get-tuple-element.375.refs_0_.refs_2_, ...), custom_call_target="tpu_custom_call" | custom-call | tf_op jit(solution)/shard_map/cond/branch_1_fun/pallas_call | solution.py:1180
  776.4 17.6 %branch_1_fun.6 = f32[128,2048]{1,0:T(8,128)} custom-call(bf16[128,2048]{1,0:T(8,128)(2,1)} %get-tuple-element.79.refs_0_.refs_5_, bf16[128,2048]{1,0:T(8,128)(2,1)} %get-tuple-element.80.refs_1_.refs_4_, bf16[128,2048]{1,0:T(8,128)(2,1)} %get-tuple-element.81.refs_2_.refs_3_, bf16[4,2048,2048]{2,1,0:T(8,128)(2,1)} %get-tuple-element.69.refs_1_.refs_3_), custom_call_target="tpu_custom_call" | custom-call | tf_op jit(solution)/shard_map/cond/branch_1_fun/pallas_call | solution.py:1154
  794.0 1.6 copy.116
  795.5 1.5 multiply_reduce_fusion.1
  797.6 2.8 subtract_add_fusion
  800.7 1.0 copy.96
  801.7 236.9 %shard_map.280 = (f32[128,2048]{1,0:T(8,128)}, f32[64,2048]{1,0:T(8,128)}, f32[64,2048]{1,0:T(8,128)}, f32[64,2048]{1,0:T(8,128)}, f32[64,2048]{1,0:T(8,128)}, /...) custom-call(bf16[4,8,128,2048]{3,2,1,0:T(8,128)(2,1)} %bitcast.138, ...), custom_call_target="tpu_custom_call" | custom-call | tf_op jit(solution)/shard_map/pallas_call | solution.py:683
  1038.6 7.3 shard_map.281
  1045.9 1.3 slice_bitcast_fusion
  1047.3 0.9 add_convert_fusion
  1048.2 5.8 shard_map.282
  1054.0 0.8 copy.174
  1054.8 0.8 copy.175
  1055.6 0.8 copy.176
  (132 shorter events, 17.6 us)
Async XLA Ops:
  175.8 9.0 copy-start.4
  175.8 54.0 %collective-permute-start = (bf16[1,512,512]{2,1,0:T(8,128)(2,1)}, bf16[1,512,512]{2,1,0:T(8,128)(2,1)}, u32[]{:S(2)}, u32[]{:S(2)}) collective-permute-start(bf16[1,512,512]{2,1,0:T(8,128)(2,1)} %get-tuple-element.194), channel_id=1, source_target_pairs={{0,24},{8,16},{16,8},{24,0},{1,25},{9,17},{17,9},{25,1},{2,26},{10... | collective-permute-start | bytes 1572872 | tf_op jit(solution)/shard_map/ppermute | solution.py:1339
  175.9 53.9 %collective-permute-start.1 = (bf16[1,512,512]{2,1,0:T(8,128)(2,1)}, bf16[1,512,512]{2,1,0:T(8,128)(2,1)}, u32[]{:S(2)}, u32[]{:S(2)}) collective-permute-start(bf16[1,512,512]{2,1,0:T(8,128)(2,1)} %get-tuple-element.195), channel_id=1, source_target_pairs={{0,16},{8,24},{16,0},{24,8},{1,17},{9,25},{17,1},{25,9},{2,18},{10... | collective-permute-start | bytes 1572872 | tf_op jit(solution)/shard_map/ppermute | solution.py:1339
  176.0 53.8 %collective-permute-start.2 = (bf16[1,512,512]{2,1,0:T(8,128)(2,1)}, bf16[1,512,512]{2,1,0:T(8,128)(2,1)}, u32[]{:S(2)}, u32[]{:S(2)}) collective-permute-start(bf16[1,512,512]{2,1,0:T(8,128)(2,1)} %get-tuple-element.196), channel_id=1, source_target_pairs={{0,8},{8,0},{16,24},{24,16},{1,9},{9,1},{17,25},{25,17},{2,10},{10... | collective-permute-start | bytes 1572872 | tf_op jit(solution)/shard_map/ppermute | solution.py:1339
  185.0 11.7 %copy-start.21 = (f32[128]{0:T(128)}, f32[128]{0:T(128)S(1)}, u32[]{:S(2)}) copy-start(f32[128]{0:T(128)S(1)} %add_rsqrt_fusion.3) | copy-start | bytes 1540
  185.2 11.5 %copy-start.11 = (bf16[128,2048]{1,0:T(8,128)(2,1)}, bf16[128,2048]{1,0:T(8,128)(2,1)S(1)}, u32[]{:S(2)}) copy-start(bf16[128,2048]{1,0:T(8,128)(2,1)S(1)} %multiply_convert_fusion.2) | copy-start | bytes 1572868
  201.4 8.0 copy-start.12
  203.9 5.2 copy-start.23
  203.9 5.2 copy-start.25
  203.9 5.1 copy-start.27
  214.3 10.8 %copy-start.6 = (bf16[128,16,128]{2,0,1:T(8,128)(2,1)}, bf16[128,16,128]{2,0,1:T(8,128)(2,1)S(1)}, u32[]{:S(2)}) copy-start(bf16[128,16,128]{2,0,1:T(8,128)(2,1)S(1)} %maximum_convert_fusion.1) | copy-start | bytes 1572868
  214.6 4.6 copy-start.8
  217.4 1.7 copy-start.1
  219.2 0.8 copy-start.10
  229.8 298.6 %copy-start.2 = (bf16[128,2048]{1,0:T(8,128)(2,1)}, bf16[128,2048]{1,0:T(8,128)(2,1)S(1)}, u32[]{:S(2)}) copy-start(bf16[128,2048]{1,0:T(8,128)(2,1)S(1)} %multiply_convert_fusion.1.refs_0_) | copy-start | bytes 1572868
  419.8 62.7 %collective-permute-start.3 = (bf16[2,512,512]{2,1,0:T(8,128)(2,1)}, bf16[2,512,512]{2,1,0:T(8,128)(2,1)}, u32[]{:S(2)}, u32[]{:S(2)}) collective-permute-start(bf16[2,512,512]{2,1,0:T(8,128)(2,1)} %get-tuple-element.208), channel_id=1, source_target_pairs={{0,24},{8,16},{16,8},{24,0},{1,25},{9,17},{17,9},{25,1},{2,26},{10... | collective-permute-start | bytes 3145736 | tf_op jit(solution)/shard_map/ppermute | solution.py:1339
  421.3 89.4 %collective-permute-start.4 = (bf16[2,512,512]{2,1,0:T(8,128)(2,1)}, bf16[2,512,512]{2,1,0:T(8,128)(2,1)}, u32[]{:S(2)}, u32[]{:S(2)}) collective-permute-start(bf16[2,512,512]{2,1,0:T(8,128)(2,1)} %get-tuple-element.209), channel_id=1, source_target_pairs={{0,16},{8,24},{16,0},{24,8},{1,17},{9,25},{17,1},{25,9},{2,18},{10... | collective-permute-start | bytes 3145736 | tf_op jit(solution)/shard_map/ppermute | solution.py:1339
  423.8 86.9 %collective-permute-start.5 = (bf16[2,512,512]{2,1,0:T(8,128)(2,1)}, bf16[2,512,512]{2,1,0:T(8,128)(2,1)}, u32[]{:S(2)}, u32[]{:S(2)}) collective-permute-start(bf16[2,512,512]{2,1,0:T(8,128)(2,1)} %get-tuple-element.210), channel_id=1, source_target_pairs={{0,8},{8,0},{16,24},{24,16},{1,9},{9,1},{17,25},{25,17},{2,10},{10... | collective-permute-start | bytes 3145736 | tf_op jit(solution)/shard_map/ppermute | solution.py:1339
  424.2 102.4 %copy-start.5 = (bf16[128,2048]{1,0:T(8,128)(2,1)S(1)}, bf16[128,2048]{1,0:T(8,128)(2,1)}, u32[]{:S(2)}) copy-start(bf16[128,2048]{1,0:T(8,128)(2,1)} %param.19) | copy-start | bytes 1572868
  510.7 74.9 %collective-permute-start.6 = (bf16[1,512,512]{2,1,0:T(8,128)(2,1)}, bf16[1,512,512]{2,1,0:T(8,128)(2,1)}, u32[]{:S(2)}, u32[]{:S(2)}) collective-permute-start(bf16[1,512,512]{2,1,0:T(8,128)(2,1)} %get-tuple-element.220), channel_id=1, source_target_pairs={{0,24},{8,16},{16,8},{24,0},{1,25},{9,17},{17,9},{25,1},{2,26},{10... | collective-permute-start | bytes 1572872 | tf_op jit(solution)/shard_map/ppermute | solution.py:1339
  526.1 59.5 %collective-permute-start.7 = (bf16[1,512,512]{2,1,0:T(8,128)(2,1)}, bf16[1,512,512]{2,1,0:T(8,128)(2,1)}, u32[]{:S(2)}, u32[]{:S(2)}) collective-permute-start(bf16[1,512,512]{2,1,0:T(8,128)(2,1)} %get-tuple-element.221), channel_id=1, source_target_pairs={{0,16},{8,24},{16,0},{24,8},{1,17},{9,25},{17,1},{25,9},{2,18},{10... | collective-permute-start | bytes 1572872 | tf_op jit(solution)/shard_map/ppermute | solution.py:1339
  526.1 59.5 %collective-permute-start.8 = (bf16[1,512,512]{2,1,0:T(8,128)(2,1)}, bf16[1,512,512]{2,1,0:T(8,128)(2,1)}, u32[]{:S(2)}, u32[]{:S(2)}) collective-permute-start(bf16[1,512,512]{2,1,0:T(8,128)(2,1)} %get-tuple-element.222), channel_id=1, source_target_pairs={{0,8},{8,0},{16,24},{24,16},{1,9},{9,1},{17,25},{25,17},{2,10},{10... | collective-permute-start | bytes 1572872 | tf_op jit(solution)/shard_map/ppermute | solution.py:1339
  710.2 337.9 %collective-permute-start.10 = (bf16[2,512,512]{2,1,0:T(8,128)(2,1)}, bf16[2,512,512]{2,1,0:T(8,128)(2,1)}, u32[]{:S(2)}, u32[]{:S(2)}) collective-permute-start(bf16[2,512,512]{2,1,0:T(8,128)(2,1)} %get-tuple-element.258), channel_id=1, source_target_pairs={{0,16},{8,24},{16,0},{24,8},{1,17},{9,25},{17,1},{25,9},{2,18},{10... | collective-permute-start | bytes 3145736 | tf_op jit(solution)/shard_map/ppermute | solution.py:1339
  710.3 337.9 %collective-permute-start.11 = (bf16[2,512,512]{2,1,0:T(8,128)(2,1)}, bf16[2,512,512]{2,1,0:T(8,128)(2,1)}, u32[]{:S(2)}, u32[]{:S(2)}) collective-permute-start(bf16[2,512,512]{2,1,0:T(8,128)(2,1)} %get-tuple-element.259), channel_id=1, source_target_pairs={{0,8},{8,0},{16,24},{24,16},{1,9},{9,1},{17,25},{25,17},{2,10},{10... | collective-permute-start | bytes 3145736 | tf_op jit(solution)/shard_map/ppermute | solution.py:1339
  711.9 336.3 %collective-permute-start.9 = (bf16[2,512,512]{2,1,0:T(8,128)(2,1)}, bf16[2,512,512]{2,1,0:T(8,128)(2,1)}, u32[]{:S(2)}, u32[]{:S(2)}) collective-permute-start(bf16[2,512,512]{2,1,0:T(8,128)(2,1)} %get-tuple-element.257), channel_id=1, source_target_pairs={{0,24},{8,16},{16,8},{24,0},{1,25},{9,17},{17,9},{25,1},{2,26},{10... | collective-permute-start | bytes 3145736 | tf_op jit(solution)/shard_map/ppermute | solution.py:1339
  720.4 3.7 copy-start
  720.4 3.8 copy-start.22
  720.4 3.8 copy-start.24
  720.5 3.8 copy-start.26
  732.7 9.7 copy-start.7
  732.7 9.7 copy-start.9
  776.4 20.8 %copy-start.20 = (f32[1,2048]{1,0:T(1,128)S(1)}, f32[1,2048]{1,0:T(1,128)}, u32[]{:S(2)}) copy-start(f32[1,2048]{1,0:T(1,128)} %get-tuple-element.91) | copy-start | bytes 24580 | tf_op jit(solution)/shard_map/cond
  776.4 20.9 %copy-start.19 = (f32[1,2048]{1,0:T(1,128)S(1)}, f32[1,2048]{1,0:T(1,128)}, u32[]{:S(2)}) copy-start(f32[1,2048]{1,0:T(1,128)} %get-tuple-element.92) | copy-start | bytes 24580 | tf_op jit(solution)/shard_map/cond
  776.4 24.0 %copy-start.3 = (bf16[128,2048]{1,0:T(8,128)(2,1)S(1)}, bf16[128,2048]{1,0:T(8,128)(2,1)}, u32[]{:S(2)}) copy-start(bf16[128,2048]{1,0:T(8,128)(2,1)} %get-tuple-element.90) | copy-start | bytes 1572868 | tf_op jit(solution)/shard_map/cond
  1038.6 8.7 copy-start.13
  1048.2 5.8 copy-start.17
  1048.2 6.6 copy-start.16
  1048.2 7.4 copy-start.15
  1048.2 8.2 copy-start.14
  1048.2 9.0 copy-start.18

commit v17 on v16

--- a/solution.py
+++ b/solution.py
@@ -1145,10 +1145,10 @@
             part = dot(lefts[i][...], weight_ref[0], (1, 1))
             if i:
                 part = part + out_ref[...]
-            out_ref[...] = part
-
-
-def through(lefts, weights, first):
+            out_ref[...] = part.astype(out_ref.dtype)
+
+
+def through(lefts, weights, first, kind=jnp.float32):
     count, (rows, depth) = len(lefts), lefts[0].shape
     piece = 512
     return pl.pallas_call(
@@ -1159,7 +1159,7 @@
             pl.BlockSpec((1, piece, depth), lambda c, i: (i + first, c, 0)),
         ],
         out_specs=pl.BlockSpec((rows, piece), lambda c, i: (0, c)),
-        out_shape=jax.ShapeDtypeStruct((rows, depth), jnp.float32),
+        out_shape=jax.ShapeDtypeStruct((rows, depth), kind),
         compiler_params=pltpu.CompilerParams(vmem_limit_bytes=BIG),
     )(*lefts, weights)
 
@@ -1393,7 +1393,8 @@
     hits_all = extras_all[:, :experts_all]
     router_weight = small_all[:, :experts_all]
     gains = small_all[:, experts_all : experts_all + 4].astype(jnp.float32)
-    attn_gain, query_gain, key_gain, mlp_gain = (gains[:, i] for i in range(4))
+    gains = lax.optimization_barrier(jnp.transpose(gains))
+    attn_gain, query_gain, key_gain, mlp_gain = (gains[i] for i in range(4))
     inputs = tokens.astype(jnp.float32)
     segment, position, places = layout(lengths[0], count)
     half = HD // 2
@@ -1586,7 +1587,7 @@
         grad_middle_part, grad_mlp_gain = rms_backward(middle, mlp_inverse, mlp_gain, grad_mlp)
         grad_middle = grad_final + grad_middle_part
         grad_branch_low = grad_middle.astype(bf16)
-        grad_attended = through([grad_branch_low], weights_all, 3).astype(bf16)
+        grad_attended = through([grad_branch_low], weights_all, 3, bf16)
         grad_query_low, grad_key_low, grad_value_low, grad_query_gain, grad_key_gain = core_back(
             scale,
             query_low.reshape(count, D),

time: 1070 us -> 1070 us (level)
  no operation moved by 1% of the time
where the time goes in v17:
time: 1070 us; the launch traced here: 1050 us
  Pallas kernels  899 us (84%)
  local copies, waits for them, and re-layouts  44 us (4%)
  starting transfers between devices  29.3 us (3%)
  waiting for transfers between devices  28.6 us (3%)
  matrix products  27 us (3%)
  other arithmetic  23.8 us (2%)
    pallas_call x2, Pallas kernels, scatter_call(): pl.pallas_call(functools.partial(scatter_kernel, n_dp, n_expert, count, i...  361 us
    pallas_call x2, Pallas kernels, gather_call(): pl.pallas_call(functools.partial(gather_kernel, n_dp, n_expert, n, places...  357 us
    pallas_call x2, Pallas kernels, expert_call(): pl.pallas_call(functools.partial(expert_kernel, steps, half, len(weights)...  88.6 us
    ppermute x12, starting transfers between devices, permuted(): got.append(lax.ppermute(piece, 'dp', paths))  29.3 us
    ppermute x12, waiting for transfers between devices, permuted(): got.append(lax.ppermute(piece, 'dp', paths))  28.6 us
    dot_general x9, matrix products, product(): return jnp.einsum(form, left, right, preferred_element_type=jnp.float32)  25.5 us
    pallas_call x2, Pallas kernels, through(): pl.pallas_call(functools.partial(through_kernel, count), grid=(depth // p...  24.3 us
    pallas_call x1, Pallas kernels, place_back(): pl.pallas_call(functools.partial(place_back_kernel, number), grid=(pairs,...  23.5 us
  transfers between devices with their start and end apart: 12, of which 1 were waited for; matrix products, arithmetic and copies ran while one was open for 8% of the time, Pallas kernels for 39%

profile of v17, /device:TPU:0, one launch (start us, length us, event | category | flops | bytes accessed | tf_op | source)
XLA Modules:
  0.0 1053.1 jit_solution(12367814501086860757)
XLA Ops:
  0.6 0.8 copy.97
  4.8 0.8 concatenate.24
  6.2 2.3 pad_maximum_fusion.2.refs_0_
  8.5 167.3 %shard_map.272 = (bf16[4,2048,2048]{2,1,0:T(8,128)(2,1)}, bf16[4096,256]{1,0:T(8,128)(2,1)}, bf16[8,2048,256]{2,1,0:T(8,128)(2,1)}, bf16[8,2048,256]{2,1,0:T(8,1...) custom-call(bf16[4,64,2048]{2,1,0:T(8,128)(2,1)} %pad_maximum_fusion, ...), custom_call_target="tpu_custom_call" | custom-call | tf_op jit(solution)/shard_map/pallas_call | solution.py:330
  176.0 4.3 collective-permute-start.2
  180.3 1.3 slice.78
  181.8 3.7 slice_reduce_fusion
  185.9 4.9 multiply_reduce_fusion.7
  190.8 5.1 multiply_reduce_fusion.6
  196.0 5.8 fusion.21
  201.8 2.3 slice.92
  204.6 1.3 fusion.44
  206.1 1.6 fusion.45
  208.1 2.0 copy.121
  210.4 3.2 multiply_subtract_fusion
  214.3 1.5 fusion.46
  215.8 1.3 broadcast_divide_fusion.1
  217.1 1.7 convolution_convert_fusion.1
  218.9 0.8 copy-done.11
  219.7 5.0 multiply_reduce_fusion.5
  224.7 1.6 constant_dynamic-slice_fusion
  228.4 0.9 pad.18.refs_7_
  229.5 190.0 %shard_map.273 = (bf16[4096,2048]{1,0:T(8,128)(2,1)}, bf16[4096,2048]{1,0:T(8,128)(2,1)}, bf16[8,2048,256]{2,1,0:T(8,128)(2,1)}, bf16[8,2048,256]{2,1,0:T(8,128)...) custom-call(bf16[128,2048]{1,0:T(8,128)(2,1)S(1)} %multiply_convert_, ...), custom_call_target="tpu_custom_call", output_to_operand_aliasing={{2}: (4, {}), {3}: (5, {})} | custom-call | tf_op jit(solution)/shard_map/pallas_call | solution.py:330
  419.5 1.6 collective-permute-start.3
  421.0 2.4 collective-permute-start.4
  423.9 55.2 %shard_map.274 = (bf16[8,768,2048]{2,1,0:T(8,128)(2,1)}, bf16[8,768,2048]{2,1,0:T(8,128)(2,1)}, bf16[8,768,128]{2,1,0:T(8,128)(2,1)}, bf16[6,2048,256]{2,1,0:T(8...) custom-call(s32[1]{0:T(128)} %bitcast.49.names_ref, ...), custom_call_target="tpu_custom_call" | custom-call | tf_op jit(solution)/shard_map/pallas_call | solution.py:1008
  479.2 2.7 dynamic-slice_bitcast_fusion
  481.9 28.5 %collective-permute-done.4.refs_2_ = bf16[2,512,512]{2,1,0:T(8,128)(2,1)} collective-permute-done((bf16[2,512,512]{2,1,0:T(8,128)(2,1)}, bf16[2,512,512]{2,1,0:T(8,128)(2,1)}, u32[]{:S(2)}, u32[]{:S(2)}) %collective-permute-start.4) | collective-permute-done | bytes 1048608 | tf_op jit(solution)/shard_map/ppermute | solution.py:1339
  510.4 15.4 %collective-permute-start.6 = (bf16[1,512,512]{2,1,0:T(8,128)(2,1)}, bf16[1,512,512]{2,1,0:T(8,128)(2,1)}, u32[]{:S(2)}, u32[]{:S(2)}) collective-permute-start(bf16[1,512,512]{2,1,0:T(8,128)(2,1)} %get-tuple-element.220), channel_id=1, source_target_pairs={{0,24},{8,16},{16,8},{24,0},{1,25},{9,17},{17,9},{25,1},{2,26},{10... | collective-permute-start | bytes 1572872 | tf_op jit(solution)/shard_map/ppermute | solution.py:1339
  526.4 1.1 convert_element_type.90
  528.4 33.4 %shard_map.275 = (bf16[8,768,2048]{2,1,0:T(8,128)(2,1)}, bf16[8,768,2048]{2,1,0:T(8,128)(2,1)}, bf16[8,768,128]{2,1,0:T(8,128)(2,1)}, bf16[2,2048,256]{2,1,0:T(8...) custom-call(s32[5]{0:T(128)} %stack.71.names_ref, ...), custom_call_target="tpu_custom_call", output_to_operand_aliasing={{0}: (9, {}), {1}: (10, {}), {2}: (11, {}), {5}: (12, {})} | custom-call | tf_op jit(solution)/shard_map/pallas_call | solution.py:1008
  561.8 23.5 %shard_map.276 = bf16[4096,2176]{1,0:T(8,128)(2,1)} custom-call(s32[16,8,256]{2,1,0:T(8,128)} %select_bitcast_fusion.refs_6_.slots_ref.refs_3_, bf16[8,768,2048]{2,1,0:T(8,128)(2,1)} %get-tuple-element.217.dx_ref, bf16[8,768,128]{2,1,0:T(8,128)(2,1)} %get-tuple-element.218.probs_ref), custom_call_target="tpu_custom_call" | custom-call | tf_op jit(solution)/shard_map/pallas_call | solution.py:1058
  585.3 124.7 %shard_map.277 = (f32[128,2176]{1,0:T(8,128)}, bf16[8,512,1024]{2,1,0:T(8,128)(2,1)}, bf16[8,512,1024]{2,1,0:T(8,128)(2,1)}, bf16[4096,2048]{1,0:T(8,128)(2,1)},...) custom-call(bf16[4,8,128,2176]{3,2,1,0:T(8,128)(2,1)} %bitcast.137, ...), custom_call_target="tpu_custom_call" | custom-call | tf_op jit(solution)/shard_map/pallas_call | solution.py:683
  710.1 1.4 collective-permute-start.11
  711.4 3.0 collective-permute-start.9
  715.1 5.1 shard_map.278
  720.2 3.7 shard_map.279
  724.0 73.6 %conditional.1 = (f32[128,2048]{1,0:T(8,128)}, bf16[4,8,64,2048]{3,2,1,0:T(8,128)(2,1)}, bf16[4,8,64,2048]{3,2,1,0:T(8,128)(2,1)}, bf16[4,8,64,2048]{3,2,1,0:T(8...) conditional(s32[]{:T(128)} %bitcast.60, () %tuple.38, ...), branch_computations={%region_12.13_spmd, %region_13.19_spmd} | conditional | flops 108151040 | bytes 35258440 | solution.py:1632
  724.3 1.1 multiply_reduce_fusion.4
  725.4 1.0 multiply_convert_fusion
  726.5 1.6 copy.110
  728.0 1.8 multiply_reduce_fusion
  729.8 2.6 fusion.43
  732.4 6.8 branch_1_fun.4.grad_ref
  739.9 1.1 copy_bitcast_fusion
  741.1 2.7 copy.113.probs_ref
  745.2 2.1 copy.114.q_gain_ref
  747.4 2.1 copy.115.k_gain_ref
  749.5 8.6 branch_1_fun.5
  758.1 1.0 copy.117.refs_0_
  759.2 13.8 %branch_1_fun.7 = (bf16[2048,2048]{1,0:T(8,128)(2,1)}, bf16[2048,2048]{1,0:T(8,128)(2,1)}, bf16[2048,2048]{1,0:T(8,128)(2,1)}, bf16[2048,2048]{1,0:T(8,128)(2,1)}) custom-call(bf16[128,2048]{1,0:T(8,128)(2,1)} %copy.117.refs_0_, bf16[128,2048]{1,0:T(8,128)(2,1)} %get-tuple-element.85.refs_1_, bf16[128,2048]{1,0:T(8,128)(2,1)} %get-tuple-element.375.refs_0_.refs_2_, ...), custom_call_target="tpu_custom_call" | custom-call | tf_op jit(solution)/shard_map/cond/branch_1_fun/pallas_call | solution.py:1180
  773.0 17.5 %branch_1_fun.6 = f32[128,2048]{1,0:T(8,128)} custom-call(bf16[128,2048]{1,0:T(8,128)(2,1)} %get-tuple-element.79.refs_0_.refs_5_, bf16[128,2048]{1,0:T(8,128)(2,1)} %get-tuple-element.80.refs_1_.refs_4_, bf16[128,2048]{1,0:T(8,128)(2,1)} %get-tuple-element.81.refs_2_.refs_3_, bf16[4,2048,2048]{2,1,0:T(8,128)(2,1)} %get-tuple-element.69.refs_1_.refs_3_), custom_call_target="tpu_custom_call" | custom-call | tf_op jit(solution)/shard_map/cond/branch_1_fun/pallas_call | solution.py:1154
  790.6 1.6 copy.116
  792.1 1.5 multiply_reduce_fusion.1
  794.2 2.8 subtract_add_fusion
  797.6 235.9 %shard_map.280 = (f32[128,2048]{1,0:T(8,128)}, f32[64,2048]{1,0:T(8,128)}, f32[64,2048]{1,0:T(8,128)}, f32[64,2048]{1,0:T(8,128)}, f32[64,2048]{1,0:T(8,128)}, /...) custom-call(bf16[4,8,128,2048]{3,2,1,0:T(8,128)(2,1)} %bitcast.138, ...), custom_call_target="tpu_custom_call" | custom-call | tf_op jit(solution)/shard_map/pallas_call | solution.py:683
  1033.5 7.3 shard_map.281
  1040.8 1.3 slice_bitcast_fusion
  1042.1 0.9 add_convert_fusion
  1043.1 5.8 shard_map.282
  1048.9 0.8 copy.174
  1049.7 0.8 copy.175
  1050.5 0.8 copy.176
  1051.3 0.8 copy.177
  (133 shorter events, 15.7 us)
Async XLA Ops:
  175.8 9.7 copy-start.4
  175.8 53.7 %collective-permute-start = (bf16[1,512,512]{2,1,0:T(8,128)(2,1)}, bf16[1,512,512]{2,1,0:T(8,128)(2,1)}, u32[]{:S(2)}, u32[]{:S(2)}) collective-permute-start(bf16[1,512,512]{2,1,0:T(8,128)(2,1)} %get-tuple-element.194), channel_id=1, source_target_pairs={{0,24},{8,16},{16,8},{24,0},{1,25},{9,17},{17,9},{25,1},{2,26},{10... | collective-permute-start | bytes 1572872 | tf_op jit(solution)/shard_map/ppermute | solution.py:1339
  175.9 53.6 %collective-permute-start.1 = (bf16[1,512,512]{2,1,0:T(8,128)(2,1)}, bf16[1,512,512]{2,1,0:T(8,128)(2,1)}, u32[]{:S(2)}, u32[]{:S(2)}) collective-permute-start(bf16[1,512,512]{2,1,0:T(8,128)(2,1)} %get-tuple-element.195), channel_id=1, source_target_pairs={{0,16},{8,24},{16,0},{24,8},{1,17},{9,25},{17,1},{25,9},{2,18},{10... | collective-permute-start | bytes 1572872 | tf_op jit(solution)/shard_map/ppermute | solution.py:1339
  176.0 53.5 %collective-permute-start.2 = (bf16[1,512,512]{2,1,0:T(8,128)(2,1)}, bf16[1,512,512]{2,1,0:T(8,128)(2,1)}, u32[]{:S(2)}, u32[]{:S(2)}) collective-permute-start(bf16[1,512,512]{2,1,0:T(8,128)(2,1)} %get-tuple-element.196), channel_id=1, source_target_pairs={{0,8},{8,0},{16,24},{24,16},{1,9},{9,1},{17,25},{25,17},{2,10},{10... | collective-permute-start | bytes 1572872 | tf_op jit(solution)/shard_map/ppermute | solution.py:1339
  185.7 10.2 copy-start.22
  185.9 10.1 copy-start.13
  190.8 13.3 %copy-start.5 = (f32[128,2048]{1,0:T(8,128)}, f32[128,2048]{1,0:T(8,128)S(1)}, u32[]{:S(2)}) copy-start(f32[128,2048]{1,0:T(8,128)S(1)} %get-tuple-element.411) | copy-start | bytes 3145732
  195.9 8.4 copy-start.6
  204.1 3.7 copy-start.24
  204.1 3.6 copy-start.26
  204.1 3.6 copy-start.28
  214.0 10.7 %copy-start.7 = (bf16[128,16,128]{2,0,1:T(8,128)(2,1)}, bf16[128,16,128]{2,0,1:T(8,128)(2,1)S(1)}, u32[]{:S(2)}) copy-start(bf16[128,16,128]{2,0,1:T(8,128)(2,1)S(1)} %maximum_convert_fusion.1) | copy-start | bytes 1572868
  214.3 10.4 copy-start.9
  217.1 1.7 copy-start.1
  218.9 0.8 copy-start.11
  229.5 298.6 %copy-start.2 = (bf16[128,2048]{1,0:T(8,128)(2,1)}, bf16[128,2048]{1,0:T(8,128)(2,1)S(1)}, u32[]{:S(2)}) copy-start(bf16[128,2048]{1,0:T(8,128)(2,1)S(1)} %multiply_convert_fusion.1.refs_0_) | copy-start | bytes 1572868
  419.5 62.4 %collective-permute-start.3 = (bf16[2,512,512]{2,1,0:T(8,128)(2,1)}, bf16[2,512,512]{2,1,0:T(8,128)(2,1)}, u32[]{:S(2)}, u32[]{:S(2)}) collective-permute-start(bf16[2,512,512]{2,1,0:T(8,128)(2,1)} %get-tuple-element.208), channel_id=1, source_target_pairs={{0,24},{8,16},{16,8},{24,0},{1,25},{9,17},{17,9},{25,1},{2,26},{10... | collective-permute-start | bytes 3145736 | tf_op jit(solution)/shard_map/ppermute | solution.py:1339
  421.0 89.4 %collective-permute-start.4 = (bf16[2,512,512]{2,1,0:T(8,128)(2,1)}, bf16[2,512,512]{2,1,0:T(8,128)(2,1)}, u32[]{:S(2)}, u32[]{:S(2)}) collective-permute-start(bf16[2,512,512]{2,1,0:T(8,128)(2,1)} %get-tuple-element.209), channel_id=1, source_target_pairs={{0,16},{8,24},{16,0},{24,8},{1,17},{9,25},{17,1},{25,9},{2,18},{10... | collective-permute-start | bytes 3145736 | tf_op jit(solution)/shard_map/ppermute | solution.py:1339
  423.5 87.0 %collective-permute-start.5 = (bf16[2,512,512]{2,1,0:T(8,128)(2,1)}, bf16[2,512,512]{2,1,0:T(8,128)(2,1)}, u32[]{:S(2)}, u32[]{:S(2)}) collective-permute-start(bf16[2,512,512]{2,1,0:T(8,128)(2,1)} %get-tuple-element.210), channel_id=1, source_target_pairs={{0,8},{8,0},{16,24},{24,16},{1,9},{9,1},{17,25},{25,17},{2,10},{10... | collective-permute-start | bytes 3145736 | tf_op jit(solution)/shard_map/ppermute | solution.py:1339
  510.4 74.9 %collective-permute-start.6 = (bf16[1,512,512]{2,1,0:T(8,128)(2,1)}, bf16[1,512,512]{2,1,0:T(8,128)(2,1)}, u32[]{:S(2)}, u32[]{:S(2)}) collective-permute-start(bf16[1,512,512]{2,1,0:T(8,128)(2,1)} %get-tuple-element.220), channel_id=1, source_target_pairs={{0,24},{8,16},{16,8},{24,0},{1,25},{9,17},{17,9},{25,1},{2,26},{10... | collective-permute-start | bytes 1572872 | tf_op jit(solution)/shard_map/ppermute | solution.py:1339
  525.8 59.5 %collective-permute-start.7 = (bf16[1,512,512]{2,1,0:T(8,128)(2,1)}, bf16[1,512,512]{2,1,0:T(8,128)(2,1)}, u32[]{:S(2)}, u32[]{:S(2)}) collective-permute-start(bf16[1,512,512]{2,1,0:T(8,128)(2,1)} %get-tuple-element.221), channel_id=1, source_target_pairs={{0,16},{8,24},{16,0},{24,8},{1,17},{9,25},{17,1},{25,9},{2,18},{10... | collective-permute-start | bytes 1572872 | tf_op jit(solution)/shard_map/ppermute | solution.py:1339
  525.8 59.5 %collective-permute-start.8 = (bf16[1,512,512]{2,1,0:T(8,128)(2,1)S(1)}, bf16[1,512,512]{2,1,0:T(8,128)(2,1)}, u32[]{:S(2)}, u32[]{:S(2)}) collective-permute-start(bf16[1,512,512]{2,1,0:T(8,128)(2,1)S(1)} %get-tuple-element.222), channel_id=1, source_target_pairs={{0,8},{8,0},{16,24},{24,16},{1,9},{9,1},{17,25},{25,17},{2,10},{10... | collective-permute-start | bytes 1572872 | tf_op jit(solution)/shard_map/ppermute | solution.py:1339
  710.0 333.1 %collective-permute-start.10 = (bf16[2,512,512]{2,1,0:T(8,128)(2,1)}, bf16[2,512,512]{2,1,0:T(8,128)(2,1)}, u32[]{:S(2)}, u32[]{:S(2)}) collective-permute-start(bf16[2,512,512]{2,1,0:T(8,128)(2,1)} %get-tuple-element.258), channel_id=1, source_target_pairs={{0,16},{8,24},{16,0},{24,8},{1,17},{9,25},{17,1},{25,9},{2,18},{10... | collective-permute-start | bytes 3145736 | tf_op jit(solution)/shard_map/ppermute | solution.py:1339
  710.1 333.0 %collective-permute-start.11 = (bf16[2,512,512]{2,1,0:T(8,128)(2,1)}, bf16[2,512,512]{2,1,0:T(8,128)(2,1)}, u32[]{:S(2)}, u32[]{:S(2)}) collective-permute-start(bf16[2,512,512]{2,1,0:T(8,128)(2,1)} %get-tuple-element.259), channel_id=1, source_target_pairs={{0,8},{8,0},{16,24},{24,16},{1,9},{9,1},{17,25},{25,17},{2,10},{10... | collective-permute-start | bytes 3145736 | tf_op jit(solution)/shard_map/ppermute | solution.py:1339
  711.4 331.6 %collective-permute-start.9 = (bf16[2,512,512]{2,1,0:T(8,128)(2,1)}, bf16[2,512,512]{2,1,0:T(8,128)(2,1)}, u32[]{:S(2)}, u32[]{:S(2)}) collective-permute-start(bf16[2,512,512]{2,1,0:T(8,128)(2,1)} %get-tuple-element.257), channel_id=1, source_target_pairs={{0,24},{8,16},{16,8},{24,0},{1,25},{9,17},{17,9},{25,1},{2,26},{10... | collective-permute-start | bytes 3145736 | tf_op jit(solution)/shard_map/ppermute | solution.py:1339
  720.1 3.8 copy-start
  720.1 3.8 copy-start.3
  720.1 3.8 copy-start.23
  720.1 3.8 copy-start.25
  720.2 3.8 copy-start.27
  732.4 7.5 copy-start.8
  732.4 7.5 copy-start.10
  741.1 17.1 %copy-start.12 = (bf16[128,2048]{0,1:T(8,128)(2,1)S(1)}, bf16[128,2048]{0,1:T(8,128)(2,1)}, u32[]{:S(2)}) copy-start(bf16[128,2048]{0,1:T(8,128)(2,1)} %get-tuple-element.359) | copy-start | bytes 1572868 | tf_op jit(solution)/shard_map/cond
  773.0 20.7 %copy-start.21 = (f32[1,2048]{1,0:T(1,128)S(1)}, f32[1,2048]{1,0:T(1,128)}, u32[]{:S(2)}) copy-start(f32[1,2048]{1,0:T(1,128)} %get-tuple-element.91) | copy-start | bytes 24580 | tf_op jit(solution)/shard_map/cond
  773.0 20.8 %copy-start.20 = (f32[1,2048]{1,0:T(1,128)S(1)}, f32[1,2048]{1,0:T(1,128)}, u32[]{:S(2)}) copy-start(f32[1,2048]{1,0:T(1,128)} %get-tuple-element.92) | copy-start | bytes 24580 | tf_op jit(solution)/shard_map/cond
  1033.5 8.7 copy-start.14
  1043.1 5.8 copy-start.18
  1043.1 6.6 copy-start.17
  1043.1 7.4 copy-start.16
  1043.1 8.2 copy-start.15
  1043.1 9.0 copy-start.19
